TPU v7x, 32 devices: a whole 2x2x4 slice. The times are simulated.
32 devices in a mesh: batch: 16 (over z, x, core), mp: 2 (over y).
Axes of the slice: x: 2, y: 2, z: 4, core: 2. Of those that a mesh axis runs over, the one named last changes fastest.
Arguments:
- inputs: float32 [32, 2048, 512], P(('batch', 'mp')), may hold values from -6 to 6
- cotangent: float32 [32, 2048, 512], P(('batch', 'mp')), may hold values from -6 to 6
- block_perm: int32 [32, 64], P(('batch', 'mp')), may hold values from 0 to 63, each once within a row
- block_mask: int32 [32, 64], P(('batch', 'mp')), may hold values from 0 to 1, as said below
- pen_weight: float32 [1], replicated, may hold values from 131072 to 262144
- w_query: float32 [512, 512], replicated, may hold values from -0.25 to 0.25
- w_key: float32 [512, 512], replicated, may hold values from -0.25 to 0.25
- w_value: float32 [512, 512], replicated, may hold values from -0.25 to 0.25
- w_out: float32 [512, 512], replicated, may hold values from -1 to 1
- w_sort: float32 [512, 512], replicated, may hold values from -0.0625 to 0.0625
- gain_one: float32 [512], replicated, may hold values from 0.5 to 1.5
- gain_two: float32 [512], replicated, may hold values from 0.5 to 1.5
- w_up: float32 [512, 2048], P(None, 'mp'), may hold values from -0.25 to 0.25
- w_down: float32 [2048, 512], P('mp'), may hold values from -0.125 to 0.125
Outputs:
- output: float32 [32, 2048, 512], P(('batch', 'mp'))
- penalty: float32 [1], replicated
- grad_input: float32 [32, 2048, 512], P(('batch', 'mp'))
- grad_query: float32 [512, 512], replicated
- grad_key: float32 [512, 512], replicated
- grad_value: float32 [512, 512], replicated
- grad_out: float32 [512, 512], replicated
- grad_sort: float32 [512, 512], replicated
- grad_gain_one: float32 [512], replicated
- grad_gain_two: float32 [512], replicated
- grad_up: float32 [512, 2048], P(None, 'mp')
- grad_down: float32 [2048, 512], P('mp')
Inputs may be any that keep to these rules, and one draw needn't show every extreme that they name: `block_mask`: block 0 of every sequence is real.
All inputs are finite; a program needn't handle non-finite values.
Results may differ from a plain program's by a relative error of at most 0.015.
Values may be sent and summed in bfloat16 or wider, within the bound.
No kernel may reach another device: no remote copies, remote signals or barrier semaphores. Data moves between devices by JAX's collectives and lax.ppermute only.
A program may use at most 384 MiB of HBM per device.

v0:
```python
import jax
import jax.numpy as jnp
from jax import lax
from jax.sharding import PartitionSpec as P

HEADS = 8
HEAD_DIM = 64
BLOCK = 32
ITERS = 8


EPSILON = 1e-05
HIGHEST = lax.Precision.HIGHEST


def norm_forward(values, gain):
    center = values - jnp.mean(values, axis=-1, keepdims=True)
    inverse = lax.rsqrt(jnp.mean(center * center, axis=-1, keepdims=True) + EPSILON)
    unit_rows = center * inverse
    return (unit_rows * gain, unit_rows, inverse)


def norm_input_grad(grad_rows, unit_rows, inverse, gain):
    scaled_rows = grad_rows * gain
    return inverse * (
        scaled_rows
        - jnp.mean(scaled_rows, axis=-1, keepdims=True)
        - unit_rows * jnp.mean(scaled_rows * unit_rows, axis=-1, keepdims=True)
    )


def balancing_states(sorting_logits):
    saved_states = [sorting_logits]
    for iteration in range(ITERS):
        sorting_logits = sorting_logits - jax.scipy.special.logsumexp(
            sorting_logits, axis=-1, keepdims=True
        )
        saved_states.append(sorting_logits)
        sorting_logits = sorting_logits - jax.scipy.special.logsumexp(
            sorting_logits, axis=-2, keepdims=True
        )
        saved_states.append(sorting_logits)
    return saved_states


def balance_plans_backward(saved_states, incoming_gradient):
    for level_index in range(2 * ITERS - 1, -1, -1):
        axis_used = -1 if level_index % 2 == 0 else -2
        share = jax.nn.softmax(saved_states[level_index], axis=axis_used)
        incoming_gradient = incoming_gradient - share * jnp.sum(
            incoming_gradient, axis=axis_used, keepdims=True
        )
    return incoming_gradient


def score_blocks(query, key_rows, key_partner, allowed):
    own_part = jnp.einsum("sithd,siuhd->sihtu", query, key_rows, preferred_element_type=jnp.float32)
    far_part = jnp.einsum(
        "sithd,siuhd->sihtu", query, key_partner, preferred_element_type=jnp.float32
    )
    scores = jnp.concatenate([own_part, far_part], axis=-1) * HEAD_DIM ** (-0.5)
    return jnp.where(allowed, scores, -1e30)


def local(
    inputs,
    cotangent,
    block_perm,
    block_mask,
    pen_weight,
    w_query,
    w_key,
    w_value,
    w_out,
    w_sort,
    gain_one,
    gain_two,
    w_up,
    w_down,
):
    seq_count, seq_len, model_width = inputs.shape
    block_count = seq_len // BLOCK
    row_count = seq_count * seq_len
    head_shape = (seq_count, block_count, BLOCK, HEADS, HEAD_DIM)
    factor = HEAD_DIM ** (-0.5)
    mask_float = block_mask.astype(jnp.float32)
    local_blocks = jnp.sum(mask_float)
    block_total = lax.psum(local_blocks, ("batch", "mp"))
    flat_in = inputs.reshape(row_count, model_width)
    normed_one, unit_one, inverse_one = norm_forward(flat_in, gain_one)
    act_one = normed_one.astype(jnp.bfloat16)
    joined_weights = jnp.concatenate([w_query, w_key, w_value], axis=1).astype(jnp.bfloat16)
    projected = jnp.dot(act_one, joined_weights, preferred_element_type=jnp.float32).astype(
        jnp.bfloat16
    )
    query = projected[:, :model_width].reshape(head_shape)
    key_rows = projected[:, model_width : 2 * model_width].reshape(head_shape)
    value_rows = projected[:, 2 * model_width :].reshape(head_shape)
    block_sums = jnp.sum(
        act_one.reshape(seq_count, block_count, BLOCK, model_width), axis=2, dtype=jnp.float32
    )
    sums_low = lax.optimization_barrier(block_sums.astype(jnp.bfloat16)).astype(jnp.float32)
    block_sorting_logits = jnp.einsum(
        "sid,de->sie", sums_low, w_sort, precision=HIGHEST, preferred_element_type=jnp.float32
    )
    block_sorting_logits = block_sorting_logits.reshape(
        seq_count, block_count, HEADS, block_count
    ).transpose(0, 2, 1, 3)
    saved_states = balancing_states(block_sorting_logits)
    plan_logarithm = saved_states[-1]
    plan = jnp.exp(plan_logarithm)
    row_real = mask_float[:, None, :, None]
    entropy_local = -jnp.sum(row_real * plan * plan_logarithm)
    positions = jnp.arange(block_count, dtype=jnp.int32)
    one_hot = block_perm[:, :, None] == positions[None, None, :]
    hot_float = one_hot.astype(jnp.float32)
    hot_low = one_hot.astype(jnp.bfloat16)
    chosen = block_count * jnp.sum(plan * hot_float[:, None], axis=-1)
    partner_real = jnp.sum(one_hot.astype(jnp.int32) * block_mask[:, None, :], axis=-1) > 0
    usable = partner_real & (block_perm < positions[None, :])
    key_partner = jnp.einsum(
        "sij,sjuhd->siuhd", hot_low, key_rows, preferred_element_type=jnp.float32
    ).astype(jnp.bfloat16)
    value_partner = jnp.einsum(
        "sij,sjuhd->siuhd", hot_low, value_rows, preferred_element_type=jnp.float32
    ).astype(jnp.bfloat16)
    chosen_rows = chosen.transpose(0, 2, 1)[:, :, None, :, None]
    scaled = (value_partner * chosen_rows).astype(jnp.bfloat16)
    lower_part = jnp.arange(BLOCK)[:, None] >= jnp.arange(BLOCK)[None, :]
    frame = (seq_count, block_count, 1, BLOCK, BLOCK)
    allowed = jnp.concatenate(
        [
            jnp.broadcast_to(lower_part, frame),
            jnp.broadcast_to(usable[:, :, None, None, None], frame),
        ],
        axis=-1,
    )
    scores = score_blocks(query, key_rows, key_partner, allowed)
    log_total = jax.scipy.special.logsumexp(scores, axis=-1, keepdims=True)
    probs_low = jnp.exp(scores - log_total).astype(jnp.bfloat16)
    attended = jnp.einsum(
        "sihtu,siuhd->sithd", probs_low[..., :BLOCK], value_rows, preferred_element_type=jnp.float32
    )
    attended = attended + jnp.einsum(
        "sihtu,siuhd->sithd", probs_low[..., BLOCK:], scaled, preferred_element_type=jnp.float32
    )
    att_low = attended.astype(jnp.bfloat16).reshape(row_count, model_width)
    out_low = w_out.astype(jnp.bfloat16)
    second = flat_in + jnp.dot(att_low, out_low, preferred_element_type=jnp.float32)
    normed_two, unit_two, inverse_two = norm_forward(second, gain_two)
    act_two = normed_two.astype(jnp.bfloat16)
    up_low = w_up.astype(jnp.bfloat16)
    down_low = w_down.astype(jnp.bfloat16)
    gathered = lax.all_gather(act_two, "mp", axis=0, tiled=True)
    up_rows = jnp.dot(gathered, up_low, preferred_element_type=jnp.float32)
    hidden_full, gelu_pull = jax.vjp(jax.nn.gelu, up_rows)
    hidden = hidden_full.astype(jnp.bfloat16)
    piece = hidden
    down = lax.psum_scatter(
        jnp.dot(piece, down_low, preferred_element_type=jnp.float32).astype(jnp.bfloat16),
        "mp",
        scatter_dimension=0,
        tiled=True,
    ).astype(jnp.float32)
    output = second + down
    cot_flat = cotangent.reshape(row_count, model_width)
    cot_low = cot_flat.astype(jnp.bfloat16)
    cot_all = lax.all_gather(cot_low, "mp", axis=0, tiled=True)
    grad_hidden = jnp.einsum("rd,fd->rf", cot_all, down_low, preferred_element_type=jnp.float32)
    grad_up_rows = gelu_pull(grad_hidden)[0].astype(jnp.bfloat16)
    part_down = jnp.einsum("rf,rd->fd", hidden, cot_all, preferred_element_type=jnp.float32)
    part_up = jnp.einsum("rd,rf->df", gathered, grad_up_rows, preferred_element_type=jnp.float32)
    piece = grad_up_rows
    grad_normed_two = lax.psum_scatter(
        jnp.einsum("rf,df->rd", piece, up_low, preferred_element_type=jnp.float32),
        "mp",
        scatter_dimension=0,
        tiled=True,
    )
    grad_up, grad_down = lax.psum((part_up, part_down), "batch")
    gain_two_part = jnp.sum(grad_normed_two * unit_two, axis=0)
    grad_second = cot_flat + norm_input_grad(grad_normed_two, unit_two, inverse_two, gain_two)
    second_low = grad_second.astype(jnp.bfloat16)
    out_part = jnp.einsum("rd,re->de", att_low, second_low, preferred_element_type=jnp.float32)
    grad_att = (
        jnp.einsum("re,de->rd", second_low, out_low, preferred_element_type=jnp.float32)
        .astype(jnp.bfloat16)
        .reshape(head_shape)
    )
    probs = jnp.exp(score_blocks(query, key_rows, key_partner, allowed) - log_total)
    grad_own = jnp.einsum(
        "sithd,siuhd->sihtu", grad_att, value_rows, preferred_element_type=jnp.float32
    )
    grad_far = jnp.einsum(
        "sithd,siuhd->sihtu", grad_att, scaled, preferred_element_type=jnp.float32
    )
    grad_probs = jnp.concatenate([grad_own, grad_far], axis=-1)
    value_own_grad = jnp.einsum(
        "sihtu,sithd->siuhd", probs_low[..., :BLOCK], grad_att, preferred_element_type=jnp.float32
    )
    far_grad = jnp.einsum(
        "sihtu,sithd->siuhd", probs_low[..., BLOCK:], grad_att, preferred_element_type=jnp.float32
    )
    grad_scores = (
        probs * (grad_probs - jnp.sum(probs * grad_probs, axis=-1, keepdims=True))
    ).astype(jnp.bfloat16)
    scores_own = grad_scores[..., :BLOCK]
    scores_far = grad_scores[..., BLOCK:]
    query_grad = (
        jnp.einsum("sihtu,siuhd->sithd", scores_own, key_rows, preferred_element_type=jnp.float32)
        + jnp.einsum(
            "sihtu,siuhd->sithd", scores_far, key_partner, preferred_element_type=jnp.float32
        )
    ) * factor
    key_own_grad = (
        jnp.einsum("sihtu,sithd->siuhd", scores_own, query, preferred_element_type=jnp.float32)
        * factor
    )
    key_far_grad = (
        jnp.einsum("sihtu,sithd->siuhd", scores_far, query, preferred_element_type=jnp.float32)
        * factor
    )
    grad_chosen = jnp.sum(far_grad * value_partner, axis=(2, 4)).transpose(0, 2, 1)
    key_grad = key_own_grad + jnp.einsum(
        "sij,siuhd->sjuhd",
        hot_float,
        key_far_grad,
        precision=HIGHEST,
        preferred_element_type=jnp.float32,
    )
    value_grad = value_own_grad + jnp.einsum(
        "sij,siuhd->sjuhd",
        hot_float,
        far_grad * chosen_rows,
        precision=HIGHEST,
        preferred_element_type=jnp.float32,
    )
    grad_joined = jnp.concatenate(
        [
            query_grad.reshape(row_count, model_width),
            key_grad.reshape(row_count, model_width),
            value_grad.reshape(row_count, model_width),
        ],
        axis=1,
    ).astype(jnp.bfloat16)
    joined_part = jnp.einsum("rd,re->de", act_one, grad_joined, preferred_element_type=jnp.float32)
    grad_act = jnp.einsum(
        "re,de->rd", grad_joined, joined_weights, preferred_element_type=jnp.float32
    )
    incoming_attention_gradient = block_count * grad_chosen[..., None] * hot_float[:, None] * plan
    incoming_penalty_gradient = -row_real * plan * (plan_logarithm + 1.0)
    block_shape = (seq_count, block_count, BLOCK, model_width)
    penalty_factor = pen_weight[0] / (HEADS * block_total)
    logits_gradient = balance_plans_backward(
        saved_states, incoming_attention_gradient + penalty_factor * incoming_penalty_gradient
    )
    logits_gradient = logits_gradient.transpose(0, 2, 1, 3).reshape(
        seq_count, block_count, HEADS * block_count
    )
    sort_part = jnp.einsum(
        "sid,sie->de",
        sums_low,
        logits_gradient,
        precision=HIGHEST,
        preferred_element_type=jnp.float32,
    )
    grad_sums = jnp.einsum(
        "sie,de->sid",
        logits_gradient,
        w_sort,
        precision=HIGHEST,
        preferred_element_type=jnp.float32,
    )
    grad_normed_one = (grad_act.reshape(block_shape) + grad_sums[:, :, None, :]).reshape(
        row_count, model_width
    )
    gain_one_part = jnp.sum(grad_normed_one * unit_one, axis=0)
    joined_sum, grad_out, grad_sort, grad_gain_one, grad_gain_two, entropy_total = lax.psum(
        (joined_part, out_part, sort_part, gain_one_part, gain_two_part, entropy_local),
        ("batch", "mp"),
    )
    grad_input = grad_second + norm_input_grad(grad_normed_one, unit_one, inverse_one, gain_one)
    penalty = (entropy_total / (HEADS * block_total)).reshape(1)
    grad_query = joined_sum[:, :model_width]
    grad_key = joined_sum[:, model_width : 2 * model_width]
    grad_value = joined_sum[:, 2 * model_width :]
    return (
        output.reshape(inputs.shape),
        penalty,
        grad_input.reshape(inputs.shape),
        grad_query,
        grad_key,
        grad_value,
        grad_out,
        grad_sort,
        grad_gain_one,
        grad_gain_two,
        grad_up,
        grad_down,
    )


def solution(mesh):
    return jax.shard_map(
        local,
        mesh=mesh,
        in_specs=(
            P(("batch", "mp"), None, None),
            P(("batch", "mp"), None, None),
            P(("batch", "mp"), None),
            P(("batch", "mp"), None),
            P(),
            P(),
            P(),
            P(),
            P(),
            P(),
            P(),
            P(),
            P(None, "mp"),
            P("mp", None),
        ),
        out_specs=(
            P(("batch", "mp"), None, None),
            P(),
            P(("batch", "mp"), None, None),
            P(),
            P(),
            P(),
            P(),
            P(),
            P(),
            P(),
            P(None, "mp"),
            P("mp", None),
        ),
        check_vma=False,
    )
```

profile of v0, /device:TPU:0, one launch (start us, length us, event | category | flops | bytes accessed | tf_op | source)
XLA Modules:
  0.0 947.4 jit_solution(7410261271224813287)
XLA Ops:
  66.0 7.8 fusion.59
  80.1 9.2 fusion.42
  89.3 11.7 %fusion.45 = f32[1,64,8,32,32]{4,3,2,1,0:T(8,128)} fusion(bf16[64,32,8,64]{3,0,2,1:T(8,128)(2,1)S(1)} %copy-done.22, bf16[64,32,8,64]{3,2,1,0:T(8,128)(2,1)S(1)} %copy-done.9), kind=kOutput, calls=%fused_computation.83 | convolution fusion | flops 67108864 | bytes 6291456 | tf_op jit(solution)/shard_map/sithd,siuhd->sihtu/dot_general | solution.py:58
  101.8 8.5 fusion.143
  127.5 8.1 fusion.7
  156.5 8.4 copy.116
  178.2 15.0 %fusion.72 = f32[4096,1024]{1,0:T(8,128)} fusion(bf16[4096,512]{0,1:T(8,128)(2,1)} %all-gather.5.cloned.1.call-done, f32[1024,512]{1,0:T(8,128)} %param.27), kind=kOutput, calls=%fused_computation.105 | convolution fusion | flops 4295491584 | bytes 23068672 | tf_op jit(solution)/shard_map/rd,fd->rf/dot_general | solution.py:169
  193.2 44.5 %all-gather.3.cloned.1.call-done = bf16[4096,512]{0,1:T(8,128)(2,1)} async-done(((bf16[2048,512]{0,1:T(8,128)(2,1)}), bf16[4096,512]{0,1:T(8,128)(2,1)}) %all-gather.3.cloned.1.call-update) | async-done | bytes 4194320 | tf_op jit(solution)/shard_map/all_gather | solution.py:154
  237.7 26.2 %fusion.6 = (bf16[4096,1024]{1,0:T(8,128)(2,1)}, bf16[4096,1024]{1,0:T(8,128)(2,1)}) fusion(f32[4096,1024]{1,0:T(8,128)} %fusion.72, bf16[4096,512]{0,1:T(8,128)(2,1)} %all-gather.3.cloned.1.call-done, f32[512,1024]{1,0:T(8,128)} %param.26), kind=kOutput, calls=%fused_computation.8 | convolution fusion | flops 4387766272 | bytes 39845888 | tf_op jit(solution)/shard_map/dot_general | solution.py:155
  263.9 10.2 %fusion.75 = f32[4096,512]{0,1:T(8,128)} fusion(bf16[4096,1024]{1,0:T(8,128)(2,1)} %get-tuple-element.107, f32[512,1024]{1,0:T(8,128)S(1)} %copy-done.130), kind=kOutput, calls=%fused_computation.108 | convolution fusion | flops 4295491584 | bytes 18874368 | tf_op jit(solution)/shard_map/rf,df->rd/dot_general | solution.py:175
  274.5 10.5 %convolution_convert_fusion.1 = bf16[4096,512]{0,1:T(8,128)(2,1)} fusion(bf16[4096,1024]{1,0:T(8,128)(2,1)} %get-tuple-element.108, f32[1024,512]{1,0:T(8,128)} %param.27), kind=kOutput, calls=%fused_computation.36 | convolution fusion | flops 4297588736 | bytes 14680064 | tf_op jit(solution)/shard_map/dot_general | solution.py:160
  285.7 40.1 %psum.64 = f32[]{:T(128)} all-reduce(f32[]{:T(128)} %convert_reduce_fusion), channel_id=1, replica_groups=mesh['batch'=16,'mp'=2] {'batch','mp'}, use_global_device_ids=true, to_apply=%region_45.46 | all-reduce | flops 1 | bytes 8 | tf_op jit(solution)/shard_map/psum | solution.py:88
  327.1 47.7 %reduce-scatter.5.cloned.1.call-done = f32[2048,512]{0,1:T(8,128)} async-done(((f32[4096,512]{0,1:T(8,128)}), f32[2048,512]{0,1:T(8,128)}) %reduce-scatter.5.cloned.1.call-update) | async-done | bytes 4194320 | tf_op jit(solution)/shard_map/reduce_scatter | solution.py:174
  380.3 51.2 %reduce-scatter.3.cloned.1.call-done = bf16[2048,512]{0,1:T(8,128)(2,1)} async-done(((bf16[4096,512]{0,1:T(8,128)(2,1)}), bf16[2048,512]{0,1:T(8,128)(2,1)}) %reduce-scatter.3.cloned.1.call-update) | async-done | bytes 2097168 | tf_op jit(solution)/shard_map/reduce_scatter | solution.py:159
  431.4 7.9 bitcast_add_fusion.2
  450.3 10.4 %fusion.27 = f32[64,8,64,32]{2,3,1,0:T(8,128)} fusion(bf16[1,64,8,32,64]{4,3,2,1,0:T(8,128)(2,1)} %copy-done.5, bf16[64,32,8,64]{3,2,1,0:T(8,128)(2,1)} %reshape.1499), kind=kOutput, calls=%fused_computation.65 | convolution fusion | flops 67108864 | bytes 8388608 | tf_op jit(solution)/shard_map/sihtu,sithd->siuhd/dot_general | solution.py:201
  472.0 11.4 %multiply_reduce_fusion = f32[64,8,32]{2,1,0:T(8,128)S(1)} fusion(f32[1,64,8,32,64]{4,3,2,1,0:T(8,128)S(1)} %bitcast.201, f32[64,8,32]{2,1,0:T(8,128)S(1)} %log_add_fusion, f32[1,64,8,32,32]{4,3,2,1,0:T(8,128)} %convolution_bitcast_fusion, f32[1,64,8,32,32]{4,3,2,1,0:T(8,128)} %fusion.48), kind=kLoop, calls=%fused_computation.30 | loop fusion | flops 4177920 | bytes 8519680 | tf_op jit(solution)/shard_map/reduce_sum | solution.py:205
  503.4 9.7 %copy.138 = f32[64,8,64,32]{0,2,1,3:T(8,128)} copy(f32[64,8,64,32]{2,3,1,0:T(8,128)} %fusion.27) | data formatting | bytes 8388608 | tf_op jit(solution)/shard_map/sihtu,sithd->siuhd/dot_general | solution.py:201
  513.1 19.0 %fusion.14 = f32[64,32,8,64]{3,0,2,1:T(8,128)} fusion(f32[64,8,64,32]{0,2,1,3:T(8,128)} %copy.138, f32[64,8]{0,1:T(8,128)S(1)} %copy-done.118, s32[64]{0:T(128)S(1)} %bitcast.217), kind=kOutput, calls=%fused_computation.24 | convolution fusion | flops 806359040 | bytes 8390912 | tf_op jit(solution)/shard_map/sij,siuhd->sjuhd/dot_general | solution.py:231
  532.1 15.4 %fusion.11 = bf16[1,64,32,8,64]{4,2,3,1,0:T(8,128)(2,1)} fusion(f32[64,32,8,64]{3,0,2,1:T(8,128)} %fusion.14, bf16[1,64,8,32,64]{4,3,2,1,0:T(8,128)(2,1)S(1)} %copy-done.6, bf16[64,32,8,64]{3,2,1,0:T(8,128)(2,1)} %reshape.1499), kind=kOutput, calls=%fused_computation.19 | convolution fusion | flops 69206016 | bytes 10485760 | tf_op jit(solution)/shard_map/sihtu,sithd->siuhd/dot_general | solution.py:198
  547.5 8.4 copy.141
  561.4 18.4 %fusion.16 = f32[64,32,8,64]{3,0,2,1:T(8,128)} fusion(f32[64,32,8,64]{3,1,2,0:T(8,128)} %multiply_bitcast_fusion, s32[64]{0:T(128)S(1)} %bitcast.218), kind=kOutput, calls=%fused_computation.25 | convolution fusion | flops 805310464 | bytes 8388864 | tf_op jit(solution)/shard_map/sij,siuhd->sjuhd/dot_general | solution.py:224
  579.8 15.8 %fusion.12 = bf16[1,64,32,8,64]{4,2,3,1,0:T(8,128)(2,1)} fusion(f32[64,32,8,64]{3,0,2,1:T(8,128)} %fusion.16, bf16[1,64,8,32,64]{4,3,2,1,0:T(8,128)(2,1)S(1)} %copy-done.8, bf16[64,32,8,64]{3,2,1,0:T(8,128)(2,1)} %reshape.1489), kind=kOutput, calls=%fused_computation.21 | convolution fusion | flops 70254592 | bytes 10485760 | tf_op jit(solution)/shard_map/sihtu,sithd->siuhd/dot_general | solution.py:216
  595.6 8.5 copy.133
  610.6 14.8 %fusion.20 = bf16[1,64,32,8,64]{4,2,3,1,0:T(8,128)(2,1)S(1)} fusion(f32[64,8,64,32]{2,3,1,0:T(8,128)} %fusion.30, bf16[64,32,8,64]{3,0,2,1:T(8,128)(2,1)} %fusion.59, bf16[1,64,8,32,64]{4,3,2,1,0:T(8,128)(2,1)} %copy-done.7), kind=kOutput, calls=%fused_computation.38 | convolution fusion | flops 70254592 | bytes 10485760 | tf_op jit(solution)/shard_map/sihtu,siuhd->sithd/dot_general | solution.py:211
  671.5 10.6 %fusion.151 = f32[1024,512]{1,0:T(8,128)} fusion(bf16[4096,1024]{1,0:T(8,128)(2,1)} %get-tuple-element.108, bf16[4096,512]{0,1:T(8,128)(2,1)} %all-gather.5.cloned.1.call-done), kind=kOutput, calls=%fused_computation.299 | convolution fusion | flops 4294967296 | bytes 14680064 | tf_op jit(solution)/shard_map/rf,rd->fd/dot_general | solution.py:171
  682.0 8.5 fusion.150
  701.1 9.7 %multiply_reduce_fusion.2 = (f32[512]{0:T(512)S(1)}, f32[2048]{0:T(1024)S(1)}, f32[2048]{0:T(1024)S(1)}, f32[2048,512]{0,1:T(8,128)}) fusion(f32[1,2048,512]{1,2,0:T(8,128)} %copy.104, f32[2048]{0:T(1024)} %add_rsqrt_fusion.1, f32[2048]{0:T(1024)S(1)} %copy-done.96, f32[512]{0:T(512)S(1)} %copy-done.127, f32[2048,512]{0,1:T(8,128)} %copy.142, ...), kind=kOutput, calls=%fused_computation.50 | convolution fusion | flops 3235376640 | bytes 20484096 | tf_op jit(solution)/shard_map/re,de->rd/dot_general | solution.py:247
  711.4 39.6 %all-reduce = (f32[]{:T(128)}, f32[512]{0:T(512)}, f32[512]{0:T(512)}) all-reduce(f32[]{:T(128)S(6)} %neg.11, f32[512]{0:T(512)S(1)} %get-tuple-element.50, f32[512]{0:T(512)S(1)} %copy-done.128), channel_id=1, replica_groups=mesh['batch'=16,'mp'=2] {'batch','mp'}, use_global_device_ids=true, to_apply=%region_43.44 | all-reduce | flops 1025 | bytes 8200 | tf_op jit(solution)/shard_map/psum | solution.py:278
  751.0 8.4 add_bitcast_fusion
  770.8 49.7 %all-reduce.6.cloned.1.call-done = (f32[512,1536]{1,0:T(8,128)}, f32[512,512]{1,0:T(8,128)}, f32[512,512]{1,0:T(8,128)}) async-done(((f32[512,1536]{1,0:T(8,128)}, f32[512,512]{1,0:T(8,128)}, f32[512,512]{1,0:T(8,128)}), (f32[512,1536]{1,0:T(8,128)}, f32[512,512]{1,0:T(8,128)}, f32[512,512]{1,0:T(8,128)})) %all-reduce.6.cloned.1.call-update) | async-done | bytes 5242896 | tf_op jit(solution)/shard_map/psum | solution.py:278
  824.2 110.4 %all-reduce.8.cloned.1.call-done = (f32[512,1024]{1,0:T(8,128)}, f32[1024,512]{1,0:T(8,128)}) async-done(((f32[512,1024]{1,0:T(8,128)}, f32[1024,512]{1,0:T(8,128)}), (f32[512,1024]{1,0:T(8,128)}, f32[1024,512]{1,0:T(8,128)})) %all-reduce.8.cloned.1.call-update) | async-done | bytes 4194320 | tf_op jit(solution)/shard_map/psum | solution.py:180
  (446 shorter events, 251.7 us)
Async XLA Ops:
  7.2 171.0 %all-gather.5.cloned.1.call-start = ((), (), s32[]{:S(2)}) async-start(), calls=%async_computation.4 | async-start | bytes 6291456 | tf_op jit(solution)/shard_map/all_gather | solution.py:168
  16.4 221.3 %all-gather.3.cloned.1.call-start = ((), (), s32[]{:S(2)}) async-start(), calls=%async_computation.2 | async-start | bytes 6291456 | tf_op jit(solution)/shard_map/all_gather | solution.py:154
  24.4 26.2 %copy-start.95 = (f32[2048]{0:T(1024)}, f32[2048]{0:T(1024)S(1)}, u32[]{:S(2)}) copy-start(f32[2048]{0:T(1024)S(1)} %broadcast_multiply_fusion.5) | copy-start | bytes 24580
  34.4 15.9 %copy-start.124 = (s32[1,64]{1,0:T(1,128)S(1)}, s32[1,64]{1,0:T(1,128)}, u32[]{:S(2)}) copy-start(s32[1,64]{1,0:T(1,128)} %param.16) | copy-start | bytes 772
  34.4 15.9 %copy-start.47 = (f32[512,512]{1,0:T(8,128)S(1)}, f32[512,512]{1,0:T(8,128)}, u32[]{:S(2)}) copy-start(f32[512,512]{1,0:T(8,128)} %param.19) | copy-start | bytes 3145732
  37.2 13.2 %copy-start.48 = (f32[512,512]{1,0:T(8,128)S(1)}, f32[512,512]{1,0:T(8,128)}, u32[]{:S(2)}) copy-start(f32[512,512]{1,0:T(8,128)} %param.20) | copy-start | bytes 3145732
  40.8 69.5 %copy-start = (f32[1,8,64,64]{2,3,1,0:T(8,128)}, f32[1,8,64,64]{2,3,1,0:T(8,128)S(1)}, u32[]{:S(2)}) copy-start(f32[1,8,64,64]{2,3,1,0:T(8,128)S(1)} %get-tuple-element.104) | copy-start | bytes 393220
  41.2 69.2 %copy-start.29 = (f32[8,64]{1,0:T(8,128)}, f32[8,64]{1,0:T(8,128)S(1)}, u32[]{:S(2)}) copy-start(f32[8,64]{1,0:T(8,128)S(1)} %log_add_fusion.9) | copy-start | bytes 6148
  41.5 68.8 %copy-start.31 = (f32[8,64]{1,0:T(8,128)}, f32[8,64]{1,0:T(8,128)S(1)}, u32[]{:S(2)}) copy-start(f32[8,64]{1,0:T(8,128)S(1)} %log_add_fusion.8) | copy-start | bytes 6148
  42.2 68.2 %copy-start.35 = (f32[8,64]{1,0:T(8,128)}, f32[8,64]{1,0:T(8,128)S(1)}, u32[]{:S(2)}) copy-start(f32[8,64]{1,0:T(8,128)S(1)} %log_add_fusion.7) | copy-start | bytes 6148
  42.7 67.7 %copy-start.41 = (f32[8,64]{1,0:T(8,128)}, f32[8,64]{1,0:T(8,128)S(1)}, u32[]{:S(2)}) copy-start(f32[8,64]{1,0:T(8,128)S(1)} %log_add_fusion.6) | copy-start | bytes 6148
  44.5 65.9 %copy-start.45 = (f32[8,64]{1,0:T(8,128)}, f32[8,64]{1,0:T(8,128)S(1)}, u32[]{:S(2)}) copy-start(f32[8,64]{1,0:T(8,128)S(1)} %log_add_fusion.5) | copy-start | bytes 6148
  45.7 64.7 %copy-start.57 = (f32[8,64]{1,0:T(8,128)}, f32[8,64]{1,0:T(8,128)S(1)}, u32[]{:S(2)}) copy-start(f32[8,64]{1,0:T(8,128)S(1)} %log_add_fusion.4) | copy-start | bytes 6148
  47.2 63.2 %copy-start.67 = (f32[8,64]{1,0:T(8,128)}, f32[8,64]{1,0:T(8,128)S(1)}, u32[]{:S(2)}) copy-start(f32[8,64]{1,0:T(8,128)S(1)} %log_add_fusion.3) | copy-start | bytes 6148
  48.2 62.2 %copy-start.93 = (f32[8,64]{1,0:T(8,128)}, f32[8,64]{1,0:T(8,128)S(1)}, u32[]{:S(2)}) copy-start(f32[8,64]{1,0:T(8,128)S(1)} %get-tuple-element.67) | copy-start | bytes 6148
  48.6 61.9 %copy-start.71 = (f32[8,64]{1,0:T(8,128)}, f32[8,64]{1,0:T(8,128)S(1)}, u32[]{:S(2)}) copy-start(f32[8,64]{1,0:T(8,128)S(1)} %log_add_fusion.2) | copy-start | bytes 6148
  50.3 60.2 %copy-start.79 = (f32[8,64]{1,0:T(8,128)}, f32[8,64]{1,0:T(8,128)S(1)}, u32[]{:S(2)}) copy-start(f32[8,64]{1,0:T(8,128)S(1)} %log_add_fusion.1) | copy-start | bytes 6148
  50.3 60.2 %copy-start.43 = (f32[64,64]{0,1:T(8,128)}, f32[64,64]{0,1:T(8,128)S(1)}, u32[]{:S(2)}) copy-start(f32[64,64]{0,1:T(8,128)S(1)} %fusion.112) | copy-start | bytes 49156
  178.0 196.9 %reduce-scatter.5.cloned.1.call-start = ((), (), s32[]{:S(2)}) async-start(), calls=%async_computation.5 | async-start | bytes 12582912 | tf_op jit(solution)/shard_map/reduce_scatter | solution.py:174
  237.7 26.2 %copy-start.130 = (f32[512,1024]{1,0:T(8,128)S(1)}, f32[512,1024]{1,0:T(8,128)}, u32[]{:S(2)}) copy-start(f32[512,1024]{1,0:T(8,128)} %param.26) | copy-start | bytes 6291460
  274.0 157.4 %reduce-scatter.3.cloned.1.call-start = ((), (), s32[]{:S(2)}) async-start(), calls=%async_computation.3 | async-start | bytes 6291456 | tf_op jit(solution)/shard_map/reduce_scatter | solution.py:159
  285.0 535.4 %all-reduce.6.cloned.1.call-start = ((), (), s32[]{:S(2)}) async-start(), calls=%async_computation.6 | async-start | bytes 10485760 | tf_op jit(solution)/shard_map/psum | solution.py:278
  513.1 19.0 %copy-start.6 = (bf16[1,64,8,32,64]{4,3,2,1,0:T(8,128)(2,1)S(1)}, bf16[1,64,8,32,64]{4,3,2,1,0:T(8,128)(2,1)}, u32[]{:S(2)}) copy-start(bf16[1,64,8,32,64]{4,3,2,1,0:T(8,128)(2,1)} %copy-done.5) | copy-start | bytes 6291460
  561.4 18.4 %copy-start.8 = (bf16[1,64,8,32,64]{4,3,2,1,0:T(8,128)(2,1)S(1)}, bf16[1,64,8,32,64]{4,3,2,1,0:T(8,128)(2,1)}, u32[]{:S(2)}) copy-start(bf16[1,64,8,32,64]{4,3,2,1,0:T(8,128)(2,1)} %copy-done.7) | copy-start | bytes 6291460
  649.8 13.6 %copy-start.90 = (f32[8,64]{1,0:T(8,128)S(1)}, f32[8,64]{1,0:T(8,128)}, u32[]{:S(2)}) copy-start(f32[8,64]{1,0:T(8,128)} %copy-done.89) | copy-start | bytes 6148
  649.8 14.6 %copy-start.106 = (f32[8,64]{1,0:T(8,128)S(1)}, f32[8,64]{1,0:T(8,128)}, u32[]{:S(2)}) copy-start(f32[8,64]{1,0:T(8,128)} %copy-done.105) | copy-start | bytes 6148
  655.3 12.9 %copy-start.100 = (f32[8,64]{1,0:T(8,128)S(1)}, f32[8,64]{1,0:T(8,128)}, u32[]{:S(2)}) copy-start(f32[8,64]{1,0:T(8,128)} %copy-done.99) | copy-start | bytes 6148
  656.0 12.7 %copy-start.74 = (f32[8,64]{1,0:T(8,128)S(1)}, f32[8,64]{1,0:T(8,128)}, u32[]{:S(2)}) copy-start(f32[8,64]{1,0:T(8,128)} %copy-done.73) | copy-start | bytes 6148
  656.0 12.7 %copy-start.111 = (f32[8,64]{1,0:T(8,128)S(1)}, f32[8,64]{1,0:T(8,128)}, u32[]{:S(2)}) copy-start(f32[8,64]{1,0:T(8,128)} %get-tuple-element.76) | copy-start | bytes 6148
  671.4 263.2 %all-reduce.8.cloned.1.call-start = ((), (), s32[]{:S(2)}) async-start(), calls=%async_computation.7 | async-start | bytes 8388608 | tf_op jit(solution)/shard_map/psum | solution.py:180
  820.5 114.1 %copy-start.51 = (f32[512,512]{1,0:T(8,128)S(1)}, f32[512,512]{1,0:T(8,128)}, u32[]{:S(2)}) copy-start(f32[512,512]{1,0:T(8,128)} %get-tuple-element.132) | copy-start | bytes 3145732
  820.5 115.1 %copy-start.50 = (f32[512,512]{1,0:T(8,128)S(1)}, f32[512,512]{1,0:T(8,128)}, u32[]{:S(2)}) copy-start(f32[512,512]{1,0:T(8,128)} %get-tuple-element.133) | copy-start | bytes 3145732
  (110 other events, 798.9 us)
Sparse Core Ops, SparseCore 0:
  16.5 59.4 all-gather.4
  178.1 59.5 all-gather.2
  274.2 100.6 reduce-scatter.4
  377.1 54.3 reduce-scatter.2
  671.5 148.9 all-reduce.5
  824.6 109.9 all-reduce.7
where the time goes:
time: 952 us; the launch traced here: 947 us
  waiting for transfers between devices  304 us (32%)
  matrix products  272 us (29%)
  local copies, waits for them, and re-layouts  157 us (16%)
  other arithmetic  114 us (12%)
  blocking collectives  79.6 us (8%)
  between operations  20.4 us (2%)
    psum x1, waiting for transfers between devices, local(): grad_up, grad_down = lax.psum((part_up, part_down), 'batch')  110 us
    reduce_scatter x1, waiting for transfers between devices, local(): lax.psum_scatter(jnp.dot(piece, down_low, preferred_element_type=jnp.floa...  51.2 us
    psum x1, waiting for transfers between devices, local(): lax.psum((joined_part, out_part, sort_part, gain_one_part, gain_two_part,...  49.7 us
    reduce_scatter x1, waiting for transfers between devices, local(): lax.psum_scatter(jnp.einsum('rf,df->rd', piece, up_low, preferred_element...  47.7 us
    another operation x7, local copies, waits for them, and re-layouts  46.4 us
    all_gather x1, waiting for transfers between devices, local(): gathered = lax.all_gather(act_two, 'mp', axis=0, tiled=True)  44.5 us
    psum x1, blocking collectives, local(): block_total = lax.psum(local_blocks, ('batch', 'mp'))  40.1 us
    unnamed x283, local copies, waits for them, and re-layouts  39.7 us
  transfers between devices with their start and end apart: 6, of which 5 were waited for; matrix products, arithmetic and copies ran while one was open for 26% of the time, Pallas kernels for 0%

commit v1 on v0

v1 whole, which is shorter than its diff:
```python
import functools

import jax
import jax.numpy as jnp
from jax import lax
from jax.experimental import pallas as pl
from jax.experimental.pallas import tpu as pltpu
from jax.sharding import PartitionSpec as P

HEADS = 8
HEAD_DIM = 64
BLOCK = 32
ITERS = 8
GROUP = 4
GROUP_WIDTH = GROUP * HEAD_DIM
GROUP_ROWS = GROUP * BLOCK
EPSILON = 1e-05
FACTOR = HEAD_DIM ** (-0.5)
HIGHEST = lax.Precision.HIGHEST
F32 = jnp.float32
BF16 = jnp.bfloat16
NT = (((1,), (1,)), ((), ()))
TN = (((0,), (0,)), ((), ()))
MIB = 1024 * 1024


def dot(left, right):
    return jnp.dot(left, right, preferred_element_type=F32)


def dot_nt(left, right):
    return lax.dot_general(left, right, NT, preferred_element_type=F32)


def dot_tn(left, right):
    return lax.dot_general(left, right, TN, preferred_element_type=F32)


def shape_of(dims, dtype):
    return jax.ShapeDtypeStruct(dims, dtype)


def whole(dims):
    return pl.BlockSpec(dims, lambda *_: (0,) * len(dims))


def rows_of(size, width):
    return pl.BlockSpec((size, width), lambda step, *_: (step, 0))


def params(mib):
    return pltpu.CompilerParams(vmem_limit_bytes=mib * MIB)


def normalize(values):
    center = values - jnp.mean(values, axis=-1, keepdims=True)
    inverse = lax.rsqrt(jnp.mean(center * center, axis=-1, keepdims=True) + EPSILON)
    return center * inverse, inverse


def norm_grad(grad_rows, unit_rows, inverse, gain):
    scaled_rows = grad_rows * gain
    return inverse * (
        scaled_rows
        - jnp.mean(scaled_rows, axis=-1, keepdims=True)
        - unit_rows * jnp.mean(scaled_rows * unit_rows, axis=-1, keepdims=True)
    )


def project_kernel(x_ref, gain_ref, wq_ref, wk_ref, wv_ref, act_ref, q_ref, k_ref, v_ref, sum_ref, w_ref):
    width = x_ref.shape[1]

    @pl.when(pl.program_id(0) == 0)
    def _():
        w_ref[:, :width] = wq_ref[...].astype(BF16)
        w_ref[:, width : 2 * width] = wk_ref[...].astype(BF16)
        w_ref[:, 2 * width :] = wv_ref[...].astype(BF16)

    unit, _ = normalize(x_ref[...])
    act = (unit * gain_ref[...]).astype(BF16)
    act_ref[...] = act
    q_ref[...] = dot(act, w_ref[:, :width]).astype(BF16)
    k_ref[...] = dot(act, w_ref[:, width : 2 * width]).astype(BF16)
    v_ref[...] = dot(act, w_ref[:, 2 * width :]).astype(BF16)
    rows = act.shape[0]
    sums = jnp.sum(act.astype(F32).reshape(rows // BLOCK, BLOCK, width), axis=1)
    sum_ref[...] = sums.astype(BF16).astype(F32)


def project(x, gain, wq, wk, wv, tile=512):
    rows, width = x.shape
    low = shape_of((rows, width), BF16)
    return pl.pallas_call(
        project_kernel,
        grid=(rows // tile,),
        in_specs=[rows_of(tile, width), whole((1, width))] + [whole((width, width))] * 3,
        out_specs=[rows_of(tile, width)] * 4 + [rows_of(tile // BLOCK, width)],
        out_shape=[low, low, low, low, shape_of((rows // BLOCK, width), F32)],
        scratch_shapes=[pltpu.VMEM((width, 3 * width), BF16)],
        compiler_params=params(48),
        cost_estimate=pl.CostEstimate(flops=6 * rows * width * width, bytes_accessed=15 * MIB, transcendentals=0),
        name="project",
    )(x, gain, wq, wk, wv)


def segment_sum(tile, first):
    left = jnp.sum(jnp.where(first, tile, 0.0), axis=1, keepdims=True)
    right = jnp.sum(jnp.where(first, 0.0, tile), axis=1, keepdims=True)
    return jnp.where(first, left, right)


def segment_max(tile, first):
    left = jnp.max(jnp.where(first, tile, -jnp.inf), axis=1, keepdims=True)
    right = jnp.max(jnp.where(first, -jnp.inf, tile), axis=1, keepdims=True)
    return jnp.where(first, left, right)


def lane_tiles(blocks):
    lane = lax.broadcasted_iota(jnp.int32, (blocks, 2 * blocks), 1)
    return lane < blocks, jnp.where(lane < blocks, lane, lane - blocks)


def balance_kernel(sum_ref, w_ref, perm_ref, mask_ref, share_ref, log_ref, chosen_ref, entropy_ref):
    blocks = sum_ref.shape[0]
    wide = 2 * blocks
    first, position = lane_tiles(blocks)
    hot = position == perm_ref[...]
    real = mask_ref[...] > 0.0
    logits = jnp.dot(sum_ref[...], w_ref[...], precision=HIGHEST, preferred_element_type=F32)
    for pair in range(logits.shape[1] // wide):
        span = slice(pair * wide, (pair + 1) * wide)
        tile = logits[:, span]
        for step in range(ITERS):
            top = segment_max(tile, first)
            powers = jnp.exp(tile - top)
            total = segment_sum(powers, first)
            tile = tile - (top + jnp.log(total))
            share_ref[2 * step, :, span] = powers * (1.0 / total)
            top = jnp.max(tile, axis=0, keepdims=True)
            powers = jnp.exp(tile - top)
            total = jnp.sum(powers, axis=0, keepdims=True)
            tile = tile - (top + jnp.log(total))
            if step < ITERS - 1:
                share_ref[2 * step + 1, :, span] = powers * (1.0 / total)
        plan = jnp.exp(tile)
        share_ref[2 * ITERS - 1, :, span] = plan
        log_ref[:, span] = tile
        chosen_ref[:, span] = blocks * segment_sum(jnp.where(hot, plan, 0.0), first)
        entropy_ref[:, span] = -jnp.sum(jnp.where(real, plan * tile, 0.0), axis=0, keepdims=True)


def balance(sums, w_sort, perm_column, mask_column):
    blocks, width = sums.shape
    cols = w_sort.shape[1]
    return pl.pallas_call(
        balance_kernel,
        out_shape=[
            shape_of((2 * ITERS, blocks, cols), F32),
            shape_of((blocks, cols), F32),
            shape_of((blocks, cols), F32),
            shape_of((1, cols), F32),
        ],
        compiler_params=params(32),
        name="balance",
    )(sums, w_sort, perm_column, mask_column)


def balance_back_kernel(
    coef_ref, gch_ref, share_ref, log_ref, sum_ref, w_ref, perm_ref, mask_ref, sort_ref, gsum_ref, glog_ref
):
    blocks = sum_ref.shape[0]
    wide = 2 * blocks
    first, position = lane_tiles(blocks)
    hot = position == perm_ref[...]
    weight = coef_ref[0] * mask_ref[...]
    for pair in range(log_ref.shape[1] // wide):
        span = slice(pair * wide, (pair + 1) * wide)
        plan = share_ref[2 * ITERS - 1, :, span]
        gch = segment_sum(gch_ref[:, span], first)
        grad = plan * (jnp.where(hot, blocks * gch, 0.0) - weight * (log_ref[:, span] + 1.0))
        for level in range(2 * ITERS - 1, -1, -1):
            if level % 2:
                total = jnp.sum(grad, axis=0, keepdims=True)
            else:
                total = segment_sum(grad, first)
            grad = grad - share_ref[level, :, span] * total
        glog_ref[:, span] = grad
    glog = glog_ref[...]
    sort_ref[...] = lax.dot_general(
        sum_ref[...], glog, TN, precision=HIGHEST, preferred_element_type=F32
    ).astype(sort_ref.dtype)
    gsum_ref[...] = lax.dot_general(glog, w_ref[...], NT, precision=HIGHEST, preferred_element_type=F32)


def balance_back(coef, gch, shares, plan_log, sums, w_sort, perm_column, mask_column):
    blocks, width = sums.shape
    cols = w_sort.shape[1]
    vmem = pl.BlockSpec(memory_space=pltpu.VMEM)
    return pl.pallas_call(
        balance_back_kernel,
        in_specs=[pl.BlockSpec(memory_space=pltpu.SMEM)] + [vmem] * 7,
        out_specs=[vmem, vmem],
        out_shape=[shape_of((width, cols), BF16), shape_of((blocks, width), F32)],
        scratch_shapes=[pltpu.VMEM((blocks, cols), F32)],
        compiler_params=params(32),
        name="balance_back",
    )(coef, gch, shares, plan_log, sums, w_sort, perm_column, mask_column)


def head_masks(rows):
    lane = lax.broadcasted_iota(jnp.int32, (rows, GROUP_WIDTH), 1)
    return [(lane >= h * HEAD_DIM) & (lane < (h + 1) * HEAD_DIM) for h in range(GROUP)]


def expand(rows, masks):
    zero = jnp.zeros_like(rows)
    return jnp.concatenate([jnp.where(mask, rows, zero) for mask in masks], axis=0)


def fold(rows, masks):
    parts = [rows[h * BLOCK : (h + 1) * BLOCK] for h in range(GROUP)]
    result = parts[GROUP - 1]
    for h in range(GROUP - 1):
        result = jnp.where(masks[h], parts[h], result)
    return result


def attend_kernel(
    perm_ref, mask_ref, q_ref, k_ref, v_ref, chosen_ref, wo_ref, x_ref, gain_ref,
    probs_ref, att_ref, second_ref, act_ref, wo_low_ref,
):
    tile_index = pl.program_id(0)
    rows, width = q_ref.shape
    blocks = rows // BLOCK

    @pl.when(tile_index == 0)
    def _():
        wo_low_ref[...] = wo_ref[...].astype(BF16)

    masks = head_masks(BLOCK)
    key_row = lax.broadcasted_iota(jnp.int32, (BLOCK, GROUP_ROWS), 0)
    query_row = lax.broadcasted_iota(jnp.int32, (BLOCK, GROUP_ROWS), 1) % BLOCK
    causal = key_row <= query_row
    for b in range(blocks):
        block = tile_index * blocks + b
        partner = perm_ref[block]
        usable = (partner < block) & (mask_ref[partner] > 0)
        far_bias = jnp.where(usable, 0.0, -1e30)
        own_at = pl.ds(pl.multiple_of(block * BLOCK, BLOCK), BLOCK)
        far_at = pl.ds(pl.multiple_of(partner * BLOCK, BLOCK), BLOCK)
        here = slice(b * BLOCK, (b + 1) * BLOCK)
        for g in range(width // GROUP_WIDTH):
            lanes = slice(g * GROUP_WIDTH, (g + 1) * GROUP_WIDTH)
            queries = expand(q_ref[here, lanes], masks)
            keys = jnp.concatenate([k_ref[own_at, lanes], k_ref[far_at, lanes]], axis=0)
            scores = dot_nt(keys, queries) * FACTOR
            own = jnp.where(causal, scores[:BLOCK], -1e30)
            far = jnp.where(usable, scores[BLOCK:], -1e30)
            top = jnp.maximum(jnp.max(own, axis=0, keepdims=True), jnp.max(far, axis=0, keepdims=True))
            powers = jnp.exp(jnp.concatenate([own, far], axis=0) - top)
            probs = (powers * (1.0 / jnp.sum(powers, axis=0, keepdims=True))).astype(BF16)
            probs_ref[b * 2 * BLOCK : (b + 1) * 2 * BLOCK, g * GROUP_ROWS : (g + 1) * GROUP_ROWS] = probs
            scaled = (v_ref[far_at, lanes].astype(F32) * chosen_ref[b : b + 1, lanes]).astype(BF16)
            values = jnp.concatenate([v_ref[own_at, lanes], scaled], axis=0)
            att_ref[here, lanes] = fold(dot_tn(probs, values), masks).astype(BF16)
    second = x_ref[...] + dot(att_ref[...], wo_low_ref[...])
    second_ref[...] = second
    unit, _ = normalize(second)
    act_ref[...] = (unit * gain_ref[...]).astype(BF16)


def attend(perm, mask, q, k, v, chosen, w_out, x, gain, tile=256):
    rows, width = q.shape
    blocks = rows // BLOCK
    grid_spec = pltpu.PrefetchScalarGridSpec(
        num_scalar_prefetch=2,
        grid=(rows // tile,),
        in_specs=[
            rows_of(tile, width),
            whole((rows, width)),
            whole((rows, width)),
            rows_of(tile // BLOCK, width),
            whole((width, width)),
            rows_of(tile, width),
            whole((1, width)),
        ],
        out_specs=[
            rows_of(2 * tile, HEADS * BLOCK),
            rows_of(tile, width),
            rows_of(tile, width),
            rows_of(tile, width),
        ],
        scratch_shapes=[pltpu.VMEM((width, width), BF16)],
    )
    return pl.pallas_call(
        attend_kernel,
        grid_spec=grid_spec,
        out_shape=[
            shape_of((2 * rows, HEADS * BLOCK), BF16),
            shape_of((rows, width), BF16),
            shape_of((rows, width), F32),
            shape_of((rows, width), BF16),
        ],
        compiler_params=params(48),
        name="attend",
    )(perm, mask, q, k, v, chosen, w_out, x, gain)


def attend_back_kernel(
    perm_ref, q_ref, gatt_ref, probs_ref, k_ref, v_ref, chosen_ref,
    gq_ref, gk_ref, gv_ref, gch_ref, own_k_ref, far_k_ref, own_v_ref, far_v_ref,
):
    tile_index = pl.program_id(0)
    rows, width = q_ref.shape
    blocks = rows // BLOCK
    masks = head_masks(BLOCK)
    for b in range(blocks):
        block = tile_index * blocks + b
        partner = perm_ref[block]
        own_at = pl.ds(pl.multiple_of(block * BLOCK, BLOCK), BLOCK)
        far_at = pl.ds(pl.multiple_of(partner * BLOCK, BLOCK), BLOCK)
        here = slice(b * BLOCK, (b + 1) * BLOCK)
        for g in range(width // GROUP_WIDTH):
            lanes = slice(g * GROUP_WIDTH, (g + 1) * GROUP_WIDTH)
            queries = expand(q_ref[here, lanes], masks)
            grads = expand(gatt_ref[here, lanes], masks)
            keys = jnp.concatenate([k_ref[own_at, lanes], k_ref[far_at, lanes]], axis=0)
            far_values = v_ref[far_at, lanes].astype(F32)
            chosen = chosen_ref[b : b + 1, lanes]
            values = jnp.concatenate([v_ref[own_at, lanes], (far_values * chosen).astype(BF16)], axis=0)
            probs_low = probs_ref[
                b * 2 * BLOCK : (b + 1) * 2 * BLOCK, g * GROUP_ROWS : (g + 1) * GROUP_ROWS
            ]
            probs = probs_low.astype(F32)
            grad_probs = dot_nt(values, grads)
            total = jnp.sum(probs * grad_probs, axis=0, keepdims=True)
            grad_scores = (probs * (grad_probs - total)).astype(BF16)
            grad_keys = dot(grad_scores, queries) * FACTOR
            grad_values = dot(probs_low, grads)
            gq_ref[here, lanes] = (fold(dot_tn(grad_scores, keys), masks) * FACTOR).astype(BF16)
            far_grad = grad_values[BLOCK:]
            gch_ref[b : b + 1, lanes] = jnp.sum(far_grad * far_values, axis=0, keepdims=True)
            own_k_ref[own_at, lanes] = grad_keys[:BLOCK]
            far_k_ref[far_at, lanes] = grad_keys[BLOCK:]
            own_v_ref[own_at, lanes] = grad_values[:BLOCK]
            far_v_ref[far_at, lanes] = far_grad * chosen

    @pl.when(tile_index == pl.num_programs(0) - 1)
    def _():
        gk_ref[...] = (own_k_ref[...] + far_k_ref[...]).astype(BF16)
        gv_ref[...] = (own_v_ref[...] + far_v_ref[...]).astype(BF16)


def attend_back(perm, q, gatt, probs, k, v, chosen, tile=256):
    rows, width = q.shape
    low = shape_of((rows, width), BF16)
    grid_spec = pltpu.PrefetchScalarGridSpec(
        num_scalar_prefetch=1,
        grid=(rows // tile,),
        in_specs=[
            rows_of(tile, width),
            rows_of(tile, width),
            rows_of(2 * tile, HEADS * BLOCK),
            whole((rows, width)),
            whole((rows, width)),
            rows_of(tile // BLOCK, width),
        ],
        out_specs=[
            rows_of(tile, width),
            whole((rows, width)),
            whole((rows, width)),
            rows_of(tile // BLOCK, width),
        ],
        scratch_shapes=[pltpu.VMEM((rows, width), F32)] * 4,
    )
    return pl.pallas_call(
        attend_back_kernel,
        grid_spec=grid_spec,
        out_shape=[low, low, low, shape_of((rows // BLOCK, width), F32)],
        compiler_params=params(56),
        name="attend_back",
    )(perm, q, gatt, probs, k, v, chosen)


def gelu_pair(up):
    square = up * up
    inner = 0.7978845608028654 * 0.044715
    half = 0.5 + 0.5 * jnp.tanh(up * (0.7978845608028654 + inner * square))
    value = up * half
    slope = half + (2.0 * value) * (1.0 - half) * (0.7978845608028654 + 3.0 * inner * square)
    return value, slope


def feed_kernel(
    act_ref, second_ref, cot_ref, att_ref, up_ref, down_ref, wo_ref, gain_ref,
    out_ref, gsec_ref, gatt_ref, gup_ref, gdown_ref, gout_ref, ggain_ref,
    wo_low_ref, up_acc, down_acc, out_acc, *, chunk
):
    tile_index = pl.program_id(0)

    @pl.when(tile_index == 0)
    def _():
        wo_low_ref[...] = wo_ref[...].astype(BF16)
        up_acc[...] = jnp.zeros_like(up_acc)
        down_acc[...] = jnp.zeros_like(down_acc)
        out_acc[...] = jnp.zeros_like(out_acc)
        ggain_ref[...] = jnp.zeros_like(ggain_ref)

    hidden_units = up_ref.shape[1]
    act = act_ref[...]
    cot = cot_ref[...]
    cot_low = cot.astype(BF16)
    act_turned = act.T
    cot_turned = cot_low.T
    second = second_ref[...]
    output = second
    grad_normed = jnp.zeros_like(second)
    for c in range(hidden_units // chunk):
        span = slice(c * chunk, (c + 1) * chunk)
        value, slope = gelu_pair(dot(act, up_ref[:, span]))
        hidden = value.astype(BF16)
        output = output + dot(hidden, down_ref[span, :])
        grad_up = (dot_nt(cot_low, down_ref[span, :]) * slope).astype(BF16)
        grad_normed = grad_normed + dot_nt(grad_up, up_ref[:, span])
        up_acc[:, span] += dot(act_turned, grad_up)
        down_acc[:, span] += dot(cot_turned, hidden)
    out_ref[...] = output
    unit, inverse = normalize(second)
    ggain_ref[...] += jnp.sum(grad_normed * unit, axis=0, keepdims=True)
    grad_second = cot + norm_grad(grad_normed, unit, inverse, gain_ref[...])
    gsec_ref[...] = grad_second
    second_low = grad_second.astype(BF16)
    gatt_ref[...] = dot_nt(second_low, wo_low_ref[...]).astype(BF16)
    out_acc[...] += dot_tn(att_ref[...], second_low)

    @pl.when(tile_index == pl.num_programs(0) - 1)
    def _():
        gup_ref[...] = up_acc[...].astype(BF16)
        gdown_ref[...] = down_acc[...].astype(BF16)
        gout_ref[...] = out_acc[...].astype(BF16)


def feed(act, second, cot, att, w_up, w_down, w_out, gain, tile=256, chunk=512):
    rows, width = act.shape
    units = w_up.shape[1]
    return pl.pallas_call(
        functools.partial(feed_kernel, chunk=chunk),
        grid=(rows // tile,),
        in_specs=[rows_of(tile, width)] * 4
        + [whole((width, units)), whole((units, width)), whole((width, width)), whole((1, width))],
        out_specs=[rows_of(tile, width)] * 3
        + [whole((width, units)), whole((width, units)), whole((width, width)), whole((1, width))],
        out_shape=[
            shape_of((rows, width), F32),
            shape_of((rows, width), F32),
            shape_of((rows, width), BF16),
            shape_of((width, units), BF16),
            shape_of((width, units), BF16),
            shape_of((width, width), BF16),
            shape_of((1, width), F32),
        ],
        scratch_shapes=[
            pltpu.VMEM((width, width), BF16),
            pltpu.VMEM((width, units), F32),
            pltpu.VMEM((width, units), F32),
            pltpu.VMEM((width, width), F32),
        ],
        compiler_params=params(60),
        cost_estimate=pl.CostEstimate(flops=12 * rows * width * units, bytes_accessed=30 * MIB, transcendentals=0),
        name="feed",
    )(act, second, cot, att, w_up, w_down, w_out, gain)


def weight_kernel(act_ref, gq_ref, gk_ref, gv_ref, out_ref, acc_ref):
    @pl.when(pl.program_id(0) == 0)
    def _():
        acc_ref[...] = jnp.zeros_like(acc_ref)

    turned = act_ref[...].T
    for which, ref in enumerate((gq_ref, gk_ref, gv_ref)):
        acc_ref[which] += dot(turned, ref[...])

    @pl.when(pl.program_id(0) == pl.num_programs(0) - 1)
    def _():
        out_ref[...] = acc_ref[...].astype(BF16)


def weight_grads(act, gq, gk, gv, tile=512):
    rows, width = act.shape
    cols = gq.shape[1]
    return pl.pallas_call(
        weight_kernel,
        grid=(rows // tile,),
        in_specs=[rows_of(tile, width)] + [rows_of(tile, cols)] * 3,
        out_specs=whole((3, width, cols)),
        out_shape=shape_of((3, width, cols), BF16),
        scratch_shapes=[pltpu.VMEM((3, width, cols), F32)],
        compiler_params=params(32),
        cost_estimate=pl.CostEstimate(flops=6 * rows * width * cols, bytes_accessed=10 * MIB, transcendentals=0),
        name="weight_grads",
    )(act, gq, gk, gv)


def input_kernel(
    gq_ref, gk_ref, gv_ref, gsum_ref, x_ref, gsec_ref, gain_ref, wq_ref, wk_ref, wv_ref, out_ref, w_ref
):
    @pl.when(pl.program_id(0) == 0)
    def _():
        for which, ref in enumerate((wq_ref, wk_ref, wv_ref)):
            w_ref[which] = ref[...].astype(BF16)

    rows, width = x_ref.shape
    grad = dot_nt(gq_ref[...], w_ref[0]) + dot_nt(gk_ref[...], w_ref[1]) + dot_nt(gv_ref[...], w_ref[2])
    grad = (grad.reshape(rows // BLOCK, BLOCK, width) + gsum_ref[...][:, None, :]).reshape(rows, width)
    unit, inverse = normalize(x_ref[...])
    out_ref[...] = gsec_ref[...] + norm_grad(grad, unit, inverse, gain_ref[...])


def input_grad(gq, gk, gv, gsum, x, gsec, gain, wq, wk, wv, tile=256):
    rows, width = x.shape
    return pl.pallas_call(
        input_kernel,
        grid=(rows // tile,),
        in_specs=[rows_of(tile, width)] * 3
        + [rows_of(tile // BLOCK, width)]
        + [rows_of(tile, width)] * 2
        + [whole((1, width))]
        + [whole((width, width))] * 3,
        out_specs=rows_of(tile, width),
        out_shape=shape_of((rows, width), F32),
        scratch_shapes=[pltpu.VMEM((3, width, width), BF16)],
        compiler_params=params(48),
        cost_estimate=pl.CostEstimate(flops=6 * rows * width * width, bytes_accessed=21 * MIB, transcendentals=0),
        name="input_grad",
    )(gq, gk, gv, gsum, x, gsec, gain, wq, wk, wv)


def local(
    inputs, cotangent, block_perm, block_mask, pen_weight, w_query, w_key, w_value, w_out, w_sort,
    gain_one, gain_two, w_up, w_down,
):
    both = ("batch", "mp")
    _, rows, width = inputs.shape
    x = inputs.reshape(rows, width)
    cot = cotangent.reshape(rows, width)
    perm = block_perm.reshape(-1)
    mask = block_mask.reshape(-1)
    perm_column = perm.reshape(-1, 1)
    mask_column = mask.reshape(-1, 1).astype(F32)
    gain_one_row = gain_one.reshape(1, width)
    gain_two_row = gain_two.reshape(1, width)
    block_total = lax.psum(jnp.sum(mask.astype(F32)), both)
    up_all = lax.all_gather(w_up.astype(BF16), "mp", axis=1, tiled=True)
    down_all = lax.all_gather(w_down.astype(BF16), "mp", axis=0, tiled=True)
    act_one, q, k, v, sums = project(x, gain_one_row, w_query, w_key, w_value)
    shares, plan_log, chosen, entropy = balance(sums, w_sort, perm_column, mask_column)
    probs, att, second, act_two = attend(perm, mask, q, k, v, chosen, w_out, x, gain_two_row)
    output, grad_second, grad_att, up_part, down_part, out_part, gain_two_part = feed(
        act_two, second, cot, att, up_all, down_all, w_out, gain_two_row
    )
    gq, gk, gv, gch = attend_back(perm, q, grad_att, probs, k, v, chosen)
    coef = (pen_weight[0] / (HEADS * block_total)).reshape(1)
    sort_part, grad_sums = balance_back(coef, gch, shares, plan_log, sums, w_sort, perm_column, mask_column)
    joined_part = weight_grads(act_one, gq, gk, gv)
    grad_input = input_grad(gq, gk, gv, grad_sums, x, grad_second, gain_one_row, w_query, w_key, w_value)
    up_sum = lax.psum(lax.psum_scatter(up_part, "mp", scatter_dimension=1, tiled=True), "batch")
    down_sum = lax.psum(lax.psum_scatter(down_part, "mp", scatter_dimension=1, tiled=True), "batch")
    joined, grad_out, grad_sort = lax.psum((joined_part, out_part, sort_part), both)
    grad_gain_two, entropy_all = lax.psum((gain_two_part, entropy), both)
    joined = joined.astype(F32)
    grad_sort = grad_sort.astype(F32)
    grad_gain_one = (
        jnp.sum(joined[0] * w_query, axis=1)
        + jnp.sum(joined[1] * w_key, axis=1)
        + jnp.sum(joined[2] * w_value, axis=1)
        + jnp.sum(grad_sort * w_sort, axis=1)
    ) / gain_one
    return (
        output.reshape(inputs.shape),
        (jnp.sum(entropy_all) / (HEADS * block_total)).reshape(1),
        grad_input.reshape(inputs.shape),
        joined[0],
        joined[1],
        joined[2],
        grad_out.astype(F32),
        grad_sort,
        grad_gain_one,
        grad_gain_two.reshape(width),
        up_sum.astype(F32),
        down_sum.T.astype(F32),
    )


def solution(mesh):
    tokens = P(("batch", "mp"), None, None)
    blocks = P(("batch", "mp"), None)
    return jax.shard_map(
        local,
        mesh=mesh,
        in_specs=(tokens, tokens, blocks, blocks) + (P(),) * 8 + (P(None, "mp"), P("mp", None)),
        out_specs=(tokens, P(), tokens) + (P(),) * 7 + (P(None, "mp"), P("mp", None)),
        check_vma=False,
    )
```

time: 952 us -> 459 us (0.48)
  matrix products: 272 us -> 0 us
  local copies, waits for them, and re-layouts: 157 us -> 22.3 us
  Pallas kernels: 0 us -> 111 us
  other arithmetic: 114 us -> 15.9 us
  waiting for transfers between devices: 304 us -> 252 us
  blocking collectives: 79.6 us -> 40 us
    dot_general x30 -> x0, matrix products: 264 us -> none  [the longest x1 26.2 us: local(): up_rows = jnp.dot(gathered, up_low, preferred_element_type=jnp.float32)]
    pallas_call x0 -> x8, Pallas kernels: none -> 111 us  [the longest x1 46.8 us: feed(): pl.pallas_call(functools.partial(feed_kernel, chunk=chunk), grid=(rows //...]
    reduce_scatter x2, waiting for transfers between devices: 98.9 us -> 0.04 us  [the longest x1 0.02 us: local(): lax.psum_scatter(down_part, 'mp', scatter_dimension=1, tiled=True)]
    reduce_sum x47 -> x3, other arithmetic: 65 us -> 3.75 us  [the longest x1 2.54 us: local(): jnp.sum(grad_sort * w_sort, axis=1)]
    psum x2, waiting for transfers between devices: 160 us -> 217 us  [the longest x1 123 us: local(): lax.psum((joined_part, out_part, sort_part), both)]
    another operation x7 -> x1, local copies, waits for them, and re-layouts: 46.4 us -> 0.1 us  [local(): perm_column = perm.reshape(-1, 1)]
    psum x2 -> x1, blocking collectives: 79.6 us -> 40 us  [local(): grad_gain_two, entropy_all = lax.psum((gain_two_part, entropy), both)]
    reshape x4 -> x0, local copies, waits for them, and re-layouts: 23.9 us -> none  [the longest x1 6.45 us: local(): key_grad.reshape(row_count, model_width)]
  transfers between devices with their start and end apart: 6 -> 6, of which waited for: 5 -> 3; matrix products, arithmetic and copies ran while one was open for 26% -> 2% of each run, Pallas kernels for 0% -> 14%
where the time goes in v1:
time: 459 us; the launch traced here: 458 us
  waiting for transfers between devices  252 us (55%)
  Pallas kernels  111 us (24%)
  blocking collectives  40 us (9%)
  local copies, waits for them, and re-layouts  22.3 us (5%)
  between operations  17.5 us (4%)
  other arithmetic  15.9 us (3%)
    psum x1, waiting for transfers between devices, local(): lax.psum((joined_part, out_part, sort_part), both)  123 us
    psum x1, waiting for transfers between devices, local(): lax.psum(lax.psum_scatter(down_part, 'mp', scatter_dimension=1, tiled=Tru...  94.3 us
    pallas_call x1, Pallas kernels, feed(): pl.pallas_call(functools.partial(feed_kernel, chunk=chunk), grid=(rows //...  46.8 us
    psum x1, blocking collectives, local(): grad_gain_two, entropy_all = lax.psum((gain_two_part, entropy), both)  40 us
    all_gather x1, waiting for transfers between devices, local(): down_all = lax.all_gather(w_down.astype(BF16), 'mp', axis=0, tiled=True)  33.6 us
    unnamed x63, local copies, waits for them, and re-layouts  22.1 us
    pallas_call x1, Pallas kernels, attend_back(): pl.pallas_call(attend_back_kernel, grid_spec=grid_spec, out_shape=[low, l...  17.9 us
    pallas_call x1, Pallas kernels, attend(): pl.pallas_call(attend_kernel, grid_spec=grid_spec, out_shape=[shape_of((2...  16.7 us
  transfers between devices with their start and end apart: 6, of which 3 were waited for; matrix products, arithmetic and copies ran while one was open for 2% of the time, Pallas kernels for 14%

profile of v1, /device:TPU:0, one launch (start us, length us, event | category | flops | bytes accessed | tf_op | source)
XLA Modules:
  0.0 458.2 jit_solution(3569473804922941398)
XLA Ops:
  7.2 2.7 convert_element_type.34
  10.1 2.8 convert_element_type.35
  13.2 1.2 copy-done.3
  14.5 7.6 %project.1 = (bf16[2048,512]{1,0:T(8,128)(2,1)S(1)}, bf16[2048,512]{1,0:T(8,128)(2,1)}, bf16[2048,512]{1,0:T(8,128)(2,1)}, bf16[2048,512]{1,0:T(8,128)(2,1)}, f32[64,512]{1,0:T(8,128)S(1)}) custom-call(f32[2048,512]{1,0:T(8,128)} %bitcast.35, f32[1,512]{1,0:T(1,128)S(1)} %bitcast.27, f32[512,512]{1,0:T(8,128)S(1)} %copy-done.1, f32[512,512]{1,0:T(8,128)S(1)} %copy-done.2, ...), custom_call_target="tpu_custom_call" | custom-call | flops 3221225472 | bytes 15728640 | tf_op jit(solution)/shard_map/project/pallas_call | solution.py:93
  22.1 1.3 copy-done.25
  23.4 2.8 balance.1
  26.3 1.3 copy-done.10
  28.3 16.7 %attend.1 = (bf16[4096,256]{1,0:T(8,128)(2,1)S(1)}, bf16[2048,512]{1,0:T(8,128)(2,1)S(1)}, f32[2048,512]{1,0:T(8,128)}, bf16[2048,512]{1,0:T(8,128)(2,1)}) custom-call(s32[64]{0:T(128)S(1)} %bitcast.31, s32[64]{0:T(128)S(1)} %bitcast.34, bf16[2048,512]{1,0:T(8,128)(2,1)} %get-tuple-element.38.q_ref, bf16[2048,512]{1,0:T(8,128)(2,1)} %get-tuple-element.39.k_ref, ...), custom_call_target="tpu_custom_call" | custom-call | tf_op jit(solution)/shard_map/attend/pallas_call | solution.py:295
  45.0 1.3 copy-done.12
  46.3 1.4 copy-done.24
  47.7 33.6 %all-gather.5.cloned.1.call-done.down_ref = bf16[2048,512]{1,0:T(8,128)(2,1)} async-done(((bf16[1024,512]{1,0:T(8,128)(2,1)}), bf16[2048,512]{1,0:T(8,128)(2,1)}) %all-gather.5.cloned.1.call-update) | async-done | bytes 2097168 | tf_op jit(solution)/shard_map/all_gather | solution.py:554
  81.3 46.8 %feed.1 = (f32[2048,512]{1,0:T(8,128)}, f32[2048,512]{1,0:T(8,128)}, bf16[2048,512]{1,0:T(8,128)(2,1)}, bf16[512,2048]{1,0:T(8,128)(2,1)}, bf16[512,2048]{1,0:T(...) custom-call(bf16[2048,512]{1,0:T(8,128)(2,1)} %get-tuple-element.43.act_ref, ...), custom_call_target="tpu_custom_call" | custom-call | flops 25769803776 | bytes 31457280 | tf_op jit(solution)/shard_map/feed/pallas_call | solution.py:446
  130.2 17.9 %attend_back.1 = (bf16[2048,512]{1,0:T(8,128)(2,1)}, bf16[2048,512]{1,0:T(8,128)(2,1)}, bf16[2048,512]{1,0:T(8,128)(2,1)}, f32[64,512]{1,0:T(8,128)}) custom-call(s32[64]{0:T(128)} %bitcast.29, bf16[2048,512]{1,0:T(8,128)(2,1)} %get-tuple-element.38.q_ref, bf16[2048,512]{1,0:T(8,128)(2,1)} %get-tuple-element.48.gatt_ref, bf16[4096,256]{1,0:T(8,128)(2,1)} %copy-done.12, ...), custom_call_target="tpu_custom_call" | custom-call | tf_op jit(solution)/shard_map/attend_back/pallas_call | solution.py:376
  148.1 40.0 %all-reduce = (f32[1,512]{1,0:T(1,128)S(1)}, f32[]{:T(128)}, f32[512]{0:T(512)}) all-reduce(f32[1,512]{1,0:T(1,128)S(1)} %get-tuple-element.47, f32[]{:T(128)} %convert_reduce_fusion, f32[512]{0:T(512)S(1)} %bitcast.40), channel_id=1, replica_groups=mesh['batch'=16,'mp'=2] {'batch','mp'}, use_global_device_ids=true, to_apply=%region_0.0 | all-reduce | flops 1025 | bytes 8200 | tf_op jit(solution)/shard_map/psum | solution.py:569
  188.8 1.8 copy-done.11
  190.6 0.9 copy-done.18
  192.4 3.2 balance_back.1
  196.5 1.6 copy-done.8
  198.1 1.6 copy-done.9
  199.7 1.6 copy-done.26
  201.3 4.4 weight_grads.1
  205.7 1.1 copy-done.13
  208.7 1.2 copy-done.4
  209.9 1.6 copy-done.7
  211.5 11.1 %input_grad.1 = f32[2048,512]{1,0:T(8,128)} custom-call(bf16[2048,512]{1,0:T(8,128)(2,1)S(1)} %copy-done.7, bf16[2048,512]{1,0:T(8,128)(2,1)} %get-tuple-element.51.gk_ref, bf16[2048,512]{1,0:T(8,128)(2,1)} %get-tuple-element.52.gv_ref, f32[64,512]{1,0:T(8,128)S(1)} %get-tuple-element.56.gsum_ref, f32[2048,512]{1,0:T(8,128)} %bitcast.37, ...), custom_call_target="tpu_custom_call" | custom-call | flops 3221225472 | bytes 22020096 | tf_op jit(solution)/shard_map/input_grad/pallas_call | solution.py:521
  222.6 122.6 %all-reduce.6.cloned.1.call-done = (bf16[3,512,512]{2,1,0:T(8,128)(2,1)}, bf16[512,512]{1,0:T(8,128)(2,1)}, bf16[512,512]{1,0:T(8,128)(2,1)}) async-done(((bf16[3,512,512]{2,1,0:T(8,128)(2,1)}, bf16[512,512]{1,0:T(8,128)(2,1)}, bf16[512,512]{1,0:T(8,128)(2,1)}), (bf16[3,512,512]{2,1,0:T(8,128)(2,1)}, bf16[512,512]{1,0:T(8,128)(2,1)}, bf16[512,512]{1,0:T(8,128)(2,1)})) %all-reduce.6.cloned.1.call-update) | async-done | bytes 2621456 | tf_op jit(solution)/shard_map/psum | solution.py:568
  345.3 2.0 convert_element_type.37
  347.3 1.1 convert_element_type.38
  348.4 2.5 multiply_reduce_fusion
  351.5 94.3 %all-reduce.8.cloned.1.call-done = (bf16[1024,512]{0,1:T(8,128)(2,1)}, bf16[512,1024]{1,0:T(8,128)(2,1)}) async-done(((bf16[1024,512]{0,1:T(8,128)(2,1)}, bf16[512,1024]{1,0:T(8,128)(2,1)}), (bf16[1024,512]{0,1:T(8,128)(2,1)}, bf16[512,1024]{1,0:T(8,128)(2,1)})) %all-reduce.8.cloned.1.call-update) | async-done | bytes 2097168 | tf_op jit(solution)/shard_map/psum | solution.py:567
  445.8 2.9 convert_element_type.40
  448.7 1.6 copy.30
  (70 shorter events, 6.0 us)
Async XLA Ops:
  7.2 40.5 %all-gather.3.cloned.1.call-start = ((), (), s32[]{:S(2)}) async-start(), calls=%async_computation.2 | async-start | bytes 3145728 | tf_op jit(solution)/shard_map/all_gather | solution.py:553
  10.0 3.0 copy-start.23
  10.0 3.1 copy-start.21
  10.0 3.2 copy-start.1
  10.0 3.2 copy-start.2
  10.0 3.2 copy-start.20
  10.0 71.2 %all-gather.5.cloned.1.call-start = ((), (), s32[]{:S(2)}) async-start(), calls=%async_computation.3 | async-start | bytes 3145728 | tf_op jit(solution)/shard_map/all_gather | solution.py:554
  12.9 194.0 %reduce-scatter.5.cloned.1.call-start = ((), (), s32[]{:S(2)}) async-start(), calls=%async_computation.5 | async-start | bytes 3145728 | tf_op jit(solution)/shard_map/reduce_scatter | solution.py:567
  13.2 1.2 copy-start.3
  14.5 9.0 %copy-start = (f32[512,512]{1,0:T(8,128)S(1)}, f32[512,512]{1,0:T(8,128)}, u32[]{:S(2)}) copy-start(f32[512,512]{1,0:T(8,128)} %w_ref.3) | copy-start | bytes 3145732
  14.5 13.8 %copy-start.14 = (f32[512,512]{1,0:T(8,128)S(1)}, f32[512,512]{1,0:T(8,128)}, u32[]{:S(2)}) copy-start(f32[512,512]{1,0:T(8,128)} %wo_ref.3) | copy-start | bytes 3145732
  14.5 13.8 %copy-start.22 = (f32[512]{0:T(512)S(1)}, f32[512]{0:T(512)}, u32[]{:S(2)}) copy-start(f32[512]{0:T(512)} %param.25) | copy-start | bytes 6148
  22.1 1.4 copy-start.25
  26.3 1.3 copy-start.10
  28.3 16.7 %copy-start.15 = (f32[64,512]{1,0:T(8,128)}, f32[64,512]{1,0:T(8,128)S(1)}, u32[]{:S(2)}) copy-start(f32[64,512]{1,0:T(8,128)S(1)} %get-tuple-element.42.chosen_ref) | copy-start | bytes 393220
  45.0 1.3 copy-start.12
  46.3 1.4 copy-start.24
  128.1 78.8 %reduce-scatter.3.cloned.1.call-start = ((), (), s32[]{:S(2)}) async-start(), calls=%async_computation.4 | async-start | bytes 3145728 | tf_op jit(solution)/shard_map/reduce_scatter | solution.py:566
  128.7 216.5 %all-reduce.6.cloned.1.call-start = ((), (), s32[]{:S(2)}) async-start(), calls=%async_computation.6 | async-start | bytes 5242880 | tf_op jit(solution)/shard_map/psum | solution.py:568
  130.2 17.9 %copy-start.30 = (f32[1,512]{1,0:T(1,128)S(1)}, f32[1,512]{1,0:T(1,128)}, u32[]{:S(2)}) copy-start(f32[1,512]{1,0:T(1,128)} %get-tuple-element.61) | copy-start | bytes 6148
  188.8 7.7 %copy-start.6 = (bf16[2048,512]{1,0:T(8,128)(2,1)S(1)}, bf16[2048,512]{1,0:T(8,128)(2,1)}, u32[]{:S(2)}) copy-start(bf16[2048,512]{1,0:T(8,128)(2,1)} %get-tuple-element.50.gq_ref) | copy-start | bytes 6291460
  188.8 1.8 copy-start.11
  196.5 1.6 copy-start.8
  198.1 1.6 copy-start.9
  199.7 1.6 copy-start.26
  206.9 238.9 %all-reduce.8.cloned.1.call-start = ((), (), s32[]{:S(2)}) async-start(), calls=%async_computation.7 | async-start | bytes 4194304 | tf_op jit(solution)/shard_map/psum | solution.py:567
  208.7 1.2 copy-start.4
  209.9 1.6 copy-start.7
  345.2 2.0 copy-start.29
  345.3 3.1 copy-start.5
  345.3 3.1 copy-start.28
  445.8 2.9 copy-start.27
  (5 other events, 4.4 us)
Sparse Core Ops, SparseCore 0:
  10.1 35.8 all-gather.2
  48.1 33.1 all-gather.4
  128.2 32.3 reduce-scatter.4
  162.8 32.5 reduce-scatter.2
  207.0 138.2 all-reduce.5
  349.1 96.5 all-reduce.7

commit v2 on v0

v2 whole, which is shorter than its diff:
```python
import functools

import jax
import jax.numpy as jnp
from jax import lax
from jax.experimental import pallas as pl
from jax.experimental.pallas import tpu as pltpu
from jax.sharding import PartitionSpec as P

HEADS = 8
HEAD_DIM = 64
BLOCK = 32
ITERS = 8
GROUP = 4
GROUP_WIDTH = GROUP * HEAD_DIM
GROUP_ROWS = GROUP * BLOCK
EPSILON = 1e-05
FACTOR = HEAD_DIM ** (-0.5)
HIGHEST = lax.Precision.HIGHEST
F32 = jnp.float32
BF16 = jnp.bfloat16
NT = (((1,), (1,)), ((), ()))
TN = (((0,), (0,)), ((), ()))
MIB = 1024 * 1024
LANES = 128


def dot(left, right):
    return jnp.dot(left, right, preferred_element_type=F32)


def dot_nt(left, right):
    return lax.dot_general(left, right, NT, preferred_element_type=F32)


def dot_tn(left, right):
    return lax.dot_general(left, right, TN, preferred_element_type=F32)


def shape_of(dims, dtype):
    return jax.ShapeDtypeStruct(dims, dtype)


def whole(dims):
    return pl.BlockSpec(dims, lambda *_: (0,) * len(dims))


def once(dims):
    return pl.BlockSpec(dims, lambda *_: (0,) * len(dims), pipeline_mode=pl.Buffered(1))


def rows_of(size, width):
    return pl.BlockSpec((size, width), lambda step, *_: (step, 0))


def params(mib):
    return pltpu.CompilerParams(vmem_limit_bytes=mib * MIB)


def far(array):
    return pltpu.with_memory_space_constraint(array, pltpu.HBM)


def near(array):
    return pltpu.with_memory_space_constraint(array, pltpu.VMEM)


def near_shape(dims, dtype):
    return pltpu.VMEM(dims, dtype)


def far_shape(dims, dtype):
    return pltpu.HBM(dims, dtype)


def cost(wide):
    return pl.CostEstimate(flops=100000000000 if wide else 1000000, bytes_accessed=0, transcendentals=0)


def normalize(values):
    center = values - jnp.mean(values, axis=-1, keepdims=True)
    inverse = lax.rsqrt(jnp.mean(center * center, axis=-1, keepdims=True) + EPSILON)
    return center * inverse, inverse


def norm_grad(grad_rows, unit_rows, inverse, gain):
    scaled_rows = grad_rows * gain
    return inverse * (
        scaled_rows
        - jnp.mean(scaled_rows, axis=-1, keepdims=True)
        - unit_rows * jnp.mean(scaled_rows * unit_rows, axis=-1, keepdims=True)
    )


def segment_sum(tile, first):
    left = jnp.sum(jnp.where(first, tile, 0.0), axis=1, keepdims=True)
    right = jnp.sum(jnp.where(first, 0.0, tile), axis=1, keepdims=True)
    return jnp.where(first, left, right)


def segment_max(tile, first):
    left = jnp.max(jnp.where(first, tile, -jnp.inf), axis=1, keepdims=True)
    right = jnp.max(jnp.where(first, -jnp.inf, tile), axis=1, keepdims=True)
    return jnp.where(first, left, right)


def head_masks(rows):
    lane = lax.broadcasted_iota(jnp.int32, (rows, GROUP_WIDTH), 1)
    return [(lane >= h * HEAD_DIM) & (lane < (h + 1) * HEAD_DIM) for h in range(GROUP)]


def expand(rows, masks):
    zero = jnp.zeros_like(rows)
    return jnp.concatenate([jnp.where(mask, rows, zero) for mask in masks], axis=0)


def fold(rows, masks):
    parts = [rows[h * BLOCK : (h + 1) * BLOCK] for h in range(GROUP)]
    result = parts[GROUP - 1]
    for h in range(GROUP - 1):
        result = jnp.where(masks[h], parts[h], result)
    return result


def lane_tiles(blocks):
    lane = lax.broadcasted_iota(jnp.int32, (blocks, 2 * blocks), 1)
    return lane < blocks, jnp.where(lane < blocks, lane, lane - blocks).astype(F32)


def down_rows(row, wide):
    return jnp.broadcast_to(row.astype(F32), (wide, row.shape[1])).T


def balance_plans(logits, perm_row, mask_row, share_ref, log_ref, chosen_ref, entropy_ref):
    blocks = logits.shape[0]
    wide = 2 * blocks
    first, position = lane_tiles(blocks)
    hot = position == down_rows(perm_row, wide)
    real = down_rows(mask_row, wide) > 0.0
    for pair in range(logits.shape[1] // wide):
        span = slice(pair * wide, (pair + 1) * wide)
        tile = logits[:, span]
        for step in range(ITERS):
            top = segment_max(tile, first)
            powers = jnp.exp(tile - top)
            total = segment_sum(powers, first)
            tile = tile - (top + jnp.log(total))
            share_ref[2 * step, :, span] = powers * (1.0 / total)
            top = jnp.max(tile, axis=0, keepdims=True)
            powers = jnp.exp(tile - top)
            total = jnp.sum(powers, axis=0, keepdims=True)
            tile = tile - (top + jnp.log(total))
            if step < ITERS - 1:
                share_ref[2 * step + 1, :, span] = powers * (1.0 / total)
        plan = jnp.exp(tile)
        share_ref[2 * ITERS - 1, :, span] = plan
        log_ref[:, span] = tile
        chosen_ref[:, span] = blocks * segment_sum(jnp.where(hot, plan, 0.0), first)
        entropy_ref[:, span] = -jnp.sum(jnp.where(real, plan * tile, 0.0), axis=0, keepdims=True)


def forward_kernel(
    perm_ref, mask_ref, perm_row_ref, mask_row_ref, gain_one_ref, gain_two_ref,
    x_far, wq_far, wk_far, wv_far, ws_far, wo_far,
    act_far, q_far, k_far, v_far, probs_far, att_far, second_far, share_far,
    act_two_ref, sum_ref, log_ref, chosen_ref, entropy_ref,
    x_ref, w_ref, w_low_ref, wo_low_ref, act_ref, q_ref, k_ref, v_ref, probs_ref, att_ref, second_ref, share_ref,
    in_sem, out_sem, share_sem, *, tile,
):
    rows, width = x_ref.shape
    tiles = rows // tile

    def x_copy(i):
        at = pl.ds(pl.multiple_of(i * tile, tile), tile)
        return pltpu.make_async_copy(x_far.at[at, :], x_ref.at[at, :], in_sem.at[i])

    def w_copy(n):
        far_ref = (wq_far, wk_far, wv_far, ws_far, wo_far)[n]
        return pltpu.make_async_copy(far_ref, w_ref.at[n], in_sem.at[tiles + n])

    outs = (
        (act_ref, act_far), (q_ref, q_far), (k_ref, k_far), (v_ref, v_far),
        (probs_ref, probs_far), (att_ref, att_far), (second_ref, second_far),
    )

    def out_copy(n, i):
        near_ref, far_ref = outs[n]
        size = near_ref.shape[0] // tiles
        at = pl.ds(pl.multiple_of(i * size, size), size)
        return pltpu.make_async_copy(near_ref.at[at, :], far_ref.at[at, :], out_sem.at[n, i])

    x_copy(0).start()
    for n in range(3):
        w_copy(n).start()
    for i in range(1, tiles):
        x_copy(i).start()
    w_copy(3).start()
    w_copy(4).start()
    for n in range(3):
        w_copy(n).wait()
        w_low_ref[:, n * width : (n + 1) * width] = w_ref[n].astype(BF16)

    def project(i, _):
        x_copy(i).wait()
        at = pl.ds(pl.multiple_of(i * tile, tile), tile)
        unit, _ = normalize(x_ref[at, :])
        act = (unit * gain_one_ref[...]).astype(BF16)
        act_ref[at, :] = act
        for n, ref in enumerate((q_ref, k_ref, v_ref)):
            ref[at, :] = dot(act, w_low_ref[:, n * width : (n + 1) * width]).astype(BF16)
        sums = jnp.sum(act.astype(F32).reshape(tile // BLOCK, BLOCK, width), axis=1)
        some = tile // BLOCK
        sum_ref[pl.ds(pl.multiple_of(i * some, some), some), :] = sums.astype(BF16).astype(F32)
        for n in range(4):
            out_copy(n, i).start()
        return 0

    lax.fori_loop(0, tiles, project, 0)
    w_copy(3).wait()
    w_copy(4).wait()
    wo_low_ref[...] = w_ref[4].astype(BF16)
    logits = jnp.dot(sum_ref[...], w_ref[3], precision=HIGHEST, preferred_element_type=F32)
    balance_plans(
        logits, perm_row_ref[...], mask_row_ref[...], share_ref, log_ref, chosen_ref, entropy_ref
    )
    pltpu.make_async_copy(share_ref, share_far, share_sem).start()

    masks = head_masks(BLOCK)
    key_row = lax.broadcasted_iota(jnp.int32, (BLOCK, GROUP_ROWS), 0)
    query_row = lax.broadcasted_iota(jnp.int32, (BLOCK, GROUP_ROWS), 1) % BLOCK
    causal = key_row <= query_row
    part = 8

    def attend(j, _):
        for b in range(part):
            block = j * part + b
            partner = perm_ref[block]
            usable = (partner < block) & (mask_ref[partner] > 0)
            own_at = pl.ds(pl.multiple_of(block * BLOCK, BLOCK), BLOCK)
            far_at = pl.ds(pl.multiple_of(partner * BLOCK, BLOCK), BLOCK)
            probs_at = pl.ds(pl.multiple_of(block * 2 * BLOCK, 2 * BLOCK), 2 * BLOCK)
            chosen_row = chosen_ref[pl.ds(block, 1), :]
            for g in range(width // GROUP_WIDTH):
                lanes = slice(g * GROUP_WIDTH, (g + 1) * GROUP_WIDTH)
                queries = expand(q_ref[own_at, lanes], masks)
                keys = jnp.concatenate([k_ref[own_at, lanes], k_ref[far_at, lanes]], axis=0)
                scores = dot_nt(keys, queries) * FACTOR
                own = jnp.where(causal, scores[:BLOCK], -1e30)
                far = jnp.where(usable, scores[BLOCK:], -1e30)
                top = jnp.maximum(jnp.max(own, axis=0, keepdims=True), jnp.max(far, axis=0, keepdims=True))
                powers = jnp.exp(jnp.concatenate([own, far], axis=0) - top)
                probs = (powers * (1.0 / jnp.sum(powers, axis=0, keepdims=True))).astype(BF16)
                probs_ref[probs_at, g * GROUP_ROWS : (g + 1) * GROUP_ROWS] = probs
                scaled = (v_ref[far_at, lanes].astype(F32) * chosen_row[:, lanes]).astype(BF16)
                values = jnp.concatenate([v_ref[own_at, lanes], scaled], axis=0)
                att_ref[own_at, lanes] = fold(dot_tn(probs, values), masks).astype(BF16)
        return 0

    def finish_tile(i, _):
        per = tile // BLOCK // part
        lax.fori_loop(i * per, (i + 1) * per, attend, 0)
        at = pl.ds(pl.multiple_of(i * tile, tile), tile)
        second = x_ref[at, :] + dot(att_ref[at, :], wo_low_ref[...])
        second_ref[at, :] = second
        unit, _ = normalize(second)
        act_two_ref[at, :] = (unit * gain_two_ref[...]).astype(BF16)
        for n in range(4, 7):
            out_copy(n, i).start()
        return 0

    lax.fori_loop(0, tiles, finish_tile, 0)
    for n in range(7):
        for i in range(tiles):
            out_copy(n, i).wait()
    pltpu.make_async_copy(share_ref, share_far, share_sem).wait()


def forward(perm, mask, perm_row, mask_row, gain_one, gain_two, x, wq, wk, wv, ws, wo, tile=512):
    rows, width = x.shape
    blocks = rows // BLOCK
    tiles = rows // tile
    smem = pl.BlockSpec(memory_space=pltpu.SMEM)
    vmem = pl.BlockSpec(memory_space=pltpu.VMEM)
    hbm = pl.BlockSpec(memory_space=pltpu.HBM)
    low = ((rows, width), BF16)
    probs = ((2 * rows, HEADS * BLOCK), BF16)
    full = ((rows, width), F32)
    share = ((2 * ITERS, blocks, width), F32)
    plan = ((blocks, width), F32)
    return pl.pallas_call(
        functools.partial(forward_kernel, tile=tile),
        in_specs=[smem] * 2 + [vmem] * 4 + [hbm] * 6,
        out_specs=[hbm] * 8 + [vmem] * 5,
        out_shape=[far_shape(*s) for s in (low, low, low, low, probs, low, full, share)]
        + [near_shape(*s) for s in (low, plan, plan, plan, ((1, width), F32))],
        scratch_shapes=[pltpu.VMEM(*full), pltpu.VMEM((5, width, width), F32), pltpu.VMEM((width, 3 * width), BF16)]
        + [pltpu.VMEM((width, width), BF16)]
        + [pltpu.VMEM(*s) for s in (low, low, low, low, probs, low, full, share)]
        + [
            pltpu.SemaphoreType.DMA((tiles + 5,)),
            pltpu.SemaphoreType.DMA((7, tiles)),
            pltpu.SemaphoreType.DMA,
        ],
        compiler_params=params(44),
        cost_estimate=cost(True),
        name="forward",
    )(perm, mask, perm_row, mask_row, gain_one, gain_two, far(x), far(wq), far(wk), far(wv), far(ws), far(wo))


def attend_back_kernel(
    perm_ref, q_ref, gatt_ref, probs_ref, k_ref, v_ref, chosen_ref,
    gq_ref, gk_ref, gv_ref, gch_ref, own_k_ref, far_k_ref, own_v_ref, far_v_ref,
):
    tile_index = pl.program_id(0)
    rows = q_ref.shape[0]
    blocks = rows // BLOCK
    masks = head_masks(BLOCK)
    for b in range(blocks):
        block = tile_index * blocks + b
        partner = perm_ref[block]
        own_at = pl.ds(pl.multiple_of(block * BLOCK, BLOCK), BLOCK)
        far_at = pl.ds(pl.multiple_of(partner * BLOCK, BLOCK), BLOCK)
        here = slice(b * BLOCK, (b + 1) * BLOCK)
        queries = expand(q_ref[here, :], masks)
        grads = expand(gatt_ref[here, :], masks)
        keys = jnp.concatenate([k_ref[own_at, :], k_ref[far_at, :]], axis=0)
        far_values = v_ref[far_at, :].astype(F32)
        chosen = chosen_ref[b : b + 1, :]
        values = jnp.concatenate([v_ref[own_at, :], (far_values * chosen).astype(BF16)], axis=0)
        probs_low = probs_ref[b * 2 * BLOCK : (b + 1) * 2 * BLOCK, :]
        probs = probs_low.astype(F32)
        grad_probs = dot_nt(values, grads)
        total = jnp.sum(probs * grad_probs, axis=0, keepdims=True)
        grad_scores = (probs * (grad_probs - total)).astype(BF16)
        grad_keys = dot(grad_scores, queries) * FACTOR
        grad_values = dot(probs_low, grads)
        gq_ref[here, :] = (fold(dot_tn(grad_scores, keys), masks) * FACTOR).astype(BF16)
        far_grad = grad_values[BLOCK:]
        gch_ref[b : b + 1, :] = jnp.sum(far_grad * far_values, axis=0, keepdims=True)
        own_k_ref[own_at, :] = grad_keys[:BLOCK]
        far_k_ref[far_at, :] = grad_keys[BLOCK:]
        own_v_ref[own_at, :] = grad_values[:BLOCK]
        far_v_ref[far_at, :] = far_grad * chosen

    @pl.when(tile_index == pl.num_programs(0) - 1)
    def _():
        gk_ref[...] = (own_k_ref[...] + far_k_ref[...]).astype(BF16)
        gv_ref[...] = (own_v_ref[...] + far_v_ref[...]).astype(BF16)


def attend_back(perm, q, gatt, probs, k, v, chosen, group, tile=256):
    rows, width = q.shape
    low = near_shape((rows, GROUP_WIDTH), BF16)

    def lanes(size, cols):
        return pl.BlockSpec((size, cols), lambda step, *_: (step, group))

    full = pl.BlockSpec((rows, GROUP_WIDTH), lambda step, *_: (0, group), pipeline_mode=pl.Buffered(1))
    grid_spec = pltpu.PrefetchScalarGridSpec(
        num_scalar_prefetch=1,
        grid=(rows // tile,),
        in_specs=[
            lanes(tile, GROUP_WIDTH),
            lanes(tile, GROUP_WIDTH),
            lanes(2 * tile, GROUP_ROWS),
            full,
            full,
            lanes(tile // BLOCK, GROUP_WIDTH),
        ],
        out_specs=[
            rows_of(tile, GROUP_WIDTH),
            whole((rows, GROUP_WIDTH)),
            whole((rows, GROUP_WIDTH)),
            rows_of(tile // BLOCK, GROUP_WIDTH),
        ],
        scratch_shapes=[pltpu.VMEM((rows, GROUP_WIDTH), F32)] * 4,
    )
    return pl.pallas_call(
        attend_back_kernel,
        grid_spec=grid_spec,
        out_shape=[low, low, low, shape_of((rows // BLOCK, GROUP_WIDTH), F32)],
        compiler_params=params(20),
        cost_estimate=cost(group > 0),
        name="attend_back",
    )(perm, near(q), near(gatt), near(probs), near(k), near(v), near(chosen))


def gelu_pair(up):
    square = up * up
    inner = 0.7978845608028654 * 0.044715
    half = 0.5 + 0.5 * jnp.tanh(up * (0.7978845608028654 + inner * square))
    value = up * half
    slope = half + (2.0 * value) * (1.0 - half) * (0.7978845608028654 + 3.0 * inner * square)
    return value, slope


def spread(out_ref, acc_ref, where, lanes):
    chunks, size = out_ref.shape[0], out_ref.shape[-2]
    for r in range(chunks):
        at = pl.multiple_of((r ^ where) * size, size)
        out_ref[r, :, lanes] = acc_ref[pl.ds(at, size), :].astype(out_ref.dtype)


def quarter_math(act, cot_low, weights_ref, hidden_ref, up_acc, down_acc):
    value, slope = gelu_pair(dot(act, weights_ref[0]))
    hidden = value.astype(BF16)
    hidden_ref[...] = hidden
    grad_up = (dot_nt(cot_low, weights_ref[1]) * slope).astype(BF16)
    up_acc[...] += dot_tn(act, grad_up)
    down_acc[...] += dot_tn(cot_low, hidden)
    return dot_nt(grad_up, weights_ref[0])


def first_quarter_kernel(
    where_ref, act_ref, cot_ref, weights_ref,
    low_ref, grad_ref, hidden_ref, piece_ref, up_acc, down_acc,
):
    @pl.when(pl.program_id(0) == 0)
    def _():
        up_acc[...] = jnp.zeros_like(up_acc)
        down_acc[...] = jnp.zeros_like(down_acc)

    cot_low = cot_ref[...].astype(BF16)
    low_ref[...] = cot_low
    grad_ref[...] = quarter_math(act_ref[...], cot_low, weights_ref, hidden_ref, up_acc, down_acc)

    @pl.when(pl.program_id(0) == pl.num_programs(0) - 1)
    def _():
        spread(piece_ref.at[:, 0], up_acc, where_ref[0], slice(None))
        spread(piece_ref.at[:, 1], down_acc, where_ref[0], slice(None))


def quarter_kernel(
    where_ref, act_ref, cot_ref, weights_ref, sofar_ref,
    grad_ref, hidden_ref, piece_ref, up_acc, down_acc,
):
    @pl.when(pl.program_id(0) == 0)
    def _():
        up_acc[...] = jnp.zeros_like(up_acc)
        down_acc[...] = jnp.zeros_like(down_acc)

    grad_ref[...] = sofar_ref[...] + quarter_math(
        act_ref[...], cot_ref[...], weights_ref, hidden_ref, up_acc, down_acc
    )

    @pl.when(pl.program_id(0) == pl.num_programs(0) - 1)
    def _():
        spread(piece_ref.at[:, 0], up_acc, where_ref[0], slice(None))
        spread(piece_ref.at[:, 1], down_acc, where_ref[0], slice(None))


def settle_kernel(
    where_ref, grad_ref, cot_ref, second_ref, att_ref, wo_ref, gain_ref, entropy_ref,
    gsec_ref, gatt_ref, gout_ref, out_acc, gain_acc, column_ref, wo_low_ref,
):
    width = grad_ref.shape[1]

    @pl.when(pl.program_id(0) == 0)
    def _():
        out_acc[...] = jnp.zeros_like(out_acc)
        gain_acc[...] = jnp.zeros_like(gain_acc)
        wo_low_ref[...] = wo_ref[...].astype(BF16)

    grad_normed = grad_ref[...]
    unit, inverse = normalize(second_ref[...])
    gain_acc[...] += jnp.sum(grad_normed * unit, axis=0, keepdims=True)
    grad_second = cot_ref[...] + norm_grad(grad_normed, unit, inverse, gain_ref[...])
    gsec_ref[...] = grad_second
    second_low = grad_second.astype(BF16)
    gatt_ref[...] = dot_nt(second_low, wo_low_ref[...]).astype(BF16)
    out_acc[...] += dot_tn(att_ref[...], second_low)

    @pl.when(pl.program_id(0) == pl.num_programs(0) - 1)
    def _():
        spread(gout_ref, out_acc, where_ref[2], slice(0, width))
        half = (LANES // 2, width)
        column_ref[...] = jnp.concatenate(
            [jnp.broadcast_to(gain_acc[...], half), jnp.broadcast_to(entropy_ref[...], half)], axis=0
        ).T
        spread(gout_ref, column_ref, where_ref[2], slice(width, width + LANES))


def settle(where, grad, cot, second, att, w_out, gain, entropy, out_chunks, tile=512):
    rows, width = grad.shape
    out_piece = (out_chunks, width // out_chunks, width + LANES)
    return pl.pallas_call(
        settle_kernel,
        grid_spec=pltpu.PrefetchScalarGridSpec(
            num_scalar_prefetch=1,
            grid=(rows // tile,),
            in_specs=[rows_of(tile, width)] * 4
            + [pl.BlockSpec((width, width), lambda *_: (0, 0), pipeline_mode=pl.Buffered(1))]
            + [whole((1, width))] * 2,
            out_specs=[rows_of(tile, width)] * 2 + [whole(out_piece)],
            scratch_shapes=[
                pltpu.VMEM((width, width), F32),
                pltpu.VMEM((1, width), F32),
                pltpu.VMEM((width, LANES), F32),
                pltpu.VMEM((width, width), BF16),
            ],
        ),
        out_shape=[far_shape((rows, width), F32), near_shape((rows, width), BF16), near_shape(out_piece, BF16)],
        compiler_params=params(20),
        cost_estimate=cost(False),
        name="settle",
    )(where, near(grad), near(cot), near(second), near(att), far(w_out), gain, entropy)


def feed_quarter(where, act, cot, weights, sofar, row_chunks, tile=512):
    rows, width = act.shape
    units = weights.shape[2]
    resident = pl.BlockSpec(weights.shape, lambda *_: (0, 0, 0), pipeline_mode=pl.Buffered(1))
    piece = (row_chunks, 2, width // row_chunks, units)
    in_specs = [rows_of(tile, width), rows_of(tile, width), resident]
    out_shape = [near_shape((rows, width), F32), far_shape((rows, units), BF16)] + [near_shape(piece, BF16)]
    out_specs = [rows_of(tile, width), rows_of(tile, units), whole(piece)]
    aliases = {}
    if sofar is None:
        kernel, operands = first_quarter_kernel, (near(act), near(cot), near(weights))
        out_shape = [near_shape((rows, width), BF16)] + out_shape
        out_specs = [rows_of(tile, width)] + out_specs
    else:
        kernel, operands = quarter_kernel, (near(act), near(cot), near(weights), near(sofar))
        in_specs = in_specs + [rows_of(tile, width)]
    return pl.pallas_call(
        kernel,
        grid_spec=pltpu.PrefetchScalarGridSpec(
            num_scalar_prefetch=1,
            grid=(rows // tile,),
            in_specs=in_specs,
            out_specs=out_specs,
            scratch_shapes=[pltpu.VMEM((width, units), F32)] * 2,
        ),
        out_shape=out_shape,
        input_output_aliases=aliases,
        compiler_params=params(18),
        cost_estimate=cost(True),
        name="feed_quarter",
    )(where, *operands)


def output_kernel(second_ref, *refs):
    out_ref = refs[-1]
    count = (len(refs) - 1) // 2
    total = second_ref[...]
    for hidden_ref, weights_ref in zip(refs[:count], refs[count : 2 * count]):
        total = total + dot(hidden_ref[...], weights_ref[0])
    out_ref[...] = total


def layer_output(second, hidden, weights, tile=512):
    rows, width = second.shape
    units = hidden[0].shape[1]
    down = pl.BlockSpec((1, units, width), lambda *_: (1, 0, 0), pipeline_mode=pl.Buffered(1))
    return pl.pallas_call(
        output_kernel,
        grid=(rows // tile,),
        in_specs=[rows_of(tile, width)] + [rows_of(tile, units)] * len(hidden) + [down] * len(hidden),
        out_specs=rows_of(tile, width),
        out_shape=far_shape((rows, width), F32),
        compiler_params=params(16),
        cost_estimate=cost(True),
        name="layer_output",
    )(near(second), *[far(array) for array in hidden], *[near(array) for array in weights])


def group_kernel(
    where_ref, coef_ref, act_ref, gq_ref, gk_ref, gv_ref,
    gch_ref, share_ref, log_ref, sum_ref, w_ref, perm_ref, mask_ref, extra_ref,
    piece_ref, gsum_ref, glog_ref, acc_ref, *, leading,
):
    blocks = sum_ref.shape[0]
    cols = gq_ref.shape[1]
    wide = 2 * blocks
    first, position = lane_tiles(blocks)
    hot = position == down_rows(perm_ref[...], wide)
    weight = coef_ref[0] * down_rows(mask_ref[...], wide)
    for pair in range(cols // wide):
        span = slice(pair * wide, (pair + 1) * wide)
        plan = share_ref[2 * ITERS - 1, :, span]
        gch = segment_sum(gch_ref[:, span], first)
        grad = plan * (jnp.where(hot, blocks * gch, 0.0) - weight * (log_ref[:, span] + 1.0))
        for level in range(2 * ITERS - 1, -1, -1):
            if level % 2:
                total = jnp.sum(grad, axis=0, keepdims=True)
            else:
                total = segment_sum(grad, first)
            grad = grad - share_ref[level, :, span] * total
        glog_ref[:, span] = grad
    act = act_ref[...]
    for index, ref in enumerate((gq_ref, gk_ref, gv_ref)):
        acc_ref[...] = dot_tn(act, ref[...])
        spread(piece_ref, acc_ref, where_ref[2], slice(index * cols, (index + 1) * cols))
    glog = glog_ref[...]
    acc_ref[...] = lax.dot_general(sum_ref[...], glog, TN, precision=HIGHEST, preferred_element_type=F32)
    spread(piece_ref, acc_ref, where_ref[2], slice(3 * cols, 4 * cols))
    gsum = lax.dot_general(glog, w_ref[...], NT, precision=HIGHEST, preferred_element_type=F32)
    if leading:
        piece_ref[:, :, 4 * cols :] = extra_ref[...]
    else:
        gsum = gsum + extra_ref[...]
    gsum_ref[...] = gsum


def group_grads(
    where, coef, act, gq, gk, gv, gch, shares, plan_log, sums, w_sort, perm_row, mask_row, extra, group, chunks
):
    rows, width = act.shape
    blocks = sums.shape[0]
    cols = gq.shape[1]
    smem = pl.BlockSpec(memory_space=pltpu.SMEM)
    one = pl.Buffered(1)

    def full(array):
        return pl.BlockSpec(array.shape, lambda *_: (0,) * array.ndim, pipeline_mode=one)

    def lanes(array):
        return pl.BlockSpec(
            array.shape[:-1] + (cols,), lambda *_: (0,) * (array.ndim - 1) + (group,), pipeline_mode=one
        )

    leading = group == 0
    piece = (chunks, width // chunks, 4 * cols + (extra.shape[2] if leading else 0))
    return pl.pallas_call(
        functools.partial(group_kernel, leading=leading),
        grid=(1,),
        in_specs=[smem, smem, full(act), full(gq), full(gk), full(gv), full(gch), lanes(shares), lanes(plan_log)]
        + [full(sums), lanes(w_sort), full(perm_row), full(mask_row), full(extra)],
        out_specs=[whole(piece), whole((blocks, width))],
        out_shape=[near_shape(piece, BF16), near_shape((blocks, width), F32)],
        scratch_shapes=[pltpu.VMEM((blocks, cols), F32), pltpu.VMEM((width, cols), F32)],
        compiler_params=params(16),
        cost_estimate=cost(group > 0),
        name="group_grads",
    )(
        where, coef, near(act), near(gq), near(gk), near(gv), gch, near(shares), near(plan_log), sums, far(w_sort),
        perm_row, mask_row, extra,
    )


def input_kernel(*refs):
    count = (len(refs) - 9) // 3
    groups = [refs[3 * g : 3 * g + 3] for g in range(count)]
    gsum_ref, x_ref, gsec_ref, gain_ref, wq_ref, wk_ref, wv_ref, out_ref, w_ref = refs[3 * count :]

    @pl.when(pl.program_id(0) == 0)
    def _():
        for which, ref in enumerate((wq_ref, wk_ref, wv_ref)):
            w_ref[which] = ref[...].astype(BF16)

    rows, width = x_ref.shape
    grad = jnp.zeros((rows, width), F32)
    for g, group in enumerate(groups):
        for which, ref in enumerate(group):
            cols = ref.shape[1]
            grad = grad + dot_nt(ref[...], w_ref[which, :, g * cols : (g + 1) * cols])
    grad = (grad.reshape(rows // BLOCK, BLOCK, width) + gsum_ref[...][:, None, :]).reshape(rows, width)
    unit, inverse = normalize(x_ref[...])
    out_ref[...] = gsec_ref[...] + norm_grad(grad, unit, inverse, gain_ref[...])


def input_grad(groups, gsum, x, gsec, gain, wq, wk, wv, tile=512):
    rows, width = x.shape
    weight = pl.BlockSpec((width, width), lambda *_: (0, 0), pipeline_mode=pl.Buffered(1))
    flat = [array for group in groups for array in group]
    return pl.pallas_call(
        input_kernel,
        grid=(rows // tile,),
        in_specs=[rows_of(tile, array.shape[1]) for array in flat]
        + [rows_of(tile // BLOCK, width)]
        + [rows_of(tile, width)] * 2
        + [whole((1, width))]
        + [weight] * 3,
        out_specs=rows_of(tile, width),
        out_shape=far_shape((rows, width), F32),
        scratch_shapes=[pltpu.VMEM((3, width, width), BF16)],
        compiler_params=params(20),
        cost_estimate=cost(True),
        name="input_grad",
    )(*[near(array) for array in flat], gsum, far(x), far(gsec), gain, far(wq), far(wk), far(wv))


def pack_kernel(where_ref, up_a_ref, down_a_ref, up_b_ref, down_b_ref, mine_ref, other_ref):
    mine_ref[0] = up_a_ref[...].astype(BF16)
    mine_ref[1] = down_a_ref[...].astype(BF16)
    other_ref[0] = up_b_ref[...].astype(BF16)
    other_ref[1] = down_b_ref[...].astype(BF16)


def pack_weights(core, w_up, w_down):
    width, units = w_up.shape
    half = units // 2

    def up(flip):
        return pl.BlockSpec((width, half), lambda step, core: (0, core[0] ^ flip))

    def down(flip):
        return pl.BlockSpec((half, width), lambda step, core: (core[0] ^ flip, 0))

    shape = (2, width, half)
    return pl.pallas_call(
        pack_kernel,
        grid_spec=pltpu.PrefetchScalarGridSpec(
            num_scalar_prefetch=1,
            grid=(1,),
            in_specs=[up(0), down(0), up(1), down(1)],
            out_specs=[whole(shape), whole(shape)],
        ),
        out_shape=[near_shape(shape, BF16)] * 2,
        compiler_params=params(16),
        cost_estimate=cost(True),
        name="pack_weights",
    )(core, far(w_up), far(w_down), far(w_up), far(w_down))


def finish_feed_kernel(where_ref, mine_ref, other_ref, up_ref, down_ref, turn_ref):
    chunks, _, size, units = mine_ref.shape
    for flip, ref in enumerate((mine_ref, other_ref)):
        column = pl.multiple_of((where_ref[1] ^ flip) * units, units)
        for r in range(chunks):
            at = pl.multiple_of((r ^ where_ref[0]) * size, size)
            up_ref[pl.ds(at, size), pl.ds(column, units)] = ref[r, 0].astype(F32)
            turn_ref[pl.ds(at, size), :] = ref[r, 1].astype(F32)
        down_ref[pl.ds(column, units), :] = turn_ref[...].T


def finish_feed(where, mine, other):
    chunks, _, size, units = mine.shape
    width = chunks * size
    vmem = pl.BlockSpec(memory_space=pltpu.VMEM)
    return pl.pallas_call(
        finish_feed_kernel,
        in_specs=[pl.BlockSpec(memory_space=pltpu.SMEM)] + [vmem] * 2,
        out_specs=[vmem, vmem],
        out_shape=[far_shape((width, 2 * units), F32), far_shape((2 * units, width), F32)],
        scratch_shapes=[pltpu.VMEM((width, units), F32)],
        compiler_params=params(16),
        cost_estimate=cost(True),
        name="finish_feed",
    )(where, mine, other)


def finish_kernel(
    where_ref, piece_a_ref, piece_b_ref, wq_ref, wk_ref, wv_ref, ws_ref, gain_ref,
    gq_ref, gk_ref, gv_ref, gs_ref, go_ref, gain_one_ref, gain_two_ref, entropy_ref, one_ref, two_ref,
):
    width = wq_ref.shape[0]
    chunks, size = piece_a_ref.shape[:2]
    cols = piece_b_ref.shape[2] // 4
    for r in range(chunks):
        rows = pl.ds(pl.multiple_of((r ^ where_ref[2]) * size, size), size)
        go_ref[rows, :] = piece_a_ref[r, :, 4 * cols : 4 * cols + width].astype(F32)
        two_ref[rows, :] = piece_a_ref[r, :, 4 * cols + width :].astype(F32)
        for g, piece in enumerate((piece_a_ref, piece_b_ref)):
            span = slice(g * cols, (g + 1) * cols)
            for index, ref in enumerate((gq_ref, gk_ref, gv_ref, gs_ref)):
                ref[rows, span] = piece[r, :, index * cols : (index + 1) * cols].astype(F32)
    total = jnp.zeros((width, LANES), F32)
    for at in range(0, width, LANES):
        span = slice(at, at + LANES)
        for grad, weight in ((gq_ref, wq_ref), (gk_ref, wk_ref), (gv_ref, wv_ref)):
            total = total + grad[:, span] * weight[:, span].astype(BF16).astype(F32)
        total = total + gs_ref[:, span] * ws_ref[:, span]
    one_ref[...] = total
    gain_one_ref[...] = jnp.sum(one_ref[...].T, axis=0, keepdims=True) / gain_ref[...]
    turned = two_ref[...].T
    gain_two_ref[...] = turned[:1, :]
    entropy_ref[...] = turned[LANES // 2 : LANES // 2 + 1, :]


def finish(where, pieces, wq, wk, wv, ws, gain):
    width = wq.shape[0]
    vmem = pl.BlockSpec(memory_space=pltpu.VMEM)
    square = far_shape((width, width), F32)
    row = shape_of((1, width), F32)
    return pl.pallas_call(
        finish_kernel,
        in_specs=[pl.BlockSpec(memory_space=pltpu.SMEM)] + [vmem] * 7,
        out_specs=[vmem] * 8,
        out_shape=[square] * 5 + [row] * 3,
        scratch_shapes=[pltpu.VMEM((width, LANES), F32)] * 2,
        compiler_params=params(16),
        cost_estimate=cost(True),
        name="finish",
    )(where, *pieces, far(wq), far(wk), far(wv), far(ws), gain)


MP, CORE, X, Z_LOW, Z_HIGH = 1, 2, 4, 8, 16
CORE_STEP = ((CORE,), (CORE,))
FEED_STEPS = ((X,), (Z_LOW, Z_HIGH, Z_LOW + Z_HIGH))
HEAD_STEPS = ((CORE,), (MP, X, MP + X), (Z_LOW, Z_HIGH, Z_LOW + Z_HIGH))


def swap(array, flip):
    count = lax.axis_size("batch") * lax.axis_size("mp")
    return lax.ppermute(array, ("batch", "mp"), [(i, i ^ flip) for i in range(count)])


def place(steps, index):
    result = jnp.int32(0)
    for step in steps:
        for bit in reversed(step[: (len(step) + 1).bit_length() - 1]):
            result = 2 * result + ((index & bit) > 0).astype(jnp.int32)
    return result


def add_low(left, right):
    return (left.astype(F32) + right.astype(F32)).astype(BF16)


class Walk:
    def __init__(self, piece, steps):
        self.value = piece
        self.down = list(steps)
        self.up = list(reversed(steps))
        self.reducing = False
        self.arrived = []

    def combine(self, plan):
        arrived = self.arrived if plan is None else [plan.after(array) for array in self.arrived]
        if arrived and self.reducing:
            self.value = self.value.astype(F32)
            for array in arrived:
                self.value = self.value + array.astype(F32)
            if not self.down:
                self.value = self.value.astype(BF16)
        elif arrived:
            self.value = jnp.concatenate([self.value] + arrived, axis=0)

    def step(self, plan=None):
        self.combine(plan)
        send = (lambda array: array) if plan is None else plan.after
        self.reducing = bool(self.down)
        if self.reducing:
            flips = self.down.pop(0)
            size = self.value.shape[0] // (len(flips) + 1)
            self.arrived = [
                swap(send(self.value[(n + 1) * size : (n + 2) * size].astype(BF16)), flip)
                for n, flip in enumerate(flips)
            ]
            self.value = self.value[:size]
        else:
            mine = send(self.value)
            self.arrived = [swap(mine, flip) for flip in self.up.pop(0)]
        return self.arrived

    def rest(self):
        while self.down or self.up:
            self.step()
        self.combine(None)
        return self.value


class Schedule:
    def __init__(self):
        self.pending, self.launched, self.done = [], [], None

    def after(self, array):
        return lax.optimization_barrier((array, self.done))[0]

    def enter(self, small):
        tied = lax.optimization_barrier((small, *self.pending))[0]
        self.pending, self.launched = self.launched, []
        return tied

    def leave(self, *arrays):
        self.pending.extend(arrays)
        self.done = arrays[0]

    def launch(self, *arrays):
        for array in arrays:
            self.launched.extend(array if isinstance(array, list) else [array])


def local_small(
    inputs, cotangent, block_perm, block_mask, pen_weight, w_query, w_key, w_value, w_out, w_sort,
    gain_one, gain_two, w_up, w_down,
):
    _, rows, width = inputs.shape
    x = inputs.reshape(rows, width)
    cot = cotangent.reshape(rows, width)
    perm = block_perm.reshape(-1)
    mask = block_mask.reshape(-1)
    perm_row = block_perm.reshape(1, -1)
    mask_row = block_mask.reshape(1, -1)
    gain_one_row = gain_one.reshape(1, width)
    gain_two_row = gain_two.reshape(1, width)
    batch, mp = lax.axis_index("batch"), lax.axis_index("mp")
    core = batch & 1
    index = batch * 2 + mp
    where = jnp.stack([place(FEED_STEPS, index), core, place(HEAD_STEPS, index)])
    row_chunks, out_chunks = 8, 32
    plan = Schedule()

    count = jnp.broadcast_to(jnp.sum(mask.astype(F32)), (8, LANES))
    flips = [CORE, MP, X, Z_LOW, Z_HIGH]

    def count_step(count):
        arrived = swap(plan.after(count), flips.pop(0))
        plan.launch(arrived)
        return count + arrived

    own_a, own_b = pack_weights(core.reshape(1), w_up, w_down)
    far_a = swap(own_a, MP)
    plan.leave(own_b)
    count = count_step(count)
    act_one, q, k, v, probs, att, second, shares, act_two, sums, plan_log, chosen, entropy = forward(
        perm, mask, perm_row, mask_row, plan.enter(gain_one_row), gain_two_row, x, w_query, w_key, w_value,
        w_sort, w_out,
    )
    plan.leave(act_two)
    count = count_step(count)
    cot_low, sofar, hid_a, piece = feed_quarter(plan.enter(where), act_two, cot, own_b, None, row_chunks)
    plan.leave(piece)
    plan.pending.append(far_a)

    far_b = swap(plan.after(far_a), CORE)
    near = swap(plan.after(piece), CORE)
    plan.launch(far_b, near)
    count = count_step(count)
    sofar, hid_b, piece = feed_quarter(plan.enter(where), act_two, cot_low, own_a, sofar, row_chunks)
    plan.leave(piece)

    own = piece.astype(F32) + plan.after(near).astype(F32)
    count = count_step(count)
    sofar, hid_c, piece = feed_quarter(plan.enter(where), act_two, cot_low, far_b, sofar, row_chunks)
    plan.leave(piece)

    near = swap(plan.after(piece), CORE)
    plan.launch(near)
    count = count_step(count)
    sofar, hid_d, piece = feed_quarter(plan.enter(where), act_two, cot_low, far_a, sofar, row_chunks)
    plan.leave(piece)

    arrived = swap(add_low(piece, plan.after(near)), MP)
    grad_second, grad_att, out_piece = settle(
        plan.enter(where), sofar, cot, second, att, w_out, gain_two_row, entropy, out_chunks
    )
    plan.leave(grad_att)

    gq, gk, gv, gch = attend_back(plan.enter(perm), q, grad_att, probs, k, v, chosen, 0)
    plan.leave(gch)
    groups = [(gq, gk, gv)]

    block_total = count[0, 0]
    coef = (pen_weight[0] / (HEADS * block_total)).reshape(1)
    piece, gsum = group_grads(
        plan.enter(where), coef, act_one, gq, gk, gv, gch, shares, plan_log, sums, w_sort,
        perm_row, mask_row, out_piece, 0, out_chunks,
    )
    plan.leave(gsum)

    first = Walk(piece, HEAD_STEPS)
    feed_sum = Walk(own + plan.after(arrived).astype(F32), FEED_STEPS)
    plan.launch(first.step(plan), feed_sum.step(plan))
    gq, gk, gv, gch = attend_back(plan.enter(perm), q, grad_att, probs, k, v, chosen, 1)
    plan.leave(gch)
    groups.append((gq, gk, gv))

    plan.launch(first.step(plan), feed_sum.step(plan))
    piece, gsum = group_grads(
        plan.enter(where), coef, act_one, gq, gk, gv, gch, shares, plan_log, sums, w_sort,
        perm_row, mask_row, gsum, 1, out_chunks,
    )
    plan.leave(gsum)

    final = Walk(piece, HEAD_STEPS)
    final.step(plan)
    plan.launch(final.step(plan), first.step(plan), feed_sum.step(plan))
    grad_input = input_grad(
        groups, gsum, x, grad_second, plan.enter(gain_one_row), w_query, w_key, w_value
    )
    plan.leave(grad_input)

    final.step(plan)
    first.step(plan)
    feed_sum.step(plan)
    final.step(plan)
    plan.launch(final.step(plan), first.step(plan))
    quarters = (own_b, own_a, far_b, far_a)
    output = layer_output(plan.enter(second), (hid_a, hid_b, hid_c, hid_d), quarters)
    plan.leave(output)
    final.step(plan)
    pieces = [first.rest(), final.rest()]
    total = feed_sum.rest()
    grad_up, grad_down = finish_feed(where, total, swap(total, CORE))
    grad_query, grad_key, grad_value, grad_sort, grad_out, grad_gain_one, grad_gain_two, entropies = finish(
        where, pieces, w_query, w_key, w_value, w_sort, gain_one_row
    )
    return (
        output.reshape(inputs.shape),
        (jnp.sum(entropies) / (HEADS * block_total)).reshape(1),
        grad_input.reshape(inputs.shape),
        grad_query,
        grad_key,
        grad_value,
        grad_out,
        grad_sort,
        grad_gain_one.reshape(width),
        grad_gain_two.reshape(width),
        grad_up,
        grad_down,
    )


def local_any(
    inputs, cotangent, block_perm, block_mask, pen_weight, w_query, w_key, w_value, w_out, w_sort,
    gain_one, gain_two, w_up, w_down,
):
    both = ("batch", "mp")
    _, rows, width = inputs.shape
    x = inputs.reshape(rows, width)
    cot = cotangent.reshape(rows, width)
    perm = block_perm.reshape(-1)
    mask = block_mask.reshape(-1)
    perm_row = block_perm.reshape(1, -1)
    mask_row = block_mask.reshape(1, -1)
    gain_one_row = gain_one.reshape(1, width)
    gain_two_row = gain_two.reshape(1, width)
    where = jnp.zeros((3,), jnp.int32)
    up_all = lax.all_gather(w_up.astype(BF16), "mp", axis=1, tiled=True)
    down_all = lax.all_gather(w_down.astype(BF16), "mp", axis=0, tiled=True)
    quarters = [
        jnp.stack([up_all[:, at : at + width], down_all[at : at + width]])
        for at in range(0, up_all.shape[1], width)
    ]
    act_one, q, k, v, probs, att, second, shares, act_two, sums, plan_log, chosen, entropy = forward(
        perm, mask, perm_row, mask_row, gain_one_row, gain_two_row, x, w_query, w_key, w_value, w_sort, w_out
    )
    block_total = lax.psum(jnp.sum(mask_row).astype(F32), both)
    hidden, parts = [], []
    sofar = None
    cot_low = cot
    for weights in quarters:
        results = feed_quarter(where, act_two, cot_low, weights, sofar, 1)
        if sofar is None:
            cot_low = results[0]
        sofar, hid, piece = results[-3:]
        hidden.append(hid)
        parts.append(piece[0])
    grad_second, grad_att, extra = settle(where, sofar, cot, second, att, w_out, gain_two_row, entropy, 1)
    coef = (pen_weight[0] / (HEADS * block_total)).reshape(1)
    groups, pieces = [], []
    for group in range(width // GROUP_WIDTH):
        gq, gk, gv, gch = attend_back(perm, q, grad_att, probs, k, v, chosen, group)
        piece, extra = group_grads(
            where, coef, act_one, gq, gk, gv, gch, shares, plan_log, sums, w_sort, perm_row, mask_row,
            extra, group, 1,
        )
        groups.append((gq, gk, gv))
        pieces.append(piece)
    grad_input = input_grad(groups, extra, x, grad_second, gain_one_row, w_query, w_key, w_value)
    output = layer_output(second, hidden, quarters)

    parts = jnp.concatenate(parts, axis=2)
    parts = lax.psum(lax.psum_scatter(parts, "mp", scatter_dimension=2, tiled=True), "batch").astype(F32)
    grad_up, grad_down = parts[0], parts[1].T
    pieces = lax.psum(pieces, both)
    grad_query, grad_key, grad_value, grad_sort, grad_out, grad_gain_one, grad_gain_two, entropies = finish(
        where, pieces, w_query, w_key, w_value, w_sort, gain_one_row
    )
    return (
        output.reshape(inputs.shape),
        (jnp.sum(entropies) / (HEADS * block_total)).reshape(1),
        grad_input.reshape(inputs.shape),
        grad_query,
        grad_key,
        grad_value,
        grad_out,
        grad_sort,
        grad_gain_one.reshape(width),
        grad_gain_two.reshape(width),
        grad_up,
        grad_down,
    )


def solution(mesh):
    tokens = P(("batch", "mp"), None, None)
    blocks = P(("batch", "mp"), None)
    small = mesh.shape["batch"] == 16 and mesh.shape["mp"] == 2
    return jax.shard_map(
        local_small if small else local_any,
        mesh=mesh,
        in_specs=(tokens, tokens, blocks, blocks) + (P(),) * 8 + (P(None, "mp"), P("mp", None)),
        out_specs=(tokens, P(), tokens) + (P(),) * 7 + (P(None, "mp"), P("mp", None)),
        check_vma=False,
    )
```

time: 952 us -> 252 us (0.26)
  matrix products: 272 us -> 0 us
  waiting for transfers between devices: 304 us -> 40.6 us
  local copies, waits for them, and re-layouts: 157 us -> 11.6 us
  Pallas kernels: 0 us -> 130 us
  other arithmetic: 114 us -> 8.55 us
  blocking collectives: 79.6 us -> 0 us
  starting transfers between devices: 0.83 us -> 55.9 us
  between operations: 20.4 us -> 4.5 us
    dot_general x30 -> x0, matrix products: 264 us -> none  [the longest x1 26.2 us: local(): up_rows = jnp.dot(gathered, up_low, preferred_element_type=jnp.float32)]
    psum x2 -> x0, waiting for transfers between devices: 160 us -> none  [the longest x1 110 us: local(): grad_up, grad_down = lax.psum((part_up, part_down), 'batch')]
    pallas_call x0 -> x15, Pallas kernels: none -> 130 us  [the longest x4 38.2 us: feed_quarter(): pl.pallas_call(kernel, grid_spec=pltpu.PrefetchScalarGridSpec(num_scalar_...]
    reduce_scatter x2 -> x0, waiting for transfers between devices: 98.9 us -> none  [the longest x1 51.2 us: local(): lax.psum_scatter(jnp.dot(piece, down_low, preferred_element_type=jnp.floa...]
    psum x2 -> x0, blocking collectives: 79.6 us -> none  [the longest x1 40.1 us: local(): block_total = lax.psum(local_blocks, ('batch', 'mp'))]
    reduce_sum x47 -> x2, other arithmetic: 65 us -> 1.87 us  [the longest x1 1.26 us: local_small(): count = jnp.broadcast_to(jnp.sum(mask.astype(F32)), (8, LANES))]
    ppermute x0 -> x47, starting transfers between devices: none -> 55.9 us  [swap(): lax.ppermute(array, ('batch', 'mp'), [(i, i ^ flip) for i in range(count)])]
    another operation x7 -> x0, local copies, waits for them, and re-layouts: 46.4 us -> none
  transfers between devices with their start and end apart: 6 -> 47, of which waited for: 5 -> 16; matrix products, arithmetic and copies ran while one was open for 26% -> 3% of each run, Pallas kernels for 0% -> 42%
where the time goes in v2:
time: 252 us; the launch traced here: 251 us
  Pallas kernels  130 us (52%)
  starting transfers between devices  55.9 us (22%)
  waiting for transfers between devices  40.6 us (16%)
  local copies, waits for them, and re-layouts  11.6 us (5%)
  other arithmetic  8.55 us (3%)
  between operations  4.5 us (2%)
    ppermute x47, starting transfers between devices, swap(): lax.ppermute(array, ('batch', 'mp'), [(i, i ^ flip) for i in range(count)])  55.9 us
    ppermute x47, waiting for transfers between devices, swap(): lax.ppermute(array, ('batch', 'mp'), [(i, i ^ flip) for i in range(count)])  40.6 us
    pallas_call x4, Pallas kernels, feed_quarter(): pl.pallas_call(kernel, grid_spec=pltpu.PrefetchScalarGridSpec(num_scalar_...  38.2 us
    pallas_call x1, Pallas kernels, forward(): pl.pallas_call(functools.partial(forward_kernel, tile=tile), in_specs=[sm...  24.3 us
    pallas_call x2, Pallas kernels, attend_back(): pl.pallas_call(attend_back_kernel, grid_spec=grid_spec, out_shape=[low, l...  18.8 us
    unnamed x85, local copies, waits for them, and re-layouts  9.91 us
    pallas_call x1, Pallas kernels, input_grad(): pl.pallas_call(input_kernel, grid=(rows // tile,), in_specs=[rows_of(tile...  9.69 us
    pallas_call x1, Pallas kernels, settle(): pl.pallas_call(settle_kernel, grid_spec=pltpu.PrefetchScalarGridSpec(num_...  9.05 us
  transfers between devices with their start and end apart: 47, of which 16 were waited for; matrix products, arithmetic and copies ran while one was open for 3% of the time, Pallas kernels for 42%

profile of v2, /device:TPU:0, one launch (start us, length us, event | category | flops | bytes accessed | tf_op | source)
XLA Modules:
  0.0 251.5 jit_solution(13989802437936543892)
XLA Ops:
  1.9 3.3 %pack_weights.1 = (bf16[2,512,512]{2,1,0:T(8,128)(2,1)}, bf16[2,512,512]{2,1,0:T(8,128)(2,1)S(1)}) custom-call(s32[1]{0:T(128)} %bitcast.3.where_ref, f32[512,1024]{1,0:T(8,128)} %up_b_ref.1, f32[1024,512]{1,0:T(8,128)} %down_b_ref.1, f32[512,1024]{1,0:T(8,128)} %up_b_ref.1, f32[1024,512]{1,0:T(8,128)} %down_b_ref.1), custom_call_target="tpu_custom_call" | custom-call | flops 99999997952 | tf_op jit(solution)/shard_map/pack_weights/pallas_call | solution.py:701
  6.4 2.6 %collective-permute-start = (bf16[2,512,512]{2,1,0:T(8,128)(2,1)}, bf16[2,512,512]{2,1,0:T(8,128)(2,1)}, u32[]{:S(2)}, u32[]{:S(2)}) collective-permute-start(bf16[2,512,512]{2,1,0:T(8,128)(2,1)} %get-tuple-element.146.weights_ref.refs_5_), channel_id=1, source_target_pairs={{0,1},{1,0},{2,3},{3,2},{4,5},{5,4},{6,7},{7,6},{8,9},{9,8},{10,11... | collective-permute-start | bytes 3145736 | tf_op jit(solution)/shard_map/ppermute | solution.py:796
  9.0 24.3 %forward.1 = (bf16[2048,512]{1,0:T(8,128)(2,1)}, bf16[2048,512]{1,0:T(8,128)(2,1)}, bf16[2048,512]{1,0:T(8,128)(2,1)}, bf16[2048,512]{1,0:T(8,128)(2,1)}, bf16[4...) custom-call(s32[64]{0:T(128)S(1)} %bitcast.21, ...), custom_call_target="tpu_custom_call" | custom-call | flops 99999997952 | tf_op jit(solution)/shard_map/forward/pallas_call | solution.py:290
  34.2 9.0 %feed_quarter.4 = (bf16[2048,512]{1,0:T(8,128)(2,1)S(1)}, f32[2048,512]{1,0:T(8,128)S(1)}, bf16[2048,512]{1,0:T(8,128)(2,1)}, bf16[8,2,64,512]{3,2,1,0:T(8,128)(2,1)S(1)}) custom-call(s32[3]{0:T(128)S(1)} %pad_add_fusion.where_ref, bf16[2048,512]{1,0:T(8,128)(2,1)S(1)} %get-tuple-element.148.act_ref, f32[2048,512]{1,0:T(8,128)S(1)} %bitcast.19, ...), custom_call_target="tpu_custom_call" | custom-call | flops 99999997952 | tf_op jit(solution)/shard_map/feed_quarter/pallas_call | solution.py:525
  47.6 9.9 %feed_quarter.5 = (f32[2048,512]{1,0:T(8,128)S(1)}, bf16[2048,512]{1,0:T(8,128)(2,1)}, bf16[8,2,64,512]{3,2,1,0:T(8,128)(2,1)S(1)}) custom-call(s32[3]{0:T(128)S(1)} %pad_add_fusion.where_ref, bf16[2048,512]{1,0:T(8,128)(2,1)S(1)} %get-tuple-element.148.act_ref, bf16[2048,512]{1,0:T(8,128)(2,1)S(1)} %get-tuple-element.156.cot_ref, ...), custom_call_target="tpu_custom_call" | custom-call | flops 99999997952 | tf_op jit(solution)/shard_map/feed_quarter/pallas_call | solution.py:525
  61.2 9.1 %feed_quarter.6 = (f32[2048,512]{1,0:T(8,128)S(1)}, bf16[2048,512]{1,0:T(8,128)(2,1)}, bf16[8,2,64,512]{3,2,1,0:T(8,128)(2,1)}) custom-call(s32[3]{0:T(128)S(1)} %pad_add_fusion.where_ref, bf16[2048,512]{1,0:T(8,128)(2,1)S(1)} %get-tuple-element.148.act_ref, bf16[2048,512]{1,0:T(8,128)(2,1)S(1)} %get-tuple-element.156.cot_ref, ...), custom_call_target="tpu_custom_call" | custom-call | flops 99999997952 | tf_op jit(solution)/shard_map/feed_quarter/pallas_call | solution.py:525
  70.3 3.1 %collective-permute-start.8 = (f32[8,128]{1,0:T(8,128)S(1)}, f32[8,128]{1,0:T(8,128)S(1)}, u32[]{:S(2)}, u32[]{:S(2)}) collective-permute-start(f32[8,128]{1,0:T(8,128)S(1)} %add.109), channel_id=1, source_target_pairs={{0,16},{1,17},{2,18},{3,19},{4,20},{5,21},{6,22},{7,23},{8,24},{9,... | collective-permute-start | bytes 12296 | tf_op jit(solution)/shard_map/ppermute | solution.py:796
  73.4 10.1 %feed_quarter.7 = (f32[2048,512]{1,0:T(8,128)S(1)}, bf16[2048,512]{1,0:T(8,128)(2,1)}, bf16[8,2,64,512]{3,2,1,0:T(8,128)(2,1)S(1)}) custom-call(s32[3]{0:T(128)S(1)} %pad_add_fusion.where_ref, bf16[2048,512]{1,0:T(8,128)(2,1)S(1)} %get-tuple-element.148.act_ref, bf16[2048,512]{1,0:T(8,128)(2,1)S(1)} %get-tuple-element.156.cot_ref, ...), custom_call_target="tpu_custom_call" | custom-call | flops 99999997952 | tf_op jit(solution)/shard_map/feed_quarter/pallas_call | solution.py:525
  83.5 2.0 copy-done.4
  87.7 2.2 copy-done.1
  89.9 2.2 copy-done.2
  92.1 2.2 copy-done.5
  94.3 9.1 %settle.1 = (f32[2048,512]{1,0:T(8,128)}, bf16[2048,512]{1,0:T(8,128)(2,1)S(1)}, bf16[32,16,640]{2,1,0:T(8,128)(2,1)S(1)}) custom-call(s32[3]{0:T(128)S(1)} %pad_add_fusion.where_ref, f32[2048,512]{1,0:T(8,128)S(1)} %copy-done.5, f32[2048,512]{1,0:T(8,128)S(1)} %bitcast.20, f32[2048,512]{1,0:T(8,128)S(1)} %copy-done.2, bf16[2048,512]{1,0:T(8,128)(2,1)S(1)} %copy-done.12, ...), custom_call_target="tpu_custom_call" | custom-call | flops 1000000 | tf_op jit(solution)/shard_map/settle/pallas_call | solution.py:486
  106.7 9.3 %attend_back.2 = (bf16[2048,256]{1,0:T(8,128)(2,1)S(1)}, bf16[2048,256]{1,0:T(8,128)(2,1)S(1)}, bf16[2048,256]{1,0:T(8,128)(2,1)S(1)}, f32[64,256]{1,0:T(8,128)S(1)}) custom-call(s32[64]{0:T(128)S(1)} %bitcast.22, bf16[2048,512]{1,0:T(8,128)(2,1)S(1)} %copy-done.8, bf16[2048,512]{1,0:T(8,128)(2,1)S(1)} %get-tuple-element.172.gatt_ref, ...), custom_call_target="tpu_custom_call" | custom-call | flops 1000000 | tf_op jit(solution)/shard_map/attend_back/pallas_call | solution.py:378
  116.0 4.5 %group_grads.2 = (bf16[32,16,1664]{2,1,0:T(8,128)(2,1)S(1)}, f32[64,512]{1,0:T(8,128)S(1)}) custom-call(s32[3]{0:T(128)S(1)} %pad_add_fusion.where_ref, f32[1]{0:T(128)} %bitcast.11.coef_ref, bf16[2048,512]{1,0:T(8,128)(2,1)S(1)} %copy-done.6, bf16[2048,256]{1,0:T(8,128)(2,1)S(1)} %get-tuple-element.182.gq_ref.refs_0_, ...), custom_call_target="tpu_custom_call" | custom-call | flops 1000000 | tf_op jit(solution)/shard_map/group_grads/pallas_call | solution.py:624
  120.9 9.5 %attend_back.3 = (bf16[2048,256]{1,0:T(8,128)(2,1)S(1)}, bf16[2048,256]{1,0:T(8,128)(2,1)S(1)}, bf16[2048,256]{1,0:T(8,128)(2,1)S(1)}, f32[64,256]{1,0:T(8,128)S(1)}) custom-call(s32[64]{0:T(128)S(1)} %bitcast.23, bf16[2048,512]{1,0:T(8,128)(2,1)S(1)} %copy-done.8, bf16[2048,512]{1,0:T(8,128)(2,1)S(1)} %get-tuple-element.172.gatt_ref, ...), custom_call_target="tpu_custom_call" | custom-call | flops 99999997952 | tf_op jit(solution)/shard_map/attend_back/pallas_call | solution.py:378
  133.7 2.5 collective-permute-start.18
  136.7 9.4 %collective-permute-done.11 = bf16[4,2,64,512]{3,2,1,0:T(8,128)(2,1)S(1)} collective-permute-done((bf16[4,2,64,512]{3,2,1,0:T(8,128)(2,1)S(1)}, bf16[4,2,64,512]{3,2,1,0:T(8,128)(2,1)S(1)}, u32[]{:S(2)}, u32[]{:S(2)}) %collective-permute-start.11) | collective-permute-done | bytes 524320 | tf_op jit(solution)/shard_map/ppermute | solution.py:796
  147.4 3.9 %collective-permute-start.24 = (bf16[1,2,64,512]{3,2,1,0:T(8,128)(2,1)S(1)}, bf16[1,2,64,512]{3,2,1,0:T(8,128)(2,1)S(1)}, u32[]{:S(2)}, u32[]{:S(2)}) collective-permute-start(bf16[1,2,64,512]{3,2,1,0:T(8,128)(2,1)S(1)} %get-tuple-element.224), channel_id=1, source_target_pairs={{0,24},{1,25},{2,26},{3,27},{4,28},{5,29},{6,30},{7,31},{8,16},{9,... | collective-permute-start | bytes 393224 | tf_op jit(solution)/shard_map/ppermute | solution.py:796
  151.3 4.2 %group_grads.3 = (bf16[32,16,1024]{2,1,0:T(8,128)(2,1)S(1)}, f32[64,512]{1,0:T(8,128)S(1)}) custom-call(s32[3]{0:T(128)S(1)} %pad_add_fusion.where_ref, f32[1]{0:T(128)} %bitcast.11.coef_ref, bf16[2048,512]{1,0:T(8,128)(2,1)S(1)} %copy-done.6, bf16[2048,256]{1,0:T(8,128)(2,1)S(1)} %get-tuple-element.199.gq_ref.refs_3_, ...), custom_call_target="tpu_custom_call" | custom-call | flops 99999997952 | tf_op jit(solution)/shard_map/group_grads/pallas_call | solution.py:624
  156.0 2.0 collective-permute-start.19
  161.3 9.7 %input_grad.1 = f32[2048,512]{1,0:T(8,128)} custom-call(bf16[2048,256]{1,0:T(8,128)(2,1)S(1)} %copy-done.14, bf16[2048,256]{1,0:T(8,128)(2,1)S(1)} %copy-done.16, bf16[2048,256]{1,0:T(8,128)(2,1)S(1)} %copy-done.18, bf16[2048,256]{1,0:T(8,128)(2,1)S(1)} %get-tuple-element.199.gq_ref.refs_3_, bf16[2048,256]{1,0:T(8,128)(2,1)S(1)} %get-tuple-element.200.gk_ref.refs_4_, ...), custom_call_target="tpu_custom_call" | custom-call | flops 99999997952 | tf_op jit(solution)/shard_map/input_grad/pallas_call | solution.py:666
  181.1 2.6 %collective-permute-start.33 = (bf16[4,16,1664]{2,1,0:T(8,128)(2,1)S(1)}, bf16[4,16,1664]{2,1,0:T(8,128)(2,1)S(1)}, u32[]{:S(2)}, u32[]{:S(2)}) collective-permute-start(bf16[4,16,1664]{2,1,0:T(8,128)(2,1)S(1)} %pad_maximum_fusion.1), channel_id=1, source_target_pairs={{0,5},{1,4},{2,7},{3,6},{4,1},{5,0},{6,3},{7,2},{8,13},{9,12},{10,... | collective-permute-start | bytes 638984 | tf_op jit(solution)/shard_map/ppermute | solution.py:796
  186.4 3.4 %collective-permute-done.26 = bf16[1,2,64,512]{3,2,1,0:T(8,128)(2,1)S(1)} collective-permute-done((bf16[1,2,64,512]{3,2,1,0:T(8,128)(2,1)S(1)}, bf16[1,2,64,512]{3,2,1,0:T(8,128)(2,1)S(1)}, u32[]{:S(2)}, u32[]{:S(2)}) %collective-permute-start.26) | collective-permute-done | bytes 131104 | tf_op jit(solution)/shard_map/ppermute | solution.py:796
  192.8 3.3 %collective-permute-done.31 = bf16[4,16,1664]{2,1,0:T(8,128)(2,1)S(1)} collective-permute-done((bf16[4,16,1664]{2,1,0:T(8,128)(2,1)S(1)}, bf16[4,16,1664]{2,1,0:T(8,128)(2,1)S(1)}, u32[]{:S(2)}, u32[]{:S(2)}) %collective-permute-start.31) | collective-permute-done | bytes 213024 | tf_op jit(solution)/shard_map/ppermute | solution.py:796
  200.2 9.5 %collective-permute-done.15 = bf16[4,16,1024]{2,1,0:T(8,128)(2,1)S(1)} collective-permute-done((bf16[4,16,1024]{2,1,0:T(8,128)(2,1)S(1)}, bf16[4,16,1024]{2,1,0:T(8,128)(2,1)S(1)}, u32[]{:S(2)}, u32[]{:S(2)}) %collective-permute-start.15) | collective-permute-done | bytes 131104 | tf_op jit(solution)/shard_map/ppermute | solution.py:796
  213.4 8.8 %layer_output.1 = f32[2048,512]{1,0:T(8,128)} custom-call(f32[2048,512]{1,0:T(8,128)S(1)} %copy-done.3, bf16[2048,512]{1,0:T(8,128)(2,1)} %get-tuple-element.230.refs_0_, bf16[2048,512]{1,0:T(8,128)(2,1)} %get-tuple-element.231.refs_1_, bf16[2048,512]{1,0:T(8,128)(2,1)} %get-tuple-element.232.refs_2_, bf16[2048,512]{1,0:T(8,128)(2,1)} %get-tuple-element.233.refs_3_, ...), custom_call_target="tpu_custom_call" | custom-call | flops 99999997952 | tf_op jit(solution)/shard_map/layer_output/pallas_call | solution.py:555
  222.3 2.2 collective-permute-start.40
  229.8 2.3 collective-permute-start.43
  233.3 4.2 %collective-permute-done.41 = bf16[4,16,1024]{2,1,0:T(8,128)(2,1)S(1)} collective-permute-done((bf16[4,16,1024]{2,1,0:T(8,128)(2,1)S(1)}, bf16[4,16,1024]{2,1,0:T(8,128)(2,1)S(1)}, u32[]{:S(2)}, u32[]{:S(2)}) %collective-permute-start.41) | collective-permute-done | bytes 131104 | tf_op jit(solution)/shard_map/ppermute | solution.py:796
  239.7 5.4 %finish.1 = (f32[512,512]{1,0:T(8,128)}, f32[512,512]{1,0:T(8,128)}, f32[512,512]{1,0:T(8,128)}, f32[512,512]{1,0:T(8,128)}, f32[512,512]{1,0:T(8,128)}, /*index...) custom-call(s32[3]{0:T(128)S(1)} %pad_add_fusion.where_ref, ...), custom_call_target="tpu_custom_call" | custom-call | flops 99999997952 | tf_op jit(solution)/shard_map/finish/pallas_call | solution.py:776
  246.3 4.0 %finish_feed.1 = (f32[512,1024]{1,0:T(8,128)}, f32[1024,512]{1,0:T(8,128)}) custom-call(s32[3]{0:T(128)S(1)} %pad_add_fusion.where_ref, bf16[8,2,64,512]{3,2,1,0:T(8,128)(2,1)S(1)} %constant_dynamic-update-slice_fusion.30.mine_ref, bf16[8,2,64,512]{3,2,1,0:T(8,128)(2,1)} %collective-permute-done.46.other_ref), custom_call_target="tpu_custom_call" | custom-call | flops 99999997952 | tf_op jit(solution)/shard_map/finish_feed/pallas_call | solution.py:731
  (198 shorter events, 57.2 us)
Async XLA Ops:
  5.9 27.5 %collective-permute-start.1 = (f32[8,128]{1,0:T(8,128)S(1)}, f32[8,128]{1,0:T(8,128)S(1)}, u32[]{:S(2)}, u32[]{:S(2)}) collective-permute-start(f32[8,128]{1,0:T(8,128)S(1)} %broadcast_in_dim.3), channel_id=1, source_target_pairs={{0,2},{1,3},{2,0},{3,1},{4,6},{5,7},{6,4},{7,5},{8,10},{9,11},{10,... | collective-permute-start | bytes 12296 | tf_op jit(solution)/shard_map/ppermute | solution.py:796
  6.4 41.2 %collective-permute-start = (bf16[2,512,512]{2,1,0:T(8,128)(2,1)}, bf16[2,512,512]{2,1,0:T(8,128)(2,1)}, u32[]{:S(2)}, u32[]{:S(2)}) collective-permute-start(bf16[2,512,512]{2,1,0:T(8,128)(2,1)} %get-tuple-element.146.weights_ref.refs_5_), channel_id=1, source_target_pairs={{0,1},{1,0},{2,3},{3,2},{4,5},{5,4},{6,7},{7,6},{8,9},{9,8},{10,11... | collective-permute-start | bytes 3145736 | tf_op jit(solution)/shard_map/ppermute | solution.py:796
  34.1 9.2 %collective-permute-start.4 = (f32[8,128]{1,0:T(8,128)S(1)}, f32[8,128]{1,0:T(8,128)S(1)}, u32[]{:S(2)}, u32[]{:S(2)}) collective-permute-start(f32[8,128]{1,0:T(8,128)S(1)} %broadcast_add_fusion), channel_id=1, source_target_pairs={{0,1},{1,0},{2,3},{3,2},{4,5},{5,4},{6,7},{7,6},{8,9},{9,8},{10,11... | collective-permute-start | bytes 12296 | tf_op jit(solution)/shard_map/ppermute | solution.py:796
  45.9 14.3 %collective-permute-start.3 = (bf16[8,2,64,512]{3,2,1,0:T(8,128)(2,1)S(1)}, bf16[8,2,64,512]{3,2,1,0:T(8,128)(2,1)S(1)}, u32[]{:S(2)}, u32[]{:S(2)}) collective-permute-start(bf16[8,2,64,512]{3,2,1,0:T(8,128)(2,1)S(1)} %get-tuple-element.152), channel_id=1, source_target_pairs={{0,2},{1,3},{2,0},{3,1},{4,6},{5,7},{6,4},{7,5},{8,10},{9,11},{10,... | collective-permute-start | bytes 3145736 | tf_op jit(solution)/shard_map/ppermute | solution.py:796
  47.6 13.5 %collective-permute-start.2 = (bf16[2,512,512]{2,1,0:T(8,128)(2,1)}, bf16[2,512,512]{2,1,0:T(8,128)(2,1)S(1)}, u32[]{:S(2)}, u32[]{:S(2)}) collective-permute-start(bf16[2,512,512]{2,1,0:T(8,128)(2,1)} %collective-permute-done.weights_ref.refs_7_), channel_id=1, source_target_pairs={{0,2},{1,3},{2,0},{3,1},{4,6},{5,7},{6,4},{7,5},{8,10},{9,11},{10,... | collective-permute-start | bytes 3145736 | tf_op jit(solution)/shard_map/ppermute | solution.py:796
  70.3 16.2 %collective-permute-start.8 = (f32[8,128]{1,0:T(8,128)S(1)}, f32[8,128]{1,0:T(8,128)S(1)}, u32[]{:S(2)}, u32[]{:S(2)}) collective-permute-start(f32[8,128]{1,0:T(8,128)S(1)} %add.109), channel_id=1, source_target_pairs={{0,16},{1,17},{2,18},{3,19},{4,20},{5,21},{6,22},{7,23},{8,24},{9,... | collective-permute-start | bytes 12296 | tf_op jit(solution)/shard_map/ppermute | solution.py:796
  73.3 14.3 %collective-permute-start.6 = (bf16[8,2,64,512]{3,2,1,0:T(8,128)(2,1)}, bf16[8,2,64,512]{3,2,1,0:T(8,128)(2,1)}, u32[]{:S(2)}, u32[]{:S(2)}) collective-permute-start(bf16[8,2,64,512]{3,2,1,0:T(8,128)(2,1)} %get-tuple-element.162), channel_id=1, source_target_pairs={{0,2},{1,3},{2,0},{3,1},{4,6},{5,7},{6,4},{7,5},{8,10},{9,11},{10,... | collective-permute-start | bytes 3145736 | tf_op jit(solution)/shard_map/ppermute | solution.py:796
  105.0 25.6 %collective-permute-start.10 = (bf16[8,2,64,512]{3,2,1,0:T(8,128)(2,1)S(1)}, bf16[8,2,64,512]{3,2,1,0:T(8,128)(2,1)S(1)}, u32[]{:S(2)}, u32[]{:S(2)}) collective-permute-start(bf16[8,2,64,512]{3,2,1,0:T(8,128)(2,1)S(1)} %add_convert_fusion), channel_id=1, source_target_pairs={{0,1},{1,0},{2,3},{3,2},{4,5},{5,4},{6,7},{7,6},{8,9},{9,8},{10,11... | collective-permute-start | bytes 3145736 | tf_op jit(solution)/shard_map/ppermute | solution.py:796
  120.6 9.8 %collective-permute-start.9 = (bf16[16,16,1664]{2,1,0:T(8,128)(2,1)S(1)}, bf16[16,16,1664]{2,1,0:T(8,128)(2,1)S(1)}, u32[]{:S(2)}, u32[]{:S(2)}) collective-permute-start(bf16[16,16,1664]{2,1,0:T(8,128)(2,1)S(1)} %slice.98), channel_id=1, source_target_pairs={{0,2},{1,3},{2,0},{3,1},{4,6},{5,7},{6,4},{7,5},{8,10},{9,11},{10,... | collective-permute-start | bytes 2555912 | tf_op jit(solution)/shard_map/ppermute | solution.py:796
  131.2 14.8 %collective-permute-start.11 = (bf16[4,2,64,512]{3,2,1,0:T(8,128)(2,1)S(1)}, bf16[4,2,64,512]{3,2,1,0:T(8,128)(2,1)S(1)}, u32[]{:S(2)}, u32[]{:S(2)}) collective-permute-start(bf16[4,2,64,512]{3,2,1,0:T(8,128)(2,1)S(1)} %slice.185), channel_id=1, source_target_pairs={{0,4},{1,5},{2,6},{3,7},{4,0},{5,1},{6,2},{7,3},{8,12},{9,13},{10,... | collective-permute-start | bytes 1572872 | tf_op jit(solution)/shard_map/ppermute | solution.py:796
  133.1 22.5 %collective-permute-start.17 = (bf16[4,16,1664]{2,1,0:T(8,128)(2,1)S(1)}, bf16[4,16,1664]{2,1,0:T(8,128)(2,1)S(1)}, u32[]{:S(2)}, u32[]{:S(2)}) collective-permute-start(bf16[4,16,1664]{2,1,0:T(8,128)(2,1)S(1)} %get-tuple-element.212), channel_id=1, source_target_pairs={{0,4},{1,5},{2,6},{3,7},{4,0},{5,1},{6,2},{7,3},{8,12},{9,13},{10,... | collective-permute-start | bytes 638984 | tf_op jit(solution)/shard_map/ppermute | solution.py:796
  133.7 22.0 %collective-permute-start.18 = (bf16[4,16,1664]{2,1,0:T(8,128)(2,1)S(1)}, bf16[4,16,1664]{2,1,0:T(8,128)(2,1)S(1)}, u32[]{:S(2)}, u32[]{:S(2)}) collective-permute-start(bf16[4,16,1664]{2,1,0:T(8,128)(2,1)S(1)} %get-tuple-element.214), channel_id=1, source_target_pairs={{0,5},{1,4},{2,7},{3,6},{4,1},{5,0},{6,3},{7,2},{8,13},{9,12},{10,... | collective-permute-start | bytes 638984 | tf_op jit(solution)/shard_map/ppermute | solution.py:796
  136.2 19.7 %collective-permute-start.16 = (bf16[4,16,1664]{2,1,0:T(8,128)(2,1)S(1)}, bf16[4,16,1664]{2,1,0:T(8,128)(2,1)S(1)}, u32[]{:S(2)}, u32[]{:S(2)}) collective-permute-start(bf16[4,16,1664]{2,1,0:T(8,128)(2,1)S(1)} %get-tuple-element.210), channel_id=1, source_target_pairs={{0,1},{1,0},{2,3},{3,2},{4,5},{5,4},{6,7},{7,6},{8,9},{9,8},{10,11... | collective-permute-start | bytes 638984 | tf_op jit(solution)/shard_map/ppermute | solution.py:796
  147.3 11.4 %collective-permute-start.23 = (bf16[1,2,64,512]{3,2,1,0:T(8,128)(2,1)S(1)}, bf16[1,2,64,512]{3,2,1,0:T(8,128)(2,1)S(1)}, u32[]{:S(2)}, u32[]{:S(2)}) collective-permute-start(bf16[1,2,64,512]{3,2,1,0:T(8,128)(2,1)S(1)} %get-tuple-element.222), channel_id=1, source_target_pairs={{0,16},{1,17},{2,18},{3,19},{4,20},{5,21},{6,22},{7,23},{8,24},{9,... | collective-permute-start | bytes 393224 | tf_op jit(solution)/shard_map/ppermute | solution.py:796
  147.4 11.3 %collective-permute-start.24 = (bf16[1,2,64,512]{3,2,1,0:T(8,128)(2,1)S(1)}, bf16[1,2,64,512]{3,2,1,0:T(8,128)(2,1)S(1)}, u32[]{:S(2)}, u32[]{:S(2)}) collective-permute-start(bf16[1,2,64,512]{3,2,1,0:T(8,128)(2,1)S(1)} %get-tuple-element.224), channel_id=1, source_target_pairs={{0,24},{1,25},{2,26},{3,27},{4,28},{5,29},{6,30},{7,31},{8,16},{9,... | collective-permute-start | bytes 393224 | tf_op jit(solution)/shard_map/ppermute | solution.py:796
  155.7 40.6 %collective-permute-start.12 = (bf16[16,16,1024]{2,1,0:T(8,128)(2,1)S(1)}, bf16[16,16,1024]{2,1,0:T(8,128)(2,1)S(1)}, u32[]{:S(2)}, u32[]{:S(2)}) collective-permute-start(bf16[16,16,1024]{2,1,0:T(8,128)(2,1)S(1)} %slice.101), channel_id=1, source_target_pairs={{0,2},{1,3},{2,0},{3,1},{4,6},{5,7},{6,4},{7,5},{8,10},{9,11},{10,... | collective-permute-start | bytes 1572872 | tf_op jit(solution)/shard_map/ppermute | solution.py:796
  156.0 15.0 %collective-permute-start.19 = (bf16[1,16,1664]{2,1,0:T(8,128)(2,1)S(1)}, bf16[1,16,1664]{2,1,0:T(8,128)(2,1)S(1)}, u32[]{:S(2)}, u32[]{:S(2)}) collective-permute-start(bf16[1,16,1664]{2,1,0:T(8,128)(2,1)S(1)} %get-tuple-element.216), channel_id=1, source_target_pairs={{0,8},{1,9},{2,10},{3,11},{4,12},{5,13},{6,14},{7,15},{8,0},{9,1},... | collective-permute-start | bytes 159752 | tf_op jit(solution)/shard_map/ppermute | solution.py:796
  158.7 12.2 %collective-permute-start.20 = (bf16[1,16,1664]{2,1,0:T(8,128)(2,1)S(1)}, bf16[1,16,1664]{2,1,0:T(8,128)(2,1)S(1)}, u32[]{:S(2)}, u32[]{:S(2)}) collective-permute-start(bf16[1,16,1664]{2,1,0:T(8,128)(2,1)S(1)} %get-tuple-element.217), channel_id=1, source_target_pairs={{0,16},{1,17},{2,18},{3,19},{4,20},{5,21},{6,22},{7,23},{8,24},{9,... | collective-permute-start | bytes 159752 | tf_op jit(solution)/shard_map/ppermute | solution.py:796
  158.7 12.2 %collective-permute-start.21 = (bf16[1,16,1664]{2,1,0:T(8,128)(2,1)S(1)}, bf16[1,16,1664]{2,1,0:T(8,128)(2,1)S(1)}, u32[]{:S(2)}, u32[]{:S(2)}) collective-permute-start(bf16[1,16,1664]{2,1,0:T(8,128)(2,1)S(1)} %get-tuple-element.218), channel_id=1, source_target_pairs={{0,24},{1,25},{2,26},{3,27},{4,28},{5,29},{6,30},{7,31},{8,16},{9,... | collective-permute-start | bytes 159752 | tf_op jit(solution)/shard_map/ppermute | solution.py:796
  178.3 11.5 %collective-permute-start.26 = (bf16[1,2,64,512]{3,2,1,0:T(8,128)(2,1)S(1)}, bf16[1,2,64,512]{3,2,1,0:T(8,128)(2,1)S(1)}, u32[]{:S(2)}, u32[]{:S(2)}) collective-permute-start(bf16[1,2,64,512]{3,2,1,0:T(8,128)(2,1)S(1)} %get-tuple-element.226), channel_id=1, source_target_pairs={{0,16},{1,17},{2,18},{3,19},{4,20},{5,21},{6,22},{7,23},{8,24},{9,... | collective-permute-start | bytes 393224 | tf_op jit(solution)/shard_map/ppermute | solution.py:796
  179.2 12.0 %collective-permute-start.25 = (bf16[1,2,64,512]{3,2,1,0:T(8,128)(2,1)S(1)}, bf16[1,2,64,512]{3,2,1,0:T(8,128)(2,1)S(1)}, u32[]{:S(2)}, u32[]{:S(2)}) collective-permute-start(bf16[1,2,64,512]{3,2,1,0:T(8,128)(2,1)S(1)} %get-tuple-element.226), channel_id=1, source_target_pairs={{0,8},{1,9},{2,10},{3,11},{4,12},{5,13},{6,14},{7,15},{8,0},{9,1},... | collective-permute-start | bytes 393224 | tf_op jit(solution)/shard_map/ppermute | solution.py:796
  181.1 19.0 %collective-permute-start.33 = (bf16[4,16,1664]{2,1,0:T(8,128)(2,1)S(1)}, bf16[4,16,1664]{2,1,0:T(8,128)(2,1)S(1)}, u32[]{:S(2)}, u32[]{:S(2)}) collective-permute-start(bf16[4,16,1664]{2,1,0:T(8,128)(2,1)S(1)} %pad_maximum_fusion.1), channel_id=1, source_target_pairs={{0,5},{1,4},{2,7},{3,6},{4,1},{5,0},{6,3},{7,2},{8,13},{9,12},{10,... | collective-permute-start | bytes 638984 | tf_op jit(solution)/shard_map/ppermute | solution.py:796
  184.9 11.3 %collective-permute-start.32 = (bf16[4,16,1664]{2,1,0:T(8,128)(2,1)S(1)}, bf16[4,16,1664]{2,1,0:T(8,128)(2,1)S(1)}, u32[]{:S(2)}, u32[]{:S(2)}) collective-permute-start(bf16[4,16,1664]{2,1,0:T(8,128)(2,1)S(1)} %pad_maximum_fusion.1), channel_id=1, source_target_pairs={{0,4},{1,5},{2,6},{3,7},{4,0},{5,1},{6,2},{7,3},{8,12},{9,13},{10,... | collective-permute-start | bytes 638984 | tf_op jit(solution)/shard_map/ppermute | solution.py:796
  191.3 46.5 %collective-permute-start.45 = (bf16[4,2,64,512]{3,2,1,0:T(8,128)(2,1)S(1)}, bf16[4,2,64,512]{3,2,1,0:T(8,128)(2,1)S(1)}, u32[]{:S(2)}, u32[]{:S(2)}) collective-permute-start(bf16[4,2,64,512]{3,2,1,0:T(8,128)(2,1)S(1)} %pad_maximum_fusion), channel_id=1, source_target_pairs={{0,4},{1,5},{2,6},{3,7},{4,0},{5,1},{6,2},{7,3},{8,12},{9,13},{10,... | collective-permute-start | bytes 1572872 | tf_op jit(solution)/shard_map/ppermute | solution.py:796
  196.6 13.2 %collective-permute-start.13 = (bf16[4,16,1024]{2,1,0:T(8,128)(2,1)S(1)}, bf16[4,16,1024]{2,1,0:T(8,128)(2,1)S(1)}, u32[]{:S(2)}, u32[]{:S(2)}) collective-permute-start(bf16[4,16,1024]{2,1,0:T(8,128)(2,1)S(1)} %get-tuple-element.206), channel_id=1, source_target_pairs={{0,1},{1,0},{2,3},{3,2},{4,5},{5,4},{6,7},{7,6},{8,9},{9,8},{10,11... | collective-permute-start | bytes 393224 | tf_op jit(solution)/shard_map/ppermute | solution.py:796
  197.8 12.0 %collective-permute-start.14 = (bf16[4,16,1024]{2,1,0:T(8,128)(2,1)S(1)}, bf16[4,16,1024]{2,1,0:T(8,128)(2,1)S(1)}, u32[]{:S(2)}, u32[]{:S(2)}) collective-permute-start(bf16[4,16,1024]{2,1,0:T(8,128)(2,1)S(1)} %get-tuple-element.207), channel_id=1, source_target_pairs={{0,4},{1,5},{2,6},{3,7},{4,0},{5,1},{6,2},{7,3},{8,12},{9,13},{10,... | collective-permute-start | bytes 393224 | tf_op jit(solution)/shard_map/ppermute | solution.py:796
  199.2 10.6 %collective-permute-start.15 = (bf16[4,16,1024]{2,1,0:T(8,128)(2,1)S(1)}, bf16[4,16,1024]{2,1,0:T(8,128)(2,1)S(1)}, u32[]{:S(2)}, u32[]{:S(2)}) collective-permute-start(bf16[4,16,1024]{2,1,0:T(8,128)(2,1)S(1)} %get-tuple-element.208), channel_id=1, source_target_pairs={{0,5},{1,4},{2,7},{3,6},{4,1},{5,0},{6,3},{7,2},{8,13},{9,12},{10,... | collective-permute-start | bytes 393224 | tf_op jit(solution)/shard_map/ppermute | solution.py:796
  200.2 38.2 %collective-permute-start.34 = (bf16[16,16,1664]{2,1,0:T(8,128)(2,1)S(1)}, bf16[16,16,1664]{2,1,0:T(8,128)(2,1)S(1)}, u32[]{:S(2)}, u32[]{:S(2)}) collective-permute-start(bf16[16,16,1664]{2,1,0:T(8,128)(2,1)S(1)} %get-tuple-element.299), channel_id=1, source_target_pairs={{0,2},{1,3},{2,0},{3,1},{4,6},{5,7},{6,4},{7,5},{8,10},{9,11},{10,... | collective-permute-start | bytes 2555912 | tf_op jit(solution)/shard_map/ppermute | solution.py:796
  209.9 12.4 %collective-permute-start.36 = (bf16[1,16,1024]{2,1,0:T(8,128)(2,1)S(1)}, bf16[1,16,1024]{2,1,0:T(8,128)(2,1)S(1)}, u32[]{:S(2)}, u32[]{:S(2)}) collective-permute-start(bf16[1,16,1024]{2,1,0:T(8,128)(2,1)S(1)} %get-tuple-element.247), channel_id=1, source_target_pairs={{0,16},{1,17},{2,18},{3,19},{4,20},{5,21},{6,22},{7,23},{8,24},{9,... | collective-permute-start | bytes 98312 | tf_op jit(solution)/shard_map/ppermute | solution.py:796
  211.8 10.5 %collective-permute-start.37 = (bf16[1,16,1024]{2,1,0:T(8,128)(2,1)S(1)}, bf16[1,16,1024]{2,1,0:T(8,128)(2,1)S(1)}, u32[]{:S(2)}, u32[]{:S(2)}) collective-permute-start(bf16[1,16,1024]{2,1,0:T(8,128)(2,1)S(1)} %get-tuple-element.249), channel_id=1, source_target_pairs={{0,24},{1,25},{2,26},{3,27},{4,28},{5,29},{6,30},{7,31},{8,16},{9,... | collective-permute-start | bytes 98312 | tf_op jit(solution)/shard_map/ppermute | solution.py:796
  213.0 9.2 %collective-permute-start.35 = (bf16[1,16,1024]{2,1,0:T(8,128)(2,1)S(1)}, bf16[1,16,1024]{2,1,0:T(8,128)(2,1)S(1)}, u32[]{:S(2)}, u32[]{:S(2)}) collective-permute-start(bf16[1,16,1024]{2,1,0:T(8,128)(2,1)S(1)} %get-tuple-element.245), channel_id=1, source_target_pairs={{0,8},{1,9},{2,10},{3,11},{4,12},{5,13},{6,14},{7,15},{8,0},{9,1},... | collective-permute-start | bytes 98312 | tf_op jit(solution)/shard_map/ppermute | solution.py:796
  237.8 8.5 %collective-permute-start.46 = (bf16[8,2,64,512]{3,2,1,0:T(8,128)(2,1)S(1)}, bf16[8,2,64,512]{3,2,1,0:T(8,128)(2,1)}, u32[]{:S(2)}, u32[]{:S(2)}) collective-permute-start(bf16[8,2,64,512]{3,2,1,0:T(8,128)(2,1)S(1)} %constant_dynamic-update-slice_fusion.30.mine_ref), channel_id=1, source_target_pairs={{0,2},{1,3},{2,0},{3,1},{4,6},{5,7},{6,4},{7,5},{8,10},{9,11},{10,... | collective-permute-start | bytes 3145736 | tf_op jit(solution)/shard_map/ppermute | solution.py:796
  (50 other events, 428.1 us)

commit v3 on v2

v3 whole, which is shorter than its diff:
```python
import functools

import jax
import jax.numpy as jnp
from jax import lax
from jax.experimental import pallas as pl
from jax.experimental.pallas import tpu as pltpu
from jax.sharding import PartitionSpec as P

HEADS = 8
HEAD_DIM = 64
BLOCK = 32
ITERS = 8
GROUP = 4
GROUP_WIDTH = GROUP * HEAD_DIM
GROUP_ROWS = GROUP * BLOCK
EPSILON = 1e-05
FACTOR = HEAD_DIM ** (-0.5)
HIGHEST = lax.Precision.HIGHEST
F32 = jnp.float32
BF16 = jnp.bfloat16
NT = (((1,), (1,)), ((), ()))
TN = (((0,), (0,)), ((), ()))
MIB = 1024 * 1024
LANES = 128
TALLY_ROWS = 16


def dot(left, right):
    return jnp.dot(left, right, preferred_element_type=F32)


def dot_nt(left, right):
    return lax.dot_general(left, right, NT, preferred_element_type=F32)


def dot_tn(left, right):
    return lax.dot_general(left, right, TN, preferred_element_type=F32)


def shape_of(dims, dtype):
    return jax.ShapeDtypeStruct(dims, dtype)


def whole(dims):
    return pl.BlockSpec(dims, lambda *_: (0,) * len(dims))


def once(dims):
    return pl.BlockSpec(dims, lambda *_: (0,) * len(dims), pipeline_mode=pl.Buffered(1))


def rows_of(size, width):
    return pl.BlockSpec((size, width), lambda step, *_: (step, 0))


def params(mib):
    return pltpu.CompilerParams(vmem_limit_bytes=mib * MIB)


def far(array):
    return pltpu.with_memory_space_constraint(array, pltpu.HBM)


def near(array):
    return pltpu.with_memory_space_constraint(array, pltpu.VMEM)


def near_shape(dims, dtype):
    return pltpu.VMEM(dims, dtype)


def far_shape(dims, dtype):
    return pltpu.HBM(dims, dtype)


def cost(micros):
    return pl.CostEstimate(flops=int(micros * 1150000000), bytes_accessed=0, transcendentals=0)


def normalize(values):
    center = values - jnp.mean(values, axis=-1, keepdims=True)
    inverse = lax.rsqrt(jnp.mean(center * center, axis=-1, keepdims=True) + EPSILON)
    return center * inverse, inverse


def norm_grad(grad_rows, unit_rows, inverse, gain):
    scaled_rows = grad_rows * gain
    return inverse * (
        scaled_rows
        - jnp.mean(scaled_rows, axis=-1, keepdims=True)
        - unit_rows * jnp.mean(scaled_rows * unit_rows, axis=-1, keepdims=True)
    )


def segment_sum(tile, first):
    left = jnp.sum(jnp.where(first, tile, 0.0), axis=1, keepdims=True)
    right = jnp.sum(jnp.where(first, 0.0, tile), axis=1, keepdims=True)
    return jnp.where(first, left, right)


def segment_max(tile, first):
    left = jnp.max(jnp.where(first, tile, -jnp.inf), axis=1, keepdims=True)
    right = jnp.max(jnp.where(first, -jnp.inf, tile), axis=1, keepdims=True)
    return jnp.where(first, left, right)


def head_masks(rows):
    lane = lax.broadcasted_iota(jnp.int32, (rows, GROUP_WIDTH), 1)
    return [(lane >= h * HEAD_DIM) & (lane < (h + 1) * HEAD_DIM) for h in range(GROUP)]


def expand(rows, masks):
    zero = jnp.zeros_like(rows)
    return jnp.concatenate([jnp.where(mask, rows, zero) for mask in masks], axis=0)


def fold(rows, masks):
    parts = [rows[h * BLOCK : (h + 1) * BLOCK] for h in range(GROUP)]
    result = parts[GROUP - 1]
    for h in range(GROUP - 1):
        result = jnp.where(masks[h], parts[h], result)
    return result


def lane_tiles(blocks):
    lane = lax.broadcasted_iota(jnp.int32, (blocks, 2 * blocks), 1)
    return lane < blocks, jnp.where(lane < blocks, lane, lane - blocks).astype(F32)


def down_rows(row, wide):
    return jnp.broadcast_to(row.astype(F32), (wide, row.shape[1])).T


def balance_plans(logits, perm_row, mask_row, share_ref, log_ref, chosen_ref, entropy_ref):
    blocks = logits.shape[0]
    wide = 2 * blocks
    first, position = lane_tiles(blocks)
    hot = position == down_rows(perm_row, wide)
    real = down_rows(mask_row, wide) > 0.0
    for pair in range(logits.shape[1] // wide):
        span = slice(pair * wide, (pair + 1) * wide)
        tile = logits[:, span]
        for step in range(ITERS):
            top = segment_max(tile, first)
            powers = jnp.exp(tile - top)
            total = segment_sum(powers, first)
            tile = tile - (top + jnp.log(total))
            share_ref[2 * step, :, span] = powers * (1.0 / total)
            top = jnp.max(tile, axis=0, keepdims=True)
            powers = jnp.exp(tile - top)
            total = jnp.sum(powers, axis=0, keepdims=True)
            tile = tile - (top + jnp.log(total))
            if step < ITERS - 1:
                share_ref[2 * step + 1, :, span] = powers * (1.0 / total)
        plan = jnp.exp(tile)
        share_ref[2 * ITERS - 1, :, span] = plan
        log_ref[:, span] = tile
        chosen_ref[:, span] = blocks * segment_sum(jnp.where(hot, plan, 0.0), first)
        entropy_ref[:, span] = -jnp.sum(jnp.where(real, plan * tile, 0.0), axis=0, keepdims=True)


def forward_kernel(
    perm_ref, mask_ref, other_ref, perm_row_ref, mask_row_ref, gain_one_ref, gain_two_ref,
    x_far, wq_far, wk_far, wv_far, ws_far, wo_far, up_far, down_far,
    act_far, q_far, k_far, v_far, probs_far, att_far, second_far, act_two_far, share_far,
    sum_ref, log_ref, chosen_ref, entropy_ref, packed_ref,
    x_ref, w_ref, w_low_ref, wo_low_ref, act_ref, q_ref, k_ref, v_ref, probs_ref, att_ref, second_ref, act_two_ref, share_ref,
    feed_ref, in_sem, out_sem, share_sem, feed_sem, *, tile,
):
    rows, width = x_ref.shape
    tiles = rows // tile

    def x_copy(i):
        at = pl.ds(pl.multiple_of(i * tile, tile), tile)
        return pltpu.make_async_copy(x_far.at[at, :], x_ref.at[at, :], in_sem.at[i])

    def w_copy(n):
        far_ref = (wq_far, wk_far, wv_far, ws_far, wo_far)[n]
        return pltpu.make_async_copy(far_ref, w_ref.at[n], in_sem.at[tiles + n])

    outs = (
        (act_ref, act_far), (q_ref, q_far), (k_ref, k_far), (v_ref, v_far),
        (probs_ref, probs_far), (att_ref, att_far), (second_ref, second_far), (act_two_ref, act_two_far),
    )
    part = 8
    some = part * BLOCK
    parts = rows // some

    def out_copy(n, i):
        near_ref, far_ref = outs[n]
        size = near_ref.shape[0] // (tiles if n < 4 else parts)
        at = pl.ds(pl.multiple_of(i * size, size), size)
        return pltpu.make_async_copy(near_ref.at[at, :], far_ref.at[at, :], out_sem.at[n, i])

    x_copy(0).start()
    for n in range(3):
        w_copy(n).start()
    for i in range(1, tiles):
        x_copy(i).start()
    w_copy(3).start()
    w_copy(4).start()
    units = packed_ref.shape[2]
    at = pl.ds(pl.multiple_of(other_ref[0] * units, units), units)
    feed_copies = [
        pltpu.make_async_copy(up_far.at[:, at], feed_ref.at[0], feed_sem.at[0]),
        pltpu.make_async_copy(down_far.at[at, :], feed_ref.at[1], feed_sem.at[1]),
    ]
    for copy in feed_copies:
        copy.start()
    for n in range(3):
        w_copy(n).wait()
        w_low_ref[:, n * width : (n + 1) * width] = w_ref[n].astype(BF16)

    def prepare(i):
        at = pl.ds(pl.multiple_of(i * tile, tile), tile)
        unit, _ = normalize(x_ref[at, :])
        act = (unit * gain_one_ref[...]).astype(BF16)
        act_ref[at, :] = act
        sums = jnp.sum(act.astype(F32).reshape(tile // BLOCK, BLOCK, width), axis=1)
        some = tile // BLOCK
        sum_ref[pl.ds(pl.multiple_of(i * some, some), some), :] = sums.astype(BF16).astype(F32)

    def project(i):
        at = pl.ds(pl.multiple_of(i * tile, tile), tile)
        act = act_ref[at, :]
        for n, ref in enumerate((q_ref, k_ref, v_ref)):
            ref[at, :] = dot(act, w_low_ref[:, n * width : (n + 1) * width]).astype(BF16)

    def project_out(i):
        for n in range(4):
            out_copy(n, i).start()

    def both(i, _):
        x_copy(i + 1).wait()
        project(i)
        prepare(i + 1)
        project_out(i)
        return 0

    x_copy(0).wait()
    prepare(0)
    lax.fori_loop(0, tiles - 2, both, 0)
    x_copy(tiles - 1).wait()
    prepare(tiles - 1)
    w_copy(3).wait()
    w_copy(4).wait()
    wo_low_ref[...] = w_ref[4].astype(BF16)
    for n, copy in enumerate(feed_copies):
        copy.wait()
        packed_ref[n] = feed_ref[n].astype(BF16)
    logits = jnp.dot(sum_ref[...], w_ref[3], precision=HIGHEST, preferred_element_type=F32)
    balance_plans(
        logits, perm_row_ref[...], mask_row_ref[...], share_ref, log_ref, chosen_ref, entropy_ref
    )
    for i in (tiles - 2, tiles - 1):
        project(i)
    for i in (tiles - 2, tiles - 1):
        project_out(i)
    pltpu.make_async_copy(share_ref, share_far, share_sem).start()

    masks = head_masks(BLOCK)
    key_row = lax.broadcasted_iota(jnp.int32, (BLOCK, GROUP_ROWS), 0)
    query_row = lax.broadcasted_iota(jnp.int32, (BLOCK, GROUP_ROWS), 1) % BLOCK
    causal = key_row <= query_row

    def attend(j):
        for b in range(part):
            block = j * part + b
            partner = perm_ref[block]
            usable = (partner < block) & (mask_ref[partner] > 0)
            own_at = pl.ds(pl.multiple_of(block * BLOCK, BLOCK), BLOCK)
            far_at = pl.ds(pl.multiple_of(partner * BLOCK, BLOCK), BLOCK)
            probs_at = pl.ds(pl.multiple_of(block * 2 * BLOCK, 2 * BLOCK), 2 * BLOCK)
            chosen_row = chosen_ref[pl.ds(block, 1), :]
            for g in range(width // GROUP_WIDTH):
                lanes = slice(g * GROUP_WIDTH, (g + 1) * GROUP_WIDTH)
                queries = expand(q_ref[own_at, lanes], masks)
                keys = jnp.concatenate([k_ref[own_at, lanes], k_ref[far_at, lanes]], axis=0)
                scores = dot_nt(keys, queries) * FACTOR
                own = jnp.where(causal, scores[:BLOCK], -1e30)
                far = jnp.where(usable, scores[BLOCK:], -1e30)
                top = jnp.maximum(jnp.max(own, axis=0, keepdims=True), jnp.max(far, axis=0, keepdims=True))
                powers = jnp.exp(jnp.concatenate([own, far], axis=0) - top)
                probs = (powers * (1.0 / jnp.sum(powers, axis=0, keepdims=True))).astype(BF16)
                probs_ref[probs_at, g * GROUP_ROWS : (g + 1) * GROUP_ROWS] = probs
                scaled = (v_ref[far_at, lanes].astype(F32) * chosen_row[:, lanes]).astype(BF16)
                values = jnp.concatenate([v_ref[own_at, lanes], scaled], axis=0)
                att_ref[own_at, lanes] = fold(dot_tn(probs, values), masks).astype(BF16)

    def settle(j):
        at = pl.ds(pl.multiple_of(j * some, some), some)
        second = x_ref[at, :] + dot(att_ref[at, :], wo_low_ref[...])
        second_ref[at, :] = second
        unit, _ = normalize(second)
        act_two_ref[at, :] = (unit * gain_two_ref[...]).astype(BF16)

    def settle_out(j):
        for n in range(4, 8):
            out_copy(n, j).start()

    def step(j, _):
        settle(j - 1)
        attend(j)
        settle_out(j - 1)
        return 0

    attend(0)
    lax.fori_loop(1, parts, step, 0)
    settle(parts - 1)
    settle_out(parts - 1)
    for n in range(8):
        for i in range(tiles if n < 4 else parts):
            out_copy(n, i).wait()
    pltpu.make_async_copy(share_ref, share_far, share_sem).wait()


def forward(perm, mask, other, perm_row, mask_row, gain_one, gain_two, x, wq, wk, wv, ws, wo, w_up, w_down, tile=512):
    rows, width = x.shape
    blocks = rows // BLOCK
    tiles = rows // tile
    smem = pl.BlockSpec(memory_space=pltpu.SMEM)
    vmem = pl.BlockSpec(memory_space=pltpu.VMEM)
    hbm = pl.BlockSpec(memory_space=pltpu.HBM)
    low = ((rows, width), BF16)
    probs = ((2 * rows, HEADS * BLOCK), BF16)
    full = ((rows, width), F32)
    share = ((2 * ITERS, blocks, width), F32)
    plan = ((blocks, width), F32)
    packed = ((2, width, width), BF16)
    return pl.pallas_call(
        functools.partial(forward_kernel, tile=tile),
        in_specs=[smem] * 3 + [vmem] * 4 + [hbm] * 8,
        out_specs=[hbm] * 9 + [vmem] * 5,
        out_shape=[far_shape(*s) for s in (low, low, low, low, probs, low, full, low, share)]
        + [near_shape(*s) for s in (plan, plan, plan, ((1, width), F32), packed)],
        scratch_shapes=[pltpu.VMEM(*full), pltpu.VMEM((5, width, width), F32), pltpu.VMEM((width, 3 * width), BF16)]
        + [pltpu.VMEM((width, width), BF16)]
        + [pltpu.VMEM(*s) for s in (low, low, low, low, probs, low, full, low, share)]
        + [
            pltpu.VMEM((2, width, width), F32),
            pltpu.SemaphoreType.DMA((tiles + 5,)),
            pltpu.SemaphoreType.DMA((8, rows // (8 * BLOCK))),
            pltpu.SemaphoreType.DMA,
            pltpu.SemaphoreType.DMA((2,)),
        ],
        compiler_params=params(40),
        cost_estimate=cost(25),
        name="forward",
    )(
        perm, mask, other, perm_row, mask_row, gain_one, gain_two, far(x), far(wq), far(wk), far(wv), far(ws), far(wo),
        far(w_up), far(w_down),
    )


def attend_back_kernel(
    perm_ref, chosen_ref, gatt_ref, q_far, probs_far, k_far, v_far,
    gq_ref, gk_ref, gv_ref, gch_ref,
    q_ref, probs_ref, k_ref, v_ref, own_k_ref, far_k_ref, own_v_ref, far_v_ref, sems, *, group, part,
):
    rows, width = q_ref.shape
    parts = rows // (part * BLOCK)
    masks = head_masks(BLOCK)

    def copies():
        for n, (far_ref, near_ref) in enumerate(((k_far, k_ref), (v_far, v_ref), (q_far, q_ref), (probs_far, probs_ref))):
            cols = near_ref.shape[1]
            lanes = pl.ds(group * cols, cols)
            yield pltpu.make_async_copy(far_ref.at[:, lanes], near_ref, sems.at[n])

    for copy in copies():
        copy.start()
    for copy in copies():
        copy.wait()

    def body(j, _):
        for b in range(part):
            block = j * part + b
            partner = perm_ref[block]
            own_at = pl.ds(pl.multiple_of(block * BLOCK, BLOCK), BLOCK)
            far_at = pl.ds(pl.multiple_of(partner * BLOCK, BLOCK), BLOCK)
            probs_at = pl.ds(pl.multiple_of(block * 2 * BLOCK, 2 * BLOCK), 2 * BLOCK)
            queries = expand(q_ref[own_at, :], masks)
            grads = expand(gatt_ref[own_at, group * width : (group + 1) * width], masks)
            keys = jnp.concatenate([k_ref[own_at, :], k_ref[far_at, :]], axis=0)
            far_values = v_ref[far_at, :].astype(F32)
            chosen = chosen_ref[pl.ds(block, 1), group * width : (group + 1) * width]
            values = jnp.concatenate([v_ref[own_at, :], (far_values * chosen).astype(BF16)], axis=0)
            probs_low = probs_ref[probs_at, :]
            probs = probs_low.astype(F32)
            grad_probs = dot_nt(values, grads)
            total = jnp.sum(probs * grad_probs, axis=0, keepdims=True)
            grad_scores = (probs * (grad_probs - total)).astype(BF16)
            grad_keys = dot(grad_scores, queries) * FACTOR
            grad_values = dot(probs_low, grads)
            gq_ref[own_at, :] = (fold(dot_tn(grad_scores, keys), masks) * FACTOR).astype(BF16)
            far_grad = grad_values[BLOCK:]
            gch_ref[pl.ds(block, 1), :] = jnp.sum(far_grad * far_values, axis=0, keepdims=True)
            own_k_ref[own_at, :] = grad_keys[:BLOCK]
            far_k_ref[far_at, :] = grad_keys[BLOCK:]
            own_v_ref[own_at, :] = grad_values[:BLOCK]
            far_v_ref[far_at, :] = far_grad * chosen
        return 0

    lax.fori_loop(0, parts, body, 0)
    gk_ref[...] = (own_k_ref[...] + far_k_ref[...]).astype(BF16)
    gv_ref[...] = (own_v_ref[...] + far_v_ref[...]).astype(BF16)


def attend_back(perm, q, gatt, probs, k, v, chosen, group, part=8):
    rows = q.shape[0]
    smem = pl.BlockSpec(memory_space=pltpu.SMEM)
    vmem = pl.BlockSpec(memory_space=pltpu.VMEM)
    hbm = pl.BlockSpec(memory_space=pltpu.HBM)
    low = ((rows, GROUP_WIDTH), BF16)
    full = ((rows, GROUP_WIDTH), F32)
    return pl.pallas_call(
        functools.partial(attend_back_kernel, group=group, part=part),
        in_specs=[smem, vmem, vmem] + [hbm] * 4,
        out_specs=[vmem] * 4,
        out_shape=[near_shape(*s) for s in (low, low, low, ((rows // BLOCK, GROUP_WIDTH), F32))],
        scratch_shapes=[pltpu.VMEM(*s) for s in (low, ((2 * rows, GROUP_ROWS), BF16), low, low, full, full, full, full)]
        + [pltpu.SemaphoreType.DMA((4,))],
        compiler_params=params(18),
        cost_estimate=cost(10),
        name="attend_back",
    )(perm, near(chosen), near(gatt), far(q), far(probs), far(k), far(v))


def gelu_pair(up):
    square = up * up
    inner = 0.7978845608028654 * 0.044715
    half = 0.5 + 0.5 * jnp.tanh(up * (0.7978845608028654 + inner * square))
    value = up * half
    slope = half + (2.0 * value) * (1.0 - half) * (0.7978845608028654 + 3.0 * inner * square)
    return value, slope


def spread(out_ref, acc_ref, where, lanes):
    chunks, size = out_ref.shape[0], out_ref.shape[-2]
    for r in range(chunks):
        at = pl.multiple_of((r ^ where) * size, size)
        out_ref[r, :, lanes] = acc_ref[pl.ds(at, size), :].astype(out_ref.dtype)


class Copies:
    def __init__(self, source, target, sems, tile):
        self.source, self.target, self.sems, self.tile = source, target, sems, tile

    def copy(self, i):
        at = pl.ds(pl.multiple_of(i * self.tile, self.tile), self.tile)
        return pltpu.make_async_copy(self.source.at[at, :], self.target.at[at, :], self.sems.at[i])

    def start(self, i):
        self.copy(i).start()

    def wait(self, i):
        self.copy(i).wait()


def quarter_math(act, cot_low, weights_ref, up_acc, down_acc):
    value, slope = gelu_pair(dot(act, weights_ref[0]))
    hidden = value.astype(BF16)
    grad_up = (dot_nt(cot_low, weights_ref[1]) * slope).astype(BF16)
    up_acc[...] += dot_tn(act, grad_up)
    down_acc[...] += dot_tn(cot_low, hidden)
    return hidden, dot_nt(grad_up, weights_ref[0])


def quarter_kernel(*refs, kind, tile, tally):
    if tally:
        mask_ref, refs = refs[0], refs[1:]
    where_ref, act_ref, weights_ref = refs[:3]
    if kind == "first":
        cot_far, hidden_far, grad_ref, piece_ref, low_ref, act_ref = refs[3:9]
        hidden_ref, up_acc, down_acc, hidden_sems, cot_ref, cot_sems, act_sems = refs[9:]
    elif kind == "middle":
        low_ref, sofar_ref, hidden_far, grad_ref, piece_ref = refs[3:8]
        hidden_ref, up_acc, down_acc, hidden_sems = refs[8:]
    else:
        low_ref, sofar_ref, gain_ref, entropy_ref, cot_far, second_far, att_far, wo_far = refs[3:11]
        hidden_far, gsec_far, piece_ref, gatt_ref, gout_ref = refs[11:16]
        hidden_ref, up_acc, down_acc, hidden_sems, cot_ref, cot_sems = refs[16:22]
        second_ref, second_sems, att_ref, att_sems, gsec_ref, gsec_sems = refs[22:28]
        wo_ref, wo_low_ref, wo_sem, out_acc, gain_acc, column_ref, sum_ref = refs[28:]
    rows, width = act_ref.shape
    tiles = rows // tile
    hidden_out = Copies(hidden_ref, hidden_far, hidden_sems, tile)
    ins = []
    if kind == "first":
        ins = [Copies(cot_far, cot_ref, cot_sems, tile), Copies(refs[1], act_ref, act_sems, tile)]
    if kind == "last":
        ins = [
            Copies(second_far, second_ref, second_sems, tile),
            Copies(cot_far, cot_ref, cot_sems, tile),
            Copies(att_far, att_ref, att_sems, tile),
        ]
        gsec_out = Copies(gsec_ref, gsec_far, gsec_sems, tile)
    for i in range(tiles):
        for copies in ins:
            copies.start(i)
        if kind == "last" and i == 0:
            wo_copy = pltpu.make_async_copy(wo_far, wo_ref, wo_sem)
            wo_copy.start()
    up_acc[...] = jnp.zeros_like(up_acc)
    down_acc[...] = jnp.zeros_like(down_acc)
    if kind == "last":
        out_acc[...] = jnp.zeros_like(out_acc)
        gain_acc[...] = jnp.zeros_like(gain_acc)
        wo_copy.wait()
        wo_low_ref[...] = wo_ref[...].astype(BF16)

    def multiply(i):
        at = pl.ds(pl.multiple_of(i * tile, tile), tile)
        if kind == "first":
            low_ref[at, :] = cot_ref[at, :].astype(BF16)
        hidden, grad = quarter_math(act_ref[at, :], low_ref[at, :], weights_ref, up_acc, down_acc)
        hidden_ref[at, :] = hidden
        if kind == "first":
            grad_ref[at, :] = grad
        elif kind == "middle":
            grad_ref[at, :] = sofar_ref[at, :] + grad
        else:
            sum_ref[i % 2] = sofar_ref[at, :] + grad

    def settle(i):
        at = pl.ds(pl.multiple_of(i * tile, tile), tile)
        grad = sum_ref[i % 2]
        unit, inverse = normalize(second_ref[at, :])
        gain_acc[...] += jnp.sum(grad * unit, axis=0, keepdims=True)
        grad_second = cot_ref[at, :] + norm_grad(grad, unit, inverse, gain_ref[...])
        gsec_ref[at, :] = grad_second
        second_low = grad_second.astype(BF16)
        gatt_ref[at, :] = dot_nt(second_low, wo_low_ref[...]).astype(BF16)
        out_acc[...] += dot_tn(att_ref[at, :], second_low)

    def body(i, _):
        for copies in ins:
            copies.wait(i - 1 if kind == "last" else i)
        if kind == "last":
            settle(i - 1)
        multiply(i)
        if kind == "last":
            gsec_out.start(i - 1)
        hidden_out.start(i)
        return 0

    if kind == "last":
        multiply(0)
        hidden_out.start(0)
        lax.fori_loop(1, tiles, body, 0)
        for copies in ins:
            copies.wait(tiles - 1)
        settle(tiles - 1)
        gsec_out.start(tiles - 1)
    else:
        lax.fori_loop(0, tiles, body, 0)
    size = width // piece_ref.shape[0]
    spread(piece_ref.at[:, :size], up_acc, where_ref[0], slice(None))
    spread(piece_ref.at[:, size : 2 * size], down_acc, where_ref[0], slice(None))
    if tally:
        shape = (TALLY_ROWS, weights_ref.shape[2])
        mine = lax.broadcasted_iota(jnp.int32, shape, 1) == where_ref[3]
        count = jnp.sum(mask_ref[...].astype(F32), axis=1, keepdims=True)
        row = jnp.where(mine, jnp.broadcast_to(count, shape), 0.0).astype(BF16)
        for r in range(piece_ref.shape[0]):
            piece_ref[r, 2 * size :, :] = row
    if kind == "last":
        spread(gout_ref, out_acc, where_ref[2], slice(0, width))
        half = (LANES // 2, width)
        column_ref[...] = jnp.concatenate(
            [jnp.broadcast_to(gain_acc[...], half), jnp.broadcast_to(entropy_ref[...], half)], axis=0
        ).T
        spread(gout_ref, column_ref, where_ref[2], slice(width, width + LANES))
    for i in range(tiles):
        hidden_out.wait(i)
        if kind == "last":
            gsec_out.wait(i)


def feed_quarter(
    kind, where, act, weights, cot, sofar=None, extra=None, mask_row=None, row_chunks=1, out_chunks=1, tile=512
):
    rows, width = act.shape
    units = weights.shape[2]
    tiles = rows // tile
    smem = pl.BlockSpec(memory_space=pltpu.SMEM)
    vmem = pl.BlockSpec(memory_space=pltpu.VMEM)
    hbm = pl.BlockSpec(memory_space=pltpu.HBM)
    tally = mask_row is not None
    size = 2 * (width // row_chunks) + (TALLY_ROWS if tally else 0)
    piece = near_shape((row_chunks, size, units), BF16)
    low = near_shape((rows, width), BF16)
    full = near_shape((rows, width), F32)
    hidden = far_shape((rows, units), BF16)
    sems = pltpu.SemaphoreType.DMA((tiles,))
    low_buffer, full_buffer = pltpu.VMEM((rows, width), BF16), pltpu.VMEM((rows, width), F32)
    square = pltpu.VMEM((width, width), F32)
    scratch = [pltpu.VMEM((rows, units), BF16), square, square, sems]
    if kind == "first":
        operands = (far(cot),)
        in_specs = [hbm]
        out_shape, out_specs = [hidden, full, piece, low, low], [hbm] + [vmem] * 4
        scratch = scratch + [full_buffer, sems, sems]
        limit = 24
    elif kind == "middle":
        operands = (near(cot), near(sofar))
        in_specs = [vmem] * 2
        out_shape, out_specs = [hidden, full, piece], [hbm] + [vmem] * 2
        limit = 18
    else:
        full_cot, second, att, w_out, gain, entropy = extra
        operands = (near(cot), near(sofar), gain, entropy, far(full_cot), far(second), far(att), far(w_out))
        in_specs = [vmem] * 4 + [hbm] * 4
        out_piece = near_shape((out_chunks, width // out_chunks, width + LANES), BF16)
        out_shape = [hidden, far_shape((rows, width), F32), piece, low, out_piece]
        out_specs = [hbm] * 2 + [vmem] * 3
        scratch = scratch + [full_buffer, sems, full_buffer, sems, low_buffer, sems, full_buffer, sems]
        scratch = scratch + [square, pltpu.VMEM((width, width), BF16), pltpu.SemaphoreType.DMA]
        scratch = scratch + [square, pltpu.VMEM((1, width), F32), pltpu.VMEM((width, LANES), F32)]
        scratch = scratch + [pltpu.VMEM((2, tile, width), F32)]
        limit = 32
    return pl.pallas_call(
        functools.partial(quarter_kernel, kind=kind, tile=tile, tally=tally),
        in_specs=([vmem] if tally else []) + [smem, hbm if kind == "first" else vmem, vmem] + in_specs,
        out_specs=out_specs,
        out_shape=out_shape,
        scratch_shapes=scratch,
        compiler_params=params(limit),
        cost_estimate=cost(9),
        name="feed_" + kind,
    )(
        *([mask_row] if tally else []), where, far(act) if kind == "first" else near(act), near(weights), *operands
    )


def output_kernel(second_ref, *refs):
    out_ref = refs[-1]
    count = (len(refs) - 1) // 2
    total = second_ref[...]
    for hidden_ref, weights_ref in zip(refs[:count], refs[count : 2 * count]):
        total = total + dot(hidden_ref[...], weights_ref[0])
    out_ref[...] = total


def layer_output(second, hidden, weights, tile=512):
    rows, width = second.shape
    units = hidden[0].shape[1]
    down = pl.BlockSpec((1, units, width), lambda *_: (1, 0, 0), pipeline_mode=pl.Buffered(1))
    return pl.pallas_call(
        output_kernel,
        grid=(rows // tile,),
        in_specs=[rows_of(tile, width)] + [rows_of(tile, units)] * len(hidden) + [down] * len(hidden),
        out_specs=rows_of(tile, width),
        out_shape=far_shape((rows, width), F32),
        compiler_params=params(16),
        cost_estimate=cost(8),
        name="layer_output",
    )(near(second), *[far(array) for array in hidden], *[near(array) for array in weights])


def head_kernel(*refs, count):
    where_ref, pen_ref, act_ref = refs[:3]
    groups = [refs[3 + 4 * g : 7 + 4 * g] for g in range(count)]
    share_ref, log_ref, sum_ref, w_ref, perm_ref, mask_ref, out_ref, tally_ref = refs[3 + 4 * count : 11 + 4 * count]
    piece_ref, gsum_ref, total_ref, glog_ref, acc_ref = refs[11 + 4 * count :]
    block_total = jnp.sum(tally_ref[...].astype(F32), axis=1, keepdims=True)
    block_total = jnp.sum(block_total, axis=0, keepdims=True)
    total_ref[...] = jnp.broadcast_to(block_total, total_ref.shape)
    coef = pen_ref[0] / (HEADS * block_total)
    blocks, width = sum_ref.shape
    cols = acc_ref.shape[1]
    wide = 2 * blocks
    first, position = lane_tiles(blocks)
    hot = position == down_rows(perm_ref[...], wide)
    weight = coef * down_rows(mask_ref[...], wide)
    act = act_ref[...]
    for g, group in enumerate(groups):
        for index in range(3):
            acc_ref[...] = dot_tn(act, group[index][...])
            at = index * width + g * cols
            spread(piece_ref, acc_ref, where_ref[2], slice(at, at + cols))
        for pair in range(cols // wide):
            at = g * cols + pair * wide
            span = slice(at, at + wide)
            plan = share_ref[2 * ITERS - 1, :, span]
            gch = segment_sum(group[3][:, pair * wide : (pair + 1) * wide], first)
            grad = plan * (jnp.where(hot, blocks * gch, 0.0) - weight * (log_ref[:, span] + 1.0))
            for level in range(2 * ITERS - 1, -1, -1):
                if level % 2:
                    total = jnp.sum(grad, axis=0, keepdims=True)
                else:
                    total = segment_sum(grad, first)
                grad = grad - share_ref[level, :, span] * total
            glog_ref[:, span] = grad
    for g in range(count):
        at = slice(g * cols, (g + 1) * cols)
        acc_ref[...] = lax.dot_general(
            sum_ref[...], glog_ref[:, at], TN, precision=HIGHEST, preferred_element_type=F32
        )
        spread(piece_ref, acc_ref, where_ref[2], slice(3 * width + g * cols, 3 * width + (g + 1) * cols))
    gsum_ref[...] = lax.dot_general(glog_ref[...], w_ref[...], NT, precision=HIGHEST, preferred_element_type=F32)
    piece_ref[:, :, 4 * width :] = out_ref[...]


def head_grads(
    where, pen_weight, act, groups, shares, plan_log, sums, w_sort, perm_row, mask_row, out_piece, tallies, chunks
):
    rows, width = act.shape
    blocks = sums.shape[0]
    cols = groups[0][0].shape[1]
    smem = pl.BlockSpec(memory_space=pltpu.SMEM)
    vmem = pl.BlockSpec(memory_space=pltpu.VMEM)
    flat = [near(array) for group in groups for array in group]
    piece = (chunks, width // chunks, 4 * width + out_piece.shape[2])
    return pl.pallas_call(
        functools.partial(head_kernel, count=len(groups)),
        in_specs=[smem] * 2 + [vmem] * (9 + len(flat)),
        out_specs=[vmem] * 3,
        out_shape=[near_shape(piece, BF16), near_shape((blocks, width), F32), near_shape((1, LANES), F32)],
        scratch_shapes=[pltpu.VMEM((blocks, width), F32), pltpu.VMEM((width, cols), F32)],
        compiler_params=params(14),
        cost_estimate=cost(6),
        name="head_grads",
    )(
        where, pen_weight, near(act), *flat, near(shares), near(plan_log), near(sums), near(w_sort), perm_row, mask_row,
        near(out_piece), tallies,
    )


def input_kernel(*refs):
    count = (len(refs) - 9) // 3
    groups = [refs[3 * g : 3 * g + 3] for g in range(count)]
    gsum_ref, x_ref, gsec_ref, gain_ref, wq_ref, wk_ref, wv_ref, out_ref, w_ref = refs[3 * count :]

    @pl.when(pl.program_id(0) == 0)
    def _():
        for which, ref in enumerate((wq_ref, wk_ref, wv_ref)):
            w_ref[which] = ref[...].astype(BF16)

    rows, width = x_ref.shape
    grad = jnp.zeros((rows, width), F32)
    for g, group in enumerate(groups):
        for which, ref in enumerate(group):
            cols = ref.shape[1]
            grad = grad + dot_nt(ref[...], w_ref[which, :, g * cols : (g + 1) * cols])
    grad = (grad.reshape(rows // BLOCK, BLOCK, width) + gsum_ref[...][:, None, :]).reshape(rows, width)
    unit, inverse = normalize(x_ref[...])
    out_ref[...] = gsec_ref[...] + norm_grad(grad, unit, inverse, gain_ref[...])


def input_grad(groups, gsum, x, gsec, gain, wq, wk, wv, tile=512):
    rows, width = x.shape
    weight = pl.BlockSpec((width, width), lambda *_: (0, 0), pipeline_mode=pl.Buffered(1))
    flat = [array for group in groups for array in group]
    return pl.pallas_call(
        input_kernel,
        grid=(rows // tile,),
        in_specs=[rows_of(tile, array.shape[1]) for array in flat]
        + [rows_of(tile // BLOCK, width)]
        + [rows_of(tile, width)] * 2
        + [whole((1, width))]
        + [weight] * 3,
        out_specs=rows_of(tile, width),
        out_shape=far_shape((rows, width), F32),
        scratch_shapes=[pltpu.VMEM((3, width, width), BF16)],
        compiler_params=params(20),
        cost_estimate=cost(10),
        name="input_grad",
    )(*[near(array) for array in flat], gsum, far(x), far(gsec), gain, far(wq), far(wk), far(wv))


def pack_kernel(core_ref, up_ref, down_ref, mine_ref):
    mine_ref[0] = up_ref[...].astype(BF16)
    mine_ref[1] = down_ref[...].astype(BF16)


def pack_weights(core, w_up, w_down):
    width, units = w_up.shape
    half = units // 2
    shape = (2, width, half)
    return pl.pallas_call(
        pack_kernel,
        grid_spec=pltpu.PrefetchScalarGridSpec(
            num_scalar_prefetch=1,
            grid=(1,),
            in_specs=[
                pl.BlockSpec((width, half), lambda step, core: (0, core[0])),
                pl.BlockSpec((half, width), lambda step, core: (core[0], 0)),
            ],
            out_specs=whole(shape),
        ),
        out_shape=near_shape(shape, BF16),
        compiler_params=params(12),
        cost_estimate=cost(2),
        name="pack_weights",
    )(core, far(w_up), far(w_down))


def finish_feed_kernel(*refs):
    where_ref, parts = refs[0], refs[1:-3]
    up_ref, down_ref, turn_ref = refs[-3:]
    some, size, units = parts[0].shape
    size = size // 2
    half = len(parts) // 2
    for flip in range(2):
        column = pl.multiple_of((where_ref[1] ^ flip) * units, units)
        for n, ref in enumerate(parts[flip * half : (flip + 1) * half]):
            for r in range(some):
                at = pl.multiple_of(((n * some + r) ^ where_ref[0]) * size, size)
                up_ref[pl.ds(at, size), pl.ds(column, units)] = ref[r, :size].astype(F32)
                turn_ref[pl.ds(at, size), :] = ref[r, size:].astype(F32)
        down_ref[pl.ds(column, units), :] = turn_ref[...].T


def finish_feed(where, parts):
    some, size, units = parts[0].shape
    width = len(parts) // 2 * some * size // 2
    vmem = pl.BlockSpec(memory_space=pltpu.VMEM)
    return pl.pallas_call(
        finish_feed_kernel,
        in_specs=[pl.BlockSpec(memory_space=pltpu.SMEM)] + [vmem] * len(parts),
        out_specs=[vmem, vmem],
        out_shape=[far_shape((width, 2 * units), F32), far_shape((2 * units, width), F32)],
        scratch_shapes=[pltpu.VMEM((width, units), F32)],
        compiler_params=params(16),
        cost_estimate=cost(3),
        name="finish_feed",
    )(where, *parts)


def finish_kernel(*refs):
    where_ref, parts = refs[0], refs[1:-22]
    weights = refs[-22:-18]
    gain_ref, total_ref = refs[-18:-16]
    fars = refs[-16:-11]
    gain_one_ref, gain_two_ref, penalty_ref = refs[-11:-8]
    nears = refs[-8:-3]
    one_ref, two_ref, sems = refs[-3:]
    width = gain_ref.shape[1]
    some, size = parts[0].shape[:2]
    total = jnp.zeros((width, LANES), F32)
    copies = []
    for index, near_ref in enumerate(nears):
        for n, part_ref in enumerate(parts):
            for r in range(some):
                rows = pl.ds(pl.multiple_of(((n * some + r) ^ where_ref[2]) * size, size), size)
                near_ref[rows, :] = part_ref[r, :, index * width : (index + 1) * width].astype(F32)
                if index == 0:
                    two_ref[rows, :] = part_ref[r, :, 5 * width :].astype(F32)
        copies.append(pltpu.make_async_copy(near_ref, fars[index], sems.at[index]))
        copies[-1].start()
    for at in range(0, width, LANES):
        span = slice(at, at + LANES)
        for grad, weight in zip(nears[:3], weights[:3]):
            total = total + grad[:, span] * weight[:, span].astype(BF16).astype(F32)
        total = total + nears[3][:, span] * weights[3][:, span]
    one_ref[...] = total
    gain_one_ref[...] = jnp.sum(one_ref[...].T, axis=0, keepdims=True) / gain_ref[...]
    turned = two_ref[...].T
    gain_two_ref[...] = turned[:1, :]
    entropy = jnp.sum(turned[LANES // 2 : LANES // 2 + 1, :], axis=1, keepdims=True)
    penalty_ref[...] = entropy / (HEADS * total_ref[:, :1])
    for copy in copies:
        copy.wait()


def finish(where, parts, wq, wk, wv, ws, gain, total):
    width = wq.shape[0]
    vmem = pl.BlockSpec(memory_space=pltpu.VMEM)
    hbm = pl.BlockSpec(memory_space=pltpu.HBM)
    square = far_shape((width, width), F32)
    row = shape_of((1, width), F32)
    return pl.pallas_call(
        finish_kernel,
        in_specs=[pl.BlockSpec(memory_space=pltpu.SMEM)] + [vmem] * (6 + len(parts)),
        out_specs=[hbm] * 5 + [vmem] * 3,
        out_shape=[square] * 5 + [row] * 2 + [shape_of((1, 1), F32)],
        scratch_shapes=[pltpu.VMEM((width, width), F32)] * 5
        + [pltpu.VMEM((width, LANES), F32)] * 2
        + [pltpu.SemaphoreType.DMA((5,))],
        compiler_params=params(16),
        cost_estimate=cost(5),
        name="finish",
    )(where, *parts, near(wq), near(wk), near(wv), near(ws), gain, total)


MP, CORE, X, Z_LOW, Z_HIGH = 1, 2, 4, 8, 16
CORE_STEP = ((CORE,), (CORE,))
FEED_STEPS = ((X,), (Z_LOW, Z_HIGH, Z_LOW + Z_HIGH))
HEAD_STEPS = ((CORE,), (MP, X, MP + X), (Z_LOW, Z_HIGH, Z_LOW + Z_HIGH))


def swap(array, flip):
    count = lax.axis_size("batch") * lax.axis_size("mp")
    return lax.ppermute(array, ("batch", "mp"), [(i, i ^ flip) for i in range(count)])


def place(steps, index):
    result = jnp.int32(0)
    for step in steps:
        for bit in reversed(step[: (len(step) + 1).bit_length() - 1]):
            result = 2 * result + ((index & bit) > 0).astype(jnp.int32)
    return result


def add_low(first, *others):
    total = first.astype(F32)
    for array in others:
        total = total + array.astype(F32)
    return total.astype(BF16)


class Walk:
    def __init__(self, pieces, steps):
        self.pieces = pieces
        self.down = list(steps)
        self.up = list(reversed(steps))
        self.parts, self.arrived = None, []

    def added(self, plan, count):
        pieces = self.pieces + [plan.after(array) for array in self.arrived]
        self.arrived = []
        size = pieces[0].shape[0] // count
        if len(pieces) == 1 and count == 1:
            return pieces
        return [
            add_low(*[piece[n * size : (n + 1) * size] for piece in pieces]) if len(pieces) > 1
            else pieces[0][n * size : (n + 1) * size]
            for n in range(count)
        ]

    def reduce(self, plan):
        flips = self.down.pop(0)
        parts = self.added(plan, len(flips) + 1)
        self.arrived = [swap(plan.after(part), flip) for part, flip in zip(parts[1:], flips)]
        self.pieces = parts[:1]
        return self.arrived

    def reduced(self, plan):
        return self.added(plan, 1)[0]

    def gather(self, plan, value):
        flips = self.up.pop(0)
        self.parts = [value]
        mine = plan.after(value)
        self.arrived = [swap(mine, flip) for flip in flips]
        return self.arrived

    def gathered(self, plan):
        parts = self.parts + [plan.after(array) for array in self.arrived]
        self.arrived = []
        return parts


class Schedule:
    def __init__(self):
        self.pending, self.launched, self.done = [], [], None

    def after(self, array):
        return lax.optimization_barrier((array, self.done))[0]

    def enter(self, small):
        tied = lax.optimization_barrier((small, *self.pending))[0]
        self.pending, self.launched = self.launched, []
        return tied

    def leave(self, *arrays):
        self.pending.extend(arrays)
        self.done = arrays[0]

    def launch(self, *arrays):
        for array in arrays:
            self.launched.extend(array if isinstance(array, list) else [array])


def local_small(
    inputs, cotangent, block_perm, block_mask, pen_weight, w_query, w_key, w_value, w_out, w_sort,
    gain_one, gain_two, w_up, w_down,
):
    _, rows, width = inputs.shape
    x = inputs.reshape(rows, width)
    cot = cotangent.reshape(rows, width)
    perm = block_perm.reshape(-1)
    mask = block_mask.reshape(-1)
    perm_row = block_perm.reshape(1, -1)
    mask_row = block_mask.reshape(1, -1)
    gain_one_row = gain_one.reshape(1, width)
    gain_two_row = gain_two.reshape(1, width)
    batch, mp = lax.axis_index("batch"), lax.axis_index("mp")
    core = batch & 1
    index = batch * 2 + mp
    where = jnp.stack([place(FEED_STEPS, index), core, place(HEAD_STEPS, index), index])
    row_chunks, out_chunks = 8, 32
    plan = Schedule()

    count = jnp.broadcast_to(jnp.sum(mask.astype(F32)), (8, LANES))
    own_a = pack_weights(core.reshape(1), w_up, w_down)
    far_a = swap(own_a, MP)
    plan.leave(own_a)
    act_one, q, k, v, probs, att, second, act_two_far, shares, sums, plan_log, chosen, entropy, own_b = forward(
        perm, mask, (1 - core).reshape(1), perm_row, mask_row, plan.enter(gain_one_row), gain_two_row, x,
        w_query, w_key, w_value, w_sort, w_out, w_up, w_down,
    )
    plan.leave(entropy)
    plan.pending.append(far_a)

    far_b = swap(plan.after(far_a), CORE)
    plan.launch(far_b)
    hid_a, sofar, other_piece, cot_low, act_two = feed_quarter(
        "first", plan.enter(where), act_two_far, far_a, cot, mask_row=mask_row, row_chunks=row_chunks
    )
    plan.leave(other_piece)

    hid_b, sofar, piece = feed_quarter(
        "middle", plan.enter(where), act_two, far_b, cot_low, sofar, mask_row=mask_row, row_chunks=row_chunks
    )
    plan.leave(piece)

    arrived = swap(plan.after(piece), CORE)
    plan.launch(arrived)
    hid_c, sofar, piece = feed_quarter(
        "middle", plan.enter(where), act_two, own_b, cot_low, sofar, row_chunks=row_chunks
    )
    plan.leave(piece)

    other = Walk([other_piece, plan.after(arrived)], FEED_STEPS)
    arrived = swap(plan.after(piece), CORE)
    plan.launch(arrived, other.reduce(plan))
    extra = (cot, second, att, w_out, gain_two_row, entropy)
    hid_d, grad_second, piece, grad_att, out_piece = feed_quarter(
        "last", plan.enter(where), act_two, own_a, cot_low, sofar, extra, None, row_chunks, out_chunks
    )
    plan.leave(grad_att)

    own = Walk([piece, plan.after(arrived)], FEED_STEPS)
    plan.launch(own.reduce(plan), other.reduce(plan))
    groups = [attend_back(plan.enter(perm), q, grad_att, probs, k, v, chosen, 0)]
    plan.leave(groups[0][3])

    other_sum = other.reduced(plan)
    crossed = swap(plan.after(other_sum), MP)
    plan.launch(crossed, own.reduce(plan))
    plan.pending.extend(own.pieces)
    groups.append(attend_back(plan.enter(perm), q, grad_att, probs, k, v, chosen, 1))
    plan.leave(groups[1][3])

    crossed = plan.after(crossed)
    rows_fed = own.pieces[0].shape[1]
    tallies = jnp.concatenate([other_sum[0, rows_fed:], crossed[0, rows_fed:]], axis=0)
    tallies = tallies.reshape(2, TALLY_ROWS, -1)[:, 0]
    own.pieces.append(crossed[:, :rows_fed])
    value = own.reduced(plan)
    plan.launch(own.gather(plan, value))
    plan.pending.append(value)
    piece, gsum, block_total = head_grads(
        plan.enter(where), pen_weight, act_one, groups, shares, plan_log, sums, w_sort, perm_row, mask_row, out_piece,
        tallies, out_chunks,
    )
    plan.leave(gsum)

    head = Walk([piece], HEAD_STEPS)
    plan.pending.extend(head.reduce(plan))
    plan.launch(head.reduce(plan))
    plan.pending.extend(head.pieces)
    grad_input = input_grad(
        [group[:3] for group in groups], gsum, x, grad_second, plan.enter(gain_one_row), w_query, w_key, w_value
    )
    plan.leave(grad_input)

    head.reduce(plan)
    own.gather(plan, jnp.concatenate(own.gathered(plan), axis=0))
    head.gather(plan, head.reduced(plan))
    value = jnp.concatenate(head.gathered(plan), axis=0)
    plan.pending.append(value)
    head.gather(plan, value)
    quarters = (far_a, far_b, own_b, own_a)
    output = layer_output(plan.enter(second), (hid_a, hid_b, hid_c, hid_d), quarters)
    plan.leave(output)

    parts = own.parts + own.arrived
    grad_up, grad_down = finish_feed(plan.enter(where), parts + [swap(part, CORE) for part in parts])
    plan.leave(grad_up)
    parts = head.gathered(plan)
    parts = parts + [swap(part, CORE) for part in parts]
    grad_query, grad_key, grad_value, grad_sort, grad_out, grad_gain_one, grad_gain_two, penalty = finish(
        where, parts, w_query, w_key, w_value, w_sort, gain_one_row, block_total
    )
    return (
        output.reshape(inputs.shape),
        penalty.reshape(1),
        grad_input.reshape(inputs.shape),
        grad_query,
        grad_key,
        grad_value,
        grad_out,
        grad_sort,
        grad_gain_one.reshape(width),
        grad_gain_two.reshape(width),
        grad_up,
        grad_down,
    )


def local_any(
    inputs, cotangent, block_perm, block_mask, pen_weight, w_query, w_key, w_value, w_out, w_sort,
    gain_one, gain_two, w_up, w_down,
):
    both = ("batch", "mp")
    _, rows, width = inputs.shape
    x = inputs.reshape(rows, width)
    cot = cotangent.reshape(rows, width)
    perm = block_perm.reshape(-1)
    mask = block_mask.reshape(-1)
    perm_row = block_perm.reshape(1, -1)
    mask_row = block_mask.reshape(1, -1)
    gain_one_row = gain_one.reshape(1, width)
    gain_two_row = gain_two.reshape(1, width)
    where = jnp.zeros((4,), jnp.int32)
    up_all = lax.all_gather(w_up.astype(BF16), "mp", axis=1, tiled=True)
    down_all = lax.all_gather(w_down.astype(BF16), "mp", axis=0, tiled=True)
    quarters = [
        jnp.stack([up_all[:, at : at + width], down_all[at : at + width]])
        for at in range(0, up_all.shape[1], width)
    ]
    act_one, q, k, v, probs, att, second, act_two_far, shares, sums, plan_log, chosen, entropy = forward(
        perm, mask, jnp.zeros((1,), jnp.int32), perm_row, mask_row, gain_one_row, gain_two_row, x,
        w_query, w_key, w_value, w_sort, w_out, w_query, w_query,
    )[:-1]
    tallies = jnp.broadcast_to(lax.psum(jnp.sum(mask_row).astype(F32), both) / width, (1, width))
    hidden, parts = [], []
    low, sofar = cot, None
    for index, weights in enumerate(quarters):
        if index == 0:
            hid, sofar, piece, low, act_two = feed_quarter("first", where, act_two_far, weights, low)
        elif index < len(quarters) - 1:
            hid, sofar, piece = feed_quarter("middle", where, act_two, weights, low, sofar)
        else:
            extra = (cot, second, att, w_out, gain_two_row, entropy)
            hid, grad_second, piece, grad_att, extra = feed_quarter(
                "last", where, act_two, weights, low, sofar, extra
            )
        hidden.append(hid)
        parts.append(piece[0])
    groups = [
        attend_back(perm, q, grad_att, probs, k, v, chosen, group) for group in range(width // GROUP_WIDTH)
    ]
    piece, gsum, block_total = head_grads(
        where, pen_weight, act_one, groups, shares, plan_log, sums, w_sort, perm_row, mask_row, extra, tallies, 1
    )
    grad_input = input_grad(
        [group[:3] for group in groups], gsum, x, grad_second, gain_one_row, w_query, w_key, w_value
    )
    output = layer_output(second, hidden, quarters)

    parts = jnp.concatenate(parts, axis=1).reshape(2, width, -1)
    parts = lax.psum(lax.psum_scatter(parts, "mp", scatter_dimension=2, tiled=True), "batch").astype(F32)
    grad_up, grad_down = parts[0], parts[1].T
    piece = lax.psum(piece, both)
    grad_query, grad_key, grad_value, grad_sort, grad_out, grad_gain_one, grad_gain_two, penalty = finish(
        where, [piece], w_query, w_key, w_value, w_sort, gain_one_row, block_total
    )
    return (
        output.reshape(inputs.shape),
        penalty.reshape(1),
        grad_input.reshape(inputs.shape),
        grad_query,
        grad_key,
        grad_value,
        grad_out,
        grad_sort,
        grad_gain_one.reshape(width),
        grad_gain_two.reshape(width),
        grad_up,
        grad_down,
    )


def solution(mesh):
    tokens = P(("batch", "mp"), None, None)
    blocks = P(("batch", "mp"), None)
    small = mesh.shape["batch"] == 16 and mesh.shape["mp"] == 2
    return jax.shard_map(
        local_small if small else local_any,
        mesh=mesh,
        in_specs=(tokens, tokens, blocks, blocks) + (P(),) * 8 + (P(None, "mp"), P("mp", None)),
        out_specs=(tokens, P(), tokens) + (P(),) * 7 + (P(None, "mp"), P("mp", None)),
        check_vma=False,
    )
```

time: 252 us -> 185 us (0.73)
  waiting for transfers between devices: 40.6 us -> 22.9 us
  starting transfers between devices: 55.9 us -> 39.7 us
  Pallas kernels: 130 us -> 118 us
  local copies, waits for them, and re-layouts: 11.6 us -> 0.73 us
  other arithmetic: 8.55 us -> 1.88 us
  between operations: 4.5 us -> 1.85 us
    ppermute x47 -> x36, waiting for transfers between devices: 40.6 us -> 22.9 us  [swap(): lax.ppermute(array, ('batch', 'mp'), [(i, i ^ flip) for i in range(count)])]
    ppermute x47 -> x36, starting transfers between devices: 55.9 us -> 39.7 us  [swap(): lax.ppermute(array, ('batch', 'mp'), [(i, i ^ flip) for i in range(count)])]
    unnamed x85 -> x27, local copies, waits for them, and re-layouts: 9.91 us -> 0.63 us
    pallas_call x1, Pallas kernels: 24.3 us -> 20 us  [forward(): pl.pallas_call(functools.partial(forward_kernel, tile=tile), in_specs=[sm...]
    pallas_call x9 -> x7, Pallas kernels: 74.7 us -> 70.5 us  [the longest x4 42.5 us: feed_quarter(): pl.pallas_call(functools.partial(quarter_kernel, kind=kind, tile=tile, ta...]
  transfers between devices with their start and end apart: 47 -> 36, of which waited for: 16 -> 11; matrix products, arithmetic and copies ran while one was open for 3% -> 1% of each run, Pallas kernels for 42% -> 53%
where the time goes in v3:
time: 185 us
  Pallas kernels  118 us (64%)
  starting transfers between devices  39.7 us (21%)
  waiting for transfers between devices  22.9 us (12%)
  other arithmetic  1.88 us (1%)
  between operations  1.85 us (1%)
    pallas_call x4, Pallas kernels, feed_quarter(): pl.pallas_call(functools.partial(quarter_kernel, kind=kind, tile=tile, ta...  42.5 us
    ppermute x36, starting transfers between devices, swap(): lax.ppermute(array, ('batch', 'mp'), [(i, i ^ flip) for i in range(count)])  39.7 us
    ppermute x36, waiting for transfers between devices, swap(): lax.ppermute(array, ('batch', 'mp'), [(i, i ^ flip) for i in range(count)])  22.9 us
    pallas_call x2, Pallas kernels, attend_back(): pl.pallas_call(functools.partial(attend_back_kernel, group=group, part=pa...  22 us
    pallas_call x1, Pallas kernels, forward(): pl.pallas_call(functools.partial(forward_kernel, tile=tile), in_specs=[sm...  20 us
    pallas_call x1, Pallas kernels, input_grad(): pl.pallas_call(input_kernel, grid=(rows // tile,), in_specs=[rows_of(tile...  9.78 us
    pallas_call x1, Pallas kernels, layer_output(): pl.pallas_call(output_kernel, grid=(rows // tile,), in_specs=[rows_of(til...  8.34 us
    pallas_call x1, Pallas kernels, head_grads(): pl.pallas_call(functools.partial(head_kernel, count=len(groups)), in_spec...  6.06 us
  transfers between devices with their start and end apart: 36, of which 11 were waited for; matrix products, arithmetic and copies ran while one was open for 1% of the time, Pallas kernels for 53%

profile of v3, /device:TPU:0, one launch (start us, length us, event | category | flops | bytes accessed | tf_op | source)
XLA Modules:
  0.0 185.1 jit_solution(16113242530001101048)
XLA Ops:
  0.7 1.7 pack_weights.1.refs_2_.refs_7_
  2.4 3.0 %collective-permute-start = (bf16[2,512,512]{2,1,0:T(8,128)(2,1)S(1)}, bf16[2,512,512]{2,1,0:T(8,128)(2,1)S(1)}, u32[]{:S(2)}, u32[]{:S(2)}) collective-permute-start(bf16[2,512,512]{2,1,0:T(8,128)(2,1)S(1)} %pack_weights.1.refs_2_.refs_7_), channel_id=1, source_target_pairs={{0,1},{1,0},{2,3},{3,2},{4,5},{5,4},{6,7},{7,6},{8,9},{9,8},{10,11... | collective-permute-start | bytes 3145736 | tf_op jit(solution)/shard_map/ppermute | solution.py:896
  5.4 20.0 %forward.1 = (bf16[2048,512]{1,0:T(8,128)(2,1)}, bf16[2048,512]{1,0:T(8,128)(2,1)}, bf16[2048,512]{1,0:T(8,128)(2,1)}, bf16[2048,512]{1,0:T(8,128)(2,1)}, bf16[4...) custom-call(s32[64]{0:T(128)S(1)} %bitcast.30, ...), custom_call_target="tpu_custom_call" | custom-call | flops 28750000128 | tf_op jit(solution)/shard_map/forward/pallas_call | solution.py:331
  26.0 2.6 %collective-permute-done.refs_3_.refs_4_ = bf16[2,512,512]{2,1,0:T(8,128)(2,1)S(1)} collective-permute-done((bf16[2,512,512]{2,1,0:T(8,128)(2,1)S(1)}, bf16[2,512,512]{2,1,0:T(8,128)(2,1)S(1)}, u32[]{:S(2)}, u32[]{:S(2)}) %collective-permute-start) | collective-permute-done | bytes 1048608 | tf_op jit(solution)/shard_map/ppermute | solution.py:896
  28.6 9.5 %feed_first.1 = (bf16[2048,512]{1,0:T(8,128)(2,1)}, f32[2048,512]{1,0:T(8,128)S(1)}, bf16[8,144,512]{2,1,0:T(8,128)(2,1)S(1)}, bf16[2048,512]{1,0:T(8,128)(2,1)S(1)}, bf16[2048,512]{1,0:T(8,128)(2,1)S(1)}) custom-call(s32[1,64]{1,0:T(1,128)S(1)} %copy-done.7, s32[4]{0:T(128)S(1)} %pad_add_fusion.refs_1_.refs_0_, ...), custom_call_target="tpu_custom_call" | custom-call | flops 10350000128 | tf_op jit(solution)/shard_map/feed_first/pallas_call | solution.py:623
  38.2 7.8 %feed_middle.2 = (bf16[2048,512]{1,0:T(8,128)(2,1)}, f32[2048,512]{1,0:T(8,128)S(1)}, bf16[8,144,512]{2,1,0:T(8,128)(2,1)S(1)}) custom-call(s32[1,64]{1,0:T(1,128)S(1)} %copy-done.7, s32[4]{0:T(128)S(1)} %pad_add_fusion.refs_1_.refs_0_, bf16[2048,512]{1,0:T(8,128)(2,1)S(1)} %get-tuple-element.132.refs_2_.refs_1_, ...), custom_call_target="tpu_custom_call" | custom-call | flops 10350000128 | tf_op jit(solution)/shard_map/feed_middle/pallas_call | solution.py:623
  47.2 8.0 %feed_middle.3 = (bf16[2048,512]{1,0:T(8,128)(2,1)}, f32[2048,512]{1,0:T(8,128)S(1)}, bf16[8,128,512]{2,1,0:T(8,128)(2,1)S(1)}) custom-call(s32[4]{0:T(128)S(1)} %pad_add_fusion.refs_1_.refs_0_, bf16[2048,512]{1,0:T(8,128)(2,1)S(1)} %get-tuple-element.132.refs_2_.refs_1_, bf16[2,512,512]{2,1,0:T(8,128)(2,1)S(1)} %get-tuple-element.138.refs_2_.refs_6_, ...), custom_call_target="tpu_custom_call" | custom-call | flops 10350000128 | tf_op jit(solution)/shard_map/feed_middle/pallas_call | solution.py:623
  55.7 1.8 collective-permute-start.3
  57.5 17.1 %feed_last.1 = (bf16[2048,512]{1,0:T(8,128)(2,1)}, f32[2048,512]{1,0:T(8,128)}, bf16[8,128,512]{2,1,0:T(8,128)(2,1)S(1)}, bf16[2048,512]{1,0:T(8,128)(2,1)S(1)}, bf16[32,16,640]{2,1,0:T(8,128)(2,1)S(1)}) custom-call(s32[4]{0:T(128)S(1)} %pad_add_fusion.refs_1_.refs_0_, bf16[2048,512]{1,0:T(8,128)(2,1)S(1)} %get-tuple-element.132.refs_2_.refs_1_, ...), custom_call_target="tpu_custom_call" | custom-call | flops 10350000128 | tf_op jit(solution)/shard_map/feed_last/pallas_call | solution.py:623
  75.4 3.9 %collective-permute-start.7 = (bf16[1,144,512]{2,1,0:T(8,128)(2,1)S(1)}, bf16[1,144,512]{2,1,0:T(8,128)(2,1)S(1)}, u32[]{:S(2)}, u32[]{:S(2)}) collective-permute-start(bf16[1,144,512]{2,1,0:T(8,128)(2,1)S(1)} %get-tuple-element.160), channel_id=1, source_target_pairs={{0,24},{1,25},{2,26},{3,27},{4,28},{5,29},{6,30},{7,31},{8,16},{9,... | collective-permute-start | bytes 442376 | tf_op jit(solution)/shard_map/ppermute | solution.py:896
  79.9 10.8 %attend_back.2 = (bf16[2048,256]{1,0:T(8,128)(2,1)S(1)}, bf16[2048,256]{1,0:T(8,128)(2,1)S(1)}, bf16[2048,256]{1,0:T(8,128)(2,1)S(1)}, f32[64,256]{1,0:T(8,128)S(1)}) custom-call(s32[64]{0:T(128)S(1)} %bitcast.31, f32[64,512]{1,0:T(8,128)S(1)} %get-tuple-element.151.chosen_ref, bf16[2048,512]{1,0:T(8,128)(2,1)S(1)} %get-tuple-element.146.gatt_ref, ...), custom_call_target="tpu_custom_call" | custom-call | flops 11500000256 | tf_op jit(solution)/shard_map/attend_back/pallas_call | solution.py:417
  92.4 2.9 %collective-permute-start.11 = (bf16[1,128,512]{2,1,0:T(8,128)(2,1)S(1)}, bf16[1,128,512]{2,1,0:T(8,128)(2,1)S(1)}, u32[]{:S(2)}, u32[]{:S(2)}) collective-permute-start(bf16[1,128,512]{2,1,0:T(8,128)(2,1)S(1)} %get-tuple-element.168), channel_id=1, source_target_pairs={{0,16},{1,17},{2,18},{3,19},{4,20},{5,21},{6,22},{7,23},{8,24},{9,... | collective-permute-start | bytes 393224 | tf_op jit(solution)/shard_map/ppermute | solution.py:896
  95.5 1.7 collective-permute-start.8
  97.2 11.2 %attend_back.3 = (bf16[2048,256]{1,0:T(8,128)(2,1)S(1)}, bf16[2048,256]{1,0:T(8,128)(2,1)S(1)}, bf16[2048,256]{1,0:T(8,128)(2,1)S(1)}, f32[64,256]{1,0:T(8,128)S(1)}) custom-call(s32[64]{0:T(128)S(1)} %bitcast.32, f32[64,512]{1,0:T(8,128)S(1)} %get-tuple-element.151.chosen_ref, bf16[2048,512]{1,0:T(8,128)(2,1)S(1)} %get-tuple-element.146.gatt_ref, ...), custom_call_target="tpu_custom_call" | custom-call | flops 11500000256 | tf_op jit(solution)/shard_map/attend_back/pallas_call | solution.py:417
  108.6 6.1 %head_grads.1 = (bf16[32,16,2688]{2,1,0:T(8,128)(2,1)S(1)}, f32[64,512]{1,0:T(8,128)S(1)}, f32[1,128]{1,0:T(1,128)S(1)}) custom-call(s32[4]{0:T(128)S(1)} %pad_add_fusion.refs_1_.refs_0_, f32[1]{0:T(128)S(6)} %copy.30.refs_1_, bf16[2048,512]{1,0:T(8,128)(2,1)S(1)} %copy-done.9, bf16[2048,256]{1,0:T(8,128)(2,1)S(1)} %get-tuple-element.178.refs_3_.refs_0_, ...), custom_call_target="tpu_custom_call" | custom-call | flops 6899999744 | tf_op jit(solution)/shard_map/head_grads/pallas_call | solution.py:716
  115.3 3.8 %collective-permute-start.18 = (bf16[1,128,512]{2,1,0:T(8,128)(2,1)S(1)}, bf16[1,128,512]{2,1,0:T(8,128)(2,1)S(1)}, u32[]{:S(2)}, u32[]{:S(2)}) collective-permute-start(bf16[1,128,512]{2,1,0:T(8,128)(2,1)S(1)} %add_convert_fusion.13), channel_id=1, source_target_pairs={{0,16},{1,17},{2,18},{3,19},{4,20},{5,21},{6,22},{7,23},{8,24},{9,... | collective-permute-start | bytes 393224 | tf_op jit(solution)/shard_map/ppermute | solution.py:896
  120.1 1.6 collective-permute-start.15
  124.7 4.4 %collective-permute-done.18 = bf16[1,128,512]{2,1,0:T(8,128)(2,1)S(1)} collective-permute-done((bf16[1,128,512]{2,1,0:T(8,128)(2,1)S(1)}, bf16[1,128,512]{2,1,0:T(8,128)(2,1)S(1)}, u32[]{:S(2)}, u32[]{:S(2)}) %collective-permute-start.18) | collective-permute-done | bytes 131104 | tf_op jit(solution)/shard_map/ppermute | solution.py:896
  129.1 9.8 %input_grad.1 = f32[2048,512]{1,0:T(8,128)} custom-call(bf16[2048,256]{1,0:T(8,128)(2,1)S(1)} %get-tuple-element.178.refs_3_.refs_0_, bf16[2048,256]{1,0:T(8,128)(2,1)S(1)} %get-tuple-element.179.refs_4_.refs_1_, bf16[2048,256]{1,0:T(8,128)(2,1)S(1)} %get-tuple-element.180.refs_5_.refs_2_, bf16[2048,256]{1,0:T(8,128)(2,1)S(1)} %get-tuple-element.181.refs_7_.refs_3_, ...), custom_call_target="tpu_custom_call" | custom-call | flops 11500000256 | tf_op jit(solution)/shard_map/input_grad/pallas_call | solution.py:756
  139.0 2.7 %collective-permute-start.22 = (bf16[1,16,2688]{2,1,0:T(8,128)(2,1)S(1)}, bf16[1,16,2688]{2,1,0:T(8,128)(2,1)S(1)}, u32[]{:S(2)}, u32[]{:S(2)}) collective-permute-start(bf16[1,16,2688]{2,1,0:T(8,128)(2,1)S(1)} %get-tuple-element.205), channel_id=1, source_target_pairs={{0,24},{1,25},{2,26},{3,27},{4,28},{5,29},{6,30},{7,31},{8,16},{9,... | collective-permute-start | bytes 258056 | tf_op jit(solution)/shard_map/ppermute | solution.py:896
  141.7 1.7 collective-permute-start.21
  143.5 1.5 collective-permute-start.27
  145.5 4.6 %collective-permute-done.21 = bf16[1,16,2688]{2,1,0:T(8,128)(2,1)S(1)} collective-permute-done((bf16[1,16,2688]{2,1,0:T(8,128)(2,1)S(1)}, bf16[1,16,2688]{2,1,0:T(8,128)(2,1)S(1)}, u32[]{:S(2)}, u32[]{:S(2)}) %collective-permute-start.21) | collective-permute-done | bytes 86048 | tf_op jit(solution)/shard_map/ppermute | solution.py:896
  150.2 2.3 %collective-permute-start.25 = (bf16[1,16,2688]{2,1,0:T(8,128)(2,1)S(1)}, bf16[1,16,2688]{2,1,0:T(8,128)(2,1)S(1)}, u32[]{:S(2)}, u32[]{:S(2)}) collective-permute-start(bf16[1,16,2688]{2,1,0:T(8,128)(2,1)S(1)} %add_convert_fusion.18), channel_id=1, source_target_pairs={{0,24},{1,25},{2,26},{3,27},{4,28},{5,29},{6,30},{7,31},{8,16},{9,... | collective-permute-start | bytes 258056 | tf_op jit(solution)/shard_map/ppermute | solution.py:896
  152.5 2.1 %collective-permute-start.23 = (bf16[1,16,2688]{2,1,0:T(8,128)(2,1)S(1)}, bf16[1,16,2688]{2,1,0:T(8,128)(2,1)S(1)}, u32[]{:S(2)}, u32[]{:S(2)}) collective-permute-start(bf16[1,16,2688]{2,1,0:T(8,128)(2,1)S(1)} %add_convert_fusion.18), channel_id=1, source_target_pairs={{0,8},{1,9},{2,10},{3,11},{4,12},{5,13},{6,14},{7,15},{8,0},{9,1},... | collective-permute-start | bytes 258056 | tf_op jit(solution)/shard_map/ppermute | solution.py:896
  154.7 3.0 %collective-permute-done.25 = bf16[1,16,2688]{2,1,0:T(8,128)(2,1)S(1)} collective-permute-done((bf16[1,16,2688]{2,1,0:T(8,128)(2,1)S(1)}, bf16[1,16,2688]{2,1,0:T(8,128)(2,1)S(1)}, u32[]{:S(2)}, u32[]{:S(2)}) %collective-permute-start.25) | collective-permute-done | bytes 86048 | tf_op jit(solution)/shard_map/ppermute | solution.py:896
  157.7 1.9 %collective-permute-done.24 = bf16[1,16,2688]{2,1,0:T(8,128)(2,1)S(1)} collective-permute-done((bf16[1,16,2688]{2,1,0:T(8,128)(2,1)S(1)}, bf16[1,16,2688]{2,1,0:T(8,128)(2,1)S(1)}, u32[]{:S(2)}, u32[]{:S(2)}) %collective-permute-start.24) | collective-permute-done | bytes 86048 | tf_op jit(solution)/shard_map/ppermute | solution.py:896
  161.7 1.5 collective-permute-start.31
  163.2 8.3 %layer_output.1 = f32[2048,512]{1,0:T(8,128)} custom-call(f32[2048,512]{1,0:T(8,128)S(1)} %copy-done.8, bf16[2048,512]{1,0:T(8,128)(2,1)} %get-tuple-element.212.refs_0_, bf16[2048,512]{1,0:T(8,128)(2,1)} %get-tuple-element.213.refs_1_, bf16[2048,512]{1,0:T(8,128)(2,1)} %get-tuple-element.214.refs_2_, bf16[2048,512]{1,0:T(8,128)(2,1)} %get-tuple-element.215.refs_3_, ...), custom_call_target="tpu_custom_call" | custom-call | flops 9200000000 | tf_op jit(solution)/shard_map/layer_output/pallas_call | solution.py:650
  172.1 3.3 %finish_feed.1 = (f32[512,1024]{1,0:T(8,128)}, f32[1024,512]{1,0:T(8,128)}) custom-call(s32[4]{0:T(128)S(1)} %pad_add_fusion.refs_1_.refs_0_, bf16[4,128,512]{2,1,0:T(8,128)(2,1)S(1)} %pad_maximum_fusion.refs_1_, bf16[4,128,512]{2,1,0:T(8,128)(2,1)S(1)} %collective-permute-done.27.refs_2_, bf16[4,128,512]{2,1,0:T(8,128)(2,1)S(1)} %collective-permute-done.28.refs_3_, ...), custom_call_target="tpu_custom_call" | custom-call | flops 3449999872 | tf_op jit(solution)/shard_map/finish_feed/pallas_call | solution.py:820
  175.4 2.3 %collective-permute-done.31.refs_4_ = bf16[4,16,2688]{2,1,0:T(8,128)(2,1)S(1)} collective-permute-done((bf16[4,16,2688]{2,1,0:T(8,128)(2,1)S(1)}, bf16[4,16,2688]{2,1,0:T(8,128)(2,1)S(1)}, u32[]{:S(2)}, u32[]{:S(2)}) %collective-permute-start.31) | collective-permute-done | bytes 344096 | tf_op jit(solution)/shard_map/ppermute | solution.py:896
  180.4 4.5 %finish.1 = (f32[512,512]{1,0:T(8,128)}, f32[512,512]{1,0:T(8,128)}, f32[512,512]{1,0:T(8,128)}, f32[512,512]{1,0:T(8,128)}, f32[512,512]{1,0:T(8,128)}, /*index...) custom-call(s32[4]{0:T(128)S(1)} %pad_add_fusion.refs_1_.refs_0_, ...), custom_call_target="tpu_custom_call" | custom-call | flops 5750000128 | tf_op jit(solution)/shard_map/finish/pallas_call | solution.py:874
  (96 shorter events, 15.6 us)
Async XLA Ops:
  2.4 26.2 %collective-permute-start = (bf16[2,512,512]{2,1,0:T(8,128)(2,1)S(1)}, bf16[2,512,512]{2,1,0:T(8,128)(2,1)S(1)}, u32[]{:S(2)}, u32[]{:S(2)}) collective-permute-start(bf16[2,512,512]{2,1,0:T(8,128)(2,1)S(1)} %pack_weights.1.refs_2_.refs_7_), channel_id=1, source_target_pairs={{0,1},{1,0},{2,3},{3,2},{4,5},{5,4},{6,7},{7,6},{8,9},{9,8},{10,11... | collective-permute-start | bytes 3145736 | tf_op jit(solution)/shard_map/ppermute | solution.py:896
  28.6 9.6 %collective-permute-start.1 = (bf16[2,512,512]{2,1,0:T(8,128)(2,1)S(1)}, bf16[2,512,512]{2,1,0:T(8,128)(2,1)S(1)}, u32[]{:S(2)}, u32[]{:S(2)}) collective-permute-start(bf16[2,512,512]{2,1,0:T(8,128)(2,1)S(1)} %collective-permute-done.refs_3_.refs_4_), channel_id=1, source_target_pairs={{0,2},{1,3},{2,0},{3,1},{4,6},{5,7},{6,4},{7,5},{8,10},{9,11},{10,... | collective-permute-start | bytes 3145736 | tf_op jit(solution)/shard_map/ppermute | solution.py:896
  46.0 9.3 %collective-permute-start.2 = (bf16[8,144,512]{2,1,0:T(8,128)(2,1)S(1)}, bf16[8,144,512]{2,1,0:T(8,128)(2,1)S(1)}, u32[]{:S(2)}, u32[]{:S(2)}) collective-permute-start(bf16[8,144,512]{2,1,0:T(8,128)(2,1)S(1)} %get-tuple-element.136), channel_id=1, source_target_pairs={{0,2},{1,3},{2,0},{3,1},{4,6},{5,7},{6,4},{7,5},{8,10},{9,11},{10,... | collective-permute-start | bytes 3538952 | tf_op jit(solution)/shard_map/ppermute | solution.py:896
  55.2 19.3 %collective-permute-start.5 = (bf16[8,128,512]{2,1,0:T(8,128)(2,1)S(1)}, bf16[8,128,512]{2,1,0:T(8,128)(2,1)S(1)}, u32[]{:S(2)}, u32[]{:S(2)}) collective-permute-start(bf16[8,128,512]{2,1,0:T(8,128)(2,1)S(1)} %get-tuple-element.149), channel_id=1, source_target_pairs={{0,2},{1,3},{2,0},{3,1},{4,6},{5,7},{6,4},{7,5},{8,10},{9,11},{10,... | collective-permute-start | bytes 3145736 | tf_op jit(solution)/shard_map/ppermute | solution.py:896
  55.7 19.6 %collective-permute-start.3 = (bf16[4,144,512]{2,1,0:T(8,128)(2,1)S(1)}, bf16[4,144,512]{2,1,0:T(8,128)(2,1)S(1)}, u32[]{:S(2)}, u32[]{:S(2)}) collective-permute-start(bf16[4,144,512]{2,1,0:T(8,128)(2,1)S(1)} %get-tuple-element.142), channel_id=1, source_target_pairs={{0,4},{1,5},{2,6},{3,7},{4,0},{5,1},{6,2},{7,3},{8,12},{9,13},{10,... | collective-permute-start | bytes 1769480 | tf_op jit(solution)/shard_map/ppermute | solution.py:896
  74.9 15.8 %collective-permute-start.9 = (bf16[4,128,512]{2,1,0:T(8,128)(2,1)S(1)}, bf16[4,128,512]{2,1,0:T(8,128)(2,1)S(1)}, u32[]{:S(2)}, u32[]{:S(2)}) collective-permute-start(bf16[4,128,512]{2,1,0:T(8,128)(2,1)S(1)} %get-tuple-element.165), channel_id=1, source_target_pairs={{0,4},{1,5},{2,6},{3,7},{4,0},{5,1},{6,2},{7,3},{8,12},{9,13},{10,... | collective-permute-start | bytes 1572872 | tf_op jit(solution)/shard_map/ppermute | solution.py:896
  75.4 19.9 %collective-permute-start.7 = (bf16[1,144,512]{2,1,0:T(8,128)(2,1)S(1)}, bf16[1,144,512]{2,1,0:T(8,128)(2,1)S(1)}, u32[]{:S(2)}, u32[]{:S(2)}) collective-permute-start(bf16[1,144,512]{2,1,0:T(8,128)(2,1)S(1)} %get-tuple-element.160), channel_id=1, source_target_pairs={{0,24},{1,25},{2,26},{3,27},{4,28},{5,29},{6,30},{7,31},{8,16},{9,... | collective-permute-start | bytes 442376 | tf_op jit(solution)/shard_map/ppermute | solution.py:896
  79.3 16.1 %collective-permute-start.6 = (bf16[1,144,512]{2,1,0:T(8,128)(2,1)S(1)}, bf16[1,144,512]{2,1,0:T(8,128)(2,1)S(1)}, u32[]{:S(2)}, u32[]{:S(2)}) collective-permute-start(bf16[1,144,512]{2,1,0:T(8,128)(2,1)S(1)} %get-tuple-element.158), channel_id=1, source_target_pairs={{0,16},{1,17},{2,18},{3,19},{4,20},{5,21},{6,22},{7,23},{8,24},{9,... | collective-permute-start | bytes 442376 | tf_op jit(solution)/shard_map/ppermute | solution.py:896
  79.3 16.1 %collective-permute-start.4 = (bf16[1,144,512]{2,1,0:T(8,128)(2,1)S(1)}, bf16[1,144,512]{2,1,0:T(8,128)(2,1)S(1)}, u32[]{:S(2)}, u32[]{:S(2)}) collective-permute-start(bf16[1,144,512]{2,1,0:T(8,128)(2,1)S(1)} %get-tuple-element.148), channel_id=1, source_target_pairs={{0,8},{1,9},{2,10},{3,11},{4,12},{5,13},{6,14},{7,15},{8,0},{9,1},... | collective-permute-start | bytes 442376 | tf_op jit(solution)/shard_map/ppermute | solution.py:896
  90.9 17.5 %collective-permute-start.10 = (bf16[1,128,512]{2,1,0:T(8,128)(2,1)S(1)}, bf16[1,128,512]{2,1,0:T(8,128)(2,1)S(1)}, u32[]{:S(2)}, u32[]{:S(2)}) collective-permute-start(bf16[1,128,512]{2,1,0:T(8,128)(2,1)S(1)} %get-tuple-element.167), channel_id=1, source_target_pairs={{0,8},{1,9},{2,10},{3,11},{4,12},{5,13},{6,14},{7,15},{8,0},{9,1},... | collective-permute-start | bytes 393224 | tf_op jit(solution)/shard_map/ppermute | solution.py:896
  92.4 16.1 %collective-permute-start.11 = (bf16[1,128,512]{2,1,0:T(8,128)(2,1)S(1)}, bf16[1,128,512]{2,1,0:T(8,128)(2,1)S(1)}, u32[]{:S(2)}, u32[]{:S(2)}) collective-permute-start(bf16[1,128,512]{2,1,0:T(8,128)(2,1)S(1)} %get-tuple-element.168), channel_id=1, source_target_pairs={{0,16},{1,17},{2,18},{3,19},{4,20},{5,21},{6,22},{7,23},{8,24},{9,... | collective-permute-start | bytes 393224 | tf_op jit(solution)/shard_map/ppermute | solution.py:896
  95.3 13.1 %collective-permute-start.12 = (bf16[1,128,512]{2,1,0:T(8,128)(2,1)S(1)}, bf16[1,128,512]{2,1,0:T(8,128)(2,1)S(1)}, u32[]{:S(2)}, u32[]{:S(2)}) collective-permute-start(bf16[1,128,512]{2,1,0:T(8,128)(2,1)S(1)} %get-tuple-element.169), channel_id=1, source_target_pairs={{0,24},{1,25},{2,26},{3,27},{4,28},{5,29},{6,30},{7,31},{8,16},{9,... | collective-permute-start | bytes 393224 | tf_op jit(solution)/shard_map/ppermute | solution.py:896
  95.5 13.0 %collective-permute-start.8 = (bf16[1,144,512]{2,1,0:T(8,128)(2,1)S(1)}, bf16[1,144,512]{2,1,0:T(8,128)(2,1)S(1)}, u32[]{:S(2)}, u32[]{:S(2)}) collective-permute-start(bf16[1,144,512]{2,1,0:T(8,128)(2,1)S(1)} %add_convert_fusion.8), channel_id=1, source_target_pairs={{0,1},{1,0},{2,3},{3,2},{4,5},{5,4},{6,7},{7,6},{8,9},{9,8},{10,11... | collective-permute-start | bytes 442376 | tf_op jit(solution)/shard_map/ppermute | solution.py:896
  114.9 8.4 %collective-permute-start.17 = (bf16[1,128,512]{2,1,0:T(8,128)(2,1)S(1)}, bf16[1,128,512]{2,1,0:T(8,128)(2,1)S(1)}, u32[]{:S(2)}, u32[]{:S(2)}) collective-permute-start(bf16[1,128,512]{2,1,0:T(8,128)(2,1)S(1)} %add_convert_fusion.13), channel_id=1, source_target_pairs={{0,8},{1,9},{2,10},{3,11},{4,12},{5,13},{6,14},{7,15},{8,0},{9,1},... | collective-permute-start | bytes 393224 | tf_op jit(solution)/shard_map/ppermute | solution.py:896
  115.3 13.8 %collective-permute-start.18 = (bf16[1,128,512]{2,1,0:T(8,128)(2,1)S(1)}, bf16[1,128,512]{2,1,0:T(8,128)(2,1)S(1)}, u32[]{:S(2)}, u32[]{:S(2)}) collective-permute-start(bf16[1,128,512]{2,1,0:T(8,128)(2,1)S(1)} %add_convert_fusion.13), channel_id=1, source_target_pairs={{0,16},{1,17},{2,18},{3,19},{4,20},{5,21},{6,22},{7,23},{8,24},{9,... | collective-permute-start | bytes 393224 | tf_op jit(solution)/shard_map/ppermute | solution.py:896
  119.1 9.9 %collective-permute-start.19 = (bf16[1,128,512]{2,1,0:T(8,128)(2,1)S(1)}, bf16[1,128,512]{2,1,0:T(8,128)(2,1)S(1)}, u32[]{:S(2)}, u32[]{:S(2)}) collective-permute-start(bf16[1,128,512]{2,1,0:T(8,128)(2,1)S(1)} %add_convert_fusion.13), channel_id=1, source_target_pairs={{0,24},{1,25},{2,26},{3,27},{4,28},{5,29},{6,30},{7,31},{8,16},{9,... | collective-permute-start | bytes 393224 | tf_op jit(solution)/shard_map/ppermute | solution.py:896
  119.7 19.2 %collective-permute-start.14 = (bf16[4,16,2688]{2,1,0:T(8,128)(2,1)S(1)}, bf16[4,16,2688]{2,1,0:T(8,128)(2,1)S(1)}, u32[]{:S(2)}, u32[]{:S(2)}) collective-permute-start(bf16[4,16,2688]{2,1,0:T(8,128)(2,1)S(1)} %get-tuple-element.192), channel_id=1, source_target_pairs={{0,1},{1,0},{2,3},{3,2},{4,5},{5,4},{6,7},{7,6},{8,9},{9,8},{10,11... | collective-permute-start | bytes 1032200 | tf_op jit(solution)/shard_map/ppermute | solution.py:896
  120.1 18.7 %collective-permute-start.15 = (bf16[4,16,2688]{2,1,0:T(8,128)(2,1)S(1)}, bf16[4,16,2688]{2,1,0:T(8,128)(2,1)S(1)}, u32[]{:S(2)}, u32[]{:S(2)}) collective-permute-start(bf16[4,16,2688]{2,1,0:T(8,128)(2,1)S(1)} %get-tuple-element.193), channel_id=1, source_target_pairs={{0,4},{1,5},{2,6},{3,7},{4,0},{5,1},{6,2},{7,3},{8,12},{9,13},{10,... | collective-permute-start | bytes 1032200 | tf_op jit(solution)/shard_map/ppermute | solution.py:896
  123.3 15.6 %collective-permute-start.16 = (bf16[4,16,2688]{2,1,0:T(8,128)(2,1)S(1)}, bf16[4,16,2688]{2,1,0:T(8,128)(2,1)S(1)}, u32[]{:S(2)}, u32[]{:S(2)}) collective-permute-start(bf16[4,16,2688]{2,1,0:T(8,128)(2,1)S(1)} %get-tuple-element.194), channel_id=1, source_target_pairs={{0,5},{1,4},{2,7},{3,6},{4,1},{5,0},{6,3},{7,2},{8,13},{9,12},{10,... | collective-permute-start | bytes 1032200 | tf_op jit(solution)/shard_map/ppermute | solution.py:896
  139.0 6.5 %collective-permute-start.22 = (bf16[1,16,2688]{2,1,0:T(8,128)(2,1)S(1)}, bf16[1,16,2688]{2,1,0:T(8,128)(2,1)S(1)}, u32[]{:S(2)}, u32[]{:S(2)}) collective-permute-start(bf16[1,16,2688]{2,1,0:T(8,128)(2,1)S(1)} %get-tuple-element.205), channel_id=1, source_target_pairs={{0,24},{1,25},{2,26},{3,27},{4,28},{5,29},{6,30},{7,31},{8,16},{9,... | collective-permute-start | bytes 258056 | tf_op jit(solution)/shard_map/ppermute | solution.py:896
  141.7 8.4 %collective-permute-start.21 = (bf16[1,16,2688]{2,1,0:T(8,128)(2,1)S(1)}, bf16[1,16,2688]{2,1,0:T(8,128)(2,1)S(1)}, u32[]{:S(2)}, u32[]{:S(2)}) collective-permute-start(bf16[1,16,2688]{2,1,0:T(8,128)(2,1)S(1)} %get-tuple-element.203), channel_id=1, source_target_pairs={{0,16},{1,17},{2,18},{3,19},{4,20},{5,21},{6,22},{7,23},{8,24},{9,... | collective-permute-start | bytes 258056 | tf_op jit(solution)/shard_map/ppermute | solution.py:896
  143.4 6.7 %collective-permute-start.20 = (bf16[1,16,2688]{2,1,0:T(8,128)(2,1)S(1)}, bf16[1,16,2688]{2,1,0:T(8,128)(2,1)S(1)}, u32[]{:S(2)}, u32[]{:S(2)}) collective-permute-start(bf16[1,16,2688]{2,1,0:T(8,128)(2,1)S(1)} %get-tuple-element.201), channel_id=1, source_target_pairs={{0,8},{1,9},{2,10},{3,11},{4,12},{5,13},{6,14},{7,15},{8,0},{9,1},... | collective-permute-start | bytes 258056 | tf_op jit(solution)/shard_map/ppermute | solution.py:896
  143.5 19.6 %collective-permute-start.27 = (bf16[4,128,512]{2,1,0:T(8,128)(2,1)S(1)}, bf16[4,128,512]{2,1,0:T(8,128)(2,1)S(1)}, u32[]{:S(2)}, u32[]{:S(2)}) collective-permute-start(bf16[4,128,512]{2,1,0:T(8,128)(2,1)S(1)} %pad_maximum_fusion.refs_1_), channel_id=1, source_target_pairs={{0,4},{1,5},{2,6},{3,7},{4,0},{5,1},{6,2},{7,3},{8,12},{9,13},{10,... | collective-permute-start | bytes 1572872 | tf_op jit(solution)/shard_map/ppermute | solution.py:896
  150.2 7.4 %collective-permute-start.25 = (bf16[1,16,2688]{2,1,0:T(8,128)(2,1)S(1)}, bf16[1,16,2688]{2,1,0:T(8,128)(2,1)S(1)}, u32[]{:S(2)}, u32[]{:S(2)}) collective-permute-start(bf16[1,16,2688]{2,1,0:T(8,128)(2,1)S(1)} %add_convert_fusion.18), channel_id=1, source_target_pairs={{0,24},{1,25},{2,26},{3,27},{4,28},{5,29},{6,30},{7,31},{8,16},{9,... | collective-permute-start | bytes 258056 | tf_op jit(solution)/shard_map/ppermute | solution.py:896
  152.5 7.0 %collective-permute-start.24 = (bf16[1,16,2688]{2,1,0:T(8,128)(2,1)S(1)}, bf16[1,16,2688]{2,1,0:T(8,128)(2,1)S(1)}, u32[]{:S(2)}, u32[]{:S(2)}) collective-permute-start(bf16[1,16,2688]{2,1,0:T(8,128)(2,1)S(1)} %add_convert_fusion.18), channel_id=1, source_target_pairs={{0,16},{1,17},{2,18},{3,19},{4,20},{5,21},{6,22},{7,23},{8,24},{9,... | collective-permute-start | bytes 258056 | tf_op jit(solution)/shard_map/ppermute | solution.py:896
  152.5 7.0 %collective-permute-start.23 = (bf16[1,16,2688]{2,1,0:T(8,128)(2,1)S(1)}, bf16[1,16,2688]{2,1,0:T(8,128)(2,1)S(1)}, u32[]{:S(2)}, u32[]{:S(2)}) collective-permute-start(bf16[1,16,2688]{2,1,0:T(8,128)(2,1)S(1)} %add_convert_fusion.18), channel_id=1, source_target_pairs={{0,8},{1,9},{2,10},{3,11},{4,12},{5,13},{6,14},{7,15},{8,0},{9,1},... | collective-permute-start | bytes 258056 | tf_op jit(solution)/shard_map/ppermute | solution.py:896
  154.7 16.9 %collective-permute-start.28 = (bf16[4,128,512]{2,1,0:T(8,128)(2,1)S(1)}, bf16[4,128,512]{2,1,0:T(8,128)(2,1)S(1)}, u32[]{:S(2)}, u32[]{:S(2)}) collective-permute-start(bf16[4,128,512]{2,1,0:T(8,128)(2,1)S(1)} %pad_maximum_fusion.refs_1_), channel_id=1, source_target_pairs={{0,2},{1,3},{2,0},{3,1},{4,6},{5,7},{6,4},{7,5},{8,10},{9,11},{10,... | collective-permute-start | bytes 1572872 | tf_op jit(solution)/shard_map/ppermute | solution.py:896
  159.6 15.8 %collective-permute-start.26 = (bf16[4,16,2688]{2,1,0:T(8,128)(2,1)S(1)}, bf16[4,16,2688]{2,1,0:T(8,128)(2,1)S(1)}, u32[]{:S(2)}, u32[]{:S(2)}) collective-permute-start(bf16[4,16,2688]{2,1,0:T(8,128)(2,1)S(1)} %pad_maximum_fusion.1.refs_1_), channel_id=1, source_target_pairs={{0,1},{1,0},{2,3},{3,2},{4,5},{5,4},{6,7},{7,6},{8,9},{9,8},{10,11... | collective-permute-start | bytes 1032200 | tf_op jit(solution)/shard_map/ppermute | solution.py:896
  160.2 15.3 %collective-permute-start.30 = (bf16[4,16,2688]{2,1,0:T(8,128)(2,1)S(1)}, bf16[4,16,2688]{2,1,0:T(8,128)(2,1)S(1)}, u32[]{:S(2)}, u32[]{:S(2)}) collective-permute-start(bf16[4,16,2688]{2,1,0:T(8,128)(2,1)S(1)} %pad_maximum_fusion.1.refs_1_), channel_id=1, source_target_pairs={{0,4},{1,5},{2,6},{3,7},{4,0},{5,1},{6,2},{7,3},{8,12},{9,13},{10,... | collective-permute-start | bytes 1032200 | tf_op jit(solution)/shard_map/ppermute | solution.py:896
  161.7 16.1 %collective-permute-start.31 = (bf16[4,16,2688]{2,1,0:T(8,128)(2,1)S(1)}, bf16[4,16,2688]{2,1,0:T(8,128)(2,1)S(1)}, u32[]{:S(2)}, u32[]{:S(2)}) collective-permute-start(bf16[4,16,2688]{2,1,0:T(8,128)(2,1)S(1)} %pad_maximum_fusion.1.refs_1_), channel_id=1, source_target_pairs={{0,5},{1,4},{2,7},{3,6},{4,1},{5,0},{6,3},{7,2},{8,13},{9,12},{10,... | collective-permute-start | bytes 1032200 | tf_op jit(solution)/shard_map/ppermute | solution.py:896
  163.2 8.9 %collective-permute-start.29 = (bf16[4,128,512]{2,1,0:T(8,128)(2,1)S(1)}, bf16[4,128,512]{2,1,0:T(8,128)(2,1)S(1)}, u32[]{:S(2)}, u32[]{:S(2)}) collective-permute-start(bf16[4,128,512]{2,1,0:T(8,128)(2,1)S(1)} %collective-permute-done.27.refs_2_), channel_id=1, source_target_pairs={{0,2},{1,3},{2,0},{3,1},{4,6},{5,7},{6,4},{7,5},{8,10},{9,11},{10,... | collective-permute-start | bytes 1572872 | tf_op jit(solution)/shard_map/ppermute | solution.py:896
  171.5 6.7 %collective-permute-start.32 = (bf16[4,16,2688]{2,1,0:T(8,128)(2,1)S(1)}, bf16[4,16,2688]{2,1,0:T(8,128)(2,1)S(1)}, u32[]{:S(2)}, u32[]{:S(2)}) collective-permute-start(bf16[4,16,2688]{2,1,0:T(8,128)(2,1)S(1)} %pad_maximum_fusion.1.refs_1_), channel_id=1, source_target_pairs={{0,2},{1,3},{2,0},{3,1},{4,6},{5,7},{6,4},{7,5},{8,10},{9,11},{10,... | collective-permute-start | bytes 1032200 | tf_op jit(solution)/shard_map/ppermute | solution.py:896
  (17 other events, 127.2 us)

commit v4 on v3

--- a/solution.py
+++ b/solution.py
@@ -333,7 +333,8 @@
         in_specs=[smem] * 3 + [vmem] * 4 + [hbm] * 8,
         out_specs=[hbm] * 9 + [vmem] * 5,
         out_shape=[far_shape(*s) for s in (low, low, low, low, probs, low, full, low, share)]
-        + [near_shape(*s) for s in (plan, plan, plan, ((1, width), F32), packed)],
+        + [near_shape(*s) for s in (plan, plan, plan)]
+        + [far_shape((1, width), F32), near_shape(*packed)],
         scratch_shapes=[pltpu.VMEM(*full), pltpu.VMEM((5, width, width), F32), pltpu.VMEM((width, 3 * width), BF16)]
         + [pltpu.VMEM((width, width), BF16)]
         + [pltpu.VMEM(*s) for s in (low, low, low, low, probs, low, full, low, share)]
@@ -354,24 +355,14 @@
 
 
 def attend_back_kernel(
-    perm_ref, chosen_ref, gatt_ref, q_far, probs_far, k_far, v_far,
+    perm_ref, chosen_ref, gatt_ref, q_ref, probs_ref, k_ref, v_ref,
     gq_ref, gk_ref, gv_ref, gch_ref,
-    q_ref, probs_ref, k_ref, v_ref, own_k_ref, far_k_ref, own_v_ref, far_v_ref, sems, *, group, part,
+    own_k_ref, far_k_ref, own_v_ref, far_v_ref, *, group, part,
 ):
-    rows, width = q_ref.shape
+    rows, width = gq_ref.shape
     parts = rows // (part * BLOCK)
     masks = head_masks(BLOCK)
-
-    def copies():
-        for n, (far_ref, near_ref) in enumerate(((k_far, k_ref), (v_far, v_ref), (q_far, q_ref), (probs_far, probs_ref))):
-            cols = near_ref.shape[1]
-            lanes = pl.ds(group * cols, cols)
-            yield pltpu.make_async_copy(far_ref.at[:, lanes], near_ref, sems.at[n])
-
-    for copy in copies():
-        copy.start()
-    for copy in copies():
-        copy.wait()
+    lanes = slice(group * width, (group + 1) * width)
 
     def body(j, _):
         for b in range(part):
@@ -380,13 +371,13 @@
             own_at = pl.ds(pl.multiple_of(block * BLOCK, BLOCK), BLOCK)
             far_at = pl.ds(pl.multiple_of(partner * BLOCK, BLOCK), BLOCK)
             probs_at = pl.ds(pl.multiple_of(block * 2 * BLOCK, 2 * BLOCK), 2 * BLOCK)
-            queries = expand(q_ref[own_at, :], masks)
-            grads = expand(gatt_ref[own_at, group * width : (group + 1) * width], masks)
-            keys = jnp.concatenate([k_ref[own_at, :], k_ref[far_at, :]], axis=0)
-            far_values = v_ref[far_at, :].astype(F32)
-            chosen = chosen_ref[pl.ds(block, 1), group * width : (group + 1) * width]
-            values = jnp.concatenate([v_ref[own_at, :], (far_values * chosen).astype(BF16)], axis=0)
-            probs_low = probs_ref[probs_at, :]
+            queries = expand(q_ref[own_at, lanes], masks)
+            grads = expand(gatt_ref[own_at, lanes], masks)
+            keys = jnp.concatenate([k_ref[own_at, lanes], k_ref[far_at, lanes]], axis=0)
+            far_values = v_ref[far_at, lanes].astype(F32)
+            chosen = chosen_ref[pl.ds(block, 1), lanes]
+            values = jnp.concatenate([v_ref[own_at, lanes], (far_values * chosen).astype(BF16)], axis=0)
+            probs_low = probs_ref[probs_at, group * GROUP_ROWS : (group + 1) * GROUP_ROWS]
             probs = probs_low.astype(F32)
             grad_probs = dot_nt(values, grads)
             total = jnp.sum(probs * grad_probs, axis=0, keepdims=True)
@@ -411,20 +402,18 @@
     rows = q.shape[0]
     smem = pl.BlockSpec(memory_space=pltpu.SMEM)
     vmem = pl.BlockSpec(memory_space=pltpu.VMEM)
-    hbm = pl.BlockSpec(memory_space=pltpu.HBM)
     low = ((rows, GROUP_WIDTH), BF16)
     full = ((rows, GROUP_WIDTH), F32)
     return pl.pallas_call(
         functools.partial(attend_back_kernel, group=group, part=part),
-        in_specs=[smem, vmem, vmem] + [hbm] * 4,
+        in_specs=[smem] + [vmem] * 6,
         out_specs=[vmem] * 4,
         out_shape=[near_shape(*s) for s in (low, low, low, ((rows // BLOCK, GROUP_WIDTH), F32))],
-        scratch_shapes=[pltpu.VMEM(*s) for s in (low, ((2 * rows, GROUP_ROWS), BF16), low, low, full, full, full, full)]
-        + [pltpu.SemaphoreType.DMA((4,))],
-        compiler_params=params(18),
+        scratch_shapes=[pltpu.VMEM(*full)] * 4,
+        compiler_params=params(12),
         cost_estimate=cost(10),
         name="attend_back",
-    )(perm, near(chosen), near(gatt), far(q), far(probs), far(k), far(v))
+    )(perm, near(chosen), near(gatt), near(q), near(probs), near(k), near(v))
 
 
 def gelu_pair(up):
@@ -482,7 +471,7 @@
         hidden_far, gsec_far, piece_ref, gatt_ref, gout_ref = refs[11:16]
         hidden_ref, up_acc, down_acc, hidden_sems, cot_ref, cot_sems = refs[16:22]
         second_ref, second_sems, att_ref, att_sems, gsec_ref, gsec_sems = refs[22:28]
-        wo_ref, wo_low_ref, wo_sem, out_acc, gain_acc, column_ref, sum_ref = refs[28:]
+        wo_ref, wo_low_ref, wo_sem, out_acc, gain_acc, column_ref, sum_ref, second_low_ref = refs[28:]
     rows, width = act_ref.shape
     tiles = rows // tile
     hidden_out = Copies(hidden_ref, hidden_far, hidden_sems, tile)
@@ -507,8 +496,6 @@
     if kind == "last":
         out_acc[...] = jnp.zeros_like(out_acc)
         gain_acc[...] = jnp.zeros_like(gain_acc)
-        wo_copy.wait()
-        wo_low_ref[...] = wo_ref[...].astype(BF16)
 
     def multiply(i):
         at = pl.ds(pl.multiple_of(i * tile, tile), tile)
@@ -530,7 +517,11 @@
         gain_acc[...] += jnp.sum(grad * unit, axis=0, keepdims=True)
         grad_second = cot_ref[at, :] + norm_grad(grad, unit, inverse, gain_ref[...])
         gsec_ref[at, :] = grad_second
-        second_low = grad_second.astype(BF16)
+        second_low_ref[...] = grad_second.astype(BF16)
+
+    def settle_back(i):
+        at = pl.ds(pl.multiple_of(i * tile, tile), tile)
+        second_low = second_low_ref[...]
         gatt_ref[at, :] = dot_nt(second_low, wo_low_ref[...]).astype(BF16)
         out_acc[...] += dot_tn(att_ref[at, :], second_low)
 
@@ -541,6 +532,7 @@
             settle(i - 1)
         multiply(i)
         if kind == "last":
+            settle_back(i - 1)
             gsec_out.start(i - 1)
         hidden_out.start(i)
         return 0
@@ -548,11 +540,14 @@
     if kind == "last":
         multiply(0)
         hidden_out.start(0)
+        wo_copy.wait()
+        wo_low_ref[...] = wo_ref[...].astype(BF16)
         lax.fori_loop(1, tiles, body, 0)
         for copies in ins:
             copies.wait(tiles - 1)
         settle(tiles - 1)
         gsec_out.start(tiles - 1)
+        settle_back(tiles - 1)
     else:
         lax.fori_loop(0, tiles, body, 0)
     size = width // piece_ref.shape[0]
@@ -618,7 +613,7 @@
         scratch = scratch + [full_buffer, sems, full_buffer, sems, low_buffer, sems, full_buffer, sems]
         scratch = scratch + [square, pltpu.VMEM((width, width), BF16), pltpu.SemaphoreType.DMA]
         scratch = scratch + [square, pltpu.VMEM((1, width), F32), pltpu.VMEM((width, LANES), F32)]
-        scratch = scratch + [pltpu.VMEM((2, tile, width), F32)]
+        scratch = scratch + [pltpu.VMEM((2, tile, width), F32), pltpu.VMEM((tile, width), BF16)]
         limit = 32
     return pl.pallas_call(
         functools.partial(quarter_kernel, kind=kind, tile=tile, tally=tally),
@@ -1051,7 +1046,6 @@
     tallies = tallies.reshape(2, TALLY_ROWS, -1)[:, 0]
     own.pieces.append(crossed[:, :rows_fed])
     value = own.reduced(plan)
-    plan.launch(own.gather(plan, value))
     plan.pending.append(value)
     piece, gsum, block_total = head_grads(
         plan.enter(where), pen_weight, act_one, groups, shares, plan_log, sums, w_sort, perm_row, mask_row, out_piece,
@@ -1061,6 +1055,7 @@
 
     head = Walk([piece], HEAD_STEPS)
     plan.pending.extend(head.reduce(plan))
+    own.gather(plan, value)
     plan.launch(head.reduce(plan))
     plan.pending.extend(head.pieces)
     grad_input = input_grad(

time: 185 us -> 177 us (0.957)
  Pallas kernels: 118 us -> 112 us
    pallas_call x2, Pallas kernels: 22 us -> 17.3 us  [attend_back(): pl.pallas_call(functools.partial(attend_back_kernel, group=group, part=pa...]
    pallas_call x4, Pallas kernels: 42.5 us -> 40.5 us  [feed_quarter(): pl.pallas_call(functools.partial(quarter_kernel, kind=kind, tile=tile, ta...]
  transfers between devices with their start and end apart: 36 -> 36, of which waited for: 11 -> 12; matrix products, arithmetic and copies ran while one was open for 1% -> 1% of each run, Pallas kernels for 53% -> 52%
where the time goes in v4:
time: 177 us; the launch traced here: 176 us
  Pallas kernels  112 us (63%)
  starting transfers between devices  38.6 us (22%)
  waiting for transfers between devices  21.9 us (12%)
  other arithmetic  1.88 us (1%)
  between operations  1.88 us (1%)
    pallas_call x4, Pallas kernels, feed_quarter(): pl.pallas_call(functools.partial(quarter_kernel, kind=kind, tile=tile, ta...  40.5 us
    ppermute x36, starting transfers between devices, swap(): lax.ppermute(array, ('batch', 'mp'), [(i, i ^ flip) for i in range(count)])  38.6 us
    ppermute x36, waiting for transfers between devices, swap(): lax.ppermute(array, ('batch', 'mp'), [(i, i ^ flip) for i in range(count)])  21.9 us
    pallas_call x1, Pallas kernels, forward(): pl.pallas_call(functools.partial(forward_kernel, tile=tile), in_specs=[sm...  20.6 us
    pallas_call x2, Pallas kernels, attend_back(): pl.pallas_call(functools.partial(attend_back_kernel, group=group, part=pa...  17.3 us
    pallas_call x1, Pallas kernels, input_grad(): pl.pallas_call(input_kernel, grid=(rows // tile,), in_specs=[rows_of(tile...  9.8 us
    pallas_call x1, Pallas kernels, layer_output(): pl.pallas_call(output_kernel, grid=(rows // tile,), in_specs=[rows_of(til...  8.34 us
    pallas_call x1, Pallas kernels, head_grads(): pl.pallas_call(functools.partial(head_kernel, count=len(groups)), in_spec...  6.08 us
  transfers between devices with their start and end apart: 36, of which 12 were waited for; matrix products, arithmetic and copies ran while one was open for 1% of the time, Pallas kernels for 52%

profile of v4, /device:TPU:0, one launch (start us, length us, event | category | flops | bytes accessed | tf_op | source)
XLA Modules:
  0.0 176.5 jit_solution(6578513596453475304)
XLA Ops:
  0.7 1.7 pack_weights.1.refs_2_.refs_7_
  2.4 3.0 %collective-permute-start = (bf16[2,512,512]{2,1,0:T(8,128)(2,1)S(1)}, bf16[2,512,512]{2,1,0:T(8,128)(2,1)S(1)}, u32[]{:S(2)}, u32[]{:S(2)}) collective-permute-start(bf16[2,512,512]{2,1,0:T(8,128)(2,1)S(1)} %pack_weights.1.refs_2_.refs_7_), channel_id=1, source_target_pairs={{0,1},{1,0},{2,3},{3,2},{4,5},{5,4},{6,7},{7,6},{8,9},{9,8},{10,11... | collective-permute-start | bytes 3145736 | tf_op jit(solution)/shard_map/ppermute | solution.py:891
  5.4 20.6 %forward.1 = (bf16[2048,512]{1,0:T(8,128)(2,1)}, bf16[2048,512]{1,0:T(8,128)(2,1)}, bf16[2048,512]{1,0:T(8,128)(2,1)}, bf16[2048,512]{1,0:T(8,128)(2,1)}, bf16[4...) custom-call(s32[64]{0:T(128)S(1)} %bitcast.30, ...), custom_call_target="tpu_custom_call" | custom-call | flops 28750000128 | tf_op jit(solution)/shard_map/forward/pallas_call | solution.py:331
  26.0 2.6 %collective-permute-done.refs_3_.refs_4_ = bf16[2,512,512]{2,1,0:T(8,128)(2,1)S(1)} collective-permute-done((bf16[2,512,512]{2,1,0:T(8,128)(2,1)S(1)}, bf16[2,512,512]{2,1,0:T(8,128)(2,1)S(1)}, u32[]{:S(2)}, u32[]{:S(2)}) %collective-permute-start) | collective-permute-done | bytes 1048608 | tf_op jit(solution)/shard_map/ppermute | solution.py:891
  28.6 9.5 %feed_first.1 = (bf16[2048,512]{1,0:T(8,128)(2,1)}, f32[2048,512]{1,0:T(8,128)S(1)}, bf16[8,144,512]{2,1,0:T(8,128)(2,1)S(1)}, bf16[2048,512]{1,0:T(8,128)(2,1)S(1)}, bf16[2048,512]{1,0:T(8,128)(2,1)S(1)}) custom-call(s32[1,64]{1,0:T(1,128)S(1)} %copy-done.7, s32[4]{0:T(128)S(1)} %pad_add_fusion.refs_1_.refs_0_, ...), custom_call_target="tpu_custom_call" | custom-call | flops 10350000128 | tf_op jit(solution)/shard_map/feed_first/pallas_call | solution.py:618
  38.2 7.8 %feed_middle.2 = (bf16[2048,512]{1,0:T(8,128)(2,1)}, f32[2048,512]{1,0:T(8,128)S(1)}, bf16[8,144,512]{2,1,0:T(8,128)(2,1)S(1)}) custom-call(s32[1,64]{1,0:T(1,128)S(1)} %copy-done.7, s32[4]{0:T(128)S(1)} %pad_add_fusion.refs_1_.refs_0_, bf16[2048,512]{1,0:T(8,128)(2,1)S(1)} %get-tuple-element.132.refs_2_.refs_1_, ...), custom_call_target="tpu_custom_call" | custom-call | flops 10350000128 | tf_op jit(solution)/shard_map/feed_middle/pallas_call | solution.py:618
  47.2 8.0 %feed_middle.3 = (bf16[2048,512]{1,0:T(8,128)(2,1)}, f32[2048,512]{1,0:T(8,128)S(1)}, bf16[8,128,512]{2,1,0:T(8,128)(2,1)S(1)}) custom-call(s32[4]{0:T(128)S(1)} %pad_add_fusion.refs_1_.refs_0_, bf16[2048,512]{1,0:T(8,128)(2,1)S(1)} %get-tuple-element.132.refs_2_.refs_1_, bf16[2,512,512]{2,1,0:T(8,128)(2,1)S(1)} %get-tuple-element.138.refs_2_.refs_6_, ...), custom_call_target="tpu_custom_call" | custom-call | flops 10350000128 | tf_op jit(solution)/shard_map/feed_middle/pallas_call | solution.py:618
  55.7 1.8 %collective-permute-start.3 = (bf16[4,144,512]{2,1,0:T(8,128)(2,1)S(1)}, bf16[4,144,512]{2,1,0:T(8,128)(2,1)S(1)}, u32[]{:S(2)}, u32[]{:S(2)}) collective-permute-start(bf16[4,144,512]{2,1,0:T(8,128)(2,1)S(1)} %get-tuple-element.142), channel_id=1, source_target_pairs={{0,4},{1,5},{2,6},{3,7},{4,0},{5,1},{6,2},{7,3},{8,12},{9,13},{10,... | collective-permute-start | bytes 1769480 | tf_op jit(solution)/shard_map/ppermute | solution.py:891
  57.5 15.2 %feed_last.1 = (bf16[2048,512]{1,0:T(8,128)(2,1)}, f32[2048,512]{1,0:T(8,128)}, bf16[8,128,512]{2,1,0:T(8,128)(2,1)S(1)}, bf16[2048,512]{1,0:T(8,128)(2,1)S(1)}, bf16[32,16,640]{2,1,0:T(8,128)(2,1)S(1)}) custom-call(s32[4]{0:T(128)S(1)} %pad_add_fusion.refs_1_.refs_0_, bf16[2048,512]{1,0:T(8,128)(2,1)S(1)} %get-tuple-element.132.refs_2_.refs_1_, ...), custom_call_target="tpu_custom_call" | custom-call | flops 10350000128 | tf_op jit(solution)/shard_map/feed_last/pallas_call | solution.py:618
  73.5 3.9 %collective-permute-start.7 = (bf16[1,144,512]{2,1,0:T(8,128)(2,1)S(1)}, bf16[1,144,512]{2,1,0:T(8,128)(2,1)S(1)}, u32[]{:S(2)}, u32[]{:S(2)}) collective-permute-start(bf16[1,144,512]{2,1,0:T(8,128)(2,1)S(1)} %get-tuple-element.160), channel_id=1, source_target_pairs={{0,24},{1,25},{2,26},{3,27},{4,28},{5,29},{6,30},{7,31},{8,16},{9,... | collective-permute-start | bytes 442376 | tf_op jit(solution)/shard_map/ppermute | solution.py:891
  78.0 8.6 %attend_back.2 = (bf16[2048,256]{1,0:T(8,128)(2,1)S(1)}, bf16[2048,256]{1,0:T(8,128)(2,1)S(1)}, bf16[2048,256]{1,0:T(8,128)(2,1)S(1)}, f32[64,256]{1,0:T(8,128)S(1)}) custom-call(s32[64]{0:T(128)S(1)} %bitcast.31, f32[64,512]{1,0:T(8,128)S(1)} %get-tuple-element.151.chosen_ref, bf16[2048,512]{1,0:T(8,128)(2,1)S(1)} %get-tuple-element.146.gatt_ref, ...), custom_call_target="tpu_custom_call" | custom-call | flops 11500000256 | tf_op jit(solution)/shard_map/attend_back/pallas_call | solution.py:407
  87.2 1.6 collective-permute-start.10
  88.9 2.6 %collective-permute-start.11 = (bf16[1,128,512]{2,1,0:T(8,128)(2,1)S(1)}, bf16[1,128,512]{2,1,0:T(8,128)(2,1)S(1)}, u32[]{:S(2)}, u32[]{:S(2)}) collective-permute-start(bf16[1,128,512]{2,1,0:T(8,128)(2,1)S(1)} %get-tuple-element.168), channel_id=1, source_target_pairs={{0,16},{1,17},{2,18},{3,19},{4,20},{5,21},{6,22},{7,23},{8,24},{9,... | collective-permute-start | bytes 393224 | tf_op jit(solution)/shard_map/ppermute | solution.py:891
  91.8 1.6 collective-permute-start.8
  93.4 8.8 %attend_back.3 = (bf16[2048,256]{1,0:T(8,128)(2,1)S(1)}, bf16[2048,256]{1,0:T(8,128)(2,1)S(1)}, bf16[2048,256]{1,0:T(8,128)(2,1)S(1)}, f32[64,256]{1,0:T(8,128)S(1)}) custom-call(s32[64]{0:T(128)S(1)} %bitcast.32, f32[64,512]{1,0:T(8,128)S(1)} %get-tuple-element.151.chosen_ref, bf16[2048,512]{1,0:T(8,128)(2,1)S(1)} %get-tuple-element.146.gatt_ref, ...), custom_call_target="tpu_custom_call" | custom-call | flops 11500000256 | tf_op jit(solution)/shard_map/attend_back/pallas_call | solution.py:407
  102.4 6.1 %head_grads.1 = (bf16[32,16,2688]{2,1,0:T(8,128)(2,1)S(1)}, f32[64,512]{1,0:T(8,128)S(1)}, f32[1,128]{1,0:T(1,128)S(1)}) custom-call(s32[4]{0:T(128)S(1)} %pad_add_fusion.refs_1_.refs_0_, f32[1]{0:T(128)S(6)} %copy.30.refs_1_, bf16[2048,512]{1,0:T(8,128)(2,1)S(1)} %copy-done.9, bf16[2048,256]{1,0:T(8,128)(2,1)S(1)} %get-tuple-element.178.refs_3_.refs_0_, ...), custom_call_target="tpu_custom_call" | custom-call | flops 6899999744 | tf_op jit(solution)/shard_map/head_grads/pallas_call | solution.py:711
  108.7 3.7 %collective-permute-start.26 = (bf16[1,128,512]{2,1,0:T(8,128)(2,1)S(1)}, bf16[1,128,512]{2,1,0:T(8,128)(2,1)S(1)}, u32[]{:S(2)}, u32[]{:S(2)}) collective-permute-start(bf16[1,128,512]{2,1,0:T(8,128)(2,1)S(1)} %add_convert_fusion.13), channel_id=1, source_target_pairs={{0,24},{1,25},{2,26},{3,27},{4,28},{5,29},{6,30},{7,31},{8,16},{9,... | collective-permute-start | bytes 393224 | tf_op jit(solution)/shard_map/ppermute | solution.py:891
  115.2 1.7 collective-permute-done.26
  118.0 9.8 %input_grad.1 = f32[2048,512]{1,0:T(8,128)} custom-call(bf16[2048,256]{1,0:T(8,128)(2,1)S(1)} %get-tuple-element.178.refs_3_.refs_0_, bf16[2048,256]{1,0:T(8,128)(2,1)S(1)} %get-tuple-element.179.refs_4_.refs_1_, bf16[2048,256]{1,0:T(8,128)(2,1)S(1)} %get-tuple-element.180.refs_5_.refs_2_, bf16[2048,256]{1,0:T(8,128)(2,1)S(1)} %get-tuple-element.181.refs_7_.refs_3_, ...), custom_call_target="tpu_custom_call" | custom-call | flops 11500000256 | tf_op jit(solution)/shard_map/input_grad/pallas_call | solution.py:751
  127.9 3.9 %collective-permute-done.16 = bf16[4,16,2688]{2,1,0:T(8,128)(2,1)S(1)} collective-permute-done((bf16[4,16,2688]{2,1,0:T(8,128)(2,1)S(1)}, bf16[4,16,2688]{2,1,0:T(8,128)(2,1)S(1)}, u32[]{:S(2)}, u32[]{:S(2)}) %collective-permute-start.16) | collective-permute-done | bytes 344096 | tf_op jit(solution)/shard_map/ppermute | solution.py:891
  131.9 3.6 %collective-permute-start.19 = (bf16[1,16,2688]{2,1,0:T(8,128)(2,1)S(1)}, bf16[1,16,2688]{2,1,0:T(8,128)(2,1)S(1)}, u32[]{:S(2)}, u32[]{:S(2)}) collective-permute-start(bf16[1,16,2688]{2,1,0:T(8,128)(2,1)S(1)} %get-tuple-element.204), channel_id=1, source_target_pairs={{0,24},{1,25},{2,26},{3,27},{4,28},{5,29},{6,30},{7,31},{8,16},{9,... | collective-permute-start | bytes 258056 | tf_op jit(solution)/shard_map/ppermute | solution.py:891
  138.9 3.2 %collective-permute-done.18 = bf16[1,16,2688]{2,1,0:T(8,128)(2,1)S(1)} collective-permute-done((bf16[1,16,2688]{2,1,0:T(8,128)(2,1)S(1)}, bf16[1,16,2688]{2,1,0:T(8,128)(2,1)S(1)}, u32[]{:S(2)}, u32[]{:S(2)}) %collective-permute-start.18) | collective-permute-done | bytes 86048 | tf_op jit(solution)/shard_map/ppermute | solution.py:891
  142.2 2.3 %collective-permute-start.22 = (bf16[1,16,2688]{2,1,0:T(8,128)(2,1)S(1)}, bf16[1,16,2688]{2,1,0:T(8,128)(2,1)S(1)}, u32[]{:S(2)}, u32[]{:S(2)}) collective-permute-start(bf16[1,16,2688]{2,1,0:T(8,128)(2,1)S(1)} %add_convert_fusion.18), channel_id=1, source_target_pairs={{0,24},{1,25},{2,26},{3,27},{4,28},{5,29},{6,30},{7,31},{8,16},{9,... | collective-permute-start | bytes 258056 | tf_op jit(solution)/shard_map/ppermute | solution.py:891
  144.5 2.1 %collective-permute-start.20 = (bf16[1,16,2688]{2,1,0:T(8,128)(2,1)S(1)}, bf16[1,16,2688]{2,1,0:T(8,128)(2,1)S(1)}, u32[]{:S(2)}, u32[]{:S(2)}) collective-permute-start(bf16[1,16,2688]{2,1,0:T(8,128)(2,1)S(1)} %add_convert_fusion.18), channel_id=1, source_target_pairs={{0,8},{1,9},{2,10},{3,11},{4,12},{5,13},{6,14},{7,15},{8,0},{9,1},... | collective-permute-start | bytes 258056 | tf_op jit(solution)/shard_map/ppermute | solution.py:891
  146.6 2.9 %collective-permute-done.22 = bf16[1,16,2688]{2,1,0:T(8,128)(2,1)S(1)} collective-permute-done((bf16[1,16,2688]{2,1,0:T(8,128)(2,1)S(1)}, bf16[1,16,2688]{2,1,0:T(8,128)(2,1)S(1)}, u32[]{:S(2)}, u32[]{:S(2)}) %collective-permute-start.22) | collective-permute-done | bytes 86048 | tf_op jit(solution)/shard_map/ppermute | solution.py:891
  149.5 2.2 %collective-permute-done.21 = bf16[1,16,2688]{2,1,0:T(8,128)(2,1)S(1)} collective-permute-done((bf16[1,16,2688]{2,1,0:T(8,128)(2,1)S(1)}, bf16[1,16,2688]{2,1,0:T(8,128)(2,1)S(1)}, u32[]{:S(2)}, u32[]{:S(2)}) %collective-permute-start.21) | collective-permute-done | bytes 86048 | tf_op jit(solution)/shard_map/ppermute | solution.py:891
  152.0 1.3 collective-permute-start.30
  153.2 2.1 %collective-permute-start.31 = (bf16[4,16,2688]{2,1,0:T(8,128)(2,1)S(1)}, bf16[4,16,2688]{2,1,0:T(8,128)(2,1)S(1)}, u32[]{:S(2)}, u32[]{:S(2)}) collective-permute-start(bf16[4,16,2688]{2,1,0:T(8,128)(2,1)S(1)} %pad_maximum_fusion.1.refs_1_), channel_id=1, source_target_pairs={{0,5},{1,4},{2,7},{3,6},{4,1},{5,0},{6,3},{7,2},{8,13},{9,12},{10,... | collective-permute-start | bytes 1032200 | tf_op jit(solution)/shard_map/ppermute | solution.py:891
  155.3 8.3 %layer_output.1 = f32[2048,512]{1,0:T(8,128)} custom-call(f32[2048,512]{1,0:T(8,128)S(1)} %copy-done.8, bf16[2048,512]{1,0:T(8,128)(2,1)} %get-tuple-element.211.refs_0_, bf16[2048,512]{1,0:T(8,128)(2,1)} %get-tuple-element.212.refs_1_, bf16[2048,512]{1,0:T(8,128)(2,1)} %get-tuple-element.213.refs_2_, bf16[2048,512]{1,0:T(8,128)(2,1)} %get-tuple-element.214.refs_3_, ...), custom_call_target="tpu_custom_call" | custom-call | flops 9200000000 | tf_op jit(solution)/shard_map/layer_output/pallas_call | solution.py:645
  164.2 3.3 %finish_feed.1 = (f32[512,1024]{1,0:T(8,128)}, f32[1024,512]{1,0:T(8,128)}) custom-call(s32[4]{0:T(128)S(1)} %pad_add_fusion.refs_1_.refs_0_, bf16[4,128,512]{2,1,0:T(8,128)(2,1)S(1)} %pad_maximum_fusion.refs_1_, bf16[4,128,512]{2,1,0:T(8,128)(2,1)S(1)} %collective-permute-done.27.refs_2_, bf16[4,128,512]{2,1,0:T(8,128)(2,1)S(1)} %collective-permute-done.28.refs_3_, ...), custom_call_target="tpu_custom_call" | custom-call | flops 3449999872 | tf_op jit(solution)/shard_map/finish_feed/pallas_call | solution.py:815
  167.6 1.6 collective-permute-done.31.refs_4_
  171.9 4.5 %finish.1 = (f32[512,512]{1,0:T(8,128)}, f32[512,512]{1,0:T(8,128)}, f32[512,512]{1,0:T(8,128)}, f32[512,512]{1,0:T(8,128)}, f32[512,512]{1,0:T(8,128)}, /*index...) custom-call(s32[4]{0:T(128)S(1)} %pad_add_fusion.refs_1_.refs_0_, ...), custom_call_target="tpu_custom_call" | custom-call | flops 5750000128 | tf_op jit(solution)/shard_map/finish/pallas_call | solution.py:869
  (102 shorter events, 14.9 us)
Async XLA Ops:
  2.4 26.2 %collective-permute-start = (bf16[2,512,512]{2,1,0:T(8,128)(2,1)S(1)}, bf16[2,512,512]{2,1,0:T(8,128)(2,1)S(1)}, u32[]{:S(2)}, u32[]{:S(2)}) collective-permute-start(bf16[2,512,512]{2,1,0:T(8,128)(2,1)S(1)} %pack_weights.1.refs_2_.refs_7_), channel_id=1, source_target_pairs={{0,1},{1,0},{2,3},{3,2},{4,5},{5,4},{6,7},{7,6},{8,9},{9,8},{10,11... | collective-permute-start | bytes 3145736 | tf_op jit(solution)/shard_map/ppermute | solution.py:891
  28.6 9.6 %collective-permute-start.1 = (bf16[2,512,512]{2,1,0:T(8,128)(2,1)S(1)}, bf16[2,512,512]{2,1,0:T(8,128)(2,1)S(1)}, u32[]{:S(2)}, u32[]{:S(2)}) collective-permute-start(bf16[2,512,512]{2,1,0:T(8,128)(2,1)S(1)} %collective-permute-done.refs_3_.refs_4_), channel_id=1, source_target_pairs={{0,2},{1,3},{2,0},{3,1},{4,6},{5,7},{6,4},{7,5},{8,10},{9,11},{10,... | collective-permute-start | bytes 3145736 | tf_op jit(solution)/shard_map/ppermute | solution.py:891
  46.0 9.3 %collective-permute-start.2 = (bf16[8,144,512]{2,1,0:T(8,128)(2,1)S(1)}, bf16[8,144,512]{2,1,0:T(8,128)(2,1)S(1)}, u32[]{:S(2)}, u32[]{:S(2)}) collective-permute-start(bf16[8,144,512]{2,1,0:T(8,128)(2,1)S(1)} %get-tuple-element.136), channel_id=1, source_target_pairs={{0,2},{1,3},{2,0},{3,1},{4,6},{5,7},{6,4},{7,5},{8,10},{9,11},{10,... | collective-permute-start | bytes 3538952 | tf_op jit(solution)/shard_map/ppermute | solution.py:891
  55.2 17.4 %collective-permute-start.5 = (bf16[8,128,512]{2,1,0:T(8,128)(2,1)S(1)}, bf16[8,128,512]{2,1,0:T(8,128)(2,1)S(1)}, u32[]{:S(2)}, u32[]{:S(2)}) collective-permute-start(bf16[8,128,512]{2,1,0:T(8,128)(2,1)S(1)} %get-tuple-element.149), channel_id=1, source_target_pairs={{0,2},{1,3},{2,0},{3,1},{4,6},{5,7},{6,4},{7,5},{8,10},{9,11},{10,... | collective-permute-start | bytes 3145736 | tf_op jit(solution)/shard_map/ppermute | solution.py:891
  55.7 17.7 %collective-permute-start.3 = (bf16[4,144,512]{2,1,0:T(8,128)(2,1)S(1)}, bf16[4,144,512]{2,1,0:T(8,128)(2,1)S(1)}, u32[]{:S(2)}, u32[]{:S(2)}) collective-permute-start(bf16[4,144,512]{2,1,0:T(8,128)(2,1)S(1)} %get-tuple-element.142), channel_id=1, source_target_pairs={{0,4},{1,5},{2,6},{3,7},{4,0},{5,1},{6,2},{7,3},{8,12},{9,13},{10,... | collective-permute-start | bytes 1769480 | tf_op jit(solution)/shard_map/ppermute | solution.py:891
  73.0 14.1 %collective-permute-start.9 = (bf16[4,128,512]{2,1,0:T(8,128)(2,1)S(1)}, bf16[4,128,512]{2,1,0:T(8,128)(2,1)S(1)}, u32[]{:S(2)}, u32[]{:S(2)}) collective-permute-start(bf16[4,128,512]{2,1,0:T(8,128)(2,1)S(1)} %get-tuple-element.165), channel_id=1, source_target_pairs={{0,4},{1,5},{2,6},{3,7},{4,0},{5,1},{6,2},{7,3},{8,12},{9,13},{10,... | collective-permute-start | bytes 1572872 | tf_op jit(solution)/shard_map/ppermute | solution.py:891
  73.5 18.0 %collective-permute-start.7 = (bf16[1,144,512]{2,1,0:T(8,128)(2,1)S(1)}, bf16[1,144,512]{2,1,0:T(8,128)(2,1)S(1)}, u32[]{:S(2)}, u32[]{:S(2)}) collective-permute-start(bf16[1,144,512]{2,1,0:T(8,128)(2,1)S(1)} %get-tuple-element.160), channel_id=1, source_target_pairs={{0,24},{1,25},{2,26},{3,27},{4,28},{5,29},{6,30},{7,31},{8,16},{9,... | collective-permute-start | bytes 442376 | tf_op jit(solution)/shard_map/ppermute | solution.py:891
  77.4 14.3 %collective-permute-start.6 = (bf16[1,144,512]{2,1,0:T(8,128)(2,1)S(1)}, bf16[1,144,512]{2,1,0:T(8,128)(2,1)S(1)}, u32[]{:S(2)}, u32[]{:S(2)}) collective-permute-start(bf16[1,144,512]{2,1,0:T(8,128)(2,1)S(1)} %get-tuple-element.158), channel_id=1, source_target_pairs={{0,16},{1,17},{2,18},{3,19},{4,20},{5,21},{6,22},{7,23},{8,24},{9,... | collective-permute-start | bytes 442376 | tf_op jit(solution)/shard_map/ppermute | solution.py:891
  77.4 14.3 %collective-permute-start.4 = (bf16[1,144,512]{2,1,0:T(8,128)(2,1)S(1)}, bf16[1,144,512]{2,1,0:T(8,128)(2,1)S(1)}, u32[]{:S(2)}, u32[]{:S(2)}) collective-permute-start(bf16[1,144,512]{2,1,0:T(8,128)(2,1)S(1)} %get-tuple-element.148), channel_id=1, source_target_pairs={{0,8},{1,9},{2,10},{3,11},{4,12},{5,13},{6,14},{7,15},{8,0},{9,1},... | collective-permute-start | bytes 442376 | tf_op jit(solution)/shard_map/ppermute | solution.py:891
  87.2 15.0 %collective-permute-start.10 = (bf16[1,128,512]{2,1,0:T(8,128)(2,1)S(1)}, bf16[1,128,512]{2,1,0:T(8,128)(2,1)S(1)}, u32[]{:S(2)}, u32[]{:S(2)}) collective-permute-start(bf16[1,128,512]{2,1,0:T(8,128)(2,1)S(1)} %get-tuple-element.167), channel_id=1, source_target_pairs={{0,8},{1,9},{2,10},{3,11},{4,12},{5,13},{6,14},{7,15},{8,0},{9,1},... | collective-permute-start | bytes 393224 | tf_op jit(solution)/shard_map/ppermute | solution.py:891
  88.9 13.3 %collective-permute-start.11 = (bf16[1,128,512]{2,1,0:T(8,128)(2,1)S(1)}, bf16[1,128,512]{2,1,0:T(8,128)(2,1)S(1)}, u32[]{:S(2)}, u32[]{:S(2)}) collective-permute-start(bf16[1,128,512]{2,1,0:T(8,128)(2,1)S(1)} %get-tuple-element.168), channel_id=1, source_target_pairs={{0,16},{1,17},{2,18},{3,19},{4,20},{5,21},{6,22},{7,23},{8,24},{9,... | collective-permute-start | bytes 393224 | tf_op jit(solution)/shard_map/ppermute | solution.py:891
  91.5 10.7 %collective-permute-start.12 = (bf16[1,128,512]{2,1,0:T(8,128)(2,1)S(1)}, bf16[1,128,512]{2,1,0:T(8,128)(2,1)S(1)}, u32[]{:S(2)}, u32[]{:S(2)}) collective-permute-start(bf16[1,128,512]{2,1,0:T(8,128)(2,1)S(1)} %get-tuple-element.169), channel_id=1, source_target_pairs={{0,24},{1,25},{2,26},{3,27},{4,28},{5,29},{6,30},{7,31},{8,16},{9,... | collective-permute-start | bytes 393224 | tf_op jit(solution)/shard_map/ppermute | solution.py:891
  91.8 10.4 %collective-permute-start.8 = (bf16[1,144,512]{2,1,0:T(8,128)(2,1)S(1)}, bf16[1,144,512]{2,1,0:T(8,128)(2,1)S(1)}, u32[]{:S(2)}, u32[]{:S(2)}) collective-permute-start(bf16[1,144,512]{2,1,0:T(8,128)(2,1)S(1)} %add_convert_fusion.8), channel_id=1, source_target_pairs={{0,1},{1,0},{2,3},{3,2},{4,5},{5,4},{6,7},{7,6},{8,9},{9,8},{10,11... | collective-permute-start | bytes 442376 | tf_op jit(solution)/shard_map/ppermute | solution.py:891
  108.7 8.3 %collective-permute-start.26 = (bf16[1,128,512]{2,1,0:T(8,128)(2,1)S(1)}, bf16[1,128,512]{2,1,0:T(8,128)(2,1)S(1)}, u32[]{:S(2)}, u32[]{:S(2)}) collective-permute-start(bf16[1,128,512]{2,1,0:T(8,128)(2,1)S(1)} %add_convert_fusion.13), channel_id=1, source_target_pairs={{0,24},{1,25},{2,26},{3,27},{4,28},{5,29},{6,30},{7,31},{8,16},{9,... | collective-permute-start | bytes 393224 | tf_op jit(solution)/shard_map/ppermute | solution.py:891
  112.3 15.5 %collective-permute-start.25 = (bf16[1,128,512]{2,1,0:T(8,128)(2,1)S(1)}, bf16[1,128,512]{2,1,0:T(8,128)(2,1)S(1)}, u32[]{:S(2)}, u32[]{:S(2)}) collective-permute-start(bf16[1,128,512]{2,1,0:T(8,128)(2,1)S(1)} %add_convert_fusion.13), channel_id=1, source_target_pairs={{0,16},{1,17},{2,18},{3,19},{4,20},{5,21},{6,22},{7,23},{8,24},{9,... | collective-permute-start | bytes 393224 | tf_op jit(solution)/shard_map/ppermute | solution.py:891
  112.3 15.5 %collective-permute-start.24 = (bf16[1,128,512]{2,1,0:T(8,128)(2,1)S(1)}, bf16[1,128,512]{2,1,0:T(8,128)(2,1)S(1)}, u32[]{:S(2)}, u32[]{:S(2)}) collective-permute-start(bf16[1,128,512]{2,1,0:T(8,128)(2,1)S(1)} %add_convert_fusion.13), channel_id=1, source_target_pairs={{0,8},{1,9},{2,10},{3,11},{4,12},{5,13},{6,14},{7,15},{8,0},{9,1},... | collective-permute-start | bytes 393224 | tf_op jit(solution)/shard_map/ppermute | solution.py:891
  113.5 18.2 %collective-permute-start.14 = (bf16[4,16,2688]{2,1,0:T(8,128)(2,1)S(1)}, bf16[4,16,2688]{2,1,0:T(8,128)(2,1)S(1)}, u32[]{:S(2)}, u32[]{:S(2)}) collective-permute-start(bf16[4,16,2688]{2,1,0:T(8,128)(2,1)S(1)} %get-tuple-element.192), channel_id=1, source_target_pairs={{0,1},{1,0},{2,3},{3,2},{4,5},{5,4},{6,7},{7,6},{8,9},{9,8},{10,11... | collective-permute-start | bytes 1032200 | tf_op jit(solution)/shard_map/ppermute | solution.py:891
  114.2 17.5 %collective-permute-start.15 = (bf16[4,16,2688]{2,1,0:T(8,128)(2,1)S(1)}, bf16[4,16,2688]{2,1,0:T(8,128)(2,1)S(1)}, u32[]{:S(2)}, u32[]{:S(2)}) collective-permute-start(bf16[4,16,2688]{2,1,0:T(8,128)(2,1)S(1)} %get-tuple-element.193), channel_id=1, source_target_pairs={{0,4},{1,5},{2,6},{3,7},{4,0},{5,1},{6,2},{7,3},{8,12},{9,13},{10,... | collective-permute-start | bytes 1032200 | tf_op jit(solution)/shard_map/ppermute | solution.py:891
  116.9 14.8 %collective-permute-start.16 = (bf16[4,16,2688]{2,1,0:T(8,128)(2,1)S(1)}, bf16[4,16,2688]{2,1,0:T(8,128)(2,1)S(1)}, u32[]{:S(2)}, u32[]{:S(2)}) collective-permute-start(bf16[4,16,2688]{2,1,0:T(8,128)(2,1)S(1)} %get-tuple-element.194), channel_id=1, source_target_pairs={{0,5},{1,4},{2,7},{3,6},{4,1},{5,0},{6,3},{7,2},{8,13},{9,12},{10,... | collective-permute-start | bytes 1032200 | tf_op jit(solution)/shard_map/ppermute | solution.py:891
  131.9 7.0 %collective-permute-start.19 = (bf16[1,16,2688]{2,1,0:T(8,128)(2,1)S(1)}, bf16[1,16,2688]{2,1,0:T(8,128)(2,1)S(1)}, u32[]{:S(2)}, u32[]{:S(2)}) collective-permute-start(bf16[1,16,2688]{2,1,0:T(8,128)(2,1)S(1)} %get-tuple-element.204), channel_id=1, source_target_pairs={{0,24},{1,25},{2,26},{3,27},{4,28},{5,29},{6,30},{7,31},{8,16},{9,... | collective-permute-start | bytes 258056 | tf_op jit(solution)/shard_map/ppermute | solution.py:891
  135.5 6.6 %collective-permute-start.18 = (bf16[1,16,2688]{2,1,0:T(8,128)(2,1)S(1)}, bf16[1,16,2688]{2,1,0:T(8,128)(2,1)S(1)}, u32[]{:S(2)}, u32[]{:S(2)}) collective-permute-start(bf16[1,16,2688]{2,1,0:T(8,128)(2,1)S(1)} %get-tuple-element.202), channel_id=1, source_target_pairs={{0,16},{1,17},{2,18},{3,19},{4,20},{5,21},{6,22},{7,23},{8,24},{9,... | collective-permute-start | bytes 258056 | tf_op jit(solution)/shard_map/ppermute | solution.py:891
  135.5 6.6 %collective-permute-start.17 = (bf16[1,16,2688]{2,1,0:T(8,128)(2,1)S(1)}, bf16[1,16,2688]{2,1,0:T(8,128)(2,1)S(1)}, u32[]{:S(2)}, u32[]{:S(2)}) collective-permute-start(bf16[1,16,2688]{2,1,0:T(8,128)(2,1)S(1)} %get-tuple-element.200), channel_id=1, source_target_pairs={{0,8},{1,9},{2,10},{3,11},{4,12},{5,13},{6,14},{7,15},{8,0},{9,1},... | collective-permute-start | bytes 258056 | tf_op jit(solution)/shard_map/ppermute | solution.py:891
  136.4 18.9 %collective-permute-start.27 = (bf16[4,128,512]{2,1,0:T(8,128)(2,1)S(1)}, bf16[4,128,512]{2,1,0:T(8,128)(2,1)S(1)}, u32[]{:S(2)}, u32[]{:S(2)}) collective-permute-start(bf16[4,128,512]{2,1,0:T(8,128)(2,1)S(1)} %pad_maximum_fusion.refs_1_), channel_id=1, source_target_pairs={{0,4},{1,5},{2,6},{3,7},{4,0},{5,1},{6,2},{7,3},{8,12},{9,13},{10,... | collective-permute-start | bytes 1572872 | tf_op jit(solution)/shard_map/ppermute | solution.py:891
  142.2 7.3 %collective-permute-start.22 = (bf16[1,16,2688]{2,1,0:T(8,128)(2,1)S(1)}, bf16[1,16,2688]{2,1,0:T(8,128)(2,1)S(1)}, u32[]{:S(2)}, u32[]{:S(2)}) collective-permute-start(bf16[1,16,2688]{2,1,0:T(8,128)(2,1)S(1)} %add_convert_fusion.18), channel_id=1, source_target_pairs={{0,24},{1,25},{2,26},{3,27},{4,28},{5,29},{6,30},{7,31},{8,16},{9,... | collective-permute-start | bytes 258056 | tf_op jit(solution)/shard_map/ppermute | solution.py:891
  144.5 7.2 %collective-permute-start.21 = (bf16[1,16,2688]{2,1,0:T(8,128)(2,1)S(1)}, bf16[1,16,2688]{2,1,0:T(8,128)(2,1)S(1)}, u32[]{:S(2)}, u32[]{:S(2)}) collective-permute-start(bf16[1,16,2688]{2,1,0:T(8,128)(2,1)S(1)} %add_convert_fusion.18), channel_id=1, source_target_pairs={{0,16},{1,17},{2,18},{3,19},{4,20},{5,21},{6,22},{7,23},{8,24},{9,... | collective-permute-start | bytes 258056 | tf_op jit(solution)/shard_map/ppermute | solution.py:891
  144.5 7.2 %collective-permute-start.20 = (bf16[1,16,2688]{2,1,0:T(8,128)(2,1)S(1)}, bf16[1,16,2688]{2,1,0:T(8,128)(2,1)S(1)}, u32[]{:S(2)}, u32[]{:S(2)}) collective-permute-start(bf16[1,16,2688]{2,1,0:T(8,128)(2,1)S(1)} %add_convert_fusion.18), channel_id=1, source_target_pairs={{0,8},{1,9},{2,10},{3,11},{4,12},{5,13},{6,14},{7,15},{8,0},{9,1},... | collective-permute-start | bytes 258056 | tf_op jit(solution)/shard_map/ppermute | solution.py:891
  146.6 17.0 %collective-permute-start.28 = (bf16[4,128,512]{2,1,0:T(8,128)(2,1)S(1)}, bf16[4,128,512]{2,1,0:T(8,128)(2,1)S(1)}, u32[]{:S(2)}, u32[]{:S(2)}) collective-permute-start(bf16[4,128,512]{2,1,0:T(8,128)(2,1)S(1)} %pad_maximum_fusion.refs_1_), channel_id=1, source_target_pairs={{0,2},{1,3},{2,0},{3,1},{4,6},{5,7},{6,4},{7,5},{8,10},{9,11},{10,... | collective-permute-start | bytes 1572872 | tf_op jit(solution)/shard_map/ppermute | solution.py:891
  151.7 15.8 %collective-permute-start.23 = (bf16[4,16,2688]{2,1,0:T(8,128)(2,1)S(1)}, bf16[4,16,2688]{2,1,0:T(8,128)(2,1)S(1)}, u32[]{:S(2)}, u32[]{:S(2)}) collective-permute-start(bf16[4,16,2688]{2,1,0:T(8,128)(2,1)S(1)} %pad_maximum_fusion.1.refs_1_), channel_id=1, source_target_pairs={{0,1},{1,0},{2,3},{3,2},{4,5},{5,4},{6,7},{7,6},{8,9},{9,8},{10,11... | collective-permute-start | bytes 1032200 | tf_op jit(solution)/shard_map/ppermute | solution.py:891
  152.0 15.6 %collective-permute-start.30 = (bf16[4,16,2688]{2,1,0:T(8,128)(2,1)S(1)}, bf16[4,16,2688]{2,1,0:T(8,128)(2,1)S(1)}, u32[]{:S(2)}, u32[]{:S(2)}) collective-permute-start(bf16[4,16,2688]{2,1,0:T(8,128)(2,1)S(1)} %pad_maximum_fusion.1.refs_1_), channel_id=1, source_target_pairs={{0,4},{1,5},{2,6},{3,7},{4,0},{5,1},{6,2},{7,3},{8,12},{9,13},{10,... | collective-permute-start | bytes 1032200 | tf_op jit(solution)/shard_map/ppermute | solution.py:891
  153.2 16.0 %collective-permute-start.31 = (bf16[4,16,2688]{2,1,0:T(8,128)(2,1)S(1)}, bf16[4,16,2688]{2,1,0:T(8,128)(2,1)S(1)}, u32[]{:S(2)}, u32[]{:S(2)}) collective-permute-start(bf16[4,16,2688]{2,1,0:T(8,128)(2,1)S(1)} %pad_maximum_fusion.1.refs_1_), channel_id=1, source_target_pairs={{0,5},{1,4},{2,7},{3,6},{4,1},{5,0},{6,3},{7,2},{8,13},{9,12},{10,... | collective-permute-start | bytes 1032200 | tf_op jit(solution)/shard_map/ppermute | solution.py:891
  155.3 8.9 %collective-permute-start.29 = (bf16[4,128,512]{2,1,0:T(8,128)(2,1)S(1)}, bf16[4,128,512]{2,1,0:T(8,128)(2,1)S(1)}, u32[]{:S(2)}, u32[]{:S(2)}) collective-permute-start(bf16[4,128,512]{2,1,0:T(8,128)(2,1)S(1)} %collective-permute-done.27.refs_2_), channel_id=1, source_target_pairs={{0,2},{1,3},{2,0},{3,1},{4,6},{5,7},{6,4},{7,5},{8,10},{9,11},{10,... | collective-permute-start | bytes 1572872 | tf_op jit(solution)/shard_map/ppermute | solution.py:891
  163.7 6.0 %collective-permute-start.32 = (bf16[4,16,2688]{2,1,0:T(8,128)(2,1)S(1)}, bf16[4,16,2688]{2,1,0:T(8,128)(2,1)S(1)}, u32[]{:S(2)}, u32[]{:S(2)}) collective-permute-start(bf16[4,16,2688]{2,1,0:T(8,128)(2,1)S(1)} %pad_maximum_fusion.1.refs_1_), channel_id=1, source_target_pairs={{0,2},{1,3},{2,0},{3,1},{4,6},{5,7},{6,4},{7,5},{8,10},{9,11},{10,... | collective-permute-start | bytes 1032200 | tf_op jit(solution)/shard_map/ppermute | solution.py:891
  (20 other events, 172.3 us)

commit v5 on v4

--- a/solution.py
+++ b/solution.py
@@ -24,6 +24,7 @@
 MIB = 1024 * 1024
 LANES = 128
 TALLY_ROWS = 16
+AHEAD = 3
 
 
 def dot(left, right):
@@ -264,29 +265,40 @@
     query_row = lax.broadcasted_iota(jnp.int32, (BLOCK, GROUP_ROWS), 1) % BLOCK
     causal = key_row <= query_row
 
+    def score(block, g):
+        partner = perm_ref[block]
+        own_at = pl.ds(pl.multiple_of(block * BLOCK, BLOCK), BLOCK)
+        far_at = pl.ds(pl.multiple_of(partner * BLOCK, BLOCK), BLOCK)
+        lanes = slice(g * GROUP_WIDTH, (g + 1) * GROUP_WIDTH)
+        queries = expand(q_ref[own_at, lanes], masks)
+        keys = jnp.concatenate([k_ref[own_at, lanes], k_ref[far_at, lanes]], axis=0)
+        return dot_nt(keys, queries) * FACTOR
+
+    def mix(block, g, scores):
+        partner = perm_ref[block]
+        usable = (partner < block) & (mask_ref[partner] > 0)
+        own_at = pl.ds(pl.multiple_of(block * BLOCK, BLOCK), BLOCK)
+        far_at = pl.ds(pl.multiple_of(partner * BLOCK, BLOCK), BLOCK)
+        probs_at = pl.ds(pl.multiple_of(block * 2 * BLOCK, 2 * BLOCK), 2 * BLOCK)
+        lanes = slice(g * GROUP_WIDTH, (g + 1) * GROUP_WIDTH)
+        own = jnp.where(causal, scores[:BLOCK], -1e30)
+        far = jnp.where(usable, scores[BLOCK:], -1e30)
+        top = jnp.maximum(jnp.max(own, axis=0, keepdims=True), jnp.max(far, axis=0, keepdims=True))
+        powers = jnp.exp(jnp.concatenate([own, far], axis=0) - top)
+        probs = (powers * (1.0 / jnp.sum(powers, axis=0, keepdims=True))).astype(BF16)
+        probs_ref[probs_at, g * GROUP_ROWS : (g + 1) * GROUP_ROWS] = probs
+        scaled = (v_ref[far_at, lanes].astype(F32) * chosen_ref[pl.ds(block, 1), lanes]).astype(BF16)
+        values = jnp.concatenate([v_ref[own_at, lanes], scaled], axis=0)
+        att_ref[own_at, lanes] = fold(dot_tn(probs, values), masks).astype(BF16)
+
     def attend(j):
-        for b in range(part):
-            block = j * part + b
-            partner = perm_ref[block]
-            usable = (partner < block) & (mask_ref[partner] > 0)
-            own_at = pl.ds(pl.multiple_of(block * BLOCK, BLOCK), BLOCK)
-            far_at = pl.ds(pl.multiple_of(partner * BLOCK, BLOCK), BLOCK)
-            probs_at = pl.ds(pl.multiple_of(block * 2 * BLOCK, 2 * BLOCK), 2 * BLOCK)
-            chosen_row = chosen_ref[pl.ds(block, 1), :]
-            for g in range(width // GROUP_WIDTH):
-                lanes = slice(g * GROUP_WIDTH, (g + 1) * GROUP_WIDTH)
-                queries = expand(q_ref[own_at, lanes], masks)
-                keys = jnp.concatenate([k_ref[own_at, lanes], k_ref[far_at, lanes]], axis=0)
-                scores = dot_nt(keys, queries) * FACTOR
-                own = jnp.where(causal, scores[:BLOCK], -1e30)
-                far = jnp.where(usable, scores[BLOCK:], -1e30)
-                top = jnp.maximum(jnp.max(own, axis=0, keepdims=True), jnp.max(far, axis=0, keepdims=True))
-                powers = jnp.exp(jnp.concatenate([own, far], axis=0) - top)
-                probs = (powers * (1.0 / jnp.sum(powers, axis=0, keepdims=True))).astype(BF16)
-                probs_ref[probs_at, g * GROUP_ROWS : (g + 1) * GROUP_ROWS] = probs
-                scaled = (v_ref[far_at, lanes].astype(F32) * chosen_row[:, lanes]).astype(BF16)
-                values = jnp.concatenate([v_ref[own_at, lanes], scaled], axis=0)
-                att_ref[own_at, lanes] = fold(dot_tn(probs, values), masks).astype(BF16)
+        units = [(j * part + b, g) for b in range(part) for g in range(width // GROUP_WIDTH)]
+        ahead = []
+        for n in range(len(units) + AHEAD):
+            if n < len(units):
+                ahead.append(score(*units[n]))
+            if n >= AHEAD:
+                mix(*units[n - AHEAD], ahead[n - AHEAD])
 
     def settle(j):
         at = pl.ds(pl.multiple_of(j * some, some), some)
@@ -364,33 +376,46 @@
     masks = head_masks(BLOCK)
     lanes = slice(group * width, (group + 1) * width)
 
+    def ahead(block):
+        partner = perm_ref[block]
+        own_at = pl.ds(pl.multiple_of(block * BLOCK, BLOCK), BLOCK)
+        far_at = pl.ds(pl.multiple_of(partner * BLOCK, BLOCK), BLOCK)
+        probs_at = pl.ds(pl.multiple_of(block * 2 * BLOCK, 2 * BLOCK), 2 * BLOCK)
+        grads = expand(gatt_ref[own_at, lanes], masks)
+        far_values = v_ref[far_at, lanes].astype(F32)
+        chosen = chosen_ref[pl.ds(block, 1), lanes]
+        values = jnp.concatenate([v_ref[own_at, lanes], (far_values * chosen).astype(BF16)], axis=0)
+        probs_low = probs_ref[probs_at, group * GROUP_ROWS : (group + 1) * GROUP_ROWS]
+        grad_probs = dot_nt(values, grads)
+        grad_values = dot(probs_low, grads)
+        far_grad = grad_values[BLOCK:]
+        gch_ref[pl.ds(block, 1), :] = jnp.sum(far_grad * far_values, axis=0, keepdims=True)
+        own_v_ref[own_at, :] = grad_values[:BLOCK]
+        far_v_ref[far_at, :] = far_grad * chosen
+        return grad_probs
+
+    def behind(block, grad_probs):
+        partner = perm_ref[block]
+        own_at = pl.ds(pl.multiple_of(block * BLOCK, BLOCK), BLOCK)
+        far_at = pl.ds(pl.multiple_of(partner * BLOCK, BLOCK), BLOCK)
+        probs_at = pl.ds(pl.multiple_of(block * 2 * BLOCK, 2 * BLOCK), 2 * BLOCK)
+        queries = expand(q_ref[own_at, lanes], masks)
+        keys = jnp.concatenate([k_ref[own_at, lanes], k_ref[far_at, lanes]], axis=0)
+        probs = probs_ref[probs_at, group * GROUP_ROWS : (group + 1) * GROUP_ROWS].astype(F32)
+        total = jnp.sum(probs * grad_probs, axis=0, keepdims=True)
+        grad_scores = (probs * (grad_probs - total)).astype(BF16)
+        grad_keys = dot(grad_scores, queries) * FACTOR
+        gq_ref[own_at, :] = (fold(dot_tn(grad_scores, keys), masks) * FACTOR).astype(BF16)
+        own_k_ref[own_at, :] = grad_keys[:BLOCK]
+        far_k_ref[far_at, :] = grad_keys[BLOCK:]
+
     def body(j, _):
-        for b in range(part):
-            block = j * part + b
-            partner = perm_ref[block]
-            own_at = pl.ds(pl.multiple_of(block * BLOCK, BLOCK), BLOCK)
-            far_at = pl.ds(pl.multiple_of(partner * BLOCK, BLOCK), BLOCK)
-            probs_at = pl.ds(pl.multiple_of(block * 2 * BLOCK, 2 * BLOCK), 2 * BLOCK)
-            queries = expand(q_ref[own_at, lanes], masks)
-            grads = expand(gatt_ref[own_at, lanes], masks)
-            keys = jnp.concatenate([k_ref[own_at, lanes], k_ref[far_at, lanes]], axis=0)
-            far_values = v_ref[far_at, lanes].astype(F32)
-            chosen = chosen_ref[pl.ds(block, 1), lanes]
-            values = jnp.concatenate([v_ref[own_at, lanes], (far_values * chosen).astype(BF16)], axis=0)
-            probs_low = probs_ref[probs_at, group * GROUP_ROWS : (group + 1) * GROUP_ROWS]
-            probs = probs_low.astype(F32)
-            grad_probs = dot_nt(values, grads)
-            total = jnp.sum(probs * grad_probs, axis=0, keepdims=True)
-            grad_scores = (probs * (grad_probs - total)).astype(BF16)
-            grad_keys = dot(grad_scores, queries) * FACTOR
-            grad_values = dot(probs_low, grads)
-            gq_ref[own_at, :] = (fold(dot_tn(grad_scores, keys), masks) * FACTOR).astype(BF16)
-            far_grad = grad_values[BLOCK:]
-            gch_ref[pl.ds(block, 1), :] = jnp.sum(far_grad * far_values, axis=0, keepdims=True)
-            own_k_ref[own_at, :] = grad_keys[:BLOCK]
-            far_k_ref[far_at, :] = grad_keys[BLOCK:]
-            own_v_ref[own_at, :] = grad_values[:BLOCK]
-            far_v_ref[far_at, :] = far_grad * chosen
+        products = []
+        for n in range(part + AHEAD):
+            if n < part:
+                products.append(ahead(j * part + n))
+            if n >= AHEAD:
+                behind(j * part + n - AHEAD, products[n - AHEAD])
         return 0
 
     lax.fori_loop(0, parts, body, 0)

time: 177 us -> 177 us (level)
  Pallas kernels: 112 us -> 109 us
  waiting for transfers between devices: 21.9 us -> 24.9 us
    pallas_call x2, Pallas kernels: 17.3 us -> 14.2 us  [attend_back(): pl.pallas_call(functools.partial(attend_back_kernel, group=group, part=pa...]
    ppermute x36, waiting for transfers between devices: 21.9 us -> 24.9 us  [swap(): lax.ppermute(array, ('batch', 'mp'), [(i, i ^ flip) for i in range(count)])]
  transfers between devices with their start and end apart: 36 -> 36, of which waited for: 12 -> 13; matrix products, arithmetic and copies ran while one was open for 1% -> 1% of each run, Pallas kernels for 52% -> 50%
where the time goes in v5:
time: 177 us
  Pallas kernels  109 us (62%)
  starting transfers between devices  39.1 us (22%)
  waiting for transfers between devices  24.9 us (14%)
  other arithmetic  1.88 us (1%)
  between operations  1.86 us (1%)
    pallas_call x4, Pallas kernels, feed_quarter(): pl.pallas_call(functools.partial(quarter_kernel, kind=kind, tile=tile, ta...  40.5 us
    ppermute x36, starting transfers between devices, swap(): lax.ppermute(array, ('batch', 'mp'), [(i, i ^ flip) for i in range(count)])  39.1 us
    ppermute x36, waiting for transfers between devices, swap(): lax.ppermute(array, ('batch', 'mp'), [(i, i ^ flip) for i in range(count)])  24.9 us
    pallas_call x1, Pallas kernels, forward(): pl.pallas_call(functools.partial(forward_kernel, tile=tile), in_specs=[sm...  20.3 us
    pallas_call x2, Pallas kernels, attend_back(): pl.pallas_call(functools.partial(attend_back_kernel, group=group, part=pa...  14.2 us
    pallas_call x1, Pallas kernels, input_grad(): pl.pallas_call(input_kernel, grid=(rows // tile,), in_specs=[rows_of(tile...  9.8 us
    pallas_call x1, Pallas kernels, layer_output(): pl.pallas_call(output_kernel, grid=(rows // tile,), in_specs=[rows_of(til...  8.34 us
    pallas_call x1, Pallas kernels, head_grads(): pl.pallas_call(functools.partial(head_kernel, count=len(groups)), in_spec...  6.07 us
  transfers between devices with their start and end apart: 36, of which 13 were waited for; matrix products, arithmetic and copies ran while one was open for 1% of the time, Pallas kernels for 50%

profile of v5, /device:TPU:0, one launch (start us, length us, event | category | flops | bytes accessed | tf_op | source)
XLA Modules:
  0.0 176.6 jit_solution(13353650468932018763)
XLA Ops:
  0.7 1.7 pack_weights.1.refs_2_.refs_7_
  2.4 3.0 %collective-permute-start = (bf16[2,512,512]{2,1,0:T(8,128)(2,1)S(1)}, bf16[2,512,512]{2,1,0:T(8,128)(2,1)S(1)}, u32[]{:S(2)}, u32[]{:S(2)}) collective-permute-start(bf16[2,512,512]{2,1,0:T(8,128)(2,1)S(1)} %pack_weights.1.refs_2_.refs_7_), channel_id=1, source_target_pairs={{0,1},{1,0},{2,3},{3,2},{4,5},{5,4},{6,7},{7,6},{8,9},{9,8},{10,11... | collective-permute-start | bytes 3145736 | tf_op jit(solution)/shard_map/ppermute | solution.py:916
  5.4 20.3 %forward.1 = (bf16[2048,512]{1,0:T(8,128)(2,1)}, bf16[2048,512]{1,0:T(8,128)(2,1)}, bf16[2048,512]{1,0:T(8,128)(2,1)}, bf16[2048,512]{1,0:T(8,128)(2,1)}, bf16[4...) custom-call(s32[64]{0:T(128)S(1)} %bitcast.30, ...), custom_call_target="tpu_custom_call" | custom-call | flops 28750000128 | tf_op jit(solution)/shard_map/forward/pallas_call | solution.py:343
  25.7 2.8 %collective-permute-done.refs_3_.refs_4_ = bf16[2,512,512]{2,1,0:T(8,128)(2,1)S(1)} collective-permute-done((bf16[2,512,512]{2,1,0:T(8,128)(2,1)S(1)}, bf16[2,512,512]{2,1,0:T(8,128)(2,1)S(1)}, u32[]{:S(2)}, u32[]{:S(2)}) %collective-permute-start) | collective-permute-done | bytes 1048608 | tf_op jit(solution)/shard_map/ppermute | solution.py:916
  28.6 9.5 %feed_first.1 = (bf16[2048,512]{1,0:T(8,128)(2,1)}, f32[2048,512]{1,0:T(8,128)S(1)}, bf16[8,144,512]{2,1,0:T(8,128)(2,1)S(1)}, bf16[2048,512]{1,0:T(8,128)(2,1)S(1)}, bf16[2048,512]{1,0:T(8,128)(2,1)S(1)}) custom-call(s32[1,64]{1,0:T(1,128)S(1)} %copy-done.7, s32[4]{0:T(128)S(1)} %pad_add_fusion.refs_1_.refs_0_, ...), custom_call_target="tpu_custom_call" | custom-call | flops 10350000128 | tf_op jit(solution)/shard_map/feed_first/pallas_call | solution.py:643
  38.2 7.8 %feed_middle.2 = (bf16[2048,512]{1,0:T(8,128)(2,1)}, f32[2048,512]{1,0:T(8,128)S(1)}, bf16[8,144,512]{2,1,0:T(8,128)(2,1)S(1)}) custom-call(s32[1,64]{1,0:T(1,128)S(1)} %copy-done.7, s32[4]{0:T(128)S(1)} %pad_add_fusion.refs_1_.refs_0_, bf16[2048,512]{1,0:T(8,128)(2,1)S(1)} %get-tuple-element.132.refs_2_.refs_1_, ...), custom_call_target="tpu_custom_call" | custom-call | flops 10350000128 | tf_op jit(solution)/shard_map/feed_middle/pallas_call | solution.py:643
  47.2 8.0 %feed_middle.3 = (bf16[2048,512]{1,0:T(8,128)(2,1)}, f32[2048,512]{1,0:T(8,128)S(1)}, bf16[8,128,512]{2,1,0:T(8,128)(2,1)S(1)}) custom-call(s32[4]{0:T(128)S(1)} %pad_add_fusion.refs_1_.refs_0_, bf16[2048,512]{1,0:T(8,128)(2,1)S(1)} %get-tuple-element.132.refs_2_.refs_1_, bf16[2,512,512]{2,1,0:T(8,128)(2,1)S(1)} %get-tuple-element.138.refs_2_.refs_6_, ...), custom_call_target="tpu_custom_call" | custom-call | flops 10350000128 | tf_op jit(solution)/shard_map/feed_middle/pallas_call | solution.py:643
  55.7 1.8 %collective-permute-start.3 = (bf16[4,144,512]{2,1,0:T(8,128)(2,1)S(1)}, bf16[4,144,512]{2,1,0:T(8,128)(2,1)S(1)}, u32[]{:S(2)}, u32[]{:S(2)}) collective-permute-start(bf16[4,144,512]{2,1,0:T(8,128)(2,1)S(1)} %get-tuple-element.142), channel_id=1, source_target_pairs={{0,4},{1,5},{2,6},{3,7},{4,0},{5,1},{6,2},{7,3},{8,12},{9,13},{10,... | collective-permute-start | bytes 1769480 | tf_op jit(solution)/shard_map/ppermute | solution.py:916
  57.5 15.2 %feed_last.1 = (bf16[2048,512]{1,0:T(8,128)(2,1)}, f32[2048,512]{1,0:T(8,128)}, bf16[8,128,512]{2,1,0:T(8,128)(2,1)S(1)}, bf16[2048,512]{1,0:T(8,128)(2,1)S(1)}, bf16[32,16,640]{2,1,0:T(8,128)(2,1)S(1)}) custom-call(s32[4]{0:T(128)S(1)} %pad_add_fusion.refs_1_.refs_0_, bf16[2048,512]{1,0:T(8,128)(2,1)S(1)} %get-tuple-element.132.refs_2_.refs_1_, ...), custom_call_target="tpu_custom_call" | custom-call | flops 10350000128 | tf_op jit(solution)/shard_map/feed_last/pallas_call | solution.py:643
  73.5 3.9 %collective-permute-start.7 = (bf16[1,144,512]{2,1,0:T(8,128)(2,1)S(1)}, bf16[1,144,512]{2,1,0:T(8,128)(2,1)S(1)}, u32[]{:S(2)}, u32[]{:S(2)}) collective-permute-start(bf16[1,144,512]{2,1,0:T(8,128)(2,1)S(1)} %get-tuple-element.160), channel_id=1, source_target_pairs={{0,24},{1,25},{2,26},{3,27},{4,28},{5,29},{6,30},{7,31},{8,16},{9,... | collective-permute-start | bytes 442376 | tf_op jit(solution)/shard_map/ppermute | solution.py:916
  78.0 7.0 %attend_back.2 = (bf16[2048,256]{1,0:T(8,128)(2,1)S(1)}, bf16[2048,256]{1,0:T(8,128)(2,1)S(1)}, bf16[2048,256]{1,0:T(8,128)(2,1)S(1)}, f32[64,256]{1,0:T(8,128)S(1)}) custom-call(s32[64]{0:T(128)S(1)} %bitcast.31, f32[64,512]{1,0:T(8,128)S(1)} %get-tuple-element.151.chosen_ref, bf16[2048,512]{1,0:T(8,128)(2,1)S(1)} %get-tuple-element.146.gatt_ref, ...), custom_call_target="tpu_custom_call" | custom-call | flops 11500000256 | tf_op jit(solution)/shard_map/attend_back/pallas_call | solution.py:432
  85.1 2.0 %collective-permute-done.9 = bf16[4,128,512]{2,1,0:T(8,128)(2,1)S(1)} collective-permute-done((bf16[4,128,512]{2,1,0:T(8,128)(2,1)S(1)}, bf16[4,128,512]{2,1,0:T(8,128)(2,1)S(1)}, u32[]{:S(2)}, u32[]{:S(2)}) %collective-permute-start.9) | collective-permute-done | bytes 524320 | tf_op jit(solution)/shard_map/ppermute | solution.py:916
  87.2 1.6 collective-permute-start.10
  88.9 2.6 %collective-permute-start.11 = (bf16[1,128,512]{2,1,0:T(8,128)(2,1)S(1)}, bf16[1,128,512]{2,1,0:T(8,128)(2,1)S(1)}, u32[]{:S(2)}, u32[]{:S(2)}) collective-permute-start(bf16[1,128,512]{2,1,0:T(8,128)(2,1)S(1)} %get-tuple-element.168), channel_id=1, source_target_pairs={{0,16},{1,17},{2,18},{3,19},{4,20},{5,21},{6,22},{7,23},{8,24},{9,... | collective-permute-start | bytes 393224 | tf_op jit(solution)/shard_map/ppermute | solution.py:916
  91.8 1.6 collective-permute-start.8
  93.4 7.2 %attend_back.3 = (bf16[2048,256]{1,0:T(8,128)(2,1)S(1)}, bf16[2048,256]{1,0:T(8,128)(2,1)S(1)}, bf16[2048,256]{1,0:T(8,128)(2,1)S(1)}, f32[64,256]{1,0:T(8,128)S(1)}) custom-call(s32[64]{0:T(128)S(1)} %bitcast.32, f32[64,512]{1,0:T(8,128)S(1)} %get-tuple-element.151.chosen_ref, bf16[2048,512]{1,0:T(8,128)(2,1)S(1)} %get-tuple-element.146.gatt_ref, ...), custom_call_target="tpu_custom_call" | custom-call | flops 11500000256 | tf_op jit(solution)/shard_map/attend_back/pallas_call | solution.py:432
  101.5 6.1 %head_grads.1 = (bf16[32,16,2688]{2,1,0:T(8,128)(2,1)S(1)}, f32[64,512]{1,0:T(8,128)S(1)}, f32[1,128]{1,0:T(1,128)S(1)}) custom-call(s32[4]{0:T(128)S(1)} %pad_add_fusion.refs_1_.refs_0_, f32[1]{0:T(128)S(6)} %copy.30.refs_1_, bf16[2048,512]{1,0:T(8,128)(2,1)S(1)} %copy-done.9, bf16[2048,256]{1,0:T(8,128)(2,1)S(1)} %get-tuple-element.178.refs_3_.refs_0_, ...), custom_call_target="tpu_custom_call" | custom-call | flops 6899999744 | tf_op jit(solution)/shard_map/head_grads/pallas_call | solution.py:736
  107.8 3.0 %collective-permute-start.26 = (bf16[1,128,512]{2,1,0:T(8,128)(2,1)S(1)}, bf16[1,128,512]{2,1,0:T(8,128)(2,1)S(1)}, u32[]{:S(2)}, u32[]{:S(2)}) collective-permute-start(bf16[1,128,512]{2,1,0:T(8,128)(2,1)S(1)} %add_convert_fusion.13), channel_id=1, source_target_pairs={{0,24},{1,25},{2,26},{3,27},{4,28},{5,29},{6,30},{7,31},{8,16},{9,... | collective-permute-start | bytes 393224 | tf_op jit(solution)/shard_map/ppermute | solution.py:916
  112.6 1.6 collective-permute-start.14
  117.6 9.8 %input_grad.1 = f32[2048,512]{1,0:T(8,128)} custom-call(bf16[2048,256]{1,0:T(8,128)(2,1)S(1)} %get-tuple-element.178.refs_3_.refs_0_, bf16[2048,256]{1,0:T(8,128)(2,1)S(1)} %get-tuple-element.179.refs_4_.refs_1_, bf16[2048,256]{1,0:T(8,128)(2,1)S(1)} %get-tuple-element.180.refs_5_.refs_2_, bf16[2048,256]{1,0:T(8,128)(2,1)S(1)} %get-tuple-element.181.refs_7_.refs_3_, ...), custom_call_target="tpu_custom_call" | custom-call | flops 11500000256 | tf_op jit(solution)/shard_map/input_grad/pallas_call | solution.py:776
  127.4 3.4 %collective-permute-done.16 = bf16[4,16,2688]{2,1,0:T(8,128)(2,1)S(1)} collective-permute-done((bf16[4,16,2688]{2,1,0:T(8,128)(2,1)S(1)}, bf16[4,16,2688]{2,1,0:T(8,128)(2,1)S(1)}, u32[]{:S(2)}, u32[]{:S(2)}) %collective-permute-start.16) | collective-permute-done | bytes 344096 | tf_op jit(solution)/shard_map/ppermute | solution.py:916
  130.9 3.0 %collective-permute-start.19 = (bf16[1,16,2688]{2,1,0:T(8,128)(2,1)S(1)}, bf16[1,16,2688]{2,1,0:T(8,128)(2,1)S(1)}, u32[]{:S(2)}, u32[]{:S(2)}) collective-permute-start(bf16[1,16,2688]{2,1,0:T(8,128)(2,1)S(1)} %get-tuple-element.204), channel_id=1, source_target_pairs={{0,24},{1,25},{2,26},{3,27},{4,28},{5,29},{6,30},{7,31},{8,16},{9,... | collective-permute-start | bytes 258056 | tf_op jit(solution)/shard_map/ppermute | solution.py:916
  136.4 1.7 collective-permute-done.19
  138.1 3.0 %collective-permute-done.18 = bf16[1,16,2688]{2,1,0:T(8,128)(2,1)S(1)} collective-permute-done((bf16[1,16,2688]{2,1,0:T(8,128)(2,1)S(1)}, bf16[1,16,2688]{2,1,0:T(8,128)(2,1)S(1)}, u32[]{:S(2)}, u32[]{:S(2)}) %collective-permute-start.18) | collective-permute-done | bytes 86048 | tf_op jit(solution)/shard_map/ppermute | solution.py:916
  141.2 3.0 %collective-permute-start.22 = (bf16[1,16,2688]{2,1,0:T(8,128)(2,1)S(1)}, bf16[1,16,2688]{2,1,0:T(8,128)(2,1)S(1)}, u32[]{:S(2)}, u32[]{:S(2)}) collective-permute-start(bf16[1,16,2688]{2,1,0:T(8,128)(2,1)S(1)} %add_convert_fusion.18), channel_id=1, source_target_pairs={{0,24},{1,25},{2,26},{3,27},{4,28},{5,29},{6,30},{7,31},{8,16},{9,... | collective-permute-start | bytes 258056 | tf_op jit(solution)/shard_map/ppermute | solution.py:916
  145.7 2.1 %collective-permute-done.22 = bf16[1,16,2688]{2,1,0:T(8,128)(2,1)S(1)} collective-permute-done((bf16[1,16,2688]{2,1,0:T(8,128)(2,1)S(1)}, bf16[1,16,2688]{2,1,0:T(8,128)(2,1)S(1)}, u32[]{:S(2)}, u32[]{:S(2)}) %collective-permute-start.22) | collective-permute-done | bytes 86048 | tf_op jit(solution)/shard_map/ppermute | solution.py:916
  147.8 3.1 %collective-permute-done.21 = bf16[1,16,2688]{2,1,0:T(8,128)(2,1)S(1)} collective-permute-done((bf16[1,16,2688]{2,1,0:T(8,128)(2,1)S(1)}, bf16[1,16,2688]{2,1,0:T(8,128)(2,1)S(1)}, u32[]{:S(2)}, u32[]{:S(2)}) %collective-permute-start.21) | collective-permute-done | bytes 86048 | tf_op jit(solution)/shard_map/ppermute | solution.py:916
  152.7 1.9 %collective-permute-start.31 = (bf16[4,16,2688]{2,1,0:T(8,128)(2,1)S(1)}, bf16[4,16,2688]{2,1,0:T(8,128)(2,1)S(1)}, u32[]{:S(2)}, u32[]{:S(2)}) collective-permute-start(bf16[4,16,2688]{2,1,0:T(8,128)(2,1)S(1)} %pad_maximum_fusion.1.refs_1_), channel_id=1, source_target_pairs={{0,5},{1,4},{2,7},{3,6},{4,1},{5,0},{6,3},{7,2},{8,13},{9,12},{10,... | collective-permute-start | bytes 1032200 | tf_op jit(solution)/shard_map/ppermute | solution.py:916
  154.5 8.3 %layer_output.1 = f32[2048,512]{1,0:T(8,128)} custom-call(f32[2048,512]{1,0:T(8,128)S(1)} %copy-done.8, bf16[2048,512]{1,0:T(8,128)(2,1)} %get-tuple-element.211.refs_0_, bf16[2048,512]{1,0:T(8,128)(2,1)} %get-tuple-element.212.refs_1_, bf16[2048,512]{1,0:T(8,128)(2,1)} %get-tuple-element.213.refs_2_, bf16[2048,512]{1,0:T(8,128)(2,1)} %get-tuple-element.214.refs_3_, ...), custom_call_target="tpu_custom_call" | custom-call | flops 9200000000 | tf_op jit(solution)/shard_map/layer_output/pallas_call | solution.py:670
  163.5 3.3 %finish_feed.1 = (f32[512,1024]{1,0:T(8,128)}, f32[1024,512]{1,0:T(8,128)}) custom-call(s32[4]{0:T(128)S(1)} %pad_add_fusion.refs_1_.refs_0_, bf16[4,128,512]{2,1,0:T(8,128)(2,1)S(1)} %pad_maximum_fusion.refs_1_, bf16[4,128,512]{2,1,0:T(8,128)(2,1)S(1)} %collective-permute-done.27.refs_2_, bf16[4,128,512]{2,1,0:T(8,128)(2,1)S(1)} %collective-permute-done.28.refs_3_, ...), custom_call_target="tpu_custom_call" | custom-call | flops 3449999872 | tf_op jit(solution)/shard_map/finish_feed/pallas_call | solution.py:840
  166.8 2.5 %collective-permute-done.31.refs_4_ = bf16[4,16,2688]{2,1,0:T(8,128)(2,1)S(1)} collective-permute-done((bf16[4,16,2688]{2,1,0:T(8,128)(2,1)S(1)}, bf16[4,16,2688]{2,1,0:T(8,128)(2,1)S(1)}, u32[]{:S(2)}, u32[]{:S(2)}) %collective-permute-start.31) | collective-permute-done | bytes 344096 | tf_op jit(solution)/shard_map/ppermute | solution.py:916
  172.0 4.5 %finish.1 = (f32[512,512]{1,0:T(8,128)}, f32[512,512]{1,0:T(8,128)}, f32[512,512]{1,0:T(8,128)}, f32[512,512]{1,0:T(8,128)}, f32[512,512]{1,0:T(8,128)}, /*index...) custom-call(s32[4]{0:T(128)S(1)} %pad_add_fusion.refs_1_.refs_0_, ...), custom_call_target="tpu_custom_call" | custom-call | flops 5750000128 | tf_op jit(solution)/shard_map/finish/pallas_call | solution.py:894
  (102 shorter events, 18.6 us)
Async XLA Ops:
  2.4 26.2 %collective-permute-start = (bf16[2,512,512]{2,1,0:T(8,128)(2,1)S(1)}, bf16[2,512,512]{2,1,0:T(8,128)(2,1)S(1)}, u32[]{:S(2)}, u32[]{:S(2)}) collective-permute-start(bf16[2,512,512]{2,1,0:T(8,128)(2,1)S(1)} %pack_weights.1.refs_2_.refs_7_), channel_id=1, source_target_pairs={{0,1},{1,0},{2,3},{3,2},{4,5},{5,4},{6,7},{7,6},{8,9},{9,8},{10,11... | collective-permute-start | bytes 3145736 | tf_op jit(solution)/shard_map/ppermute | solution.py:916
  28.6 9.6 %collective-permute-start.1 = (bf16[2,512,512]{2,1,0:T(8,128)(2,1)S(1)}, bf16[2,512,512]{2,1,0:T(8,128)(2,1)S(1)}, u32[]{:S(2)}, u32[]{:S(2)}) collective-permute-start(bf16[2,512,512]{2,1,0:T(8,128)(2,1)S(1)} %collective-permute-done.refs_3_.refs_4_), channel_id=1, source_target_pairs={{0,2},{1,3},{2,0},{3,1},{4,6},{5,7},{6,4},{7,5},{8,10},{9,11},{10,... | collective-permute-start | bytes 3145736 | tf_op jit(solution)/shard_map/ppermute | solution.py:916
  46.0 9.3 %collective-permute-start.2 = (bf16[8,144,512]{2,1,0:T(8,128)(2,1)S(1)}, bf16[8,144,512]{2,1,0:T(8,128)(2,1)S(1)}, u32[]{:S(2)}, u32[]{:S(2)}) collective-permute-start(bf16[8,144,512]{2,1,0:T(8,128)(2,1)S(1)} %get-tuple-element.136), channel_id=1, source_target_pairs={{0,2},{1,3},{2,0},{3,1},{4,6},{5,7},{6,4},{7,5},{8,10},{9,11},{10,... | collective-permute-start | bytes 3538952 | tf_op jit(solution)/shard_map/ppermute | solution.py:916
  55.2 17.4 %collective-permute-start.5 = (bf16[8,128,512]{2,1,0:T(8,128)(2,1)S(1)}, bf16[8,128,512]{2,1,0:T(8,128)(2,1)S(1)}, u32[]{:S(2)}, u32[]{:S(2)}) collective-permute-start(bf16[8,128,512]{2,1,0:T(8,128)(2,1)S(1)} %get-tuple-element.149), channel_id=1, source_target_pairs={{0,2},{1,3},{2,0},{3,1},{4,6},{5,7},{6,4},{7,5},{8,10},{9,11},{10,... | collective-permute-start | bytes 3145736 | tf_op jit(solution)/shard_map/ppermute | solution.py:916
  55.7 17.7 %collective-permute-start.3 = (bf16[4,144,512]{2,1,0:T(8,128)(2,1)S(1)}, bf16[4,144,512]{2,1,0:T(8,128)(2,1)S(1)}, u32[]{:S(2)}, u32[]{:S(2)}) collective-permute-start(bf16[4,144,512]{2,1,0:T(8,128)(2,1)S(1)} %get-tuple-element.142), channel_id=1, source_target_pairs={{0,4},{1,5},{2,6},{3,7},{4,0},{5,1},{6,2},{7,3},{8,12},{9,13},{10,... | collective-permute-start | bytes 1769480 | tf_op jit(solution)/shard_map/ppermute | solution.py:916
  73.0 14.1 %collective-permute-start.9 = (bf16[4,128,512]{2,1,0:T(8,128)(2,1)S(1)}, bf16[4,128,512]{2,1,0:T(8,128)(2,1)S(1)}, u32[]{:S(2)}, u32[]{:S(2)}) collective-permute-start(bf16[4,128,512]{2,1,0:T(8,128)(2,1)S(1)} %get-tuple-element.165), channel_id=1, source_target_pairs={{0,4},{1,5},{2,6},{3,7},{4,0},{5,1},{6,2},{7,3},{8,12},{9,13},{10,... | collective-permute-start | bytes 1572872 | tf_op jit(solution)/shard_map/ppermute | solution.py:916
  73.5 18.0 %collective-permute-start.7 = (bf16[1,144,512]{2,1,0:T(8,128)(2,1)S(1)}, bf16[1,144,512]{2,1,0:T(8,128)(2,1)S(1)}, u32[]{:S(2)}, u32[]{:S(2)}) collective-permute-start(bf16[1,144,512]{2,1,0:T(8,128)(2,1)S(1)} %get-tuple-element.160), channel_id=1, source_target_pairs={{0,24},{1,25},{2,26},{3,27},{4,28},{5,29},{6,30},{7,31},{8,16},{9,... | collective-permute-start | bytes 442376 | tf_op jit(solution)/shard_map/ppermute | solution.py:916
  77.4 14.3 %collective-permute-start.6 = (bf16[1,144,512]{2,1,0:T(8,128)(2,1)S(1)}, bf16[1,144,512]{2,1,0:T(8,128)(2,1)S(1)}, u32[]{:S(2)}, u32[]{:S(2)}) collective-permute-start(bf16[1,144,512]{2,1,0:T(8,128)(2,1)S(1)} %get-tuple-element.158), channel_id=1, source_target_pairs={{0,16},{1,17},{2,18},{3,19},{4,20},{5,21},{6,22},{7,23},{8,24},{9,... | collective-permute-start | bytes 442376 | tf_op jit(solution)/shard_map/ppermute | solution.py:916
  77.4 14.3 %collective-permute-start.4 = (bf16[1,144,512]{2,1,0:T(8,128)(2,1)S(1)}, bf16[1,144,512]{2,1,0:T(8,128)(2,1)S(1)}, u32[]{:S(2)}, u32[]{:S(2)}) collective-permute-start(bf16[1,144,512]{2,1,0:T(8,128)(2,1)S(1)} %get-tuple-element.148), channel_id=1, source_target_pairs={{0,8},{1,9},{2,10},{3,11},{4,12},{5,13},{6,14},{7,15},{8,0},{9,1},... | collective-permute-start | bytes 442376 | tf_op jit(solution)/shard_map/ppermute | solution.py:916
  87.2 14.1 %collective-permute-start.10 = (bf16[1,128,512]{2,1,0:T(8,128)(2,1)S(1)}, bf16[1,128,512]{2,1,0:T(8,128)(2,1)S(1)}, u32[]{:S(2)}, u32[]{:S(2)}) collective-permute-start(bf16[1,128,512]{2,1,0:T(8,128)(2,1)S(1)} %get-tuple-element.167), channel_id=1, source_target_pairs={{0,8},{1,9},{2,10},{3,11},{4,12},{5,13},{6,14},{7,15},{8,0},{9,1},... | collective-permute-start | bytes 393224 | tf_op jit(solution)/shard_map/ppermute | solution.py:916
  88.9 12.5 %collective-permute-start.11 = (bf16[1,128,512]{2,1,0:T(8,128)(2,1)S(1)}, bf16[1,128,512]{2,1,0:T(8,128)(2,1)S(1)}, u32[]{:S(2)}, u32[]{:S(2)}) collective-permute-start(bf16[1,128,512]{2,1,0:T(8,128)(2,1)S(1)} %get-tuple-element.168), channel_id=1, source_target_pairs={{0,16},{1,17},{2,18},{3,19},{4,20},{5,21},{6,22},{7,23},{8,24},{9,... | collective-permute-start | bytes 393224 | tf_op jit(solution)/shard_map/ppermute | solution.py:916
  91.5 9.1 %collective-permute-start.12 = (bf16[1,128,512]{2,1,0:T(8,128)(2,1)S(1)}, bf16[1,128,512]{2,1,0:T(8,128)(2,1)S(1)}, u32[]{:S(2)}, u32[]{:S(2)}) collective-permute-start(bf16[1,128,512]{2,1,0:T(8,128)(2,1)S(1)} %get-tuple-element.169), channel_id=1, source_target_pairs={{0,24},{1,25},{2,26},{3,27},{4,28},{5,29},{6,30},{7,31},{8,16},{9,... | collective-permute-start | bytes 393224 | tf_op jit(solution)/shard_map/ppermute | solution.py:916
  91.8 9.5 %collective-permute-start.8 = (bf16[1,144,512]{2,1,0:T(8,128)(2,1)S(1)}, bf16[1,144,512]{2,1,0:T(8,128)(2,1)S(1)}, u32[]{:S(2)}, u32[]{:S(2)}) collective-permute-start(bf16[1,144,512]{2,1,0:T(8,128)(2,1)S(1)} %add_convert_fusion.8), channel_id=1, source_target_pairs={{0,1},{1,0},{2,3},{3,2},{4,5},{5,4},{6,7},{7,6},{8,9},{9,8},{10,11... | collective-permute-start | bytes 442376 | tf_op jit(solution)/shard_map/ppermute | solution.py:916
  107.8 8.3 %collective-permute-start.26 = (bf16[1,128,512]{2,1,0:T(8,128)(2,1)S(1)}, bf16[1,128,512]{2,1,0:T(8,128)(2,1)S(1)}, u32[]{:S(2)}, u32[]{:S(2)}) collective-permute-start(bf16[1,128,512]{2,1,0:T(8,128)(2,1)S(1)} %add_convert_fusion.13), channel_id=1, source_target_pairs={{0,24},{1,25},{2,26},{3,27},{4,28},{5,29},{6,30},{7,31},{8,16},{9,... | collective-permute-start | bytes 393224 | tf_op jit(solution)/shard_map/ppermute | solution.py:916
  110.7 16.7 %collective-permute-start.25 = (bf16[1,128,512]{2,1,0:T(8,128)(2,1)S(1)}, bf16[1,128,512]{2,1,0:T(8,128)(2,1)S(1)}, u32[]{:S(2)}, u32[]{:S(2)}) collective-permute-start(bf16[1,128,512]{2,1,0:T(8,128)(2,1)S(1)} %add_convert_fusion.13), channel_id=1, source_target_pairs={{0,16},{1,17},{2,18},{3,19},{4,20},{5,21},{6,22},{7,23},{8,24},{9,... | collective-permute-start | bytes 393224 | tf_op jit(solution)/shard_map/ppermute | solution.py:916
  111.3 16.1 %collective-permute-start.24 = (bf16[1,128,512]{2,1,0:T(8,128)(2,1)S(1)}, bf16[1,128,512]{2,1,0:T(8,128)(2,1)S(1)}, u32[]{:S(2)}, u32[]{:S(2)}) collective-permute-start(bf16[1,128,512]{2,1,0:T(8,128)(2,1)S(1)} %add_convert_fusion.13), channel_id=1, source_target_pairs={{0,8},{1,9},{2,10},{3,11},{4,12},{5,13},{6,14},{7,15},{8,0},{9,1},... | collective-permute-start | bytes 393224 | tf_op jit(solution)/shard_map/ppermute | solution.py:916
  112.6 18.2 %collective-permute-start.14 = (bf16[4,16,2688]{2,1,0:T(8,128)(2,1)S(1)}, bf16[4,16,2688]{2,1,0:T(8,128)(2,1)S(1)}, u32[]{:S(2)}, u32[]{:S(2)}) collective-permute-start(bf16[4,16,2688]{2,1,0:T(8,128)(2,1)S(1)} %get-tuple-element.192), channel_id=1, source_target_pairs={{0,1},{1,0},{2,3},{3,2},{4,5},{5,4},{6,7},{7,6},{8,9},{9,8},{10,11... | collective-permute-start | bytes 1032200 | tf_op jit(solution)/shard_map/ppermute | solution.py:916
  114.2 16.6 %collective-permute-start.15 = (bf16[4,16,2688]{2,1,0:T(8,128)(2,1)S(1)}, bf16[4,16,2688]{2,1,0:T(8,128)(2,1)S(1)}, u32[]{:S(2)}, u32[]{:S(2)}) collective-permute-start(bf16[4,16,2688]{2,1,0:T(8,128)(2,1)S(1)} %get-tuple-element.193), channel_id=1, source_target_pairs={{0,4},{1,5},{2,6},{3,7},{4,0},{5,1},{6,2},{7,3},{8,12},{9,13},{10,... | collective-permute-start | bytes 1032200 | tf_op jit(solution)/shard_map/ppermute | solution.py:916
  116.0 14.7 %collective-permute-start.16 = (bf16[4,16,2688]{2,1,0:T(8,128)(2,1)S(1)}, bf16[4,16,2688]{2,1,0:T(8,128)(2,1)S(1)}, u32[]{:S(2)}, u32[]{:S(2)}) collective-permute-start(bf16[4,16,2688]{2,1,0:T(8,128)(2,1)S(1)} %get-tuple-element.194), channel_id=1, source_target_pairs={{0,5},{1,4},{2,7},{3,6},{4,1},{5,0},{6,3},{7,2},{8,13},{9,12},{10,... | collective-permute-start | bytes 1032200 | tf_op jit(solution)/shard_map/ppermute | solution.py:916
  130.9 7.2 %collective-permute-start.19 = (bf16[1,16,2688]{2,1,0:T(8,128)(2,1)S(1)}, bf16[1,16,2688]{2,1,0:T(8,128)(2,1)S(1)}, u32[]{:S(2)}, u32[]{:S(2)}) collective-permute-start(bf16[1,16,2688]{2,1,0:T(8,128)(2,1)S(1)} %get-tuple-element.204), channel_id=1, source_target_pairs={{0,24},{1,25},{2,26},{3,27},{4,28},{5,29},{6,30},{7,31},{8,16},{9,... | collective-permute-start | bytes 258056 | tf_op jit(solution)/shard_map/ppermute | solution.py:916
  133.9 7.3 %collective-permute-start.18 = (bf16[1,16,2688]{2,1,0:T(8,128)(2,1)S(1)}, bf16[1,16,2688]{2,1,0:T(8,128)(2,1)S(1)}, u32[]{:S(2)}, u32[]{:S(2)}) collective-permute-start(bf16[1,16,2688]{2,1,0:T(8,128)(2,1)S(1)} %get-tuple-element.202), channel_id=1, source_target_pairs={{0,16},{1,17},{2,18},{3,19},{4,20},{5,21},{6,22},{7,23},{8,24},{9,... | collective-permute-start | bytes 258056 | tf_op jit(solution)/shard_map/ppermute | solution.py:916
  134.7 6.4 %collective-permute-start.17 = (bf16[1,16,2688]{2,1,0:T(8,128)(2,1)S(1)}, bf16[1,16,2688]{2,1,0:T(8,128)(2,1)S(1)}, u32[]{:S(2)}, u32[]{:S(2)}) collective-permute-start(bf16[1,16,2688]{2,1,0:T(8,128)(2,1)S(1)} %get-tuple-element.200), channel_id=1, source_target_pairs={{0,8},{1,9},{2,10},{3,11},{4,12},{5,13},{6,14},{7,15},{8,0},{9,1},... | collective-permute-start | bytes 258056 | tf_op jit(solution)/shard_map/ppermute | solution.py:916
  135.4 19.1 %collective-permute-start.27 = (bf16[4,128,512]{2,1,0:T(8,128)(2,1)S(1)}, bf16[4,128,512]{2,1,0:T(8,128)(2,1)S(1)}, u32[]{:S(2)}, u32[]{:S(2)}) collective-permute-start(bf16[4,128,512]{2,1,0:T(8,128)(2,1)S(1)} %pad_maximum_fusion.refs_1_), channel_id=1, source_target_pairs={{0,4},{1,5},{2,6},{3,7},{4,0},{5,1},{6,2},{7,3},{8,12},{9,13},{10,... | collective-permute-start | bytes 1572872 | tf_op jit(solution)/shard_map/ppermute | solution.py:916
  141.2 6.6 %collective-permute-start.22 = (bf16[1,16,2688]{2,1,0:T(8,128)(2,1)S(1)}, bf16[1,16,2688]{2,1,0:T(8,128)(2,1)S(1)}, u32[]{:S(2)}, u32[]{:S(2)}) collective-permute-start(bf16[1,16,2688]{2,1,0:T(8,128)(2,1)S(1)} %add_convert_fusion.18), channel_id=1, source_target_pairs={{0,24},{1,25},{2,26},{3,27},{4,28},{5,29},{6,30},{7,31},{8,16},{9,... | collective-permute-start | bytes 258056 | tf_op jit(solution)/shard_map/ppermute | solution.py:916
  144.2 6.7 %collective-permute-start.21 = (bf16[1,16,2688]{2,1,0:T(8,128)(2,1)S(1)}, bf16[1,16,2688]{2,1,0:T(8,128)(2,1)S(1)}, u32[]{:S(2)}, u32[]{:S(2)}) collective-permute-start(bf16[1,16,2688]{2,1,0:T(8,128)(2,1)S(1)} %add_convert_fusion.18), channel_id=1, source_target_pairs={{0,16},{1,17},{2,18},{3,19},{4,20},{5,21},{6,22},{7,23},{8,24},{9,... | collective-permute-start | bytes 258056 | tf_op jit(solution)/shard_map/ppermute | solution.py:916
  144.2 6.7 %collective-permute-start.20 = (bf16[1,16,2688]{2,1,0:T(8,128)(2,1)S(1)}, bf16[1,16,2688]{2,1,0:T(8,128)(2,1)S(1)}, u32[]{:S(2)}, u32[]{:S(2)}) collective-permute-start(bf16[1,16,2688]{2,1,0:T(8,128)(2,1)S(1)} %add_convert_fusion.18), channel_id=1, source_target_pairs={{0,8},{1,9},{2,10},{3,11},{4,12},{5,13},{6,14},{7,15},{8,0},{9,1},... | collective-permute-start | bytes 258056 | tf_op jit(solution)/shard_map/ppermute | solution.py:916
  145.7 17.2 %collective-permute-start.28 = (bf16[4,128,512]{2,1,0:T(8,128)(2,1)S(1)}, bf16[4,128,512]{2,1,0:T(8,128)(2,1)S(1)}, u32[]{:S(2)}, u32[]{:S(2)}) collective-permute-start(bf16[4,128,512]{2,1,0:T(8,128)(2,1)S(1)} %pad_maximum_fusion.refs_1_), channel_id=1, source_target_pairs={{0,2},{1,3},{2,0},{3,1},{4,6},{5,7},{6,4},{7,5},{8,10},{9,11},{10,... | collective-permute-start | bytes 1572872 | tf_op jit(solution)/shard_map/ppermute | solution.py:916
  151.0 15.8 %collective-permute-start.23 = (bf16[4,16,2688]{2,1,0:T(8,128)(2,1)S(1)}, bf16[4,16,2688]{2,1,0:T(8,128)(2,1)S(1)}, u32[]{:S(2)}, u32[]{:S(2)}) collective-permute-start(bf16[4,16,2688]{2,1,0:T(8,128)(2,1)S(1)} %pad_maximum_fusion.1.refs_1_), channel_id=1, source_target_pairs={{0,1},{1,0},{2,3},{3,2},{4,5},{5,4},{6,7},{7,6},{8,9},{9,8},{10,11... | collective-permute-start | bytes 1032200 | tf_op jit(solution)/shard_map/ppermute | solution.py:916
  151.6 15.2 %collective-permute-start.30 = (bf16[4,16,2688]{2,1,0:T(8,128)(2,1)S(1)}, bf16[4,16,2688]{2,1,0:T(8,128)(2,1)S(1)}, u32[]{:S(2)}, u32[]{:S(2)}) collective-permute-start(bf16[4,16,2688]{2,1,0:T(8,128)(2,1)S(1)} %pad_maximum_fusion.1.refs_1_), channel_id=1, source_target_pairs={{0,4},{1,5},{2,6},{3,7},{4,0},{5,1},{6,2},{7,3},{8,12},{9,13},{10,... | collective-permute-start | bytes 1032200 | tf_op jit(solution)/shard_map/ppermute | solution.py:916
  152.7 16.7 %collective-permute-start.31 = (bf16[4,16,2688]{2,1,0:T(8,128)(2,1)S(1)}, bf16[4,16,2688]{2,1,0:T(8,128)(2,1)S(1)}, u32[]{:S(2)}, u32[]{:S(2)}) collective-permute-start(bf16[4,16,2688]{2,1,0:T(8,128)(2,1)S(1)} %pad_maximum_fusion.1.refs_1_), channel_id=1, source_target_pairs={{0,5},{1,4},{2,7},{3,6},{4,1},{5,0},{6,3},{7,2},{8,13},{9,12},{10,... | collective-permute-start | bytes 1032200 | tf_op jit(solution)/shard_map/ppermute | solution.py:916
  154.5 8.9 %collective-permute-start.29 = (bf16[4,128,512]{2,1,0:T(8,128)(2,1)S(1)}, bf16[4,128,512]{2,1,0:T(8,128)(2,1)S(1)}, u32[]{:S(2)}, u32[]{:S(2)}) collective-permute-start(bf16[4,128,512]{2,1,0:T(8,128)(2,1)S(1)} %collective-permute-done.27.refs_2_), channel_id=1, source_target_pairs={{0,2},{1,3},{2,0},{3,1},{4,6},{5,7},{6,4},{7,5},{8,10},{9,11},{10,... | collective-permute-start | bytes 1572872 | tf_op jit(solution)/shard_map/ppermute | solution.py:916
  162.9 6.9 %collective-permute-start.32 = (bf16[4,16,2688]{2,1,0:T(8,128)(2,1)S(1)}, bf16[4,16,2688]{2,1,0:T(8,128)(2,1)S(1)}, u32[]{:S(2)}, u32[]{:S(2)}) collective-permute-start(bf16[4,16,2688]{2,1,0:T(8,128)(2,1)S(1)} %pad_maximum_fusion.1.refs_1_), channel_id=1, source_target_pairs={{0,2},{1,3},{2,0},{3,1},{4,6},{5,7},{6,4},{7,5},{8,10},{9,11},{10,... | collective-permute-start | bytes 1032200 | tf_op jit(solution)/shard_map/ppermute | solution.py:916
  (20 other events, 172.1 us)

commit v6 on v5

--- a/solution.py
+++ b/solution.py
@@ -679,72 +679,123 @@
     )(near(second), *[far(array) for array in hidden], *[near(array) for array in weights])
 
 
-def head_kernel(*refs, count):
-    where_ref, pen_ref, act_ref = refs[:3]
-    groups = [refs[3 + 4 * g : 7 + 4 * g] for g in range(count)]
-    share_ref, log_ref, sum_ref, w_ref, perm_ref, mask_ref, out_ref, tally_ref = refs[3 + 4 * count : 11 + 4 * count]
-    piece_ref, gsum_ref, total_ref, glog_ref, acc_ref = refs[11 + 4 * count :]
+def plans_back(grad, share_ref, span, first):
+    for level in range(2 * ITERS - 1, -1, -1):
+        if level % 2:
+            total = jnp.sum(grad, axis=0, keepdims=True)
+        else:
+            total = segment_sum(grad, first)
+        grad = grad - share_ref[level, :, span] * total
+    return grad
+
+
+def first_heads_kernel(
+    where_ref, act_ref, gq_ref, gk_ref, gv_ref, out_ref, gch_ref, share_ref, log_ref, perm_ref, mask_ref,
+    piece_ref, chosen_part_ref, penalty_part_ref, acc_ref,
+):
+    blocks = log_ref.shape[0]
+    wide = 2 * blocks
+    first, position = lane_tiles(blocks)
+    hot = position == down_rows(perm_ref[...], wide)
+    real = down_rows(mask_ref[...], wide)
+    for pair in range(gch_ref.shape[1] // wide):
+        span = slice(pair * wide, (pair + 1) * wide)
+        plan = share_ref[2 * ITERS - 1, :, span]
+        gch = segment_sum(gch_ref[:, span], first)
+        chosen_part_ref[:, span] = plans_back(plan * jnp.where(hot, blocks * gch, 0.0), share_ref, span, first)
+        penalty_part_ref[:, span] = plans_back(plan * real * (log_ref[:, span] + 1.0), share_ref, span, first)
+    act = act_ref[...]
+    cols = acc_ref.shape[1]
+    for index, ref in enumerate((gq_ref, gk_ref, gv_ref)):
+        acc_ref[...] = dot_tn(act, ref[...])
+        spread(piece_ref, acc_ref, where_ref[2], slice(index * cols, (index + 1) * cols))
+    piece_ref[:, :, 3 * cols :] = out_ref[...]
+
+
+def first_heads(where, act, group, out_piece, shares, plan_log, perm_row, mask_row, chunks):
+    width = act.shape[1]
+    blocks = plan_log.shape[0]
+    cols = group[0].shape[1]
+    vmem = pl.BlockSpec(memory_space=pltpu.VMEM)
+    return pl.pallas_call(
+        first_heads_kernel,
+        in_specs=[pl.BlockSpec(memory_space=pltpu.SMEM)] + [vmem] * 10,
+        out_specs=[vmem] * 3,
+        out_shape=[near_shape((chunks, width // chunks, 3 * cols + out_piece.shape[2]), BF16)]
+        + [near_shape((blocks, cols), F32)] * 2,
+        scratch_shapes=[pltpu.VMEM((width, cols), F32)],
+        compiler_params=params(12),
+        cost_estimate=cost(3),
+        name="first_heads",
+    )(
+        where, near(act), *[near(array) for array in group[:3]], near(out_piece), near(group[3]), near(shares),
+        near(plan_log), perm_row, mask_row,
+    )
+
+
+def last_heads_kernel(
+    where_ref, pen_ref, act_ref, gq_ref, gk_ref, gv_ref, gch_ref,
+    first_ref, chosen_part_ref, penalty_part_ref, share_ref, log_ref, sum_ref, w_ref, perm_ref, mask_ref, tally_ref,
+    piece_ref, gsum_ref, total_ref, glog_ref, acc_ref,
+):
+    blocks, width = sum_ref.shape
+    cols = acc_ref.shape[1]
+    wide = 2 * blocks
     block_total = jnp.sum(tally_ref[...].astype(F32), axis=1, keepdims=True)
     block_total = jnp.sum(block_total, axis=0, keepdims=True)
     total_ref[...] = jnp.broadcast_to(block_total, total_ref.shape)
     coef = pen_ref[0] / (HEADS * block_total)
-    blocks, width = sum_ref.shape
-    cols = acc_ref.shape[1]
-    wide = 2 * blocks
     first, position = lane_tiles(blocks)
     hot = position == down_rows(perm_ref[...], wide)
     weight = coef * down_rows(mask_ref[...], wide)
     act = act_ref[...]
-    for g, group in enumerate(groups):
-        for index in range(3):
-            acc_ref[...] = dot_tn(act, group[index][...])
-            at = index * width + g * cols
-            spread(piece_ref, acc_ref, where_ref[2], slice(at, at + cols))
-        for pair in range(cols // wide):
-            at = g * cols + pair * wide
-            span = slice(at, at + wide)
-            plan = share_ref[2 * ITERS - 1, :, span]
-            gch = segment_sum(group[3][:, pair * wide : (pair + 1) * wide], first)
-            grad = plan * (jnp.where(hot, blocks * gch, 0.0) - weight * (log_ref[:, span] + 1.0))
-            for level in range(2 * ITERS - 1, -1, -1):
-                if level % 2:
-                    total = jnp.sum(grad, axis=0, keepdims=True)
-                else:
-                    total = segment_sum(grad, first)
-                grad = grad - share_ref[level, :, span] * total
-            glog_ref[:, span] = grad
-    for g in range(count):
+    start = first_ref.shape[2]
+    piece_ref[:, :, :start] = first_ref[...]
+    for index, ref in enumerate((gq_ref, gk_ref, gv_ref)):
+        acc_ref[...] = dot_tn(act, ref[...])
+        spread(piece_ref, acc_ref, where_ref[2], slice(start + index * cols, start + (index + 1) * cols))
+    glog_ref[:, :cols] = chosen_part_ref[...] - coef * penalty_part_ref[...]
+    for pair in range(cols // wide):
+        span = slice(cols + pair * wide, cols + (pair + 1) * wide)
+        plan = share_ref[2 * ITERS - 1, :, span]
+        gch = segment_sum(gch_ref[:, pair * wide : (pair + 1) * wide], first)
+        grad = plan * (jnp.where(hot, blocks * gch, 0.0) - weight * (log_ref[:, span] + 1.0))
+        glog_ref[:, span] = plans_back(grad, share_ref, span, first)
+    for g in range(2):
         at = slice(g * cols, (g + 1) * cols)
         acc_ref[...] = lax.dot_general(
             sum_ref[...], glog_ref[:, at], TN, precision=HIGHEST, preferred_element_type=F32
         )
-        spread(piece_ref, acc_ref, where_ref[2], slice(3 * width + g * cols, 3 * width + (g + 1) * cols))
+        spread(piece_ref, acc_ref, where_ref[2], slice(start + (3 + g) * cols, start + (4 + g) * cols))
     gsum_ref[...] = lax.dot_general(glog_ref[...], w_ref[...], NT, precision=HIGHEST, preferred_element_type=F32)
-    piece_ref[:, :, 4 * width :] = out_ref[...]
-
-
-def head_grads(
-    where, pen_weight, act, groups, shares, plan_log, sums, w_sort, perm_row, mask_row, out_piece, tallies, chunks
+
+
+def last_heads(
+    where, pen_weight, act, group, first, shares, plan_log, sums, w_sort, perm_row, mask_row, tallies, chunks
 ):
-    rows, width = act.shape
+    width = act.shape[1]
     blocks = sums.shape[0]
-    cols = groups[0][0].shape[1]
+    cols = group[0].shape[1]
     smem = pl.BlockSpec(memory_space=pltpu.SMEM)
     vmem = pl.BlockSpec(memory_space=pltpu.VMEM)
-    flat = [near(array) for group in groups for array in group]
-    piece = (chunks, width // chunks, 4 * width + out_piece.shape[2])
+    gq, gk, gv, gch = group
     return pl.pallas_call(
-        functools.partial(head_kernel, count=len(groups)),
-        in_specs=[smem] * 2 + [vmem] * (9 + len(flat)),
+        last_heads_kernel,
+        in_specs=[smem] * 2 + [vmem] * 15,
         out_specs=[vmem] * 3,
-        out_shape=[near_shape(piece, BF16), near_shape((blocks, width), F32), near_shape((1, LANES), F32)],
+        out_shape=[
+            near_shape((chunks, width // chunks, first[0].shape[2] + 5 * cols), BF16),
+            near_shape((blocks, width), F32),
+            near_shape((1, LANES), F32),
+        ],
         scratch_shapes=[pltpu.VMEM((blocks, width), F32), pltpu.VMEM((width, cols), F32)],
         compiler_params=params(14),
-        cost_estimate=cost(6),
-        name="head_grads",
+        cost_estimate=cost(5),
+        name="last_heads",
     )(
-        where, pen_weight, near(act), *flat, near(shares), near(plan_log), near(sums), near(w_sort), perm_row, mask_row,
-        near(out_piece), tallies,
+        where, pen_weight, near(act), near(gq), near(gk), near(gv), near(gch),
+        *[near(array) for array in first], near(shares),
+        near(plan_log), near(sums), near(w_sort), perm_row, mask_row, tallies,
     )
 
 
@@ -861,13 +912,19 @@
     some, size = parts[0].shape[:2]
     total = jnp.zeros((width, LANES), F32)
     copies = []
+    cols = width // 2
+    second_at = 3 * cols + width + LANES
+    spans = [[(n * cols, 0, cols), (second_at + n * cols, cols, cols)] for n in range(3)]
+    spans = spans + [[(second_at + 3 * cols, 0, width)], [(3 * cols, 0, width)]]
     for index, near_ref in enumerate(nears):
         for n, part_ref in enumerate(parts):
             for r in range(some):
                 rows = pl.ds(pl.multiple_of(((n * some + r) ^ where_ref[2]) * size, size), size)
-                near_ref[rows, :] = part_ref[r, :, index * width : (index + 1) * width].astype(F32)
+                for source, target, count in spans[index]:
+                    near_ref[rows, target : target + count] = part_ref[r, :, source : source + count].astype(F32)
                 if index == 0:
-                    two_ref[rows, :] = part_ref[r, :, 5 * width :].astype(F32)
+                    at = 3 * cols + width
+                    two_ref[rows, :] = part_ref[r, :, at : at + LANES].astype(F32)
         copies.append(pltpu.make_async_copy(near_ref, fars[index], sems.at[index]))
         copies[-1].start()
     for at in range(0, width, LANES):
@@ -1056,7 +1113,13 @@
     own = Walk([piece, plan.after(arrived)], FEED_STEPS)
     plan.launch(own.reduce(plan), other.reduce(plan))
     groups = [attend_back(plan.enter(perm), q, grad_att, probs, k, v, chosen, 0)]
+    held, plan.pending = plan.pending, []
     plan.leave(groups[0][3])
+    firsts = first_heads(
+        plan.enter(where), act_one, groups[0], out_piece, shares, plan_log, perm_row, mask_row, out_chunks
+    )
+    plan.leave(firsts[0])
+    plan.pending.extend(held)
 
     other_sum = other.reduced(plan)
     crossed = swap(plan.after(other_sum), MP)
@@ -1072,9 +1135,9 @@
     own.pieces.append(crossed[:, :rows_fed])
     value = own.reduced(plan)
     plan.pending.append(value)
-    piece, gsum, block_total = head_grads(
-        plan.enter(where), pen_weight, act_one, groups, shares, plan_log, sums, w_sort, perm_row, mask_row, out_piece,
-        tallies, out_chunks,
+    piece, gsum, block_total = last_heads(
+        plan.enter(where), pen_weight, act_one, groups[1], firsts, shares, plan_log, sums, w_sort,
+        perm_row, mask_row, tallies, out_chunks,
     )
     plan.leave(gsum)
 
@@ -1165,8 +1228,10 @@
     groups = [
         attend_back(perm, q, grad_att, probs, k, v, chosen, group) for group in range(width // GROUP_WIDTH)
     ]
-    piece, gsum, block_total = head_grads(
-        where, pen_weight, act_one, groups, shares, plan_log, sums, w_sort, perm_row, mask_row, extra, tallies, 1
+    firsts = first_heads(where, act_one, groups[0], extra, shares, plan_log, perm_row, mask_row, 1)
+    piece, gsum, block_total = last_heads(
+        where, pen_weight, act_one, groups[1], firsts, shares, plan_log, sums, w_sort, perm_row, mask_row,
+        tallies, 1,
     )
     grad_input = input_grad(
         [group[:3] for group in groups], gsum, x, grad_second, gain_one_row, w_query, w_key, w_value

time: 177 us -> 177 us (level)
    pallas_call x1 -> x2, Pallas kernels: 6.07 us -> 7.27 us  [the longest x1 4.27 us: last_heads(): pl.pallas_call(last_heads_kernel, in_specs=[smem] * 2 + [vmem] * 15, out_...]
  transfers between devices with their start and end apart: 36 -> 36, of which waited for: 13 -> 12; matrix products, arithmetic and copies ran while one was open for 1% -> 1% of each run, Pallas kernels for 50% -> 52%
where the time goes in v6:
time: 177 us; the launch traced here: 176 us
  Pallas kernels  110 us (62%)
  starting transfers between devices  39.4 us (22%)
  waiting for transfers between devices  23.2 us (13%)
  between operations  1.9 us (1%)
  other arithmetic  1.83 us (1%)
    pallas_call x4, Pallas kernels, feed_quarter(): pl.pallas_call(functools.partial(quarter_kernel, kind=kind, tile=tile, ta...  40.5 us
    ppermute x36, starting transfers between devices, swap(): lax.ppermute(array, ('batch', 'mp'), [(i, i ^ flip) for i in range(count)])  39.4 us
    ppermute x36, waiting for transfers between devices, swap(): lax.ppermute(array, ('batch', 'mp'), [(i, i ^ flip) for i in range(count)])  23.2 us
    pallas_call x1, Pallas kernels, forward(): pl.pallas_call(functools.partial(forward_kernel, tile=tile), in_specs=[sm...  20.3 us
    pallas_call x2, Pallas kernels, attend_back(): pl.pallas_call(functools.partial(attend_back_kernel, group=group, part=pa...  14.2 us
    pallas_call x1, Pallas kernels, input_grad(): pl.pallas_call(input_kernel, grid=(rows // tile,), in_specs=[rows_of(tile...  9.76 us
    pallas_call x1, Pallas kernels, layer_output(): pl.pallas_call(output_kernel, grid=(rows // tile,), in_specs=[rows_of(til...  8.34 us
    pallas_call x1, Pallas kernels, finish(): pl.pallas_call(finish_kernel, in_specs=[pl.BlockSpec(memory_space=pltpu.S...  4.46 us
  transfers between devices with their start and end apart: 36, of which 12 were waited for; matrix products, arithmetic and copies ran while one was open for 1% of the time, Pallas kernels for 52%

profile of v6, /device:TPU:0, one launch (start us, length us, event | category | flops | bytes accessed | tf_op | source)
XLA Modules:
  0.0 176.3 jit_solution(15208158468531684217)
XLA Ops:
  0.7 1.7 pack_weights.1.refs_2_.refs_7_
  2.4 3.0 %collective-permute-start = (bf16[2,512,512]{2,1,0:T(8,128)(2,1)S(1)}, bf16[2,512,512]{2,1,0:T(8,128)(2,1)S(1)}, u32[]{:S(2)}, u32[]{:S(2)}) collective-permute-start(bf16[2,512,512]{2,1,0:T(8,128)(2,1)S(1)} %pack_weights.1.refs_2_.refs_7_), channel_id=1, source_target_pairs={{0,1},{1,0},{2,3},{3,2},{4,5},{5,4},{6,7},{7,6},{8,9},{9,8},{10,11... | collective-permute-start | bytes 3145736 | tf_op jit(solution)/shard_map/ppermute | solution.py:973
  5.4 20.3 %forward.1 = (bf16[2048,512]{1,0:T(8,128)(2,1)}, bf16[2048,512]{1,0:T(8,128)(2,1)}, bf16[2048,512]{1,0:T(8,128)(2,1)}, bf16[2048,512]{1,0:T(8,128)(2,1)}, bf16[4...) custom-call(s32[64]{0:T(128)S(1)} %bitcast.30, ...), custom_call_target="tpu_custom_call" | custom-call | flops 28750000128 | tf_op jit(solution)/shard_map/forward/pallas_call | solution.py:343
  25.7 2.8 %collective-permute-done.refs_3_.refs_4_ = bf16[2,512,512]{2,1,0:T(8,128)(2,1)S(1)} collective-permute-done((bf16[2,512,512]{2,1,0:T(8,128)(2,1)S(1)}, bf16[2,512,512]{2,1,0:T(8,128)(2,1)S(1)}, u32[]{:S(2)}, u32[]{:S(2)}) %collective-permute-start) | collective-permute-done | bytes 1048608 | tf_op jit(solution)/shard_map/ppermute | solution.py:973
  28.6 9.5 %feed_first.1 = (bf16[2048,512]{1,0:T(8,128)(2,1)}, f32[2048,512]{1,0:T(8,128)S(1)}, bf16[8,144,512]{2,1,0:T(8,128)(2,1)S(1)}, bf16[2048,512]{1,0:T(8,128)(2,1)S(1)}, bf16[2048,512]{1,0:T(8,128)(2,1)S(1)}) custom-call(s32[1,64]{1,0:T(1,128)S(1)} %copy-done.7, s32[4]{0:T(128)S(1)} %pad_add_fusion.refs_1_.refs_0_.where_ref, ...), custom_call_target="tpu_custom_call" | custom-call | flops 10350000128 | tf_op jit(solution)/shard_map/feed_first/pallas_call | solution.py:643
  38.2 7.8 %feed_middle.2 = (bf16[2048,512]{1,0:T(8,128)(2,1)}, f32[2048,512]{1,0:T(8,128)S(1)}, bf16[8,144,512]{2,1,0:T(8,128)(2,1)S(1)}) custom-call(s32[1,64]{1,0:T(1,128)S(1)} %copy-done.7, s32[4]{0:T(128)S(1)} %pad_add_fusion.refs_1_.refs_0_.where_ref, bf16[2048,512]{1,0:T(8,128)(2,1)S(1)} %get-tuple-element.136.refs_2_.refs_1_, ...), custom_call_target="tpu_custom_call" | custom-call | flops 10350000128 | tf_op jit(solution)/shard_map/feed_middle/pallas_call | solution.py:643
  47.2 8.0 %feed_middle.3 = (bf16[2048,512]{1,0:T(8,128)(2,1)}, f32[2048,512]{1,0:T(8,128)S(1)}, bf16[8,128,512]{2,1,0:T(8,128)(2,1)S(1)}) custom-call(s32[4]{0:T(128)S(1)} %pad_add_fusion.refs_1_.refs_0_.where_ref, bf16[2048,512]{1,0:T(8,128)(2,1)S(1)} %get-tuple-element.136.refs_2_.refs_1_, bf16[2,512,512]{2,1,0:T(8,128)(2,1)S(1)} %get-tuple-element.142.refs_2_.refs_6_, ...), custom_call_target="tpu_custom_call" | custom-call | flops 10350000128 | tf_op jit(solution)/shard_map/feed_middle/pallas_call | solution.py:643
  55.7 1.8 %collective-permute-start.3 = (bf16[4,144,512]{2,1,0:T(8,128)(2,1)S(1)}, bf16[4,144,512]{2,1,0:T(8,128)(2,1)S(1)}, u32[]{:S(2)}, u32[]{:S(2)}) collective-permute-start(bf16[4,144,512]{2,1,0:T(8,128)(2,1)S(1)} %get-tuple-element.146), channel_id=1, source_target_pairs={{0,4},{1,5},{2,6},{3,7},{4,0},{5,1},{6,2},{7,3},{8,12},{9,13},{10,... | collective-permute-start | bytes 1769480 | tf_op jit(solution)/shard_map/ppermute | solution.py:973
  57.5 15.1 %feed_last.1 = (bf16[2048,512]{1,0:T(8,128)(2,1)}, f32[2048,512]{1,0:T(8,128)}, bf16[8,128,512]{2,1,0:T(8,128)(2,1)S(1)}, bf16[2048,512]{1,0:T(8,128)(2,1)S(1)}, bf16[32,16,640]{2,1,0:T(8,128)(2,1)S(1)}) custom-call(s32[4]{0:T(128)S(1)} %pad_add_fusion.refs_1_.refs_0_.where_ref, bf16[2048,512]{1,0:T(8,128)(2,1)S(1)} %get-tuple-element.136.refs_2_.refs_1_, ...), custom_call_target="tpu_custom_call" | custom-call | flops 10350000128 | tf_op jit(solution)/shard_map/feed_last/pallas_call | solution.py:643
  73.5 3.9 %collective-permute-start.7 = (bf16[1,144,512]{2,1,0:T(8,128)(2,1)S(1)}, bf16[1,144,512]{2,1,0:T(8,128)(2,1)S(1)}, u32[]{:S(2)}, u32[]{:S(2)}) collective-permute-start(bf16[1,144,512]{2,1,0:T(8,128)(2,1)S(1)} %get-tuple-element.173), channel_id=1, source_target_pairs={{0,24},{1,25},{2,26},{3,27},{4,28},{5,29},{6,30},{7,31},{8,16},{9,... | collective-permute-start | bytes 442376 | tf_op jit(solution)/shard_map/ppermute | solution.py:973
  77.4 7.0 %attend_back.2 = (bf16[2048,256]{1,0:T(8,128)(2,1)S(1)}, bf16[2048,256]{1,0:T(8,128)(2,1)S(1)}, bf16[2048,256]{1,0:T(8,128)(2,1)S(1)}, f32[64,256]{1,0:T(8,128)S(1)}) custom-call(s32[64]{0:T(128)S(1)} %bitcast.31, f32[64,512]{1,0:T(8,128)S(1)} %get-tuple-element.155.chosen_ref, bf16[2048,512]{1,0:T(8,128)(2,1)S(1)} %get-tuple-element.150.gatt_ref, ...), custom_call_target="tpu_custom_call" | custom-call | flops 11500000256 | tf_op jit(solution)/shard_map/attend_back/pallas_call | solution.py:432
  84.5 1.6 collective-permute-start.4
  86.1 3.0 %first_heads.1 = (bf16[32,16,1408]{2,1,0:T(8,128)(2,1)S(1)}, f32[64,256]{1,0:T(8,128)S(1)}, f32[64,256]{1,0:T(8,128)S(1)}) custom-call(s32[4]{0:T(128)S(1)} %pad_add_fusion.refs_1_.refs_0_.where_ref, bf16[2048,512]{1,0:T(8,128)(2,1)S(1)} %copy-done.8, bf16[2048,256]{1,0:T(8,128)(2,1)S(1)} %get-tuple-element.163.gq_ref.refs_0_, ...), custom_call_target="tpu_custom_call" | custom-call | flops 3449999872 | tf_op jit(solution)/shard_map/first_heads/pallas_call | solution.py:720
  89.8 2.8 %collective-permute-start.11 = (bf16[1,128,512]{2,1,0:T(8,128)(2,1)S(1)}, bf16[1,128,512]{2,1,0:T(8,128)(2,1)S(1)}, u32[]{:S(2)}, u32[]{:S(2)}) collective-permute-start(bf16[1,128,512]{2,1,0:T(8,128)(2,1)S(1)} %get-tuple-element.181), channel_id=1, source_target_pairs={{0,16},{1,17},{2,18},{3,19},{4,20},{5,21},{6,22},{7,23},{8,24},{9,... | collective-permute-start | bytes 393224 | tf_op jit(solution)/shard_map/ppermute | solution.py:973
  93.7 1.7 collective-permute-done.4
  95.5 1.6 collective-permute-start.8
  97.1 7.2 %attend_back.3 = (bf16[2048,256]{1,0:T(8,128)(2,1)S(1)}, bf16[2048,256]{1,0:T(8,128)(2,1)S(1)}, bf16[2048,256]{1,0:T(8,128)(2,1)S(1)}, f32[64,256]{1,0:T(8,128)S(1)}) custom-call(s32[64]{0:T(128)S(1)} %bitcast.32, f32[64,512]{1,0:T(8,128)S(1)} %get-tuple-element.155.chosen_ref, bf16[2048,512]{1,0:T(8,128)(2,1)S(1)} %get-tuple-element.150.gatt_ref, ...), custom_call_target="tpu_custom_call" | custom-call | flops 11500000256 | tf_op jit(solution)/shard_map/attend_back/pallas_call | solution.py:432
  104.5 4.3 %last_heads.1 = (bf16[32,16,2688]{2,1,0:T(8,128)(2,1)S(1)}, f32[64,512]{1,0:T(8,128)S(1)}, f32[1,128]{1,0:T(1,128)S(1)}) custom-call(s32[4]{0:T(128)S(1)} %pad_add_fusion.refs_1_.refs_0_.where_ref, f32[1]{0:T(128)S(6)} %copy.30.pen_ref, bf16[2048,512]{1,0:T(8,128)(2,1)S(1)} %copy-done.8, bf16[2048,256]{1,0:T(8,128)(2,1)S(1)} %get-tuple-element.190.gq_ref.refs_3_, ...), custom_call_target="tpu_custom_call" | custom-call | flops 5750000128 | tf_op jit(solution)/shard_map/last_heads/pallas_call | solution.py:782
  111.0 2.4 %collective-permute-start.24 = (bf16[1,128,512]{2,1,0:T(8,128)(2,1)S(1)}, bf16[1,128,512]{2,1,0:T(8,128)(2,1)S(1)}, u32[]{:S(2)}, u32[]{:S(2)}) collective-permute-start(bf16[1,128,512]{2,1,0:T(8,128)(2,1)S(1)} %add_convert_fusion.13), channel_id=1, source_target_pairs={{0,8},{1,9},{2,10},{3,11},{4,12},{5,13},{6,14},{7,15},{8,0},{9,1},... | collective-permute-start | bytes 393224 | tf_op jit(solution)/shard_map/ppermute | solution.py:973
  115.4 1.8 %collective-permute-done.26 = bf16[1,128,512]{2,1,0:T(8,128)(2,1)S(1)} collective-permute-done((bf16[1,128,512]{2,1,0:T(8,128)(2,1)S(1)}, bf16[1,128,512]{2,1,0:T(8,128)(2,1)S(1)}, u32[]{:S(2)}, u32[]{:S(2)}) %collective-permute-start.26) | collective-permute-done | bytes 131104 | tf_op jit(solution)/shard_map/ppermute | solution.py:973
  118.3 9.8 %input_grad.1 = f32[2048,512]{1,0:T(8,128)} custom-call(bf16[2048,256]{1,0:T(8,128)(2,1)S(1)} %get-tuple-element.163.gq_ref.refs_0_, bf16[2048,256]{1,0:T(8,128)(2,1)S(1)} %get-tuple-element.164.gk_ref.refs_1_, bf16[2048,256]{1,0:T(8,128)(2,1)S(1)} %get-tuple-element.165.gv_ref.refs_2_, bf16[2048,256]{1,0:T(8,128)(2,1)S(1)} %get-tuple-element.190.gq_ref.refs_3_, ...), custom_call_target="tpu_custom_call" | custom-call | flops 11500000256 | tf_op jit(solution)/shard_map/input_grad/pallas_call | solution.py:827
  128.1 3.9 %collective-permute-done.16 = bf16[4,16,2688]{2,1,0:T(8,128)(2,1)S(1)} collective-permute-done((bf16[4,16,2688]{2,1,0:T(8,128)(2,1)S(1)}, bf16[4,16,2688]{2,1,0:T(8,128)(2,1)S(1)}, u32[]{:S(2)}, u32[]{:S(2)}) %collective-permute-start.16) | collective-permute-done | bytes 344096 | tf_op jit(solution)/shard_map/ppermute | solution.py:973
  133.2 2.1 %collective-permute-start.18 = (bf16[1,16,2688]{2,1,0:T(8,128)(2,1)S(1)}, bf16[1,16,2688]{2,1,0:T(8,128)(2,1)S(1)}, u32[]{:S(2)}, u32[]{:S(2)}) collective-permute-start(bf16[1,16,2688]{2,1,0:T(8,128)(2,1)S(1)} %get-tuple-element.210), channel_id=1, source_target_pairs={{0,16},{1,17},{2,18},{3,19},{4,20},{5,21},{6,22},{7,23},{8,24},{9,... | collective-permute-start | bytes 258056 | tf_op jit(solution)/shard_map/ppermute | solution.py:973
  139.2 3.0 %collective-permute-done.18 = bf16[1,16,2688]{2,1,0:T(8,128)(2,1)S(1)} collective-permute-done((bf16[1,16,2688]{2,1,0:T(8,128)(2,1)S(1)}, bf16[1,16,2688]{2,1,0:T(8,128)(2,1)S(1)}, u32[]{:S(2)}, u32[]{:S(2)}) %collective-permute-start.18) | collective-permute-done | bytes 86048 | tf_op jit(solution)/shard_map/ppermute | solution.py:973
  143.6 3.2 %collective-permute-start.20 = (bf16[1,16,2688]{2,1,0:T(8,128)(2,1)S(1)}, bf16[1,16,2688]{2,1,0:T(8,128)(2,1)S(1)}, u32[]{:S(2)}, u32[]{:S(2)}) collective-permute-start(bf16[1,16,2688]{2,1,0:T(8,128)(2,1)S(1)} %add_convert_fusion.18), channel_id=1, source_target_pairs={{0,8},{1,9},{2,10},{3,11},{4,12},{5,13},{6,14},{7,15},{8,0},{9,1},... | collective-permute-start | bytes 258056 | tf_op jit(solution)/shard_map/ppermute | solution.py:973
  146.7 3.0 %collective-permute-done.22 = bf16[1,16,2688]{2,1,0:T(8,128)(2,1)S(1)} collective-permute-done((bf16[1,16,2688]{2,1,0:T(8,128)(2,1)S(1)}, bf16[1,16,2688]{2,1,0:T(8,128)(2,1)S(1)}, u32[]{:S(2)}, u32[]{:S(2)}) %collective-permute-start.22) | collective-permute-done | bytes 86048 | tf_op jit(solution)/shard_map/ppermute | solution.py:973
  149.7 1.5 collective-permute-done.21
  152.6 2.2 %collective-permute-start.31 = (bf16[4,16,2688]{2,1,0:T(8,128)(2,1)S(1)}, bf16[4,16,2688]{2,1,0:T(8,128)(2,1)S(1)}, u32[]{:S(2)}, u32[]{:S(2)}) collective-permute-start(bf16[4,16,2688]{2,1,0:T(8,128)(2,1)S(1)} %pad_maximum_fusion.1.refs_1_), channel_id=1, source_target_pairs={{0,5},{1,4},{2,7},{3,6},{4,1},{5,0},{6,3},{7,2},{8,13},{9,12},{10,... | collective-permute-start | bytes 1032200 | tf_op jit(solution)/shard_map/ppermute | solution.py:973
  154.9 8.3 %layer_output.1 = f32[2048,512]{1,0:T(8,128)} custom-call(f32[2048,512]{1,0:T(8,128)S(1)} %copy-done.10, bf16[2048,512]{1,0:T(8,128)(2,1)} %get-tuple-element.219.refs_0_, bf16[2048,512]{1,0:T(8,128)(2,1)} %get-tuple-element.220.refs_1_, bf16[2048,512]{1,0:T(8,128)(2,1)} %get-tuple-element.221.refs_2_, bf16[2048,512]{1,0:T(8,128)(2,1)} %get-tuple-element.222.refs_3_, ...), custom_call_target="tpu_custom_call" | custom-call | flops 9200000000 | tf_op jit(solution)/shard_map/layer_output/pallas_call | solution.py:670
  163.8 3.3 %finish_feed.1 = (f32[512,1024]{1,0:T(8,128)}, f32[1024,512]{1,0:T(8,128)}) custom-call(s32[4]{0:T(128)S(1)} %pad_add_fusion.refs_1_.refs_0_.where_ref, bf16[4,128,512]{2,1,0:T(8,128)(2,1)S(1)} %pad_maximum_fusion.refs_1_, bf16[4,128,512]{2,1,0:T(8,128)(2,1)S(1)} %collective-permute-done.27.refs_2_, ...), custom_call_target="tpu_custom_call" | custom-call | flops 3449999872 | tf_op jit(solution)/shard_map/finish_feed/pallas_call | solution.py:891
  167.1 1.9 %collective-permute-done.31.refs_4_ = bf16[4,16,2688]{2,1,0:T(8,128)(2,1)S(1)} collective-permute-done((bf16[4,16,2688]{2,1,0:T(8,128)(2,1)S(1)}, bf16[4,16,2688]{2,1,0:T(8,128)(2,1)S(1)}, u32[]{:S(2)}, u32[]{:S(2)}) %collective-permute-start.31) | collective-permute-done | bytes 344096 | tf_op jit(solution)/shard_map/ppermute | solution.py:973
  171.7 4.5 %finish.1 = (f32[512,512]{1,0:T(8,128)}, f32[512,512]{1,0:T(8,128)}, f32[512,512]{1,0:T(8,128)}, f32[512,512]{1,0:T(8,128)}, f32[512,512]{1,0:T(8,128)}, /*index...) custom-call(s32[4]{0:T(128)S(1)} %pad_add_fusion.refs_1_.refs_0_.where_ref, ...), custom_call_target="tpu_custom_call" | custom-call | flops 5750000128 | tf_op jit(solution)/shard_map/finish/pallas_call | solution.py:951
  (103 shorter events, 20.5 us)
Async XLA Ops:
  2.4 26.2 %collective-permute-start = (bf16[2,512,512]{2,1,0:T(8,128)(2,1)S(1)}, bf16[2,512,512]{2,1,0:T(8,128)(2,1)S(1)}, u32[]{:S(2)}, u32[]{:S(2)}) collective-permute-start(bf16[2,512,512]{2,1,0:T(8,128)(2,1)S(1)} %pack_weights.1.refs_2_.refs_7_), channel_id=1, source_target_pairs={{0,1},{1,0},{2,3},{3,2},{4,5},{5,4},{6,7},{7,6},{8,9},{9,8},{10,11... | collective-permute-start | bytes 3145736 | tf_op jit(solution)/shard_map/ppermute | solution.py:973
  28.6 9.6 %collective-permute-start.1 = (bf16[2,512,512]{2,1,0:T(8,128)(2,1)S(1)}, bf16[2,512,512]{2,1,0:T(8,128)(2,1)S(1)}, u32[]{:S(2)}, u32[]{:S(2)}) collective-permute-start(bf16[2,512,512]{2,1,0:T(8,128)(2,1)S(1)} %collective-permute-done.refs_3_.refs_4_), channel_id=1, source_target_pairs={{0,2},{1,3},{2,0},{3,1},{4,6},{5,7},{6,4},{7,5},{8,10},{9,11},{10,... | collective-permute-start | bytes 3145736 | tf_op jit(solution)/shard_map/ppermute | solution.py:973
  46.0 9.3 %collective-permute-start.2 = (bf16[8,144,512]{2,1,0:T(8,128)(2,1)S(1)}, bf16[8,144,512]{2,1,0:T(8,128)(2,1)S(1)}, u32[]{:S(2)}, u32[]{:S(2)}) collective-permute-start(bf16[8,144,512]{2,1,0:T(8,128)(2,1)S(1)} %get-tuple-element.140), channel_id=1, source_target_pairs={{0,2},{1,3},{2,0},{3,1},{4,6},{5,7},{6,4},{7,5},{8,10},{9,11},{10,... | collective-permute-start | bytes 3538952 | tf_op jit(solution)/shard_map/ppermute | solution.py:973
  55.2 17.4 %collective-permute-start.5 = (bf16[8,128,512]{2,1,0:T(8,128)(2,1)S(1)}, bf16[8,128,512]{2,1,0:T(8,128)(2,1)S(1)}, u32[]{:S(2)}, u32[]{:S(2)}) collective-permute-start(bf16[8,128,512]{2,1,0:T(8,128)(2,1)S(1)} %get-tuple-element.153), channel_id=1, source_target_pairs={{0,2},{1,3},{2,0},{3,1},{4,6},{5,7},{6,4},{7,5},{8,10},{9,11},{10,... | collective-permute-start | bytes 3145736 | tf_op jit(solution)/shard_map/ppermute | solution.py:973
  55.7 17.7 %collective-permute-start.3 = (bf16[4,144,512]{2,1,0:T(8,128)(2,1)S(1)}, bf16[4,144,512]{2,1,0:T(8,128)(2,1)S(1)}, u32[]{:S(2)}, u32[]{:S(2)}) collective-permute-start(bf16[4,144,512]{2,1,0:T(8,128)(2,1)S(1)} %get-tuple-element.146), channel_id=1, source_target_pairs={{0,4},{1,5},{2,6},{3,7},{4,0},{5,1},{6,2},{7,3},{8,12},{9,13},{10,... | collective-permute-start | bytes 1769480 | tf_op jit(solution)/shard_map/ppermute | solution.py:973
  73.0 16.1 %collective-permute-start.9 = (bf16[4,128,512]{2,1,0:T(8,128)(2,1)S(1)}, bf16[4,128,512]{2,1,0:T(8,128)(2,1)S(1)}, u32[]{:S(2)}, u32[]{:S(2)}) collective-permute-start(bf16[4,128,512]{2,1,0:T(8,128)(2,1)S(1)} %get-tuple-element.178), channel_id=1, source_target_pairs={{0,4},{1,5},{2,6},{3,7},{4,0},{5,1},{6,2},{7,3},{8,12},{9,13},{10,... | collective-permute-start | bytes 1572872 | tf_op jit(solution)/shard_map/ppermute | solution.py:973
  73.5 19.2 %collective-permute-start.7 = (bf16[1,144,512]{2,1,0:T(8,128)(2,1)S(1)}, bf16[1,144,512]{2,1,0:T(8,128)(2,1)S(1)}, u32[]{:S(2)}, u32[]{:S(2)}) collective-permute-start(bf16[1,144,512]{2,1,0:T(8,128)(2,1)S(1)} %get-tuple-element.173), channel_id=1, source_target_pairs={{0,24},{1,25},{2,26},{3,27},{4,28},{5,29},{6,30},{7,31},{8,16},{9,... | collective-permute-start | bytes 442376 | tf_op jit(solution)/shard_map/ppermute | solution.py:973
  84.4 9.3 %collective-permute-start.6 = (bf16[1,144,512]{2,1,0:T(8,128)(2,1)S(1)}, bf16[1,144,512]{2,1,0:T(8,128)(2,1)S(1)}, u32[]{:S(2)}, u32[]{:S(2)}) collective-permute-start(bf16[1,144,512]{2,1,0:T(8,128)(2,1)S(1)} %get-tuple-element.171), channel_id=1, source_target_pairs={{0,16},{1,17},{2,18},{3,19},{4,20},{5,21},{6,22},{7,23},{8,24},{9,... | collective-permute-start | bytes 442376 | tf_op jit(solution)/shard_map/ppermute | solution.py:973
  84.5 10.9 %collective-permute-start.4 = (bf16[1,144,512]{2,1,0:T(8,128)(2,1)S(1)}, bf16[1,144,512]{2,1,0:T(8,128)(2,1)S(1)}, u32[]{:S(2)}, u32[]{:S(2)}) collective-permute-start(bf16[1,144,512]{2,1,0:T(8,128)(2,1)S(1)} %get-tuple-element.152), channel_id=1, source_target_pairs={{0,8},{1,9},{2,10},{3,11},{4,12},{5,13},{6,14},{7,15},{8,0},{9,1},... | collective-permute-start | bytes 442376 | tf_op jit(solution)/shard_map/ppermute | solution.py:973
  89.3 15.0 %collective-permute-start.10 = (bf16[1,128,512]{2,1,0:T(8,128)(2,1)S(1)}, bf16[1,128,512]{2,1,0:T(8,128)(2,1)S(1)}, u32[]{:S(2)}, u32[]{:S(2)}) collective-permute-start(bf16[1,128,512]{2,1,0:T(8,128)(2,1)S(1)} %get-tuple-element.180), channel_id=1, source_target_pairs={{0,8},{1,9},{2,10},{3,11},{4,12},{5,13},{6,14},{7,15},{8,0},{9,1},... | collective-permute-start | bytes 393224 | tf_op jit(solution)/shard_map/ppermute | solution.py:973
  89.8 14.5 %collective-permute-start.11 = (bf16[1,128,512]{2,1,0:T(8,128)(2,1)S(1)}, bf16[1,128,512]{2,1,0:T(8,128)(2,1)S(1)}, u32[]{:S(2)}, u32[]{:S(2)}) collective-permute-start(bf16[1,128,512]{2,1,0:T(8,128)(2,1)S(1)} %get-tuple-element.181), channel_id=1, source_target_pairs={{0,16},{1,17},{2,18},{3,19},{4,20},{5,21},{6,22},{7,23},{8,24},{9,... | collective-permute-start | bytes 393224 | tf_op jit(solution)/shard_map/ppermute | solution.py:973
  92.7 11.6 %collective-permute-start.12 = (bf16[1,128,512]{2,1,0:T(8,128)(2,1)S(1)}, bf16[1,128,512]{2,1,0:T(8,128)(2,1)S(1)}, u32[]{:S(2)}, u32[]{:S(2)}) collective-permute-start(bf16[1,128,512]{2,1,0:T(8,128)(2,1)S(1)} %get-tuple-element.182), channel_id=1, source_target_pairs={{0,24},{1,25},{2,26},{3,27},{4,28},{5,29},{6,30},{7,31},{8,16},{9,... | collective-permute-start | bytes 393224 | tf_op jit(solution)/shard_map/ppermute | solution.py:973
  95.5 8.8 %collective-permute-start.8 = (bf16[1,144,512]{2,1,0:T(8,128)(2,1)S(1)}, bf16[1,144,512]{2,1,0:T(8,128)(2,1)S(1)}, u32[]{:S(2)}, u32[]{:S(2)}) collective-permute-start(bf16[1,144,512]{2,1,0:T(8,128)(2,1)S(1)} %add_convert_fusion.8), channel_id=1, source_target_pairs={{0,1},{1,0},{2,3},{3,2},{4,5},{5,4},{6,7},{7,6},{8,9},{9,8},{10,11... | collective-permute-start | bytes 442376 | tf_op jit(solution)/shard_map/ppermute | solution.py:973
  109.0 8.3 %collective-permute-start.26 = (bf16[1,128,512]{2,1,0:T(8,128)(2,1)S(1)}, bf16[1,128,512]{2,1,0:T(8,128)(2,1)S(1)}, u32[]{:S(2)}, u32[]{:S(2)}) collective-permute-start(bf16[1,128,512]{2,1,0:T(8,128)(2,1)S(1)} %add_convert_fusion.13), channel_id=1, source_target_pairs={{0,24},{1,25},{2,26},{3,27},{4,28},{5,29},{6,30},{7,31},{8,16},{9,... | collective-permute-start | bytes 393224 | tf_op jit(solution)/shard_map/ppermute | solution.py:973
  110.1 17.9 %collective-permute-start.25 = (bf16[1,128,512]{2,1,0:T(8,128)(2,1)S(1)}, bf16[1,128,512]{2,1,0:T(8,128)(2,1)S(1)}, u32[]{:S(2)}, u32[]{:S(2)}) collective-permute-start(bf16[1,128,512]{2,1,0:T(8,128)(2,1)S(1)} %add_convert_fusion.13), channel_id=1, source_target_pairs={{0,16},{1,17},{2,18},{3,19},{4,20},{5,21},{6,22},{7,23},{8,24},{9,... | collective-permute-start | bytes 393224 | tf_op jit(solution)/shard_map/ppermute | solution.py:973
  111.0 17.1 %collective-permute-start.24 = (bf16[1,128,512]{2,1,0:T(8,128)(2,1)S(1)}, bf16[1,128,512]{2,1,0:T(8,128)(2,1)S(1)}, u32[]{:S(2)}, u32[]{:S(2)}) collective-permute-start(bf16[1,128,512]{2,1,0:T(8,128)(2,1)S(1)} %add_convert_fusion.13), channel_id=1, source_target_pairs={{0,8},{1,9},{2,10},{3,11},{4,12},{5,13},{6,14},{7,15},{8,0},{9,1},... | collective-permute-start | bytes 393224 | tf_op jit(solution)/shard_map/ppermute | solution.py:973
  113.7 18.2 %collective-permute-start.14 = (bf16[4,16,2688]{2,1,0:T(8,128)(2,1)S(1)}, bf16[4,16,2688]{2,1,0:T(8,128)(2,1)S(1)}, u32[]{:S(2)}, u32[]{:S(2)}) collective-permute-start(bf16[4,16,2688]{2,1,0:T(8,128)(2,1)S(1)} %get-tuple-element.200), channel_id=1, source_target_pairs={{0,1},{1,0},{2,3},{3,2},{4,5},{5,4},{6,7},{7,6},{8,9},{9,8},{10,11... | collective-permute-start | bytes 1032200 | tf_op jit(solution)/shard_map/ppermute | solution.py:973
  114.3 17.6 %collective-permute-start.15 = (bf16[4,16,2688]{2,1,0:T(8,128)(2,1)S(1)}, bf16[4,16,2688]{2,1,0:T(8,128)(2,1)S(1)}, u32[]{:S(2)}, u32[]{:S(2)}) collective-permute-start(bf16[4,16,2688]{2,1,0:T(8,128)(2,1)S(1)} %get-tuple-element.201), channel_id=1, source_target_pairs={{0,4},{1,5},{2,6},{3,7},{4,0},{5,1},{6,2},{7,3},{8,12},{9,13},{10,... | collective-permute-start | bytes 1032200 | tf_op jit(solution)/shard_map/ppermute | solution.py:973
  117.3 14.7 %collective-permute-start.16 = (bf16[4,16,2688]{2,1,0:T(8,128)(2,1)S(1)}, bf16[4,16,2688]{2,1,0:T(8,128)(2,1)S(1)}, u32[]{:S(2)}, u32[]{:S(2)}) collective-permute-start(bf16[4,16,2688]{2,1,0:T(8,128)(2,1)S(1)} %get-tuple-element.202), channel_id=1, source_target_pairs={{0,5},{1,4},{2,7},{3,6},{4,1},{5,0},{6,3},{7,2},{8,13},{9,12},{10,... | collective-permute-start | bytes 1032200 | tf_op jit(solution)/shard_map/ppermute | solution.py:973
  132.1 7.2 %collective-permute-start.19 = (bf16[1,16,2688]{2,1,0:T(8,128)(2,1)S(1)}, bf16[1,16,2688]{2,1,0:T(8,128)(2,1)S(1)}, u32[]{:S(2)}, u32[]{:S(2)}) collective-permute-start(bf16[1,16,2688]{2,1,0:T(8,128)(2,1)S(1)} %get-tuple-element.212), channel_id=1, source_target_pairs={{0,24},{1,25},{2,26},{3,27},{4,28},{5,29},{6,30},{7,31},{8,16},{9,... | collective-permute-start | bytes 258056 | tf_op jit(solution)/shard_map/ppermute | solution.py:973
  133.2 8.9 %collective-permute-start.18 = (bf16[1,16,2688]{2,1,0:T(8,128)(2,1)S(1)}, bf16[1,16,2688]{2,1,0:T(8,128)(2,1)S(1)}, u32[]{:S(2)}, u32[]{:S(2)}) collective-permute-start(bf16[1,16,2688]{2,1,0:T(8,128)(2,1)S(1)} %get-tuple-element.210), channel_id=1, source_target_pairs={{0,16},{1,17},{2,18},{3,19},{4,20},{5,21},{6,22},{7,23},{8,24},{9,... | collective-permute-start | bytes 258056 | tf_op jit(solution)/shard_map/ppermute | solution.py:973
  135.3 6.9 %collective-permute-start.17 = (bf16[1,16,2688]{2,1,0:T(8,128)(2,1)S(1)}, bf16[1,16,2688]{2,1,0:T(8,128)(2,1)S(1)}, u32[]{:S(2)}, u32[]{:S(2)}) collective-permute-start(bf16[1,16,2688]{2,1,0:T(8,128)(2,1)S(1)} %get-tuple-element.208), channel_id=1, source_target_pairs={{0,8},{1,9},{2,10},{3,11},{4,12},{5,13},{6,14},{7,15},{8,0},{9,1},... | collective-permute-start | bytes 258056 | tf_op jit(solution)/shard_map/ppermute | solution.py:973
  136.6 18.3 %collective-permute-start.27 = (bf16[4,128,512]{2,1,0:T(8,128)(2,1)S(1)}, bf16[4,128,512]{2,1,0:T(8,128)(2,1)S(1)}, u32[]{:S(2)}, u32[]{:S(2)}) collective-permute-start(bf16[4,128,512]{2,1,0:T(8,128)(2,1)S(1)} %pad_maximum_fusion.refs_1_), channel_id=1, source_target_pairs={{0,4},{1,5},{2,6},{3,7},{4,0},{5,1},{6,2},{7,3},{8,12},{9,13},{10,... | collective-permute-start | bytes 1572872 | tf_op jit(solution)/shard_map/ppermute | solution.py:973
  142.3 7.4 %collective-permute-start.22 = (bf16[1,16,2688]{2,1,0:T(8,128)(2,1)S(1)}, bf16[1,16,2688]{2,1,0:T(8,128)(2,1)S(1)}, u32[]{:S(2)}, u32[]{:S(2)}) collective-permute-start(bf16[1,16,2688]{2,1,0:T(8,128)(2,1)S(1)} %add_convert_fusion.18), channel_id=1, source_target_pairs={{0,24},{1,25},{2,26},{3,27},{4,28},{5,29},{6,30},{7,31},{8,16},{9,... | collective-permute-start | bytes 258056 | tf_op jit(solution)/shard_map/ppermute | solution.py:973
  143.6 7.7 %collective-permute-start.21 = (bf16[1,16,2688]{2,1,0:T(8,128)(2,1)S(1)}, bf16[1,16,2688]{2,1,0:T(8,128)(2,1)S(1)}, u32[]{:S(2)}, u32[]{:S(2)}) collective-permute-start(bf16[1,16,2688]{2,1,0:T(8,128)(2,1)S(1)} %add_convert_fusion.18), channel_id=1, source_target_pairs={{0,16},{1,17},{2,18},{3,19},{4,20},{5,21},{6,22},{7,23},{8,24},{9,... | collective-permute-start | bytes 258056 | tf_op jit(solution)/shard_map/ppermute | solution.py:973
  143.6 7.7 %collective-permute-start.20 = (bf16[1,16,2688]{2,1,0:T(8,128)(2,1)S(1)}, bf16[1,16,2688]{2,1,0:T(8,128)(2,1)S(1)}, u32[]{:S(2)}, u32[]{:S(2)}) collective-permute-start(bf16[1,16,2688]{2,1,0:T(8,128)(2,1)S(1)} %add_convert_fusion.18), channel_id=1, source_target_pairs={{0,8},{1,9},{2,10},{3,11},{4,12},{5,13},{6,14},{7,15},{8,0},{9,1},... | collective-permute-start | bytes 258056 | tf_op jit(solution)/shard_map/ppermute | solution.py:973
  146.7 16.5 %collective-permute-start.28 = (bf16[4,128,512]{2,1,0:T(8,128)(2,1)S(1)}, bf16[4,128,512]{2,1,0:T(8,128)(2,1)S(1)}, u32[]{:S(2)}, u32[]{:S(2)}) collective-permute-start(bf16[4,128,512]{2,1,0:T(8,128)(2,1)S(1)} %pad_maximum_fusion.refs_1_), channel_id=1, source_target_pairs={{0,2},{1,3},{2,0},{3,1},{4,6},{5,7},{6,4},{7,5},{8,10},{9,11},{10,... | collective-permute-start | bytes 1572872 | tf_op jit(solution)/shard_map/ppermute | solution.py:973
  151.3 15.8 %collective-permute-start.23 = (bf16[4,16,2688]{2,1,0:T(8,128)(2,1)S(1)}, bf16[4,16,2688]{2,1,0:T(8,128)(2,1)S(1)}, u32[]{:S(2)}, u32[]{:S(2)}) collective-permute-start(bf16[4,16,2688]{2,1,0:T(8,128)(2,1)S(1)} %pad_maximum_fusion.1.refs_1_), channel_id=1, source_target_pairs={{0,1},{1,0},{2,3},{3,2},{4,5},{5,4},{6,7},{7,6},{8,9},{9,8},{10,11... | collective-permute-start | bytes 1032200 | tf_op jit(solution)/shard_map/ppermute | solution.py:973
  152.3 14.9 %collective-permute-start.30 = (bf16[4,16,2688]{2,1,0:T(8,128)(2,1)S(1)}, bf16[4,16,2688]{2,1,0:T(8,128)(2,1)S(1)}, u32[]{:S(2)}, u32[]{:S(2)}) collective-permute-start(bf16[4,16,2688]{2,1,0:T(8,128)(2,1)S(1)} %pad_maximum_fusion.1.refs_1_), channel_id=1, source_target_pairs={{0,4},{1,5},{2,6},{3,7},{4,0},{5,1},{6,2},{7,3},{8,12},{9,13},{10,... | collective-permute-start | bytes 1032200 | tf_op jit(solution)/shard_map/ppermute | solution.py:973
  152.6 16.4 %collective-permute-start.31 = (bf16[4,16,2688]{2,1,0:T(8,128)(2,1)S(1)}, bf16[4,16,2688]{2,1,0:T(8,128)(2,1)S(1)}, u32[]{:S(2)}, u32[]{:S(2)}) collective-permute-start(bf16[4,16,2688]{2,1,0:T(8,128)(2,1)S(1)} %pad_maximum_fusion.1.refs_1_), channel_id=1, source_target_pairs={{0,5},{1,4},{2,7},{3,6},{4,1},{5,0},{6,3},{7,2},{8,13},{9,12},{10,... | collective-permute-start | bytes 1032200 | tf_op jit(solution)/shard_map/ppermute | solution.py:973
  154.9 8.9 %collective-permute-start.29 = (bf16[4,128,512]{2,1,0:T(8,128)(2,1)S(1)}, bf16[4,128,512]{2,1,0:T(8,128)(2,1)S(1)}, u32[]{:S(2)}, u32[]{:S(2)}) collective-permute-start(bf16[4,128,512]{2,1,0:T(8,128)(2,1)S(1)} %collective-permute-done.27.refs_2_), channel_id=1, source_target_pairs={{0,2},{1,3},{2,0},{3,1},{4,6},{5,7},{6,4},{7,5},{8,10},{9,11},{10,... | collective-permute-start | bytes 1572872 | tf_op jit(solution)/shard_map/ppermute | solution.py:973
  163.2 6.3 %collective-permute-start.32 = (bf16[4,16,2688]{2,1,0:T(8,128)(2,1)S(1)}, bf16[4,16,2688]{2,1,0:T(8,128)(2,1)S(1)}, u32[]{:S(2)}, u32[]{:S(2)}) collective-permute-start(bf16[4,16,2688]{2,1,0:T(8,128)(2,1)S(1)} %pad_maximum_fusion.1.refs_1_), channel_id=1, source_target_pairs={{0,2},{1,3},{2,0},{3,1},{4,6},{5,7},{6,4},{7,5},{8,10},{9,11},{10,... | collective-permute-start | bytes 1032200 | tf_op jit(solution)/shard_map/ppermute | solution.py:973
  (20 other events, 167.6 us)
